TPU v7x, 32 devices: a whole 2x2x4 slice. The times are simulated.
32 devices in a mesh: fsdp: 8 (over z, core), tp: 4 (over y, x).
Axes of the slice: x: 2, y: 2, z: 4, core: 2. Of those that a mesh axis runs over, the one named last changes fastest.
Arguments:
- momentum: float32 [1024, 16384], P('fsdp', 'tp'), may hold values from -6 to 6
- grad: bfloat16 [1024, 16384], P('fsdp', 'tp'), may hold values from -6 to 6
- q_stored: bfloat16 [256, 16384], P('fsdp', 'tp'), may hold values from -6 to 6
- perm: int32 [8], replicated, may hold values from 0 to 7, each once
Outputs:
- momentum_next: float32 [1024, 16384], P('fsdp', 'tp')
- q_next: float32 [16384, 256], P('tp')
- update: bfloat16 [1024, 16384], P('fsdp', 'tp')
Inputs may be any that keep to these rules, and one draw needn't show every extreme that they name: perm names every rank block exactly once.
All inputs are finite; a program needn't handle non-finite values.
Results may differ from a plain program's by a relative error of at most 0.0008.
Values may be sent and summed in bfloat16 or wider, within the bound.
No kernel may reach another device: no remote copies, remote signals or barrier semaphores. Data moves between devices by JAX's collectives and lax.ppermute only.
A program may use at most 64 MiB of HBM per device.

v0:
```python
import math

import jax
import jax.numpy as jnp
from jax import lax
from jax.sharding import PartitionSpec as P

EPSILON = 1e-06
KEEP_SHARE = 0.5
HIGH = lax.Precision.HIGHEST


def gram_local(matrix):
    return lax.dot_general(matrix, matrix, (((0,), (0,)), ((), ())), precision=HIGH)


def make_orthonormal(projected, gram_total):
    factor_low = jnp.linalg.cholesky(gram_total)
    return jax.scipy.linalg.solve_triangular(factor_low, projected.T, lower=True).T


def on_device(momentum, grad, q_stored, perm):
    combined = momentum + grad.astype(jnp.float32)
    block_rows = q_stored.shape[0]
    num_blocks = lax.axis_size("fsdp")
    rank_total = block_rows * num_blocks
    row_total = momentum.shape[0] * num_blocks
    stored_order = lax.dot_general(
        combined,
        lax.all_gather(q_stored, "fsdp", axis=0, tiled=True).astype(jnp.float32),
        (((1,), (1,)), ((), ())),
        precision=HIGH,
    )
    blocks = jnp.arange(num_blocks, dtype=jnp.int32)
    inverse = jnp.sum(jnp.where(perm[:, None] == blocks[None, :], blocks[:, None], 0), axis=0)
    row_ids = jnp.arange(rank_total, dtype=jnp.int32)
    order_index = inverse[row_ids // block_rows] * block_rows + row_ids % block_rows
    partial_proj = jnp.take(stored_order, order_index, axis=1)
    projected = lax.psum(partial_proj, "tp")
    gram_total = lax.psum(gram_local(projected), "fsdp")
    orthonormal = make_orthonormal(projected, gram_total)
    right_share = lax.psum_scatter(
        lax.dot_general(combined, orthonormal, (((0,), (0,)), ((), ())), precision=HIGH),
        "fsdp",
        scatter_dimension=0,
        tiled=True,
    )
    right = lax.all_gather(right_share, "fsdp", axis=0, tiled=True)
    square_sums = lax.psum(jnp.sum(right * right, axis=0), "tp")
    col_total = combined.shape[1] * lax.axis_size("tp")
    scale = lax.rsqrt(square_sums / col_total + EPSILON)
    q_next = right * scale[None, :]
    outer = lax.dot_general(orthonormal, right, (((1,), (1,)), ((), ())), precision=HIGH)
    momentum_next = combined - KEEP_SHARE * outer
    direction = lax.dot_general(orthonormal, q_next, (((1,), (1,)), ((), ())), precision=HIGH)
    update = (direction * math.sqrt(row_total / rank_total)).astype(jnp.bfloat16)
    return (momentum_next, q_next, update)


def solution(mesh):
    return jax.shard_map(
        on_device,
        mesh=mesh,
        in_specs=(P("fsdp", "tp"), P("fsdp", "tp"), P("fsdp", "tp"), P()),
        out_specs=(P("fsdp", "tp"), P("tp", None), P("fsdp", "tp")),
        check_vma=False,
    )
```

profile of v0, /device:TPU:0, one launch (start us, length us, event | category | flops | bytes accessed | tf_op | source)
XLA Modules:
  0.0 352.4 jit_solution(12799127491824650412)
XLA Ops:
  7.2 0.0 all-gather.3.cloned.1.call-start
  7.2 0.7 all-gather.3.cloned.1.call-update
  7.9 0.0 all-reduce.4.cloned.1.call-start
  8.0 0.7 select_reduce_fusion.2
  8.7 0.7 fusion.18
  9.4 4.3 %compare_select_fusion.2 = s32[256,1]{0,1:T(1,128)S(1)} fusion(s32[]{:T(128)} %bitcast.1, s32[]{:T(128)} %bitcast.2, s32[]{:T(128)} %bitcast.3, s32[]{:T(128)} %bitcast.4, s32[]{:T(128)} %bitcast.5, s32[]{:T(128)} %bitcast.7, s32[]{:T(128)} %bitcast.6), kind=kLoop, calls=%fused_computation.40 | loop fusion | flops 5888 | bytes 1052 | tf_op jit(solution)/shard_map/gather | solution.py:37
  13.7 0.7 compare_and_fusion
  14.4 27.0 %all-gather.3.cloned.1.call-done = bf16[256,4096]{1,0:T(8,128)(2,1)} async-done(((bf16[32,4096]{1,0:T(8,128)(2,1)}), bf16[256,4096]{1,0:T(8,128)(2,1)}) %all-gather.3.cloned.1.call-update) | async-done | bytes 2097168 | tf_op jit(solution)/shard_map/all_gather | solution.py:30
  41.4 4.4 %fusion.3 = f32[128,256]{0,1:T(8,128)S(1)} fusion(bf16[256,4096]{1,0:T(8,128)(2,1)} %all-gather.3.cloned.1.call-done, f32[128,4096]{1,0:T(8,128)} %param.4, bf16[128,4096]{1,0:T(8,128)(2,1)} %param.5), kind=kOutput, calls=%fused_computation.13 | convolution fusion | flops 1611661312 | bytes 5373952 | tf_op jit(solution)/shard_map/dot_general | solution.py:28
  45.9 0.7 gather_fusion
  46.6 0.8 select_bitcast_fusion
  47.4 0.0 all-reduce.4.cloned.1.call-update
  47.4 0.0 all-reduce.6.cloned.1.call-start
  47.4 41.6 %all-reduce.4.cloned.1.call-done = f32[128,256]{0,1:T(8,128)} async-done(((f32[128,256]{0,1:T(8,128)}), f32[128,256]{0,1:T(8,128)}) %all-reduce.4.cloned.1.call-update) | async-done | bytes 131088 | tf_op jit(solution)/shard_map/psum | solution.py:39
  89.0 2.1 fusion.19
  91.1 0.0 all-reduce.6.cloned.1.call-update
  91.1 0.2 reduce-scatter.2.cloned.1.call-start
  91.4 55.6 %all-reduce.6.cloned.1.call-done = f32[256,256]{0,1:T(8,128)} async-done(((f32[256,256]{0,1:T(8,128)}), f32[256,256]{0,1:T(8,128)}) %all-reduce.6.cloned.1.call-update) | async-done | bytes 262160 | tf_op jit(solution)/shard_map/psum | solution.py:40
  147.0 1.1 copy.15
  148.1 0.0 copy-start.1
  148.1 0.0 copy-start.3
  148.1 1.1 fusion.4
  149.3 0.0 copy-start.5
  149.3 0.7 copy-done.5
  150.0 11.7 %cholesky.50 = f32[128,128]{1,0:T(8,128)S(1)} custom-call(f32[128,128]{1,0:T(8,128)S(1)} %cholesky.118), custom_call_target="Cholesky" | custom-call | tf_op jit(solution)/shard_map/jit(cholesky)/cholesky | solution.py:18
  161.7 9.8 %custom-call.15 = f32[1,128,128]{1,2,0:T(8,128)S(1)} custom-call(f32[1,128,128]{2,1,0:T(8,128)S(1)} %get-tuple-element.26), custom_call_target="InvertDiagBlocksLowerTriangular" | custom-call | tf_op jit(solution)/shard_map/jit(cholesky)/cholesky | solution.py:18
  171.6 1.0 constant_dynamic-update-slice_fusion.1
  172.6 1.1 convolution_subtract_fusion.1
  173.7 11.7 %cholesky.105 = f32[128,128]{1,0:T(8,128)S(1)} custom-call(f32[128,128]{1,0:T(8,128)S(1)} %convolution_subtract_fusion.1), custom_call_target="Cholesky" | custom-call | tf_op jit(solution)/shard_map/jit(cholesky)/cholesky | solution.py:18
  185.5 0.0 copy-start.4
  185.5 0.7 compare_reduce_fusion.1
  187.4 0.0 copy-done.4
  187.5 1.0 select_select_fusion
  188.4 0.1 triangular_solve.63
  188.5 5.5 %while.1 = (s32[]{:T(128)}, f32[256,256]{1,0:T(8,128)S(1)}, s32[2,2]{1,0:T(2,128)S(1)}, f32[2,128,128]{2,1,0:T(8,128)}, s32[]{:T(128)}) while((s32[]{:T(128)}, f32[256,256]{1,0:T(8,128)S(1)}, s32[2,2]{1,0:T(2,128)S(1)}, f32[2,128,128]{2,1,0:T(8,128)}, s32[]{:T(128)}) %tuple.35), condition=%wide.while_cond, body=%wide.while_body.sunk | while | flops 2 | bytes 132205 | solution.py:19
  188.7 0.6 fusion.30
  189.3 2.1 bitcast_dynamic-update-slice_fusion.2
  191.4 0.6 fusion.30
  192.0 2.1 bitcast_dynamic-update-slice_fusion.2
  194.0 21.1 %custom-call.16 = f32[2,128,128]{1,2,0:T(8,128)} custom-call(f32[2,128,128]{2,1,0:T(8,128)} %get-tuple-element.10), custom_call_target="InvertDiagBlocksLowerTriangular" | custom-call | tf_op jit(solution)/shard_map/jit(_solve_triangular)/triangular_solve | solution.py:19
  215.1 1.2 fusion.7
  216.3 1.0 convolution_subtract_fusion
  217.3 1.1 fusion.6
  218.5 0.0 copy-done.1
  218.5 0.0 copy-done.3
  218.5 5.0 %fusion.2 = f32[4096,256]{1,0:T(8,128)} fusion(f32[128,4096]{1,0:T(8,128)S(1)} %copy-done.1, bf16[128,4096]{1,0:T(8,128)(2,1)S(1)} %copy-done.3, f32[128,128]{1,0:T(8,128)S(1)} %fusion.6, f32[128,128]{1,0:T(8,128)S(1)} %fusion.7), kind=kOutput, calls=%fused_computation.12 | convolution fusion | flops 1611694080 | bytes 7471104 | tf_op jit(solution)/shard_map/dot_general | solution.py:43
  223.5 0.0 reduce-scatter.2.cloned.1.call-update
  223.6 0.0 all-gather.5.cloned.1.call-start
  223.6 49.1 %reduce-scatter.2.cloned.1.call-done = f32[512,256]{1,0:T(8,128)} async-done(((f32[4096,256]{1,0:T(8,128)}), f32[512,256]{1,0:T(8,128)}) %reduce-scatter.2.cloned.1.call-update) | async-done | bytes 524304 | tf_op jit(solution)/shard_map/reduce_scatter | solution.py:42
  272.7 0.0 all-gather.5.cloned.1.call-update
  272.7 46.7 %all-gather.5.cloned.1.call-done = f32[4096,256]{1,0:T(8,128)} async-done(((f32[512,256]{1,0:T(8,128)}), f32[4096,256]{1,0:T(8,128)}) %all-gather.5.cloned.1.call-update) | async-done | bytes 4194320 | tf_op jit(solution)/shard_map/all_gather | solution.py:48
  319.5 2.7 multiply_reduce_fusion
  322.2 9.8 %psum.23 = f32[256]{0:T(256)S(1)} all-reduce(f32[256]{0:T(256)S(1)} %multiply_reduce_fusion), channel_id=1, replica_groups=mesh['fsdp'=8,'tp'=4] {'tp'}, use_global_device_ids=true, to_apply=%region_9.10 | all-reduce | flops 256 | bytes 2048 | tf_op jit(solution)/shard_map/psum | solution.py:49
  332.1 2.5 broadcast_multiply_fusion
  334.5 0.0 copy-start.2
  334.5 0.0 copy-start
  334.5 5.5 %fusion.1 = bf16[128,4096]{1,0:T(8,128)(2,1)} fusion(f32[4096,256]{1,0:T(8,128)S(1)} %broadcast_multiply_fusion, f32[128,128]{1,0:T(8,128)S(1)} %fusion.6, f32[128,128]{1,0:T(8,128)S(1)} %fusion.7), kind=kOutput, calls=%fused_computation.6 | convolution fusion | flops 1611694080 | bytes 5373952 | tf_op jit(solution)/shard_map/dot_general | solution.py:55
  340.0 0.0 copy-done.2
  340.0 0.0 copy-done
  340.0 5.8 %fusion = f32[128,4096]{1,0:T(8,128)} fusion(f32[4096,256]{1,0:T(8,128)S(1)} %copy-done, f32[128,4096]{1,0:T(8,128)S(1)} %copy-done.1, bf16[128,4096]{1,0:T(8,128)(2,1)S(1)} %copy-done.3, f32[128,128]{1,0:T(8,128)S(1)} %fusion.6, f32[128,128]{1,0:T(8,128)S(1)} %fusion.7), kind=kOutput, calls=%fused_computation.5 | convolution fusion | flops 1612742656 | bytes 9568256 | tf_op jit(solution)/shard_map/dot_general | solution.py:53
  (12 shorter events, 0.2 us)
Async XLA Ops:
  7.2 34.3 %all-gather.3.cloned.1.call-start = ((), (), s32[]{:S(2)}) async-start(), calls=%async_computation.1 | async-start | bytes 2359296 | tf_op jit(solution)/shard_map/all_gather | solution.py:30
  7.9 81.1 %all-reduce.4.cloned.1.call-start = ((), (), s32[]{:S(2)}) async-start(), calls=%async_computation.2 | async-start | bytes 262144 | tf_op jit(solution)/shard_map/psum | solution.py:39
  47.4 99.6 %all-reduce.6.cloned.1.call-start = ((), (), s32[]{:S(2)}) async-start(), calls=%async_computation.3 | async-start | bytes 524288 | tf_op jit(solution)/shard_map/psum | solution.py:40
  91.1 181.6 %reduce-scatter.2.cloned.1.call-start = ((), (), s32[]{:S(2)}) async-start(), calls=%async_computation.4 | async-start | bytes 4718592 | tf_op jit(solution)/shard_map/reduce_scatter | solution.py:42
  148.1 70.4 %copy-start.1 = (f32[128,4096]{1,0:T(8,128)S(1)}, f32[128,4096]{1,0:T(8,128)}, u32[]{:S(2)}) copy-start(f32[128,4096]{1,0:T(8,128)} %param.4) | copy-start | bytes 6291460
  148.1 70.4 %copy-start.3 = (bf16[128,4096]{1,0:T(8,128)(2,1)S(1)}, bf16[128,4096]{1,0:T(8,128)(2,1)}, u32[]{:S(2)}) copy-start(bf16[128,4096]{1,0:T(8,128)(2,1)} %param.5) | copy-start | bytes 3145732
  149.3 0.7 copy-start.5
  185.5 2.0 copy-start.4
  223.6 95.9 %all-gather.5.cloned.1.call-start = ((), (), s32[]{:S(2)}) async-start(), calls=%async_computation.5 | async-start | bytes 4718592 | tf_op jit(solution)/shard_map/all_gather | solution.py:48
  334.5 5.5 %copy-start.2 = (f32[4096,256]{1,0:T(8,128)}, f32[4096,256]{1,0:T(8,128)S(1)}, u32[]{:S(2)}) copy-start(f32[4096,256]{1,0:T(8,128)S(1)} %broadcast_multiply_fusion) | copy-start | bytes 12582916
  334.5 5.5 %copy-start = (f32[4096,256]{1,0:T(8,128)S(1)}, f32[4096,256]{1,0:T(8,128)}, u32[]{:S(2)}) copy-start(f32[4096,256]{1,0:T(8,128)} %all-gather.5.cloned.1.call-done) | copy-start | bytes 12582916
Sparse Core Ops, SparseCore 0:
  9.6 31.7 all-gather.2
  47.5 41.4 all-reduce.3
  92.0 54.9 all-reduce.5
  223.7 48.9 reduce-scatter.1
  274.1 45.2 all-gather.4
where the time goes:
time: 353 us; the launch traced here: 352 us
  waiting for transfers between devices  221 us (63%)
  other arithmetic  69 us (20%)
  matrix products  28.3 us (8%)
  between operations  15.2 us (4%)
  blocking collectives  9.84 us (3%)
  local copies, waits for them, and re-layouts  8.61 us (2%)
    psum x1, waiting for transfers between devices, on_device(): gram_total = lax.psum(gram_local(projected), 'fsdp')  55.6 us
    reduce_scatter x1, waiting for transfers between devices, on_device(): lax.psum_scatter(lax.dot_general(combined, orthonormal, (((0,), (0,)), ((...  49.1 us
    all_gather x1, waiting for transfers between devices, on_device(): right = lax.all_gather(right_share, 'fsdp', axis=0, tiled=True)  46.7 us
    psum x1, waiting for transfers between devices, on_device(): projected = lax.psum(partial_proj, 'tp')  41.6 us
    another operation x6, other arithmetic, make_orthonormal(): factor_low = jnp.linalg.cholesky(gram_total)  34 us
    all_gather x1, waiting for transfers between devices, on_device(): lax.all_gather(q_stored, 'fsdp', axis=0, tiled=True).astype(jnp.float32)  27 us
    another operation x3, other arithmetic, make_orthonormal(): jax.scipy.linalg.solve_triangular(factor_low, projected.T, lower=True)  22.1 us
    psum x1, blocking collectives, on_device(): square_sums = lax.psum(jnp.sum(right * right, axis=0), 'tp')  9.84 us
  transfers between devices with their start and end apart: 5, of which 5 were waited for; matrix products, arithmetic and copies ran while one was open for 2% of the time, Pallas kernels for 0%

commit v1 on v0

v1 whole, which is shorter than its diff:
```python
import math

import jax
import jax.numpy as jnp
from jax import lax
from jax.experimental import pallas as pl
from jax.experimental.pallas import tpu as pltpu
from jax.sharding import PartitionSpec as P

EPSILON = 1e-06
KEEP_SHARE = 0.5
HIGH = lax.Precision.HIGHEST
PANEL = 64
TILE = 8


def split_two(x):
    high = lax.reduce_precision(x, 8, 7)
    return high.astype(jnp.bfloat16), (x - high).astype(jnp.bfloat16)


def butterfly_sum(x, axis):
    n = lax.axis_size(axis)
    step = 1
    while step < n:
        x = x + lax.ppermute(x, axis, [(i, i ^ step) for i in range(n)])
        step *= 2
    return x


def gather_list(x, axis):
    n = lax.axis_size(axis)
    return [x] + [lax.ppermute(x, axis, [(i, i ^ k) for i in range(n)]) for k in range(1, n)]


def spread(row):
    return jnp.broadcast_to(row, (TILE, 2 * PANEL))


def panel_inverse(block):
    rows = lax.broadcasted_iota(jnp.int32, (PANEL, PANEL), 0)
    cols = lax.broadcasted_iota(jnp.int32, (PANEL, PANEL), 1)
    both = jnp.concatenate([block, (rows == cols).astype(jnp.float32)], axis=1)
    count = PANEL // TILE
    tiles = [both[TILE * i : TILE * (i + 1)] for i in range(count)]
    sub = lax.broadcasted_iota(jnp.int32, (TILE, 2 * PANEL), 0)
    done = []
    for k in range(count):
        columns = [
            [spread(tiles[i][:, TILE * k + j : TILE * k + j + 1]) for j in range(TILE)] for i in range(k, count)
        ]
        own, body = columns[0], tiles[k]
        final = jnp.zeros_like(body)
        for j in range(TILE):
            here = sub == j
            pivot = spread(own[j][j : j + 1])
            inverse = 1.0 / pivot
            final = jnp.where(here, body * lax.rsqrt(pivot), final)
            reduced = spread(body[j : j + 1]) * inverse
            body = jnp.where(here, reduced, body - own[j] * reduced)
            for other in range(j + 1, TILE):
                ratio = spread(own[other][j : j + 1]) * inverse
                own[other] = jnp.where(here, ratio, own[other] - own[j] * ratio)
        done.append(final)
        for i in range(k + 1, count):
            tile = tiles[i]
            for j in range(TILE):
                tile = tile - columns[i - k][j] * spread(body[j : j + 1])
            tiles[i] = tile
    return jnp.concatenate(done, axis=0)[:, PANEL:]


def factor_kernel(gram_ref, out_ref, work):
    rank = gram_ref.shape[0]
    work[:, :rank] = gram_ref[...]
    rows = lax.broadcasted_iota(jnp.int32, (rank, rank), 0)
    cols = lax.broadcasted_iota(jnp.int32, (rank, rank), 1)
    work[:, rank:] = (rows == cols).astype(jnp.float32)
    for start in range(0, rank, PANEL):
        end = start + PANEL
        inverse = panel_inverse(work[start:end, start:end])
        scaled = jnp.dot(inverse, work[start:end, :], precision=HIGH, preferred_element_type=jnp.float32)
        out_ref[start:end, :] = scaled[:, rank:]
        if end < rank:
            low = end // 128 * 128
            change = lax.dot_general(
                scaled[:, low:rank],
                scaled,
                (((0,), (0,)), ((), ())),
                precision=HIGH,
                preferred_element_type=jnp.float32,
            )
            work[end:, :] = work[end:, :] - change[end - low :, :]


def factor_inverse(gram):
    rank = gram.shape[0]
    return pl.pallas_call(
        factor_kernel,
        out_shape=jax.ShapeDtypeStruct((rank, rank), jnp.float32),
        scratch_shapes=[pltpu.VMEM((rank, 2 * rank), jnp.float32)],
        compiler_params=pltpu.CompilerParams(vmem_limit_bytes=32 * 1024 * 1024),
        cost_estimate=pl.CostEstimate(flops=6 * 2 * rank**3, bytes_accessed=2 * rank * rank * 4, transcendentals=rank),
    )(gram)


def finish_kernel(momentum_ref, grad_ref, right_ref, high_ref, low_ref, scale_ref, next_ref, basis_ref, update_ref):
    right = right_ref[...]
    basis_ref[...] = right * scale_ref[...]
    right_high = right.astype(jnp.bfloat16)
    right_low = (right - right_high.astype(jnp.float32)).astype(jnp.bfloat16)

    def times(a, b):
        return lax.dot_general(a, b, (((1,), (1,)), ((), ())), preferred_element_type=jnp.float32)

    high = high_ref[...]
    both = times(high, right_high) + (times(low_ref[...], right_high) + times(high, right_low))
    rows = momentum_ref.shape[0]
    next_ref[...] = momentum_ref[...] + grad_ref[...].astype(jnp.float32) + both[:rows]
    update_ref[...] = both[rows:].astype(jnp.bfloat16)


def finish(momentum, grad, right, factors, scale):
    rows, cols = momentum.shape
    rank = right.shape[1]
    block = min(512, cols)
    high, low = split_two(factors)
    wide = lambda: pl.BlockSpec((rows, block), lambda i: (0, i))
    tall = lambda: pl.BlockSpec((block, rank), lambda i: (i, 0))
    whole = lambda a: pl.BlockSpec(a.shape, lambda i: (0, 0))
    return pl.pallas_call(
        finish_kernel,
        grid=(cols // block,),
        in_specs=[wide(), wide(), tall(), whole(high), whole(low), whole(scale)],
        out_specs=[wide(), tall(), wide()],
        out_shape=[
            jax.ShapeDtypeStruct((rows, cols), jnp.float32),
            jax.ShapeDtypeStruct((cols, rank), jnp.float32),
            jax.ShapeDtypeStruct((rows, cols), jnp.bfloat16),
        ],
        compiler_params=pltpu.CompilerParams(vmem_limit_bytes=32 * 1024 * 1024),
        cost_estimate=pl.CostEstimate(
            flops=6 * 2 * rows * cols * rank, bytes_accessed=rows * cols * 12 + cols * rank * 8, transcendentals=0
        ),
    )(momentum, grad, right, high, low, scale)


def on_device(momentum, grad, q_stored, perm):
    block_rows = q_stored.shape[0]
    num_blocks = lax.axis_size("fsdp")
    num_cols = lax.axis_size("tp")
    rank_total = block_rows * num_blocks
    row_total = momentum.shape[0] * num_blocks
    col_total = momentum.shape[1] * num_cols
    rows = momentum.shape[0]

    combined = momentum + grad.astype(jnp.float32)
    comb_high, comb_low = split_two(combined)
    basis = lax.all_gather(q_stored, "fsdp", axis=0, tiled=True)
    stacked = lax.dot_general(
        jnp.concatenate([comb_high, comb_low], axis=0),
        basis,
        (((1,), (1,)), ((), ())),
        preferred_element_type=jnp.float32,
    )
    stored_order = stacked[:rows] + stacked[rows:]
    blocks = jnp.arange(num_blocks, dtype=jnp.int32)
    inverse = jnp.sum(jnp.where(perm[:, None] == blocks[None, :], blocks[:, None], 0), axis=0)
    row_ids = jnp.arange(rank_total, dtype=jnp.int32)
    order_index = inverse[row_ids // block_rows] * block_rows + row_ids % block_rows
    projected = butterfly_sum(jnp.take(stored_order, order_index, axis=1), "tp")

    mixed = lax.dot_general(combined, projected, (((0,), (0,)), ((), ())), precision=HIGH)
    mixed_share = lax.psum_scatter(mixed, "fsdp", scatter_dimension=0, tiled=True)

    gram_part = lax.dot_general(projected, projected, (((0,), (0,)), ((), ())), precision=HIGH)
    piece_rows = rank_total // num_cols
    piece = lax.dynamic_slice_in_dim(gram_part, lax.axis_index("tp") * piece_rows, piece_rows, axis=0)
    pieces = gather_list(butterfly_sum(piece, "fsdp"), "tp")
    gram = jnp.zeros((rank_total, rank_total), jnp.float32)
    for k, part in enumerate(pieces):
        place = (lax.axis_index("tp") ^ k) * piece_rows
        gram = lax.dynamic_update_slice_in_dim(gram, part, place, axis=0)
    inverse_low = factor_inverse(gram)

    orthonormal = lax.dot_general(projected, inverse_low, (((1,), (1,)), ((), ())), precision=HIGH)
    right_share = lax.dot_general(mixed_share, inverse_low, (((1,), (1,)), ((), ())), precision=HIGH)
    right = lax.all_gather(right_share, "fsdp", axis=0, tiled=True)
    squares = butterfly_sum(butterfly_sum(jnp.sum(right_share * right_share, axis=0, keepdims=True), "fsdp"), "tp")
    scale = lax.rsqrt(squares / col_total + EPSILON)
    factors = jnp.concatenate(
        [-KEEP_SHARE * orthonormal, math.sqrt(row_total / rank_total) * orthonormal * scale], axis=0
    )
    return tuple(finish(momentum, grad, right, factors, scale))


def solution(mesh):
    return jax.shard_map(
        on_device,
        mesh=mesh,
        in_specs=(P("fsdp", "tp"), P("fsdp", "tp"), P("fsdp", "tp"), P()),
        out_specs=(P("fsdp", "tp"), P("tp", None), P("fsdp", "tp")),
        check_vma=False,
    )
```

time: 353 us -> 175 us (0.50)
  waiting for transfers between devices: 221 us -> 103 us
  other arithmetic: 69 us -> 9.18 us
  matrix products: 28.3 us -> 10.7 us
  Pallas kernels: 0 us -> 15.8 us
  starting transfers between devices: 0.38 us -> 15.7 us
  blocking collectives: 9.84 us -> 0 us
    psum x2 -> x0, waiting for transfers between devices: 97.2 us -> none  [the longest x1 55.6 us: on_device(): gram_total = lax.psum(gram_local(projected), 'fsdp')]
    another operation x9 -> x0, other arithmetic: 56.1 us -> none  [the longest x6 34 us: make_orthonormal(): factor_low = jnp.linalg.cholesky(gram_total)]
    reduce_scatter x1, waiting for transfers between devices: 49.1 us -> 14.8 us  [on_device(): lax.psum_scatter(mixed, 'fsdp', scatter_dimension=0, tiled=True)]
    ppermute x0 -> x13, waiting for transfers between devices: none -> 33.4 us  [the longest x10 29.4 us: butterfly_sum(): x = x + lax.ppermute(x, axis, [(i, i ^ step) for i in range(n)])]
    all_gather x1, waiting for transfers between devices: 46.7 us -> 29.2 us  [on_device(): right = lax.all_gather(right_share, 'fsdp', axis=0, tiled=True)]
    pallas_call x0 -> x2, Pallas kernels: none -> 15.8 us  [the longest x1 10.7 us: factor_inverse(): pl.pallas_call(factor_kernel, out_shape=jax.ShapeDtypeStruct((rank, rank)...]
    ppermute x0 -> x13, starting transfers between devices: none -> 15.4 us  [the longest x10 12 us: butterfly_sum(): x = x + lax.ppermute(x, axis, [(i, i ^ step) for i in range(n)])]
    dot_general x5, matrix products: 22.8 us -> 10.7 us  [the longest x1 5.03 us: on_device(): lax.dot_general(combined, projected, (((0,), (0,)), ((), ())), precision=...]
  transfers between devices with their start and end apart: 5 -> 16, of which waited for: 5 -> 16; matrix products, arithmetic and copies ran while one was open for 2% -> 6% of each run, Pallas kernels for 0% -> 6%
where the time goes in v1:
time: 175 us; the launch traced here: 174 us
  waiting for transfers between devices  103 us (59%)
  Pallas kernels  15.8 us (9%)
  starting transfers between devices  15.7 us (9%)
  between operations  13.9 us (8%)
  matrix products  10.7 us (6%)
  other arithmetic  9.18 us (5%)
  local copies, waits for them, and re-layouts  6.25 us (4%)
    ppermute x10, waiting for transfers between devices, butterfly_sum(): x = x + lax.ppermute(x, axis, [(i, i ^ step) for i in range(n)])  29.4 us
    all_gather x1, waiting for transfers between devices, on_device(): right = lax.all_gather(right_share, 'fsdp', axis=0, tiled=True)  29.2 us
    all_gather x1, waiting for transfers between devices, on_device(): basis = lax.all_gather(q_stored, 'fsdp', axis=0, tiled=True)  24.5 us
    reduce_scatter x1, waiting for transfers between devices, on_device(): lax.psum_scatter(mixed, 'fsdp', scatter_dimension=0, tiled=True)  14.8 us
    ppermute x10, starting transfers between devices, butterfly_sum(): x = x + lax.ppermute(x, axis, [(i, i ^ step) for i in range(n)])  12 us
    pallas_call x1, Pallas kernels, factor_inverse(): pl.pallas_call(factor_kernel, out_shape=jax.ShapeDtypeStruct((rank, rank)...  10.7 us
    pallas_call x1, Pallas kernels, finish(): pl.pallas_call(finish_kernel, grid=(cols // block,), in_specs=[wide(), wi...  5.05 us
    dot_general x1, matrix products, on_device(): lax.dot_general(combined, projected, (((0,), (0,)), ((), ())), precision=...  5.03 us
  transfers between devices with their start and end apart: 16, of which 16 were waited for; matrix products, arithmetic and copies ran while one was open for 6% of the time, Pallas kernels for 6%

profile of v1, /device:TPU:0, one launch (start us, length us, event | category | flops | bytes accessed | tf_op | source)
XLA Modules:
  0.0 174.2 jit_solution(17052950336223574734)
XLA Ops:
  7.2 0.0 all-gather.3.cloned.1.call-start
  7.2 0.7 all-gather.3.cloned.1.call-update
  7.9 0.0 reduce-scatter.2.cloned.1.call-start
  8.0 0.7 select_reduce_fusion
  8.7 0.7 fusion.10
  9.4 4.5 %compare_select_fusion.2 = s32[256,1]{0,1:T(1,128)S(1)} fusion(s32[]{:T(128)} %bitcast.1, s32[]{:T(128)} %bitcast.2, s32[]{:T(128)} %bitcast.3, s32[]{:T(128)} %bitcast.4, s32[]{:T(128)} %bitcast.5, s32[]{:T(128)} %bitcast.7, s32[]{:T(128)} %bitcast.6), kind=kLoop, calls=%fused_computation.25 | loop fusion | flops 5888 | bytes 1052 | tf_op jit(solution)/shard_map/gather | solution.py:170
  13.9 0.7 compare_and_fusion
  14.6 2.3 %reduce-precision_convert_fusion = (bf16[128,4096]{1,0:T(8,128)(2,1)S(1)}, bf16[128,4096]{1,0:T(8,128)(2,1)S(1)}) fusion(f32[128,4096]{1,0:T(8,128)} %momentum_ref.1, bf16[128,4096]{1,0:T(8,128)(2,1)} %grad_ref.1), kind=kLoop, calls=%fused_computation.2 | loop fusion | flops 3145728 | bytes 5242880 | tf_op jit(solution)/shard_map/convert_element_type | solution.py:19
  16.9 24.5 %all-gather.3.cloned.1.call-done = bf16[256,4096]{1,0:T(8,128)(2,1)} async-done(((bf16[32,4096]{1,0:T(8,128)(2,1)}), bf16[256,4096]{1,0:T(8,128)(2,1)}) %all-gather.3.cloned.1.call-update) | async-done | bytes 2097168 | tf_op jit(solution)/shard_map/all_gather | solution.py:159
  41.4 0.0 copy-start.1
  41.4 2.4 %fusion.1 = f32[256,256]{1,0:T(8,128)S(1)} fusion(bf16[256,4096]{1,0:T(8,128)(2,1)} %all-gather.3.cloned.1.call-done, bf16[128,4096]{1,0:T(8,128)(2,1)S(1)} %get-tuple-element.10, bf16[128,4096]{1,0:T(8,128)(2,1)S(1)} %get-tuple-element.9), kind=kOutput, calls=%fused_computation.4 | convolution fusion | flops 541065216 | bytes 4456448 | tf_op jit(solution)/shard_map/dot_general | solution.py:160
  43.9 0.0 copy-start
  43.9 0.1 copy.9
  44.0 0.7 gather_fusion
  44.7 0.1 select_bitcast_fusion
  44.8 1.5 collective-permute-start
  46.4 4.2 %collective-permute-done = f32[128,256]{0,1:T(8,128)S(1)} collective-permute-done((f32[128,256]{0,1:T(8,128)S(1)}, f32[128,256]{0,1:T(8,128)S(1)}, u32[]{:S(2)}, u32[]{:S(2)}) %collective-permute-start) | collective-permute-done | bytes 131104 | tf_op jit(solution)/shard_map/ppermute | solution.py:26
  50.5 0.1 fusion.21
  50.6 1.5 collective-permute-start.1
  52.2 3.5 %collective-permute-done.1 = f32[128,256]{0,1:T(8,128)S(1)} collective-permute-done((f32[128,256]{0,1:T(8,128)S(1)}, f32[128,256]{0,1:T(8,128)S(1)}, u32[]{:S(2)}, u32[]{:S(2)}) %collective-permute-start.1) | collective-permute-done | bytes 131104 | tf_op jit(solution)/shard_map/ppermute | solution.py:26
  55.7 0.0 copy-done.1
  55.7 0.0 copy-done
  55.7 5.0 %fusion.5 = f32[4096,256]{1,0:T(8,128)} fusion(f32[128,256]{0,1:T(8,128)S(1)} %add.143, f32[128,4096]{1,0:T(8,128)S(1)} %copy-done, bf16[128,4096]{1,0:T(8,128)(2,1)S(1)} %copy-done.1), kind=kOutput, calls=%fused_computation.9 | convolution fusion | flops 1611661312 | bytes 7471104 | tf_op jit(solution)/shard_map/dot_general | solution.py:173
  60.7 0.0 reduce-scatter.2.cloned.1.call-update
  60.8 0.2 all-gather.5.cloned.1.call-start
  61.0 0.4 fusion.11
  61.4 0.1 collective-permute-start.2
  61.5 1.2 collective-permute-done.2
  62.7 1.6 collective-permute-start.3
  64.3 2.8 %collective-permute-done.3 = f32[64,256]{1,0:T(8,128)S(1)} collective-permute-done((f32[64,256]{1,0:T(8,128)S(1)}, f32[64,256]{1,0:T(8,128)S(1)}, u32[]{:S(2)}, u32[]{:S(2)}) %collective-permute-start.3) | collective-permute-done | bytes 65568 | tf_op jit(solution)/shard_map/ppermute | solution.py:26
  67.1 2.0 %collective-permute-start.4 = (f32[64,256]{1,0:T(8,128)S(1)}, f32[64,256]{1,0:T(8,128)S(1)}, u32[]{:S(2)}, u32[]{:S(2)}) collective-permute-start(f32[64,256]{1,0:T(8,128)S(1)} %add.146), channel_id=1, source_target_pairs={{0,16},{4,20},{8,24},{12,28},{16,0},{20,4},{24,8},{28,12},{1,17},{... | collective-permute-start | bytes 196616 | tf_op jit(solution)/shard_map/ppermute | solution.py:26
  69.1 6.7 %collective-permute-done.4 = f32[64,256]{1,0:T(8,128)S(1)} collective-permute-done((f32[64,256]{1,0:T(8,128)S(1)}, f32[64,256]{1,0:T(8,128)S(1)}, u32[]{:S(2)}, u32[]{:S(2)}) %collective-permute-start.4) | collective-permute-done | bytes 65568 | tf_op jit(solution)/shard_map/ppermute | solution.py:26
  75.8 0.6 constant_dynamic-update-slice_fusion.2
  76.4 1.5 collective-permute-start.5
  77.9 1.5 collective-permute-start.6
  79.4 0.5 collective-permute-start.7
  79.9 1.1 collective-permute-done.5
  81.0 0.8 constant_dynamic-update-slice_fusion.1
  81.8 0.5 collective-permute-done.6
  82.4 2.4 %collective-permute-done.7 = f32[64,256]{1,0:T(8,128)S(1)} collective-permute-done((f32[64,256]{1,0:T(8,128)}, f32[64,256]{1,0:T(8,128)S(1)}, u32[]{:S(2)}, u32[]{:S(2)}) %collective-permute-start.7) | collective-permute-done | bytes 65568 | tf_op jit(solution)/shard_map/ppermute | solution.py:33
  84.8 0.0 copy-start.3
  84.8 0.7 copy-done.3
  85.5 0.0 copy-start.4
  85.5 0.9 copy-done.4
  86.4 10.7 %shard_map.67 = f32[256,256]{1,0:T(8,128)S(1)} custom-call(f32[256,256]{1,0:T(8,128)S(1)} %copy-done.4), custom_call_target="tpu_custom_call" | custom-call | flops 201326592 | bytes 524288 | tf_op jit(solution)/shard_map/pallas_call | solution.py:98
  97.1 14.8 %reduce-scatter.2.cloned.1.call-done = f32[512,256]{1,0:T(8,128)} async-done(((f32[4096,256]{1,0:T(8,128)}), f32[512,256]{1,0:T(8,128)}) %reduce-scatter.2.cloned.1.call-update) | async-done | bytes 524304 | tf_op jit(solution)/shard_map/reduce_scatter | solution.py:174
  111.9 2.5 %multiply_reduce_fusion = (f32[256]{0:T(256)S(1)}, f32[512,256]{1,0:T(8,128)}) fusion(f32[512,256]{1,0:T(8,128)} %reduce-scatter.2.cloned.1.call-done, f32[256,256]{1,0:T(8,128)S(1)} %shard_map.67), kind=kOutput, calls=%fused_computation.10 | convolution fusion | flops 402915072 | bytes 1311744 | tf_op jit(solution)/shard_map/dot_general | solution.py:187
  114.3 0.0 all-gather.5.cloned.1.call-update
  114.4 0.1 collective-permute-start.8
  114.4 1.1 collective-permute-done.8
  115.6 1.1 collective-permute-start.9
  116.6 2.5 %collective-permute-done.9 = f32[1,256]{1,0:T(1,128)S(1)} collective-permute-done((f32[1,256]{1,0:T(1,128)S(1)}, f32[1,256]{1,0:T(1,128)S(1)}, u32[]{:S(2)}, u32[]{:S(2)}) %collective-permute-start.9) | collective-permute-done | bytes 1056 | tf_op jit(solution)/shard_map/ppermute | solution.py:26
  119.1 1.2 collective-permute-start.10
  120.3 3.3 %collective-permute-done.10 = f32[1,256]{1,0:T(1,128)S(1)} collective-permute-done((f32[1,256]{1,0:T(1,128)S(1)}, f32[1,256]{1,0:T(1,128)S(1)}, u32[]{:S(2)}, u32[]{:S(2)}) %collective-permute-start.10) | collective-permute-done | bytes 1056 | tf_op jit(solution)/shard_map/ppermute | solution.py:26
  123.6 1.5 collective-permute-start.11
  125.1 2.1 %collective-permute-done.11 = f32[1,256]{1,0:T(1,128)S(1)} collective-permute-done((f32[1,256]{1,0:T(1,128)S(1)}, f32[1,256]{1,0:T(1,128)S(1)}, u32[]{:S(2)}, u32[]{:S(2)}) %collective-permute-start.11) | collective-permute-done | bytes 1056 | tf_op jit(solution)/shard_map/ppermute | solution.py:26
  127.2 1.5 collective-permute-start.12
  128.7 2.1 %collective-permute-done.12 = f32[1,256]{1,0:T(1,128)S(1)} collective-permute-done((f32[1,256]{1,0:T(1,128)S(1)}, f32[1,256]{1,0:T(1,128)S(1)}, u32[]{:S(2)}, u32[]{:S(2)}) %collective-permute-start.12) | collective-permute-done | bytes 1056 | tf_op jit(solution)/shard_map/ppermute | solution.py:26
  130.8 0.4 broadcast_multiply_fusion.1
  131.2 29.2 %all-gather.5.cloned.1.call-done.right_ref = f32[4096,256]{1,0:T(8,128)} async-done(((f32[512,256]{1,0:T(8,128)}), f32[4096,256]{1,0:T(8,128)}) %all-gather.5.cloned.1.call-update) | async-done | bytes 4194320 | tf_op jit(solution)/shard_map/all_gather | solution.py:188
  160.4 0.0 copy-start.2
  160.4 2.2 %copy-done.2 = f32[4096,256]{1,0:T(8,128)S(1)} copy-done((f32[4096,256]{1,0:T(8,128)S(1)}, f32[4096,256]{1,0:T(8,128)}, u32[]{:S(2)}) %copy-start.2) | copy-done | bytes 4194328
  162.6 5.0 %shard_map.68 = (f32[128,4096]{1,0:T(8,128)}, f32[4096,256]{1,0:T(8,128)}, bf16[128,4096]{1,0:T(8,128)(2,1)}) custom-call(f32[128,4096]{1,0:T(8,128)S(1)} %copy-done, bf16[128,4096]{1,0:T(8,128)(2,1)S(1)} %copy-done.1, f32[4096,256]{1,0:T(8,128)S(1)} %copy-done.2, bf16[256,256]{1,0:T(8,128)(2,1)S(1)} %get-tuple-element.12.high_ref, ...), custom_call_target="tpu_custom_call" | custom-call | flops 1610612736 | bytes 14680064 | tf_op jit(solution)/shard_map/pallas_call | solution.py:131
  (17 shorter events, 0.2 us)
Async XLA Ops:
  7.2 34.3 %all-gather.3.cloned.1.call-start = ((), (), s32[]{:S(2)}) async-start(), calls=%async_computation.1 | async-start | bytes 2359296 | tf_op jit(solution)/shard_map/all_gather | solution.py:159
  7.9 104.0 %reduce-scatter.2.cloned.1.call-start = ((), (), s32[]{:S(2)}) async-start(), calls=%async_computation.2 | async-start | bytes 4718592 | tf_op jit(solution)/shard_map/reduce_scatter | solution.py:174
  41.4 14.3 %copy-start.1 = (bf16[128,4096]{1,0:T(8,128)(2,1)S(1)}, bf16[128,4096]{1,0:T(8,128)(2,1)}, u32[]{:S(2)}) copy-start(bf16[128,4096]{1,0:T(8,128)(2,1)} %grad_ref.1) | copy-start | bytes 3145732
  43.9 11.8 %copy-start = (f32[128,4096]{1,0:T(8,128)S(1)}, f32[128,4096]{1,0:T(8,128)}, u32[]{:S(2)}) copy-start(f32[128,4096]{1,0:T(8,128)} %momentum_ref.1) | copy-start | bytes 6291460
  44.8 5.7 %collective-permute-start = (f32[128,256]{0,1:T(8,128)S(1)}, f32[128,256]{0,1:T(8,128)S(1)}, u32[]{:S(2)}, u32[]{:S(2)}) collective-permute-start(f32[128,256]{0,1:T(8,128)S(1)} %select_bitcast_fusion), channel_id=1, source_target_pairs={{0,1},{1,0},{2,3},{3,2},{4,5},{5,4},{6,7},{7,6},{8,9},{9,8},{10,11... | collective-permute-start | bytes 393224 | tf_op jit(solution)/shard_map/ppermute | solution.py:26
  50.6 5.0 %collective-permute-start.1 = (f32[128,256]{0,1:T(8,128)S(1)}, f32[128,256]{0,1:T(8,128)S(1)}, u32[]{:S(2)}, u32[]{:S(2)}) collective-permute-start(f32[128,256]{0,1:T(8,128)S(1)} %fusion.21), channel_id=1, source_target_pairs={{0,2},{1,3},{2,0},{3,1},{4,6},{5,7},{6,4},{7,5},{8,10},{9,11},{10,... | collective-permute-start | bytes 393224 | tf_op jit(solution)/shard_map/ppermute | solution.py:26
  60.8 99.7 %all-gather.5.cloned.1.call-start = ((), (), s32[]{:S(2)}) async-start(), calls=%async_computation.3 | async-start | bytes 4718592 | tf_op jit(solution)/shard_map/all_gather | solution.py:188
  61.4 1.3 collective-permute-start.2
  62.7 4.3 %collective-permute-start.3 = (f32[64,256]{1,0:T(8,128)S(1)}, f32[64,256]{1,0:T(8,128)S(1)}, u32[]{:S(2)}, u32[]{:S(2)}) collective-permute-start(f32[64,256]{1,0:T(8,128)S(1)} %fusion.20), channel_id=1, source_target_pairs={{0,8},{4,12},{8,0},{12,4},{16,24},{20,28},{24,16},{28,20},{1,9},{5... | collective-permute-start | bytes 196616 | tf_op jit(solution)/shard_map/ppermute | solution.py:26
  67.1 8.6 %collective-permute-start.4 = (f32[64,256]{1,0:T(8,128)S(1)}, f32[64,256]{1,0:T(8,128)S(1)}, u32[]{:S(2)}, u32[]{:S(2)}) collective-permute-start(f32[64,256]{1,0:T(8,128)S(1)} %add.146), channel_id=1, source_target_pairs={{0,16},{4,20},{8,24},{12,28},{16,0},{20,4},{24,8},{28,12},{1,17},{... | collective-permute-start | bytes 196616 | tf_op jit(solution)/shard_map/ppermute | solution.py:26
  76.4 4.6 %collective-permute-start.5 = (f32[64,256]{1,0:T(8,128)}, f32[64,256]{1,0:T(8,128)}, u32[]{:S(2)}, u32[]{:S(2)}) collective-permute-start(f32[64,256]{1,0:T(8,128)} %get-tuple-element.6), channel_id=1, source_target_pairs={{0,1},{1,0},{2,3},{3,2},{4,5},{5,4},{6,7},{7,6},{8,9},{9,8},{10,11... | collective-permute-start | bytes 196616 | tf_op jit(solution)/shard_map/ppermute | solution.py:33
  77.9 4.5 %collective-permute-start.6 = (f32[64,256]{1,0:T(8,128)}, f32[64,256]{1,0:T(8,128)S(1)}, u32[]{:S(2)}, u32[]{:S(2)}) collective-permute-start(f32[64,256]{1,0:T(8,128)} %get-tuple-element.6), channel_id=1, source_target_pairs={{0,2},{1,3},{2,0},{3,1},{4,6},{5,7},{6,4},{7,5},{8,10},{9,11},{10,... | collective-permute-start | bytes 196616 | tf_op jit(solution)/shard_map/ppermute | solution.py:33
  79.4 5.4 %collective-permute-start.7 = (f32[64,256]{1,0:T(8,128)}, f32[64,256]{1,0:T(8,128)S(1)}, u32[]{:S(2)}, u32[]{:S(2)}) collective-permute-start(f32[64,256]{1,0:T(8,128)} %get-tuple-element.6), channel_id=1, source_target_pairs={{0,3},{1,2},{2,1},{3,0},{4,7},{5,6},{6,5},{7,4},{8,11},{9,10},{10,... | collective-permute-start | bytes 196616 | tf_op jit(solution)/shard_map/ppermute | solution.py:33
  84.8 0.7 copy-start.3
  85.5 0.9 copy-start.4
  114.4 1.2 collective-permute-start.8
  115.6 3.6 %collective-permute-start.9 = (f32[1,256]{1,0:T(1,128)S(1)}, f32[1,256]{1,0:T(1,128)S(1)}, u32[]{:S(2)}, u32[]{:S(2)}) collective-permute-start(f32[1,256]{1,0:T(1,128)S(1)} %add.151), channel_id=1, source_target_pairs={{0,8},{4,12},{8,0},{12,4},{16,24},{20,28},{24,16},{28,20},{1,9},{5... | collective-permute-start | bytes 3080 | tf_op jit(solution)/shard_map/ppermute | solution.py:26
  119.1 4.5 %collective-permute-start.10 = (f32[1,256]{1,0:T(1,128)S(1)}, f32[1,256]{1,0:T(1,128)S(1)}, u32[]{:S(2)}, u32[]{:S(2)}) collective-permute-start(f32[1,256]{1,0:T(1,128)S(1)} %add.152), channel_id=1, source_target_pairs={{0,16},{4,20},{8,24},{12,28},{16,0},{20,4},{24,8},{28,12},{1,17},{... | collective-permute-start | bytes 3080 | tf_op jit(solution)/shard_map/ppermute | solution.py:26
  123.6 3.6 %collective-permute-start.11 = (f32[1,256]{1,0:T(1,128)S(1)}, f32[1,256]{1,0:T(1,128)S(1)}, u32[]{:S(2)}, u32[]{:S(2)}) collective-permute-start(f32[1,256]{1,0:T(1,128)S(1)} %add.153), channel_id=1, source_target_pairs={{0,1},{1,0},{2,3},{3,2},{4,5},{5,4},{6,7},{7,6},{8,9},{9,8},{10,11... | collective-permute-start | bytes 3080 | tf_op jit(solution)/shard_map/ppermute | solution.py:26
  127.2 3.6 %collective-permute-start.12 = (f32[1,256]{1,0:T(1,128)S(1)}, f32[1,256]{1,0:T(1,128)S(1)}, u32[]{:S(2)}, u32[]{:S(2)}) collective-permute-start(f32[1,256]{1,0:T(1,128)S(1)} %add.154), channel_id=1, source_target_pairs={{0,2},{1,3},{2,0},{3,1},{4,6},{5,7},{6,4},{7,5},{8,10},{9,11},{10,... | collective-permute-start | bytes 3080 | tf_op jit(solution)/shard_map/ppermute | solution.py:26
  160.4 2.2 %copy-start.2 = (f32[4096,256]{1,0:T(8,128)S(1)}, f32[4096,256]{1,0:T(8,128)}, u32[]{:S(2)}) copy-start(f32[4096,256]{1,0:T(8,128)} %all-gather.5.cloned.1.call-done.right_ref) | copy-start | bytes 12582916
Sparse Core Ops, SparseCore 0:
  9.6 31.7 all-gather.2
  60.9 50.9 reduce-scatter.1
  114.5 45.9 all-gather.4

commit v2 on v1

--- a/solution.py
+++ b/solution.py
@@ -12,6 +12,7 @@
 HIGH = lax.Precision.HIGHEST
 PANEL = 64
 TILE = 8
+HEAD = 16
 
 
 def split_two(x):
@@ -19,9 +20,8 @@
     return high.astype(jnp.bfloat16), (x - high).astype(jnp.bfloat16)
 
 
-def butterfly_sum(x, axis):
+def butterfly_sum(x, axis, step=1):
     n = lax.axis_size(axis)
-    step = 1
     while step < n:
         x = x + lax.ppermute(x, axis, [(i, i ^ step) for i in range(n)])
         step *= 2
@@ -104,11 +104,87 @@
     )(gram)
 
 
-def finish_kernel(momentum_ref, grad_ref, right_ref, high_ref, low_ref, scale_ref, next_ref, basis_ref, update_ref):
-    right = right_ref[...]
+def dot_rows(a, b):
+    return lax.dot_general(a, b, (((1,), (1,)), ((), ())), precision=HIGH, preferred_element_type=jnp.float32)
+
+
+def halves(x):
+    high = x.astype(jnp.bfloat16)
+    return high, (x - high.astype(jnp.float32)).astype(jnp.bfloat16)
+
+
+def mix_kernel(core_ref, high_ref, low_ref, proj_ref, out_ref):
+    def times(a, b):
+        return lax.dot_general(a, b, (((0,), (0,)), ((), ())), preferred_element_type=jnp.float32)
+
+    proj_high, proj_low = halves(proj_ref[...])
+    high = high_ref[...]
+    out_ref[...] = times(high, proj_high) + (times(low_ref[...], proj_high) + times(high, proj_low))
+
+
+def mix(core, pair_high, pair_low, projected):
+    rows, cols = pair_high.shape
+    rank = projected.shape[1]
+    block = min(512, cols // 2)
+    steps = cols // 2 // block
+    wide = pl.BlockSpec((rows, block), lambda i, core: (0, core[0] * steps + i))
+    return pl.pallas_call(
+        mix_kernel,
+        grid_spec=pltpu.PrefetchScalarGridSpec(
+            num_scalar_prefetch=1,
+            grid=(steps,),
+            in_specs=[wide, wide, pl.BlockSpec(projected.shape, lambda i, core: (0, 0))],
+            out_specs=pl.BlockSpec((block, rank), lambda i, core: (i, 0)),
+        ),
+        out_shape=jax.ShapeDtypeStruct((cols // 2, rank), jnp.float32),
+        compiler_params=pltpu.CompilerParams(vmem_limit_bytes=32 * 1024 * 1024),
+        cost_estimate=pl.CostEstimate(
+            flops=3 * rows * cols * rank, bytes_accessed=rows * cols * 2 + cols * rank * 2, transcendentals=0
+        ),
+    )(core, pair_high, pair_low, projected)
+
+
+def unit_of(exponent, mantissa):
+    return mantissa * jnp.exp2(exponent - 13.0)
+
+
+def encode_kernel(share_ref, inverse_ref, code_ref, squares_ref):
+    right = dot_rows(share_ref[...], inverse_ref[...])
+    rows, rank = right.shape
+    squares_ref[...] = jnp.broadcast_to(jnp.sum(right * right, axis=0, keepdims=True), squares_ref.shape)
+    top = jnp.maximum(jnp.max(jnp.abs(right), axis=0, keepdims=True), 1e-30) * (1.0 / 32766.0)
+    exponent = jnp.floor(jnp.log2(top))
+    mantissa = jnp.floor(top * jnp.exp2(13.0 - exponent)) + 1.0
+    unit = unit_of(exponent, mantissa)
+    code_ref[:rows, :] = jnp.floor(right * (1.0 / unit) + 0.5).astype(jnp.int32).astype(jnp.int16)
+    place = lax.broadcasted_iota(jnp.int32, (HEAD, rank), 0)
+    head = jnp.where(place == 0, exponent, mantissa)
+    code_ref[rows:, :] = head.astype(jnp.int32).astype(jnp.int16)
+
+
+def encode(share, inverse_low):
+    rows, rank = share.shape
+    return pl.pallas_call(
+        encode_kernel,
+        out_shape=[
+            jax.ShapeDtypeStruct((rows + HEAD, rank), jnp.int16),
+            jax.ShapeDtypeStruct((TILE, rank), jnp.float32),
+        ],
+        compiler_params=pltpu.CompilerParams(vmem_limit_bytes=32 * 1024 * 1024),
+        cost_estimate=pl.CostEstimate(flops=12 * rows * rank * rank, bytes_accessed=rows * rank * 6, transcendentals=0),
+    )(share, inverse_low)
+
+
+def finish_kernel(
+    core_ref, momentum_ref, grad_ref, mine_ref, other_ref, high_ref, low_ref, scale_ref, next_ref, basis_ref, update_ref
+):
+    code = jnp.where(pl.program_id(0) == 0, mine_ref[...].astype(jnp.int32), other_ref[...].astype(jnp.int32))
+    code = code.astype(jnp.float32)
+    share = code.shape[1] - HEAD
+    right = code[:, :share] * unit_of(code[:, share : share + 1], code[:, share + 1 : share + 2])
+    right = right.reshape(basis_ref.shape)
     basis_ref[...] = right * scale_ref[...]
-    right_high = right.astype(jnp.bfloat16)
-    right_low = (right - right_high.astype(jnp.float32)).astype(jnp.bfloat16)
+    right_high, right_low = halves(right)
 
     def times(a, b):
         return lax.dot_general(a, b, (((1,), (1,)), ((), ())), preferred_element_type=jnp.float32)
@@ -120,19 +196,27 @@
     update_ref[...] = both[rows:].astype(jnp.bfloat16)
 
 
-def finish(momentum, grad, right, factors, scale):
+def finish(core, momentum, grad, mine, other, factors, scale):
     rows, cols = momentum.shape
-    rank = right.shape[1]
-    block = min(512, cols)
+    shares, share, rank = mine.shape
+    share -= HEAD
+    group = max(1, min(512 // share, shares))
+    block, steps = group * share, shares // group
     high, low = split_two(factors)
-    wide = lambda: pl.BlockSpec((rows, block), lambda i: (0, i))
-    tall = lambda: pl.BlockSpec((block, rank), lambda i: (i, 0))
-    whole = lambda a: pl.BlockSpec(a.shape, lambda i: (0, 0))
+    column = lambda a, i, core: (a ^ core[0]) * steps + i
+    wide = lambda: pl.BlockSpec((rows, block), lambda a, i, core: (0, column(a, i, core)))
+    tall = lambda: pl.BlockSpec((block, rank), lambda a, i, core: (column(a, i, core), 0))
+    whole = lambda x: pl.BlockSpec(x.shape, lambda a, i, core: (0, 0))
+    first = pl.BlockSpec((group, share + HEAD, rank), lambda a, i, core: (jnp.where(a == 0, i, steps - 1), 0, 0))
+    second = pl.BlockSpec((group, share + HEAD, rank), lambda a, i, core: (jnp.where(a == 0, 0, i), 0, 0))
     return pl.pallas_call(
         finish_kernel,
-        grid=(cols // block,),
-        in_specs=[wide(), wide(), tall(), whole(high), whole(low), whole(scale)],
-        out_specs=[wide(), tall(), wide()],
+        grid_spec=pltpu.PrefetchScalarGridSpec(
+            num_scalar_prefetch=1,
+            grid=(2, steps),
+            in_specs=[wide(), wide(), first, second, whole(high), whole(low), whole(scale)],
+            out_specs=[wide(), tall(), wide()],
+        ),
         out_shape=[
             jax.ShapeDtypeStruct((rows, cols), jnp.float32),
             jax.ShapeDtypeStruct((cols, rank), jnp.float32),
@@ -142,7 +226,7 @@
         cost_estimate=pl.CostEstimate(
             flops=6 * 2 * rows * cols * rank, bytes_accessed=rows * cols * 12 + cols * rank * 8, transcendentals=0
         ),
-    )(momentum, grad, right, high, low, scale)
+    )(core, momentum, grad, mine, other, high, low, scale)
 
 
 def on_device(momentum, grad, q_stored, perm):
@@ -153,45 +237,53 @@
     row_total = momentum.shape[0] * num_blocks
     col_total = momentum.shape[1] * num_cols
     rows = momentum.shape[0]
-
-    combined = momentum + grad.astype(jnp.float32)
-    comb_high, comb_low = split_two(combined)
-    basis = lax.all_gather(q_stored, "fsdp", axis=0, tiled=True)
-    stacked = lax.dot_general(
-        jnp.concatenate([comb_high, comb_low], axis=0),
+    core = lax.axis_index("fsdp") % 2
+    lines = [list(range(0, num_blocks, 2)), list(range(1, num_blocks, 2))]
+    swap = lambda x: lax.ppermute(x, "fsdp", [(i, i ^ 1) for i in range(num_blocks)])
+
+    comb_high, comb_low = split_two(momentum + grad.astype(jnp.float32))
+    pair_high = jnp.concatenate([comb_high, swap(comb_high)], axis=0)
+    pair_low = jnp.concatenate([comb_low, swap(comb_low)], axis=0)
+
+    basis = lax.all_gather(q_stored, "fsdp", axis=0, tiled=True, axis_index_groups=lines)
+    product = lax.dot_general(
+        jnp.concatenate([pair_high, pair_low], axis=0),
         basis,
         (((1,), (1,)), ((), ())),
         preferred_element_type=jnp.float32,
     )
-    stored_order = stacked[:rows] + stacked[rows:]
+    mine = butterfly_sum(product[: 2 * rows] + product[2 * rows :], "tp")
+    other = swap(mine)
+    other = jnp.concatenate([other[rows:], other[:rows]], axis=0)
     blocks = jnp.arange(num_blocks, dtype=jnp.int32)
     inverse = jnp.sum(jnp.where(perm[:, None] == blocks[None, :], blocks[:, None], 0), axis=0)
+    inverse = ((inverse % 2) ^ core) * (num_blocks // 2) + inverse // 2
     row_ids = jnp.arange(rank_total, dtype=jnp.int32)
     order_index = inverse[row_ids // block_rows] * block_rows + row_ids % block_rows
-    projected = butterfly_sum(jnp.take(stored_order, order_index, axis=1), "tp")
-
-    mixed = lax.dot_general(combined, projected, (((0,), (0,)), ((), ())), precision=HIGH)
-    mixed_share = lax.psum_scatter(mixed, "fsdp", scatter_dimension=0, tiled=True)
+    projected = jnp.take(jnp.concatenate([mine, other], axis=1), order_index, axis=1)
+
+    mixed = mix(core.reshape(1), pair_high, pair_low, projected)
+    mixed_share = lax.psum_scatter(mixed, "fsdp", scatter_dimension=0, tiled=True, axis_index_groups=lines)
 
     gram_part = lax.dot_general(projected, projected, (((0,), (0,)), ((), ())), precision=HIGH)
     piece_rows = rank_total // num_cols
     piece = lax.dynamic_slice_in_dim(gram_part, lax.axis_index("tp") * piece_rows, piece_rows, axis=0)
-    pieces = gather_list(butterfly_sum(piece, "fsdp"), "tp")
+    pieces = gather_list(butterfly_sum(piece, "fsdp", 2), "tp")
     gram = jnp.zeros((rank_total, rank_total), jnp.float32)
     for k, part in enumerate(pieces):
         place = (lax.axis_index("tp") ^ k) * piece_rows
         gram = lax.dynamic_update_slice_in_dim(gram, part, place, axis=0)
     inverse_low = factor_inverse(gram)
 
-    orthonormal = lax.dot_general(projected, inverse_low, (((1,), (1,)), ((), ())), precision=HIGH)
-    right_share = lax.dot_general(mixed_share, inverse_low, (((1,), (1,)), ((), ())), precision=HIGH)
-    right = lax.all_gather(right_share, "fsdp", axis=0, tiled=True)
-    squares = butterfly_sum(butterfly_sum(jnp.sum(right_share * right_share, axis=0, keepdims=True), "fsdp"), "tp")
+    orthonormal = dot_rows(projected[:rows], inverse_low)
+    code, squares = encode(mixed_share, inverse_low)
+    codes = lax.all_gather(code, "fsdp", axis=0, axis_index_groups=lines)
+    squares = butterfly_sum(butterfly_sum(squares[:1], "fsdp"), "tp")
     scale = lax.rsqrt(squares / col_total + EPSILON)
     factors = jnp.concatenate(
         [-KEEP_SHARE * orthonormal, math.sqrt(row_total / rank_total) * orthonormal * scale], axis=0
     )
-    return tuple(finish(momentum, grad, right, factors, scale))
+    return tuple(finish(core.reshape(1), momentum, grad, codes, swap(codes), factors, scale))
 
 
 def solution(mesh):

time: 175 us -> 163 us (0.931)
  waiting for transfers between devices: 103 us -> 63.1 us
  blocking collectives: 0 us -> 21.7 us
  Pallas kernels: 15.8 us -> 21.1 us
  matrix products: 10.7 us -> 6.19 us
  other arithmetic: 9.18 us -> 11.8 us
  local copies, waits for them, and re-layouts: 6.25 us -> 8.82 us
    all_gather x2 -> x1, waiting for transfers between devices: 53.8 us -> 23.2 us  [on_device(): lax.all_gather(q_stored, 'fsdp', axis=0, tiled=True, axis_index_groups=li...]
    all_gather x0 -> x1, blocking collectives: none -> 21.7 us  [on_device(): codes = lax.all_gather(code, 'fsdp', axis=0, axis_index_groups=lines)]
    reduce_scatter x1, waiting for transfers between devices: 14.8 us -> 6.2 us  [on_device(): lax.psum_scatter(mixed, 'fsdp', scatter_dimension=0, tiled=True, axis_ind...]
    dot_general x4 -> x2, matrix products: 10.3 us -> 4.42 us  [the longest x1 3.07 us: on_device(): lax.dot_general(jnp.concatenate([pair_high, pair_low], axis=0), basis, ((...]
    pallas_call x1 -> x3, Pallas kernels: 5.05 us -> 9.46 us  [the longest x1 5.67 us: finish(): pl.pallas_call(finish_kernel, grid_spec=pltpu.PrefetchScalarGridSpec(num_...]
    concatenate x0 -> x3, other arithmetic: none -> 3.2 us  [the longest x1 1.68 us: on_device(): pair_high = jnp.concatenate([comb_high, swap(comb_high)], axis=0)]
    unnamed x10 -> x22, local copies, waits for them, and re-layouts: 3.84 us -> 4.38 us
    ppermute x10 -> x9, starting transfers between devices: 12 us -> 11.5 us  [butterfly_sum(): x = x + lax.ppermute(x, axis, [(i, i ^ step) for i in range(n)])]
  transfers between devices with their start and end apart: 16 -> 18, of which waited for: 16 -> 14; matrix products, arithmetic and copies ran while one was open for 6% -> 11% of each run, Pallas kernels for 6% -> 7%
where the time goes in v2:
time: 163 us
  waiting for transfers between devices  63.1 us (39%)
  blocking collectives  21.7 us (13%)
  Pallas kernels  21.1 us (13%)
  starting transfers between devices  15.8 us (10%)
  between operations  14.3 us (9%)
  other arithmetic  11.8 us (7%)
  local copies, waits for them, and re-layouts  8.82 us (5%)
  matrix products  6.19 us (4%)
    ppermute x9, waiting for transfers between devices, butterfly_sum(): x = x + lax.ppermute(x, axis, [(i, i ^ step) for i in range(n)])  29.7 us
    all_gather x1, waiting for transfers between devices, on_device(): lax.all_gather(q_stored, 'fsdp', axis=0, tiled=True, axis_index_groups=li...  23.2 us
    all_gather x1, blocking collectives, on_device(): codes = lax.all_gather(code, 'fsdp', axis=0, axis_index_groups=lines)  21.7 us
    pallas_call x1, Pallas kernels, factor_inverse(): pl.pallas_call(factor_kernel, out_shape=jax.ShapeDtypeStruct((rank, rank)...  11.7 us
    ppermute x9, starting transfers between devices, butterfly_sum(): x = x + lax.ppermute(x, axis, [(i, i ^ step) for i in range(n)])  11.5 us
    reduce_scatter x1, waiting for transfers between devices, on_device(): lax.psum_scatter(mixed, 'fsdp', scatter_dimension=0, tiled=True, axis_ind...  6.2 us
    pallas_call x1, Pallas kernels, finish(): pl.pallas_call(finish_kernel, grid_spec=pltpu.PrefetchScalarGridSpec(num_...  5.67 us
    gather x2, other arithmetic, on_device(): inverse[row_ids // block_rows] * block_rows + row_ids % block_rows  4.73 us
  transfers between devices with their start and end apart: 18, of which 14 were waited for; matrix products, arithmetic and copies ran while one was open for 11% of the time, Pallas kernels for 7%

profile of v2, /device:TPU:0, one launch (start us, length us, event | category | flops | bytes accessed | tf_op | source)
XLA Modules:
  0.0 162.8 jit_solution(12775654357757124218)
XLA Ops:
  7.2 0.0 all-gather.4.cloned.1.call-start
  7.2 0.7 all-gather.4.cloned.1.call-update
  7.9 0.0 reduce-scatter.2.cloned.1.call-start
  8.0 2.3 %fusion.8 = (bf16[128,4096]{1,0:T(8,128)(2,1)S(1)}, bf16[128,4096]{1,0:T(8,128)(2,1)S(1)}) fusion(f32[128,4096]{1,0:T(8,128)} %momentum_ref.1, bf16[128,4096]{1,0:T(8,128)(2,1)} %grad_ref.1), kind=kLoop, calls=%fused_computation.11 | loop fusion | flops 3145728 | bytes 5242880 | tf_op jit(solution)/shard_map/convert_element_type | solution.py:20
  10.2 0.0 copy-start.6
  10.3 0.5 collective-permute-start.1
  10.8 0.1 collective-permute-start
  10.9 0.1 select_reduce_fusion
  11.0 0.7 fusion.24
  11.7 4.7 %compare_select_fusion.2 = s32[256,1]{0,1:T(1,128)S(1)} fusion(s32[]{:T(128)} %bitcast.2, s32[]{:T(128)} %bitcast.3, s32[]{:T(128)} %bitcast.4, s32[]{:T(128)} %bitcast.5, s32[]{:T(128)} %bitcast.6, s32[]{:T(128)} %bitcast.8, s32[]{:T(128)} %bitcast.7), kind=kLoop, calls=%fused_computation.36 | loop fusion | flops 5888 | bytes 1052 | tf_op jit(solution)/shard_map/gather | solution.py:262
  16.4 0.7 compare_and_fusion
  17.1 0.0 copy-start.8
  17.1 23.2 %all-gather.4.cloned.1.call-done = bf16[128,4096]{1,0:T(8,128)(2,1)} async-done(((bf16[32,4096]{1,0:T(8,128)(2,1)}), bf16[128,4096]{1,0:T(8,128)(2,1)}) %all-gather.4.cloned.1.call-update) | async-done | bytes 1048592 | tf_op jit(solution)/shard_map/all_gather | solution.py:248
  40.2 3.1 %fusion = f32[512,128]{0,1:T(8,128)S(1)} fusion(bf16[128,4096]{1,0:T(8,128)(2,1)} %all-gather.4.cloned.1.call-done, bf16[128,4096]{1,0:T(8,128)(2,1)S(1)} %collective-permute-done.1, bf16[128,4096]{1,0:T(8,128)(2,1)S(1)} %get-tuple-element.13, bf16[128,4096]{1,0:T(8,128)(2,1)} %collective-permute-done, bf16[128,4096]{1,0:T(8,128)(2,1)S(1)} %get-tuple-element.14), kind=kOutput, calls=%fused_computation.1 | convolution fusion | flops 553648128 | bytes 5505024 | tf_op jit(solution)/shard_map/dot_general | solution.py:249
  43.4 0.0 copy-start.9
  43.4 1.5 collective-permute-start.2
  44.9 3.6 %collective-permute-done.2 = f32[256,128]{0,1:T(8,128)S(1)} collective-permute-done((f32[256,128]{0,1:T(8,128)S(1)}, f32[256,128]{0,1:T(8,128)S(1)}, u32[]{:S(2)}, u32[]{:S(2)}) %collective-permute-start.2) | collective-permute-done | bytes 131104 | tf_op jit(solution)/shard_map/ppermute | solution.py:26
  48.6 1.5 collective-permute-start.3
  50.1 1.7 %pad_maximum_fusion.high_ref = bf16[256,4096]{1,0:T(8,128)(2,1)S(1)} fusion(bf16[128,4096]{1,0:T(8,128)(2,1)} %collective-permute-done, bf16[128,4096]{1,0:T(8,128)(2,1)} %copy-done.6), kind=kLoop, calls=%fused_computation.12 | loop fusion | flops 4194304 | bytes 4194304 | tf_op jit(solution)/shard_map/concatenate | solution.py:245
  51.8 1.8 %collective-permute-done.3 = f32[256,128]{0,1:T(8,128)S(1)} collective-permute-done((f32[256,128]{0,1:T(8,128)S(1)}, f32[256,128]{0,1:T(8,128)S(1)}, u32[]{:S(2)}, u32[]{:S(2)}) %collective-permute-start.3) | collective-permute-done | bytes 131104 | tf_op jit(solution)/shard_map/ppermute | solution.py:26
  53.6 0.1 collective-permute-start.4
  53.7 1.5 pad_maximum_fusion.1.low_ref
  55.3 1.0 gather_fusion
  56.2 0.1 copy.9
  56.4 0.0 copy-start.7
  56.4 1.7 %copy-done = bf16[256,4096]{1,0:T(8,128)(2,1)S(1)} copy-done((bf16[256,4096]{1,0:T(8,128)(2,1)S(1)}, bf16[256,4096]{1,0:T(8,128)(2,1)}, u32[]{:S(2)}) %copy-start) | copy-done | bytes 2097176
  58.1 3.0 %shard_map.67 = f32[2048,256]{1,0:T(8,128)} custom-call(s32[1]{0:T(128)} %bitcast.core_ref, bf16[256,4096]{1,0:T(8,128)(2,1)S(1)} %pad_maximum_fusion.high_ref, bf16[256,4096]{1,0:T(8,128)(2,1)S(1)} %copy-done, f32[256,256]{1,0:T(8,128)S(1)} %select_bitcast_fusion.proj_ref), custom_call_target="tpu_custom_call" | custom-call | flops 805306368 | bytes 4194304 | tf_op jit(solution)/shard_map/pallas_call | solution.py:131
  61.1 0.0 reduce-scatter.2.cloned.1.call-update
  61.1 1.8 %fusion.10 = f32[256,256]{1,0:T(8,128)S(1)} fusion(f32[256,256]{0,1:T(8,128)} %copy-done.7, pred[256]{0:T(512)(128)(4,1)S(1)} %get-tuple-element.11), kind=kOutput, calls=%fused_computation.20 | convolution fusion | flops 201392128 | bytes 524544 | tf_op jit(solution)/shard_map/dot_general | solution.py:268
  62.9 1.4 collective-permute-start.5
  64.4 3.1 %collective-permute-done.5 = f32[64,256]{1,0:T(8,128)S(1)} collective-permute-done((f32[64,256]{1,0:T(8,128)S(1)}, f32[64,256]{1,0:T(8,128)S(1)}, u32[]{:S(2)}, u32[]{:S(2)}) %collective-permute-start.5) | collective-permute-done | bytes 65568 | tf_op jit(solution)/shard_map/ppermute | solution.py:26
  67.5 2.1 %collective-permute-start.6 = (f32[64,256]{1,0:T(8,128)S(1)}, f32[64,256]{1,0:T(8,128)S(1)}, u32[]{:S(2)}, u32[]{:S(2)}) collective-permute-start(f32[64,256]{1,0:T(8,128)S(1)} %fusion.27), channel_id=1, source_target_pairs={{0,16},{4,20},{8,24},{12,28},{16,0},{20,4},{24,8},{28,12},{1,17},{... | collective-permute-start | bytes 196616 | tf_op jit(solution)/shard_map/ppermute | solution.py:26
  69.6 8.2 %collective-permute-done.6 = f32[64,256]{1,0:T(8,128)S(1)} collective-permute-done((f32[64,256]{1,0:T(8,128)S(1)}, f32[64,256]{1,0:T(8,128)S(1)}, u32[]{:S(2)}, u32[]{:S(2)}) %collective-permute-start.6) | collective-permute-done | bytes 65568 | tf_op jit(solution)/shard_map/ppermute | solution.py:26
  77.8 0.7 broadcast_in_dim.33
  78.5 0.6 constant_dynamic-update-slice_fusion.2
  79.2 1.5 collective-permute-start.7
  80.6 1.5 collective-permute-start.8
  82.1 0.6 collective-permute-start.9
  82.7 0.8 collective-permute-done.7
  83.4 0.6 constant_dynamic-update-slice_fusion.1
  84.1 1.5 collective-permute-done.8
  85.6 0.6 constant_dynamic-update-slice_fusion
  86.2 1.0 collective-permute-done.9
  87.3 0.6 constant_dynamic-update-slice_fusion.3.gram_ref
  87.9 11.7 %shard_map.68.inverse_ref = f32[256,256]{1,0:T(8,128)S(1)} custom-call(f32[256,256]{1,0:T(8,128)} %constant_dynamic-update-slice_fusion.3.gram_ref), custom_call_target="tpu_custom_call" | custom-call | flops 201326592 | bytes 524288 | tf_op jit(solution)/shard_map/pallas_call | solution.py:98
  99.6 0.0 copy-start.3
  99.6 0.7 copy-done.3
  100.3 6.2 %reduce-scatter.2.cloned.1.call-done.share_ref = f32[512,256]{1,0:T(8,128)} async-done(((f32[2048,256]{1,0:T(8,128)}), f32[512,256]{1,0:T(8,128)}) %reduce-scatter.2.cloned.1.call-update) | async-done | bytes 524304 | tf_op jit(solution)/shard_map/reduce_scatter | solution.py:266
  106.5 0.9 copy-done.4
  107.4 1.0 copy-done.5
  108.5 0.8 shard_map.69
  109.3 21.7 %all-gather.5 = s16[2112,256]{1,0:T(8,128)(2,1)S(1)} all-gather(s16[528,256]{1,0:T(8,128)(2,1)S(1)} %get-tuple-element.5), channel_id=2, replica_groups={{0,8,16,24},{4,12,20,28},{1,9,17,25},{5,13,21,29},{2,10,18,26},{6,14,22..., dimensions={0}, use_global_device_ids=true | all-gather | bytes 1351680 | tf_op jit(solution)/shard_map/all_gather | solution.py:280
  131.0 0.5 collective-permute-start.11
  131.5 2.2 %collective-permute-done.11 = f32[1,256]{1,0:T(1,128)S(1)} collective-permute-done((f32[1,256]{1,0:T(1,128)S(1)}, f32[1,256]{1,0:T(1,128)S(1)}, u32[]{:S(2)}, u32[]{:S(2)}) %collective-permute-start.11) | collective-permute-done | bytes 1056 | tf_op jit(solution)/shard_map/ppermute | solution.py:26
  133.7 0.6 collective-permute-start.12
  134.3 3.0 %collective-permute-done.12 = f32[1,256]{1,0:T(1,128)S(1)} collective-permute-done((f32[1,256]{1,0:T(1,128)S(1)}, f32[1,256]{1,0:T(1,128)S(1)}, u32[]{:S(2)}, u32[]{:S(2)}) %collective-permute-start.12) | collective-permute-done | bytes 1056 | tf_op jit(solution)/shard_map/ppermute | solution.py:26
  137.3 0.9 collective-permute-start.13
  138.2 3.5 %collective-permute-done.13 = f32[1,256]{1,0:T(1,128)S(1)} collective-permute-done((f32[1,256]{1,0:T(1,128)S(1)}, f32[1,256]{1,0:T(1,128)S(1)}, u32[]{:S(2)}, u32[]{:S(2)}) %collective-permute-start.13) | collective-permute-done | bytes 1056 | tf_op jit(solution)/shard_map/ppermute | solution.py:26
  141.7 1.5 collective-permute-start.14
  143.2 2.1 %collective-permute-done.14 = f32[1,256]{1,0:T(1,128)S(1)} collective-permute-done((f32[1,256]{1,0:T(1,128)S(1)}, f32[1,256]{1,0:T(1,128)S(1)}, u32[]{:S(2)}, u32[]{:S(2)}) %collective-permute-start.14) | collective-permute-done | bytes 1056 | tf_op jit(solution)/shard_map/ppermute | solution.py:26
  145.3 1.5 collective-permute-start.15
  146.8 2.1 %collective-permute-done.15 = f32[1,256]{1,0:T(1,128)S(1)} collective-permute-done((f32[1,256]{1,0:T(1,128)S(1)}, f32[1,256]{1,0:T(1,128)S(1)}, u32[]{:S(2)}, u32[]{:S(2)}) %collective-permute-start.15) | collective-permute-done | bytes 1056 | tf_op jit(solution)/shard_map/ppermute | solution.py:26
  148.9 1.4 broadcast_multiply_fusion.1
  150.3 5.7 %shard_map.70 = (f32[128,4096]{1,0:T(8,128)}, f32[4096,256]{1,0:T(8,128)}, bf16[128,4096]{1,0:T(8,128)(2,1)}) custom-call(s32[1]{0:T(128)} %bitcast.core_ref, f32[128,4096]{1,0:T(8,128)S(1)} %copy-done.1, bf16[128,4096]{1,0:T(8,128)(2,1)S(1)} %copy-done.2, s16[4,528,256]{2,1,0:T(8,128)(2,1)S(1)} %bitcast.19, ...), custom_call_target="tpu_custom_call" | custom-call | flops 1610612736 | bytes 14680064 | tf_op jit(solution)/shard_map/pallas_call | solution.py:212
  (37 shorter events, 0.3 us)
Async XLA Ops:
  7.2 3.7 %copy-start.10 = (s32[8]{0:T(128)S(1)}, s32[8]{0:T(128)}, u32[]{:S(2)}) copy-start(s32[8]{0:T(128)} %param.7) | copy-start | bytes 100
  7.2 33.1 %all-gather.4.cloned.1.call-start = ((), (), s32[]{:S(2)}) async-start(), calls=%async_computation.1 | async-start | bytes 1310720 | tf_op jit(solution)/shard_map/all_gather | solution.py:248
  7.9 98.6 %reduce-scatter.2.cloned.1.call-start = ((), (), s32[]{:S(2)}) async-start(), calls=%async_computation.2 | async-start | bytes 2621440 | tf_op jit(solution)/shard_map/reduce_scatter | solution.py:266
  10.2 33.1 %copy-start.6 = (bf16[128,4096]{1,0:T(8,128)(2,1)}, bf16[128,4096]{1,0:T(8,128)(2,1)S(1)}, u32[]{:S(2)}) copy-start(bf16[128,4096]{1,0:T(8,128)(2,1)S(1)} %get-tuple-element.14) | copy-start | bytes 3145732
  10.3 6.8 %collective-permute-start.1 = (bf16[128,4096]{1,0:T(8,128)(2,1)S(1)}, bf16[128,4096]{1,0:T(8,128)(2,1)S(1)}, u32[]{:S(2)}, u32[]{:S(2)}) collective-permute-start(bf16[128,4096]{1,0:T(8,128)(2,1)S(1)} %get-tuple-element.13), channel_id=1, source_target_pairs={{0,4},{4,0},{8,12},{12,8},{16,20},{20,16},{24,28},{28,24},{1,5},{5... | collective-permute-start | bytes 3145736 | tf_op jit(solution)/shard_map/ppermute | solution.py:242
  10.8 6.3 %collective-permute-start = (bf16[128,4096]{1,0:T(8,128)(2,1)S(1)}, bf16[128,4096]{1,0:T(8,128)(2,1)}, u32[]{:S(2)}, u32[]{:S(2)}) collective-permute-start(bf16[128,4096]{1,0:T(8,128)(2,1)S(1)} %get-tuple-element.14), channel_id=1, source_target_pairs={{0,4},{4,0},{8,12},{12,8},{16,20},{20,16},{24,28},{28,24},{1,5},{5... | collective-permute-start | bytes 3145736 | tf_op jit(solution)/shard_map/ppermute | solution.py:242
  17.1 26.3 %copy-start.8 = (bf16[128,4096]{1,0:T(8,128)(2,1)}, bf16[128,4096]{1,0:T(8,128)(2,1)S(1)}, u32[]{:S(2)}) copy-start(bf16[128,4096]{1,0:T(8,128)(2,1)S(1)} %collective-permute-done.1) | copy-start | bytes 3145732
  43.4 10.3 %copy-start.9 = (bf16[128,4096]{1,0:T(8,128)(2,1)S(1)}, bf16[128,4096]{1,0:T(8,128)(2,1)}, u32[]{:S(2)}) copy-start(bf16[128,4096]{1,0:T(8,128)(2,1)} %copy-done.8) | copy-start | bytes 3145732
  43.4 5.2 %collective-permute-start.2 = (f32[256,128]{0,1:T(8,128)S(1)}, f32[256,128]{0,1:T(8,128)S(1)}, u32[]{:S(2)}, u32[]{:S(2)}) collective-permute-start(f32[256,128]{0,1:T(8,128)S(1)} %slice_add_fusion), channel_id=1, source_target_pairs={{0,1},{1,0},{2,3},{3,2},{4,5},{5,4},{6,7},{7,6},{8,9},{9,8},{10,11... | collective-permute-start | bytes 393224 | tf_op jit(solution)/shard_map/ppermute | solution.py:26
  48.6 5.0 %collective-permute-start.3 = (f32[256,128]{0,1:T(8,128)S(1)}, f32[256,128]{0,1:T(8,128)S(1)}, u32[]{:S(2)}, u32[]{:S(2)}) collective-permute-start(f32[256,128]{0,1:T(8,128)S(1)} %fusion.28), channel_id=1, source_target_pairs={{0,2},{1,3},{2,0},{3,1},{4,6},{5,7},{6,4},{7,5},{8,10},{9,11},{10,... | collective-permute-start | bytes 393224 | tf_op jit(solution)/shard_map/ppermute | solution.py:26
  53.6 1.6 collective-permute-start.4
  56.4 4.7 %copy-start.7 = (f32[256,256]{0,1:T(8,128)}, f32[256,256]{0,1:T(8,128)S(1)}, u32[]{:S(2)}) copy-start(f32[256,256]{0,1:T(8,128)S(1)} %copy.9) | copy-start | bytes 786436
  56.4 1.7 %copy-start = (bf16[256,4096]{1,0:T(8,128)(2,1)S(1)}, bf16[256,4096]{1,0:T(8,128)(2,1)}, u32[]{:S(2)}) copy-start(bf16[256,4096]{1,0:T(8,128)(2,1)} %pad_maximum_fusion.1.low_ref) | copy-start | bytes 6291460
  61.1 89.2 %copy-start.1 = (f32[128,4096]{1,0:T(8,128)S(1)}, f32[128,4096]{1,0:T(8,128)}, u32[]{:S(2)}) copy-start(f32[128,4096]{1,0:T(8,128)} %momentum_ref.1) | copy-start | bytes 6291460
  61.1 89.2 %copy-start.2 = (bf16[128,4096]{1,0:T(8,128)(2,1)S(1)}, bf16[128,4096]{1,0:T(8,128)(2,1)}, u32[]{:S(2)}) copy-start(bf16[128,4096]{1,0:T(8,128)(2,1)} %grad_ref.1) | copy-start | bytes 3145732
  62.9 4.5 %collective-permute-start.5 = (f32[64,256]{1,0:T(8,128)S(1)}, f32[64,256]{1,0:T(8,128)S(1)}, u32[]{:S(2)}, u32[]{:S(2)}) collective-permute-start(f32[64,256]{1,0:T(8,128)S(1)} %constant_dynamic-slice_fusion), channel_id=1, source_target_pairs={{0,8},{4,12},{8,0},{12,4},{16,24},{20,28},{24,16},{28,20},{1,9},{5... | collective-permute-start | bytes 196616 | tf_op jit(solution)/shard_map/ppermute | solution.py:26
  67.5 10.3 %collective-permute-start.6 = (f32[64,256]{1,0:T(8,128)S(1)}, f32[64,256]{1,0:T(8,128)S(1)}, u32[]{:S(2)}, u32[]{:S(2)}) collective-permute-start(f32[64,256]{1,0:T(8,128)S(1)} %fusion.27), channel_id=1, source_target_pairs={{0,16},{4,20},{8,24},{12,28},{16,0},{20,4},{24,8},{28,12},{1,17},{... | collective-permute-start | bytes 196616 | tf_op jit(solution)/shard_map/ppermute | solution.py:26
  79.2 4.3 %collective-permute-start.7 = (f32[64,256]{1,0:T(8,128)S(1)}, f32[64,256]{1,0:T(8,128)S(1)}, u32[]{:S(2)}, u32[]{:S(2)}) collective-permute-start(f32[64,256]{1,0:T(8,128)S(1)} %get-tuple-element.10), channel_id=1, source_target_pairs={{0,1},{1,0},{2,3},{3,2},{4,5},{5,4},{6,7},{7,6},{8,9},{9,8},{10,11... | collective-permute-start | bytes 196616 | tf_op jit(solution)/shard_map/ppermute | solution.py:33
  80.6 5.0 %collective-permute-start.8 = (f32[64,256]{1,0:T(8,128)S(1)}, f32[64,256]{1,0:T(8,128)S(1)}, u32[]{:S(2)}, u32[]{:S(2)}) collective-permute-start(f32[64,256]{1,0:T(8,128)S(1)} %get-tuple-element.10), channel_id=1, source_target_pairs={{0,2},{1,3},{2,0},{3,1},{4,6},{5,7},{6,4},{7,5},{8,10},{9,11},{10,... | collective-permute-start | bytes 196616 | tf_op jit(solution)/shard_map/ppermute | solution.py:33
  82.1 5.2 %collective-permute-start.9 = (f32[64,256]{1,0:T(8,128)S(1)}, f32[64,256]{1,0:T(8,128)S(1)}, u32[]{:S(2)}, u32[]{:S(2)}) collective-permute-start(f32[64,256]{1,0:T(8,128)S(1)} %get-tuple-element.10), channel_id=1, source_target_pairs={{0,3},{1,2},{2,1},{3,0},{4,7},{5,6},{6,5},{7,4},{8,11},{9,10},{10,... | collective-permute-start | bytes 196616 | tf_op jit(solution)/shard_map/ppermute | solution.py:33
  99.6 0.7 copy-start.3
  106.5 0.9 copy-start.4
  107.4 1.0 copy-start.5
  131.0 19.3 %collective-permute-start.10 = (s16[4,528,256]{2,1,0:T(8,128)(2,1)S(1)}, s16[4,528,256]{2,1,0:T(8,128)(2,1)S(1)}, u32[]{:S(2)}, u32[]{:S(2)}) collective-permute-start(s16[4,528,256]{2,1,0:T(8,128)(2,1)S(1)} %bitcast.18), channel_id=1, source_target_pairs={{0,4},{4,0},{8,12},{12,8},{16,20},{20,16},{24,28},{28,24},{1,5},{5... | collective-permute-start | bytes 3244040 | tf_op jit(solution)/shard_map/ppermute | solution.py:242
  131.0 2.7 %collective-permute-start.11 = (f32[1,256]{1,0:T(1,128)S(1)}, f32[1,256]{1,0:T(1,128)S(1)}, u32[]{:S(2)}, u32[]{:S(2)}) collective-permute-start(f32[1,256]{1,0:T(1,128)S(1)} %slice.23), channel_id=1, source_target_pairs={{0,4},{4,0},{8,12},{12,8},{16,20},{20,16},{24,28},{28,24},{1,5},{5... | collective-permute-start | bytes 3080 | tf_op jit(solution)/shard_map/ppermute | solution.py:26
  133.7 3.6 %collective-permute-start.12 = (f32[1,256]{1,0:T(1,128)S(1)}, f32[1,256]{1,0:T(1,128)S(1)}, u32[]{:S(2)}, u32[]{:S(2)}) collective-permute-start(f32[1,256]{1,0:T(1,128)S(1)} %slice_add_fusion.1), channel_id=1, source_target_pairs={{0,8},{4,12},{8,0},{12,4},{16,24},{20,28},{24,16},{28,20},{1,9},{5... | collective-permute-start | bytes 3080 | tf_op jit(solution)/shard_map/ppermute | solution.py:26
  137.3 4.5 %collective-permute-start.13 = (f32[1,256]{1,0:T(1,128)S(1)}, f32[1,256]{1,0:T(1,128)S(1)}, u32[]{:S(2)}, u32[]{:S(2)}) collective-permute-start(f32[1,256]{1,0:T(1,128)S(1)} %add.165), channel_id=1, source_target_pairs={{0,16},{4,20},{8,24},{12,28},{16,0},{20,4},{24,8},{28,12},{1,17},{... | collective-permute-start | bytes 3080 | tf_op jit(solution)/shard_map/ppermute | solution.py:26
  141.7 3.6 %collective-permute-start.14 = (f32[1,256]{1,0:T(1,128)S(1)}, f32[1,256]{1,0:T(1,128)S(1)}, u32[]{:S(2)}, u32[]{:S(2)}) collective-permute-start(f32[1,256]{1,0:T(1,128)S(1)} %add.166), channel_id=1, source_target_pairs={{0,1},{1,0},{2,3},{3,2},{4,5},{5,4},{6,7},{7,6},{8,9},{9,8},{10,11... | collective-permute-start | bytes 3080 | tf_op jit(solution)/shard_map/ppermute | solution.py:26
  145.3 3.6 %collective-permute-start.15 = (f32[1,256]{1,0:T(1,128)S(1)}, f32[1,256]{1,0:T(1,128)S(1)}, u32[]{:S(2)}, u32[]{:S(2)}) collective-permute-start(f32[1,256]{1,0:T(1,128)S(1)} %add.167), channel_id=1, source_target_pairs={{0,2},{1,3},{2,0},{3,1},{4,6},{5,7},{6,4},{7,5},{8,10},{9,11},{10,... | collective-permute-start | bytes 3080 | tf_op jit(solution)/shard_map/ppermute | solution.py:26
Sparse Core Ops, SparseCore 0:
  9.6 30.6 all-gather.3
  61.2 45.1 reduce-scatter.1

commit v3 on v2

--- a/solution.py
+++ b/solution.py
@@ -1,3 +1,4 @@
+import functools
 import math
 
 import jax
@@ -28,9 +29,43 @@
     return x
 
 
+def quad_sum(x, axis, step=1):
+    if lax.axis_size(axis) != 4 * step:
+        return butterfly_sum(x, axis, step)
+    near, far, across = [
+        lax.ppermute(x, axis, [(i, i ^ (k * step)) for i in range(4 * step)]) for k in range(1, 4)
+    ]
+    return (x + near) + (far + across)
+
+
 def gather_list(x, axis):
     n = lax.axis_size(axis)
     return [x] + [lax.ppermute(x, axis, [(i, i ^ k) for i in range(n)]) for k in range(1, n)]
+
+
+def line_gather(chunks):
+    n = lax.axis_size("fsdp")
+    length = n // 2
+    place = lax.axis_index("fsdp") // 2
+    if length > 4:
+        groups = [list(range(0, n, 2)), list(range(1, n, 2))]
+        order = (place - jnp.arange(length)) % length
+        return [jnp.take(lax.all_gather(c, "fsdp", axis_index_groups=groups), order, axis=0) for c in chunks]
+    ups = [(i, i + 2) for i in range(n - 2)]
+    downs = [(i + 2, i) for i in range(n - 2)]
+    from_below, from_above = [list(chunks)], [list(chunks)]
+    for _ in range(length - 1):
+        below, above = from_below[-1], from_above[-1]
+        moved = [(lax.ppermute(b, "fsdp", ups), lax.ppermute(a, "fsdp", downs)) for b, a in zip(below, above)]
+        from_below.append([m[0] for m in moved])
+        from_above.append([m[1] for m in moved])
+    results = []
+    for c, chunk in enumerate(chunks):
+        blocks = [chunk]
+        for k in range(1, length):
+            blocks.append(jnp.where(place >= k, from_below[k][c], from_above[length - k][c]))
+        results.append(blocks)
+    return results
 
 
 def spread(row):
@@ -148,41 +183,51 @@
     return mantissa * jnp.exp2(exponent - 13.0)
 
 
-def encode_kernel(share_ref, inverse_ref, code_ref, squares_ref):
+def encode_kernel(share_ref, inverse_ref, *out_refs):
+    squares_ref, code_refs = out_refs[-1], out_refs[:-1]
     right = dot_rows(share_ref[...], inverse_ref[...])
-    rows, rank = right.shape
     squares_ref[...] = jnp.broadcast_to(jnp.sum(right * right, axis=0, keepdims=True), squares_ref.shape)
-    top = jnp.maximum(jnp.max(jnp.abs(right), axis=0, keepdims=True), 1e-30) * (1.0 / 32766.0)
-    exponent = jnp.floor(jnp.log2(top))
-    mantissa = jnp.floor(top * jnp.exp2(13.0 - exponent)) + 1.0
-    unit = unit_of(exponent, mantissa)
-    code_ref[:rows, :] = jnp.floor(right * (1.0 / unit) + 0.5).astype(jnp.int32).astype(jnp.int16)
-    place = lax.broadcasted_iota(jnp.int32, (HEAD, rank), 0)
-    head = jnp.where(place == 0, exponent, mantissa)
-    code_ref[rows:, :] = head.astype(jnp.int32).astype(jnp.int16)
+    rows = right.shape[0] // len(code_refs)
+    place = lax.broadcasted_iota(jnp.int32, (HEAD, right.shape[1]), 0)
+    for c, code_ref in enumerate(code_refs):
+        part = right[rows * c : rows * (c + 1)]
+        top = jnp.maximum(jnp.max(jnp.abs(part), axis=0, keepdims=True), 1e-28) * (1.0 / 32766.0)
+        exponent = jnp.floor(jnp.log2(top))
+        mantissa = jnp.floor(top * jnp.exp2(13.0 - exponent)) + 1.0
+        scaled = part * (1.0 / unit_of(exponent, mantissa))
+        code_ref[:rows, :] = jnp.floor(scaled + 0.5).astype(jnp.int32).astype(jnp.int16)
+        head = jnp.where(place == 0, exponent, mantissa)
+        code_ref[rows:, :] = head.astype(jnp.int32).astype(jnp.int16)
 
 
 def encode(share, inverse_low):
     rows, rank = share.shape
-    return pl.pallas_call(
+    parts = 2 if rows % 256 == 0 else 1
+    out = pl.pallas_call(
         encode_kernel,
-        out_shape=[
-            jax.ShapeDtypeStruct((rows + HEAD, rank), jnp.int16),
-            jax.ShapeDtypeStruct((TILE, rank), jnp.float32),
-        ],
+        out_shape=[jax.ShapeDtypeStruct((rows // parts + HEAD, rank), jnp.int16)] * parts
+        + [jax.ShapeDtypeStruct((TILE, rank), jnp.float32)],
         compiler_params=pltpu.CompilerParams(vmem_limit_bytes=32 * 1024 * 1024),
         cost_estimate=pl.CostEstimate(flops=12 * rows * rank * rank, bytes_accessed=rows * rank * 6, transcendentals=0),
     )(share, inverse_low)
-
-
-def finish_kernel(
-    core_ref, momentum_ref, grad_ref, mine_ref, other_ref, high_ref, low_ref, scale_ref, next_ref, basis_ref, update_ref
-):
-    code = jnp.where(pl.program_id(0) == 0, mine_ref[...].astype(jnp.int32), other_ref[...].astype(jnp.int32))
-    code = code.astype(jnp.float32)
-    share = code.shape[1] - HEAD
-    right = code[:, :share] * unit_of(code[:, share : share + 1], code[:, share + 1 : share + 2])
-    right = right.reshape(basis_ref.shape)
+    return out[:-1], out[-1]
+
+
+def finish_kernel(parts, pieces, column_ref, momentum_ref, grad_ref, high_ref, low_ref, scale_ref, *refs):
+    code_refs, (next_ref, basis_ref, update_ref, right_ref) = refs[: parts * pieces], refs[parts * pieces :]
+    rank = basis_ref.shape[1]
+    for piece in range(pieces):
+
+        @pl.when(pl.program_id(0) == piece)
+        def _():
+            for c, code_ref in enumerate(code_refs[parts * piece : parts * (piece + 1)]):
+                code = code_ref[...].astype(jnp.int32).astype(jnp.float32)
+                share = code.shape[1] - HEAD
+                decoded = code[:, :share] * unit_of(code[:, share : share + 1], code[:, share + 1 : share + 2])
+                size = code.shape[0] * share
+                right_ref[size * c : size * (c + 1), :] = decoded.reshape(size, rank)
+
+    right = right_ref[...]
     basis_ref[...] = right * scale_ref[...]
     right_high, right_low = halves(right)
 
@@ -196,37 +241,34 @@
     update_ref[...] = both[rows:].astype(jnp.bfloat16)
 
 
-def finish(core, momentum, grad, mine, other, factors, scale):
+def finish(momentum, grad, codes, columns, factors, scale):
     rows, cols = momentum.shape
-    shares, share, rank = mine.shape
-    share -= HEAD
-    group = max(1, min(512 // share, shares))
-    block, steps = group * share, shares // group
+    pieces, parts, rank = len(codes), len(codes[0]), scale.shape[1]
+    block = cols // pieces
     high, low = split_two(factors)
-    column = lambda a, i, core: (a ^ core[0]) * steps + i
-    wide = lambda: pl.BlockSpec((rows, block), lambda a, i, core: (0, column(a, i, core)))
-    tall = lambda: pl.BlockSpec((block, rank), lambda a, i, core: (column(a, i, core), 0))
-    whole = lambda x: pl.BlockSpec(x.shape, lambda a, i, core: (0, 0))
-    first = pl.BlockSpec((group, share + HEAD, rank), lambda a, i, core: (jnp.where(a == 0, i, steps - 1), 0, 0))
-    second = pl.BlockSpec((group, share + HEAD, rank), lambda a, i, core: (jnp.where(a == 0, 0, i), 0, 0))
+    wide = lambda: pl.BlockSpec((rows, block), lambda i, column: (0, column[i]))
+    tall = lambda: pl.BlockSpec((block, rank), lambda i, column: (column[i], 0))
+    whole = lambda x: pl.BlockSpec(x.shape, lambda i, column: (0,) * x.ndim)
+    flat = [c for piece in codes for c in piece]
     return pl.pallas_call(
-        finish_kernel,
+        functools.partial(finish_kernel, parts, pieces),
         grid_spec=pltpu.PrefetchScalarGridSpec(
             num_scalar_prefetch=1,
-            grid=(2, steps),
-            in_specs=[wide(), wide(), first, second, whole(high), whole(low), whole(scale)],
+            grid=(pieces,),
+            in_specs=[wide(), wide(), whole(high), whole(low), whole(scale)] + [whole(c) for c in flat],
             out_specs=[wide(), tall(), wide()],
+            scratch_shapes=[pltpu.VMEM((block, rank), jnp.float32)],
         ),
         out_shape=[
             jax.ShapeDtypeStruct((rows, cols), jnp.float32),
             jax.ShapeDtypeStruct((cols, rank), jnp.float32),
             jax.ShapeDtypeStruct((rows, cols), jnp.bfloat16),
         ],
-        compiler_params=pltpu.CompilerParams(vmem_limit_bytes=32 * 1024 * 1024),
+        compiler_params=pltpu.CompilerParams(vmem_limit_bytes=40 * 1024 * 1024),
         cost_estimate=pl.CostEstimate(
             flops=6 * 2 * rows * cols * rank, bytes_accessed=rows * cols * 12 + cols * rank * 8, transcendentals=0
         ),
-    )(core, momentum, grad, mine, other, high, low, scale)
+    )(columns, momentum, grad, high, low, scale, *flat)
 
 
 def on_device(momentum, grad, q_stored, perm):
@@ -245,7 +287,10 @@
     pair_high = jnp.concatenate([comb_high, swap(comb_high)], axis=0)
     pair_low = jnp.concatenate([comb_low, swap(comb_low)], axis=0)
 
-    basis = lax.all_gather(q_stored, "fsdp", axis=0, tiled=True, axis_index_groups=lines)
+    parts = 2 if block_rows % 32 == 0 else 1
+    chunk_rows = block_rows // parts
+    chunks = line_gather([q_stored[chunk_rows * c : chunk_rows * (c + 1)] for c in range(parts)])
+    basis = jnp.concatenate([jnp.concatenate(list(blocks), axis=0) for blocks in chunks], axis=0)
     product = lax.dot_general(
         jnp.concatenate([pair_high, pair_low], axis=0),
         basis,
@@ -257,9 +302,13 @@
     other = jnp.concatenate([other[rows:], other[:rows]], axis=0)
     blocks = jnp.arange(num_blocks, dtype=jnp.int32)
     inverse = jnp.sum(jnp.where(perm[:, None] == blocks[None, :], blocks[:, None], 0), axis=0)
-    inverse = ((inverse % 2) ^ core) * (num_blocks // 2) + inverse // 2
+    line = num_blocks // 2
     row_ids = jnp.arange(rank_total, dtype=jnp.int32)
-    order_index = inverse[row_ids // block_rows] * block_rows + row_ids % block_rows
+    source = inverse[row_ids // block_rows]
+    within = row_ids % block_rows
+    away = (lax.axis_index("fsdp") // 2 - source // 2) % line
+    order_index = ((source % 2) ^ core) * (rank_total // 2)
+    order_index += (within // chunk_rows * line + away) * chunk_rows + within % chunk_rows
     projected = jnp.take(jnp.concatenate([mine, other], axis=1), order_index, axis=1)
 
     mixed = mix(core.reshape(1), pair_high, pair_low, projected)
@@ -276,14 +325,26 @@
     inverse_low = factor_inverse(gram)
 
     orthonormal = dot_rows(projected[:rows], inverse_low)
-    code, squares = encode(mixed_share, inverse_low)
-    codes = lax.all_gather(code, "fsdp", axis=0, axis_index_groups=lines)
-    squares = butterfly_sum(butterfly_sum(squares[:1], "fsdp"), "tp")
+    codes, squares = encode(mixed_share, inverse_low)
+    squares = quad_sum(quad_sum(squares[:1], "tp"), "fsdp", 2)
+    squares = squares + swap(squares)
     scale = lax.rsqrt(squares / col_total + EPSILON)
     factors = jnp.concatenate(
         [-KEEP_SHARE * orthonormal, math.sqrt(row_total / rank_total) * orthonormal * scale], axis=0
     )
-    return tuple(finish(core.reshape(1), momentum, grad, codes, swap(codes), factors, scale))
+
+    place = lax.axis_index("fsdp") // 2
+    if line > 4:
+        gathered = lax.all_gather(codes[0], "fsdp", axis_index_groups=lines)
+        count = max(1, mixed.shape[0] // 512)
+        mine = [[x] for x in jnp.split(gathered, count, axis=0)]
+        spots = list(range(count))
+    else:
+        mine = [[x[None] for x in blocks] for blocks in zip(*line_gather(codes))]
+        spots = [(place - k) % line for k in range(line)]
+    other = [[swap(x) for x in blocks] for blocks in mine]
+    columns = [core * len(spots) + spot for spot in spots] + [(1 - core) * len(spots) + spot for spot in spots]
+    return tuple(finish(momentum, grad, mine + other, jnp.stack(columns).astype(jnp.int32), factors, scale))
 
 
 def solution(mesh):

time: 163 us -> 220 us (1.35)
  starting transfers between devices: 15.8 us -> 93.1 us
  blocking collectives: 21.7 us -> 0 us
  waiting for transfers between devices: 63.1 us -> 46.6 us
  other arithmetic: 11.8 us -> 22.3 us
  local copies, waits for them, and re-layouts: 8.82 us -> 14.5 us
    ppermute x0 -> x30, starting transfers between devices: none -> 77.7 us  [the longest x12 54.3 us: line_gather(): lax.ppermute(b, 'fsdp', ups)]
    all_gather x1 -> x0, waiting for transfers between devices: 23.2 us -> none  [on_device(): lax.all_gather(q_stored, 'fsdp', axis=0, tiled=True, axis_index_groups=li...]
    ppermute x0 -> x30, waiting for transfers between devices: none -> 22 us  [the longest x12 13 us: line_gather(): lax.ppermute(a, 'fsdp', downs)]
    all_gather x1 -> x0, blocking collectives: 21.7 us -> none  [on_device(): codes = lax.all_gather(code, 'fsdp', axis=0, axis_index_groups=lines)]
    ppermute x9 -> x4, waiting for transfers between devices: 29.7 us -> 14.9 us  [butterfly_sum(): x = x + lax.ppermute(x, axis, [(i, i ^ step) for i in range(n)])]
    unnamed x0 -> x5, other arithmetic: none -> 5.27 us
    unnamed x22 -> x29, local copies, waits for them, and re-layouts: 4.38 us -> 7.77 us
    slice x1 -> x2, local copies, waits for them, and re-layouts: 0.01 us -> 2.26 us  [the longest x1 1.69 us: on_device(): q_stored[chunk_rows * c:chunk_rows * (c + 1)]]
  transfers between devices with their start and end apart: 18 -> 50, of which waited for: 14 -> 18; matrix products, arithmetic and copies ran while one was open for 11% -> 13% of each run, Pallas kernels for 7% -> 5%
where the time goes in v3:
time: 220 us; the launch traced here: 219 us
  starting transfers between devices  93.1 us (42%)
  waiting for transfers between devices  46.6 us (21%)
  other arithmetic  22.3 us (10%)
  Pallas kernels  21.6 us (10%)
  between operations  14.8 us (7%)
  local copies, waits for them, and re-layouts  14.5 us (7%)
  matrix products  6.25 us (3%)
    ppermute x12, starting transfers between devices, line_gather(): lax.ppermute(b, 'fsdp', ups)  54.3 us
    ppermute x12, starting transfers between devices, line_gather(): lax.ppermute(a, 'fsdp', downs)  15.4 us
    ppermute x4, waiting for transfers between devices, butterfly_sum(): x = x + lax.ppermute(x, axis, [(i, i ^ step) for i in range(n)])  14.9 us
    ppermute x12, waiting for transfers between devices, line_gather(): lax.ppermute(a, 'fsdp', downs)  13 us
    pallas_call x1, Pallas kernels, factor_inverse(): pl.pallas_call(factor_kernel, out_shape=jax.ShapeDtypeStruct((rank, rank)...  11.6 us
    ppermute x4, starting transfers between devices, butterfly_sum(): x = x + lax.ppermute(x, axis, [(i, i ^ step) for i in range(n)])  10.3 us
    ppermute x6, starting transfers between devices, quad_sum(): lax.ppermute(x, axis, [(i, i ^ k * step) for i in range(4 * step)])  7.88 us
    unnamed x29, local copies, waits for them, and re-layouts  7.77 us
  transfers between devices with their start and end apart: 50, of which 18 were waited for; matrix products, arithmetic and copies ran while one was open for 13% of the time, Pallas kernels for 5%

profile of v3, /device:TPU:0, one launch (start us, length us, event | category | flops | bytes accessed | tf_op | source)
XLA Modules:
  0.0 219.1 jit_solution(4374178571867426373)
XLA Ops:
  7.2 1.7 fusion.29
  8.9 1.3 collective-permute-start.9
  10.2 6.2 %collective-permute-start.8 = (bf16[16,4096]{1,0:T(8,128)(2,1)}, bf16[16,4096]{1,0:T(8,128)(2,1)}, u32[]{:S(2)}, u32[]{:S(2)}) collective-permute-start(bf16[16,4096]{1,0:T(8,128)(2,1)} %get-tuple-element.19), channel_id=1, source_target_pairs={{0,8},{4,12},{8,16},{12,20},{16,24},{20,28},{1,9},{5,13},{9,17},{1... | collective-permute-start | bytes 393224 | tf_op jit(solution)/shard_map/ppermute | solution.py:59
  16.4 1.3 collective-permute-start.3
  17.7 5.2 %collective-permute-start.2 = (bf16[16,4096]{1,0:T(8,128)(2,1)S(1)}, bf16[16,4096]{1,0:T(8,128)(2,1)}, u32[]{:S(2)}, u32[]{:S(2)}) collective-permute-start(bf16[16,4096]{1,0:T(8,128)(2,1)S(1)} %get-tuple-element.21), channel_id=1, source_target_pairs={{0,8},{4,12},{8,16},{12,20},{16,24},{20,28},{1,9},{5,13},{9,17},{1... | collective-permute-start | bytes 393224 | tf_op jit(solution)/shard_map/ppermute | solution.py:59
  22.9 2.3 %reduce-precision_convert_fusion = (bf16[128,4096]{1,0:T(8,128)(2,1)S(1)}, bf16[128,4096]{1,0:T(8,128)(2,1)S(1)}) fusion(f32[128,4096]{1,0:T(8,128)} %momentum_ref.1, bf16[128,4096]{1,0:T(8,128)(2,1)} %grad_ref.1), kind=kLoop, calls=%fused_computation.10 | loop fusion | flops 3145728 | bytes 5242880 | tf_op jit(solution)/shard_map/convert_element_type | solution.py:21
  25.4 1.3 collective-permute-start.4
  27.4 4.5 %compare_select_fusion.4 = s32[256,1]{0,1:T(1,128)S(1)} fusion(s32[]{:T(128)} %bitcast.9, s32[]{:T(128)} %bitcast.10, s32[]{:T(128)} %bitcast.11, s32[]{:T(128)} %bitcast.12, s32[]{:T(128)} %bitcast.13, s32[]{:T(128)} %bitcast.15, s32[]{:T(128)} %bitcast.14), kind=kLoop, calls=%fused_computation.52 | loop fusion | flops 5888 | bytes 1052 | tf_op jit(solution)/shard_map/gather | solution.py:307
  31.9 1.3 collective-permute-start.10
  33.2 5.2 %collective-permute-start.12 = (bf16[16,4096]{1,0:T(8,128)(2,1)}, bf16[16,4096]{1,0:T(8,128)(2,1)S(1)}, u32[]{:S(2)}, u32[]{:S(2)}) collective-permute-start(bf16[16,4096]{1,0:T(8,128)(2,1)} %collective-permute-done.8), channel_id=1, source_target_pairs={{0,8},{4,12},{8,16},{12,20},{16,24},{20,28},{1,9},{5,13},{9,17},{1... | collective-permute-start | bytes 393224 | tf_op jit(solution)/shard_map/ppermute | solution.py:59
  38.4 3.9 %collective-permute-start.6 = (bf16[16,4096]{1,0:T(8,128)(2,1)}, bf16[16,4096]{1,0:T(8,128)(2,1)S(1)}, u32[]{:S(2)}, u32[]{:S(2)}) collective-permute-start(bf16[16,4096]{1,0:T(8,128)(2,1)} %collective-permute-done.2), channel_id=1, source_target_pairs={{0,8},{4,12},{8,16},{12,20},{16,24},{20,28},{1,9},{5,13},{9,17},{1... | collective-permute-start | bytes 393224 | tf_op jit(solution)/shard_map/ppermute | solution.py:59
  42.4 1.3 collective-permute-start.5
  44.4 1.3 collective-permute-start.11
  45.7 5.2 %collective-permute-start.13 = (bf16[16,4096]{1,0:T(8,128)(2,1)S(1)}, bf16[16,4096]{1,0:T(8,128)(2,1)S(1)}, u32[]{:S(2)}, u32[]{:S(2)}) collective-permute-start(bf16[16,4096]{1,0:T(8,128)(2,1)S(1)} %collective-permute-done.12), channel_id=1, source_target_pairs={{0,8},{4,12},{8,16},{12,20},{16,24},{20,28},{1,9},{5,13},{9,17},{1... | collective-permute-start | bytes 393224 | tf_op jit(solution)/shard_map/ppermute | solution.py:59
  50.9 3.9 %collective-permute-start.7 = (bf16[16,4096]{1,0:T(8,128)(2,1)S(1)}, bf16[16,4096]{1,0:T(8,128)(2,1)S(1)}, u32[]{:S(2)}, u32[]{:S(2)}) collective-permute-start(bf16[16,4096]{1,0:T(8,128)(2,1)S(1)} %collective-permute-done.6), channel_id=1, source_target_pairs={{0,8},{4,12},{8,16},{12,20},{16,24},{20,28},{1,9},{5,13},{9,17},{1... | collective-permute-start | bytes 393224 | tf_op jit(solution)/shard_map/ppermute | solution.py:59
  55.6 1.6 select_dynamic-update-slice_fusion.4
  57.7 1.6 select_dynamic-update-slice_fusion.3
  61.3 1.6 select_dynamic-update-slice_fusion
  62.9 3.1 %fusion = f32[512,128]{0,1:T(8,128)S(1)} fusion(bf16[128,4096]{1,0:T(8,128)(2,1)} %select_dynamic-update-slice_fusion, bf16[128,4096]{1,0:T(8,128)(2,1)S(1)} %collective-permute-done.1, bf16[128,4096]{1,0:T(8,128)(2,1)S(1)} %get-tuple-element.16, bf16[128,4096]{1,0:T(8,128)(2,1)S(1)} %collective-permute-done, bf16[128,4096]{1,0:T(8,128)(2,1)S(1)} %get-tuple-element.15), kind=kOutput, calls=%fused_computation.1 | convolution fusion | flops 553648128 | bytes 5505024 | tf_op jit(solution)/shard_map/dot_general | solution.py:294
  66.1 2.0 collective-permute-start.14
  68.2 3.0 %collective-permute-done.14 = f32[256,128]{0,1:T(8,128)S(1)} collective-permute-done((f32[256,128]{0,1:T(8,128)S(1)}, f32[256,128]{0,1:T(8,128)S(1)}, u32[]{:S(2)}, u32[]{:S(2)}) %collective-permute-start.14) | collective-permute-done | bytes 131104 | tf_op jit(solution)/shard_map/ppermute | solution.py:27
  71.2 2.0 collective-permute-start.15
  73.2 1.7 pad_maximum_fusion.high_ref
  75.0 1.2 collective-permute-done.15
  76.3 1.5 pad_maximum_fusion.1.low_ref
  79.6 1.6 copy-done
  81.2 3.0 %shard_map.68 = f32[2048,256]{1,0:T(8,128)} custom-call(s32[1]{0:T(128)} %bitcast.20.core_ref, bf16[256,4096]{1,0:T(8,128)(2,1)S(1)} %pad_maximum_fusion.high_ref, bf16[256,4096]{1,0:T(8,128)(2,1)S(1)} %copy-done, f32[256,256]{1,0:T(8,128)S(1)} %select_bitcast_fusion.proj_ref), custom_call_target="tpu_custom_call" | custom-call | flops 805306368 | bytes 4194304 | tf_op jit(solution)/shard_map/pallas_call | solution.py:166
  84.3 1.8 fusion.10
  86.1 3.4 %collective-permute-start.17 = (f32[64,256]{1,0:T(8,128)S(1)}, f32[64,256]{1,0:T(8,128)S(1)}, u32[]{:S(2)}, u32[]{:S(2)}) collective-permute-start(f32[64,256]{1,0:T(8,128)S(1)} %constant_dynamic-slice_fusion), channel_id=1, source_target_pairs={{0,8},{4,12},{8,0},{12,4},{16,24},{20,28},{24,16},{28,20},{1,9},{5... | collective-permute-start | bytes 196616 | tf_op jit(solution)/shard_map/ppermute | solution.py:27
  89.5 2.8 %collective-permute-done.17 = f32[64,256]{1,0:T(8,128)S(1)} collective-permute-done((f32[64,256]{1,0:T(8,128)S(1)}, f32[64,256]{1,0:T(8,128)S(1)}, u32[]{:S(2)}, u32[]{:S(2)}) %collective-permute-start.17) | collective-permute-done | bytes 65568 | tf_op jit(solution)/shard_map/ppermute | solution.py:27
  92.3 2.8 %collective-permute-start.18 = (f32[64,256]{1,0:T(8,128)S(1)}, f32[64,256]{1,0:T(8,128)S(1)}, u32[]{:S(2)}, u32[]{:S(2)}) collective-permute-start(f32[64,256]{1,0:T(8,128)S(1)} %fusion.34), channel_id=1, source_target_pairs={{0,16},{4,20},{8,24},{12,28},{16,0},{20,4},{24,8},{28,12},{1,17},{... | collective-permute-start | bytes 196616 | tf_op jit(solution)/shard_map/ppermute | solution.py:27
  95.2 7.9 %collective-permute-done.18 = f32[64,256]{1,0:T(8,128)S(1)} collective-permute-done((f32[64,256]{1,0:T(8,128)S(1)}, f32[64,256]{1,0:T(8,128)S(1)}, u32[]{:S(2)}, u32[]{:S(2)}) %collective-permute-start.18) | collective-permute-done | bytes 65568 | tf_op jit(solution)/shard_map/ppermute | solution.py:27
  104.4 1.7 collective-permute-start.19
  106.1 1.5 collective-permute-start.20
  109.3 1.8 collective-permute-done.20
  111.7 1.1 collective-permute-done.21
  113.4 11.6 %shard_map.67.inverse_ref = f32[256,256]{1,0:T(8,128)S(1)} custom-call(f32[256,256]{1,0:T(8,128)} %constant_dynamic-update-slice_fusion.5.gram_ref), custom_call_target="tpu_custom_call" | custom-call | flops 201326592 | bytes 524288 | tf_op jit(solution)/shard_map/pallas_call | solution.py:133
  125.7 6.1 %reduce-scatter.2.cloned.1.call-done.share_ref = f32[512,256]{1,0:T(8,128)} async-done(((f32[2048,256]{1,0:T(8,128)}), f32[512,256]{1,0:T(8,128)}) %reduce-scatter.2.cloned.1.call-update) | async-done | bytes 524304 | tf_op jit(solution)/shard_map/reduce_scatter | solution.py:315
  135.8 1.5 collective-permute-start.23
  137.3 1.5 collective-permute-start.24
  139.7 2.4 %collective-permute-done.24 = f32[1,256]{1,0:T(1,128)} collective-permute-done((f32[1,256]{1,0:T(1,128)}, f32[1,256]{1,0:T(1,128)}, u32[]{:S(2)}, u32[]{:S(2)}) %collective-permute-start.24) | collective-permute-done | bytes 1056 | tf_op jit(solution)/shard_map/ppermute | solution.py:36
  142.7 1.2 add_add_fusion.1
  143.9 1.7 collective-permute-start.27
  145.7 1.5 collective-permute-start.26
  147.2 1.1 collective-permute-start.25
  148.3 1.3 collective-permute-start.30
  149.6 5.2 %collective-permute-start.29 = (s16[272,256]{1,0:T(8,128)(2,1)S(1)}, s16[272,256]{1,0:T(8,128)(2,1)}, u32[]{:S(2)}, u32[]{:S(2)}) collective-permute-start(s16[272,256]{1,0:T(8,128)(2,1)S(1)} %get-tuple-element.7), channel_id=1, source_target_pairs={{0,8},{4,12},{8,16},{12,20},{16,24},{20,28},{1,9},{5,13},{9,17},{1... | collective-permute-start | bytes 417800 | tf_op jit(solution)/shard_map/ppermute | solution.py:59
  156.2 1.3 collective-permute-start.34
  157.5 4.6 %collective-permute-start.33 = (s16[272,256]{1,0:T(8,128)(2,1)}, s16[272,256]{1,0:T(8,128)(2,1)S(1)}, u32[]{:S(2)}, u32[]{:S(2)}) collective-permute-start(s16[272,256]{1,0:T(8,128)(2,1)} %copy-done.6), channel_id=1, source_target_pairs={{0,8},{4,12},{8,16},{12,20},{16,24},{20,28},{1,9},{5,13},{9,17},{1... | collective-permute-start | bytes 417800 | tf_op jit(solution)/shard_map/ppermute | solution.py:59
  162.2 1.3 collective-permute-start.31
  163.5 4.6 %collective-permute-start.37 = (s16[272,256]{1,0:T(8,128)(2,1)}, s16[272,256]{1,0:T(8,128)(2,1)S(1)}, u32[]{:S(2)}, u32[]{:S(2)}) collective-permute-start(s16[272,256]{1,0:T(8,128)(2,1)} %collective-permute-done.29), channel_id=1, source_target_pairs={{0,8},{4,12},{8,16},{12,20},{16,24},{20,28},{1,9},{5,13},{9,17},{1... | collective-permute-start | bytes 417800 | tf_op jit(solution)/shard_map/ppermute | solution.py:59
  168.8 1.3 collective-permute-start.35
  170.3 4.4 %collective-permute-start.38 = (s16[272,256]{1,0:T(8,128)(2,1)S(1)}, s16[272,256]{1,0:T(8,128)(2,1)S(1)}, u32[]{:S(2)}, u32[]{:S(2)}) collective-permute-start(s16[272,256]{1,0:T(8,128)(2,1)S(1)} %collective-permute-done.33), channel_id=1, source_target_pairs={{0,8},{4,12},{8,16},{12,20},{16,24},{20,28},{1,9},{5,13},{9,17},{1... | collective-permute-start | bytes 417800 | tf_op jit(solution)/shard_map/ppermute | solution.py:59
  174.8 1.9 collective-permute-done.35
  176.8 1.3 collective-permute-start.32
  178.2 5.7 %collective-permute-done.32 = s16[272,256]{1,0:T(8,128)(2,1)S(1)} collective-permute-done((s16[272,256]{1,0:T(8,128)(2,1)S(1)}, s16[272,256]{1,0:T(8,128)(2,1)S(1)}, u32[]{:S(2)}, u32[]{:S(2)}) %collective-permute-start.32) | collective-permute-done | bytes 139296 | tf_op jit(solution)/shard_map/ppermute | solution.py:59
  183.9 2.2 collective-permute-start.39
  186.1 2.5 %collective-permute-done.39 = s16[272,256]{1,0:T(8,128)(2,1)S(1)} collective-permute-done((s16[272,256]{1,0:T(8,128)(2,1)S(1)}, s16[272,256]{1,0:T(8,128)(2,1)S(1)}, u32[]{:S(2)}, u32[]{:S(2)}) %collective-permute-start.39) | collective-permute-done | bytes 139296 | tf_op jit(solution)/shard_map/ppermute | solution.py:59
  188.6 1.3 collective-permute-start.36
  190.9 5.1 %collective-permute-done.36 = s16[272,256]{1,0:T(8,128)(2,1)S(1)} collective-permute-done((s16[272,256]{1,0:T(8,128)(2,1)S(1)}, s16[272,256]{1,0:T(8,128)(2,1)S(1)}, u32[]{:S(2)}, u32[]{:S(2)}) %collective-permute-start.36) | collective-permute-done | bytes 139296 | tf_op jit(solution)/shard_map/ppermute | solution.py:59
  196.0 3.9 %collective-permute-start.40 = (s16[272,256]{1,0:T(8,128)(2,1)S(1)}, s16[272,256]{1,0:T(8,128)(2,1)S(1)}, u32[]{:S(2)}, u32[]{:S(2)}) collective-permute-start(s16[272,256]{1,0:T(8,128)(2,1)S(1)} %collective-permute-done.38), channel_id=1, source_target_pairs={{0,8},{4,12},{8,16},{12,20},{16,24},{20,28},{1,9},{5,13},{9,17},{1... | collective-permute-start | bytes 417800 | tf_op jit(solution)/shard_map/ppermute | solution.py:59
  200.0 2.5 %collective-permute-done.40 = s16[272,256]{1,0:T(8,128)(2,1)S(1)} collective-permute-done((s16[272,256]{1,0:T(8,128)(2,1)S(1)}, s16[272,256]{1,0:T(8,128)(2,1)S(1)}, u32[]{:S(2)}, u32[]{:S(2)}) %collective-permute-start.40) | collective-permute-done | bytes 139296 | tf_op jit(solution)/shard_map/ppermute | solution.py:59
  203.7 1.3 broadcast_multiply_fusion.1
  206.0 6.2 %shard_map.70 = (f32[128,4096]{1,0:T(8,128)}, f32[4096,256]{1,0:T(8,128)}, bf16[128,4096]{1,0:T(8,128)(2,1)}) custom-call(s32[8]{0:T(128)S(1)} %stack.35.column_ref, f32[128,4096]{1,0:T(8,128)S(1)} %copy-done.1, bf16[128,4096]{1,0:T(8,128)(2,1)S(1)} %copy-done.2, bf16[256,256]{1,0:T(8,128)(2,1)S(1)} %get-tuple-element.18.high_ref, ...), custom_call_target="tpu_custom_call" | custom-call | flops 1610612736 | bytes 14680064 | tf_op jit(solution)/shard_map/pallas_call | solution.py:253
  (117 shorter events, 23.2 us)
Async XLA Ops:
  7.2 52.1 %copy-start.11 = (bf16[32,4096]{1,0:T(8,128)(2,1)S(1)}, bf16[32,4096]{1,0:T(8,128)(2,1)}, u32[]{:S(2)}) copy-start(bf16[32,4096]{1,0:T(8,128)(2,1)} %param.6) | copy-start | bytes 786436
  7.2 18.1 %copy-start.13 = (s32[8]{0:T(128)S(1)}, s32[8]{0:T(128)}, u32[]{:S(2)}) copy-start(s32[8]{0:T(128)} %param.7) | copy-start | bytes 100
  7.2 124.7 %reduce-scatter.2.cloned.1.call-start = ((), (), s32[]{:S(2)}) async-start(), calls=%async_computation.1 | async-start | bytes 2621440 | tf_op jit(solution)/shard_map/reduce_scatter | solution.py:315
  8.9 23.0 %collective-permute-start.9 = (bf16[16,4096]{1,0:T(8,128)(2,1)}, bf16[16,4096]{1,0:T(8,128)(2,1)}, u32[]{:S(2)}, u32[]{:S(2)}) collective-permute-start(bf16[16,4096]{1,0:T(8,128)(2,1)} %get-tuple-element.19), channel_id=1, source_target_pairs={{8,0},{12,4},{16,8},{20,12},{24,16},{28,20},{9,1},{13,5},{17,9},{2... | collective-permute-start | bytes 393224 | tf_op jit(solution)/shard_map/ppermute | solution.py:59
  10.2 23.0 %collective-permute-start.8 = (bf16[16,4096]{1,0:T(8,128)(2,1)}, bf16[16,4096]{1,0:T(8,128)(2,1)}, u32[]{:S(2)}, u32[]{:S(2)}) collective-permute-start(bf16[16,4096]{1,0:T(8,128)(2,1)} %get-tuple-element.19), channel_id=1, source_target_pairs={{0,8},{4,12},{8,16},{12,20},{16,24},{20,28},{1,9},{5,13},{9,17},{1... | collective-permute-start | bytes 393224 | tf_op jit(solution)/shard_map/ppermute | solution.py:59
  16.4 9.0 %collective-permute-start.3 = (bf16[16,4096]{1,0:T(8,128)(2,1)S(1)}, bf16[16,4096]{1,0:T(8,128)(2,1)}, u32[]{:S(2)}, u32[]{:S(2)}) collective-permute-start(bf16[16,4096]{1,0:T(8,128)(2,1)S(1)} %get-tuple-element.21), channel_id=1, source_target_pairs={{8,0},{12,4},{16,8},{20,12},{24,16},{28,20},{9,1},{13,5},{17,9},{2... | collective-permute-start | bytes 393224 | tf_op jit(solution)/shard_map/ppermute | solution.py:59
  17.7 20.7 %collective-permute-start.2 = (bf16[16,4096]{1,0:T(8,128)(2,1)S(1)}, bf16[16,4096]{1,0:T(8,128)(2,1)}, u32[]{:S(2)}, u32[]{:S(2)}) collective-permute-start(bf16[16,4096]{1,0:T(8,128)(2,1)S(1)} %get-tuple-element.21), channel_id=1, source_target_pairs={{0,8},{4,12},{8,16},{12,20},{16,24},{20,28},{1,9},{5,13},{9,17},{1... | collective-permute-start | bytes 393224 | tf_op jit(solution)/shard_map/ppermute | solution.py:59
  25.2 40.9 %copy-start.8 = (bf16[128,4096]{1,0:T(8,128)(2,1)}, bf16[128,4096]{1,0:T(8,128)(2,1)S(1)}, u32[]{:S(2)}) copy-start(bf16[128,4096]{1,0:T(8,128)(2,1)S(1)} %get-tuple-element.15) | copy-start | bytes 3145732
  25.2 37.7 %collective-permute-start = (bf16[128,4096]{1,0:T(8,128)(2,1)S(1)}, bf16[128,4096]{1,0:T(8,128)(2,1)S(1)}, u32[]{:S(2)}, u32[]{:S(2)}) collective-permute-start(bf16[128,4096]{1,0:T(8,128)(2,1)S(1)} %get-tuple-element.15), channel_id=1, source_target_pairs={{0,4},{4,0},{8,12},{12,8},{16,20},{20,16},{24,28},{28,24},{1,5},{5... | collective-permute-start | bytes 3145736 | tf_op jit(solution)/shard_map/ppermute | solution.py:284
  25.4 17.0 %collective-permute-start.4 = (bf16[16,4096]{1,0:T(8,128)(2,1)}, bf16[16,4096]{1,0:T(8,128)(2,1)}, u32[]{:S(2)}, u32[]{:S(2)}) collective-permute-start(bf16[16,4096]{1,0:T(8,128)(2,1)} %collective-permute-done.3), channel_id=1, source_target_pairs={{8,0},{12,4},{16,8},{20,12},{24,16},{28,20},{9,1},{13,5},{17,9},{2... | collective-permute-start | bytes 393224 | tf_op jit(solution)/shard_map/ppermute | solution.py:59
  31.9 12.4 %collective-permute-start.10 = (bf16[16,4096]{1,0:T(8,128)(2,1)}, bf16[16,4096]{1,0:T(8,128)(2,1)S(1)}, u32[]{:S(2)}, u32[]{:S(2)}) collective-permute-start(bf16[16,4096]{1,0:T(8,128)(2,1)} %collective-permute-done.9), channel_id=1, source_target_pairs={{8,0},{12,4},{16,8},{20,12},{24,16},{28,20},{9,1},{13,5},{17,9},{2... | collective-permute-start | bytes 393224 | tf_op jit(solution)/shard_map/ppermute | solution.py:59
  33.2 11.2 %collective-permute-start.12 = (bf16[16,4096]{1,0:T(8,128)(2,1)}, bf16[16,4096]{1,0:T(8,128)(2,1)S(1)}, u32[]{:S(2)}, u32[]{:S(2)}) collective-permute-start(bf16[16,4096]{1,0:T(8,128)(2,1)} %collective-permute-done.8), channel_id=1, source_target_pairs={{0,8},{4,12},{8,16},{12,20},{16,24},{20,28},{1,9},{5,13},{9,17},{1... | collective-permute-start | bytes 393224 | tf_op jit(solution)/shard_map/ppermute | solution.py:59
  38.4 7.3 %collective-permute-start.6 = (bf16[16,4096]{1,0:T(8,128)(2,1)}, bf16[16,4096]{1,0:T(8,128)(2,1)S(1)}, u32[]{:S(2)}, u32[]{:S(2)}) collective-permute-start(bf16[16,4096]{1,0:T(8,128)(2,1)} %collective-permute-done.2), channel_id=1, source_target_pairs={{0,8},{4,12},{8,16},{12,20},{16,24},{20,28},{1,9},{5,13},{9,17},{1... | collective-permute-start | bytes 393224 | tf_op jit(solution)/shard_map/ppermute | solution.py:59
  42.4 8.5 %collective-permute-start.5 = (bf16[16,4096]{1,0:T(8,128)(2,1)}, bf16[16,4096]{1,0:T(8,128)(2,1)S(1)}, u32[]{:S(2)}, u32[]{:S(2)}) collective-permute-start(bf16[16,4096]{1,0:T(8,128)(2,1)} %collective-permute-done.4), channel_id=1, source_target_pairs={{8,0},{12,4},{16,8},{20,12},{24,16},{28,20},{9,1},{13,5},{17,9},{2... | collective-permute-start | bytes 393224 | tf_op jit(solution)/shard_map/ppermute | solution.py:59
  44.3 18.6 %collective-permute-start.1 = (bf16[128,4096]{1,0:T(8,128)(2,1)S(1)}, bf16[128,4096]{1,0:T(8,128)(2,1)S(1)}, u32[]{:S(2)}, u32[]{:S(2)}) collective-permute-start(bf16[128,4096]{1,0:T(8,128)(2,1)S(1)} %get-tuple-element.16), channel_id=1, source_target_pairs={{0,4},{4,0},{8,12},{12,8},{16,20},{20,16},{24,28},{28,24},{1,5},{5... | collective-permute-start | bytes 3145736 | tf_op jit(solution)/shard_map/ppermute | solution.py:284
  44.4 15.5 %collective-permute-start.11 = (bf16[16,4096]{1,0:T(8,128)(2,1)S(1)}, bf16[16,4096]{1,0:T(8,128)(2,1)S(1)}, u32[]{:S(2)}, u32[]{:S(2)}) collective-permute-start(bf16[16,4096]{1,0:T(8,128)(2,1)S(1)} %collective-permute-done.10), channel_id=1, source_target_pairs={{8,0},{12,4},{16,8},{20,12},{24,16},{28,20},{9,1},{13,5},{17,9},{2... | collective-permute-start | bytes 393224 | tf_op jit(solution)/shard_map/ppermute | solution.py:59
  45.7 15.6 %collective-permute-start.13 = (bf16[16,4096]{1,0:T(8,128)(2,1)S(1)}, bf16[16,4096]{1,0:T(8,128)(2,1)S(1)}, u32[]{:S(2)}, u32[]{:S(2)}) collective-permute-start(bf16[16,4096]{1,0:T(8,128)(2,1)S(1)} %collective-permute-done.12), channel_id=1, source_target_pairs={{0,8},{4,12},{8,16},{12,20},{16,24},{20,28},{1,9},{5,13},{9,17},{1... | collective-permute-start | bytes 393224 | tf_op jit(solution)/shard_map/ppermute | solution.py:59
  50.9 6.7 %collective-permute-start.7 = (bf16[16,4096]{1,0:T(8,128)(2,1)S(1)}, bf16[16,4096]{1,0:T(8,128)(2,1)S(1)}, u32[]{:S(2)}, u32[]{:S(2)}) collective-permute-start(bf16[16,4096]{1,0:T(8,128)(2,1)S(1)} %collective-permute-done.6), channel_id=1, source_target_pairs={{0,8},{4,12},{8,16},{12,20},{16,24},{20,28},{1,9},{5,13},{9,17},{1... | collective-permute-start | bytes 393224 | tf_op jit(solution)/shard_map/ppermute | solution.py:59
  62.9 3.2 %copy-start.10 = (bf16[128,4096]{1,0:T(8,128)(2,1)}, bf16[128,4096]{1,0:T(8,128)(2,1)S(1)}, u32[]{:S(2)}) copy-start(bf16[128,4096]{1,0:T(8,128)(2,1)S(1)} %collective-permute-done) | copy-start | bytes 3145732
  66.1 5.0 %collective-permute-start.14 = (f32[256,128]{0,1:T(8,128)S(1)}, f32[256,128]{0,1:T(8,128)S(1)}, u32[]{:S(2)}, u32[]{:S(2)}) collective-permute-start(f32[256,128]{0,1:T(8,128)S(1)} %slice_add_fusion), channel_id=1, source_target_pairs={{0,1},{1,0},{2,3},{3,2},{4,5},{5,4},{6,7},{7,6},{8,9},{9,8},{10,11... | collective-permute-start | bytes 393224 | tf_op jit(solution)/shard_map/ppermute | solution.py:27
  71.2 5.0 %collective-permute-start.15 = (f32[256,128]{0,1:T(8,128)S(1)}, f32[256,128]{0,1:T(8,128)S(1)}, u32[]{:S(2)}, u32[]{:S(2)}) collective-permute-start(f32[256,128]{0,1:T(8,128)S(1)} %fusion.35), channel_id=1, source_target_pairs={{0,2},{1,3},{2,0},{3,1},{4,6},{5,7},{6,4},{7,5},{8,10},{9,11},{10,... | collective-permute-start | bytes 393224 | tf_op jit(solution)/shard_map/ppermute | solution.py:27
  76.2 1.6 collective-permute-start.16
  78.9 0.7 copy-start.9
  79.6 1.6 copy-start
  84.3 120.9 %copy-start.1 = (f32[128,4096]{1,0:T(8,128)S(1)}, f32[128,4096]{1,0:T(8,128)}, u32[]{:S(2)}) copy-start(f32[128,4096]{1,0:T(8,128)} %momentum_ref.1) | copy-start | bytes 6291460
  84.3 120.9 %copy-start.2 = (bf16[128,4096]{1,0:T(8,128)(2,1)S(1)}, bf16[128,4096]{1,0:T(8,128)(2,1)}, u32[]{:S(2)}) copy-start(bf16[128,4096]{1,0:T(8,128)(2,1)} %grad_ref.1) | copy-start | bytes 3145732
  86.1 6.2 %collective-permute-start.17 = (f32[64,256]{1,0:T(8,128)S(1)}, f32[64,256]{1,0:T(8,128)S(1)}, u32[]{:S(2)}, u32[]{:S(2)}) collective-permute-start(f32[64,256]{1,0:T(8,128)S(1)} %constant_dynamic-slice_fusion), channel_id=1, source_target_pairs={{0,8},{4,12},{8,0},{12,4},{16,24},{20,28},{24,16},{28,20},{1,9},{5... | collective-permute-start | bytes 196616 | tf_op jit(solution)/shard_map/ppermute | solution.py:27
  92.3 10.7 %collective-permute-start.18 = (f32[64,256]{1,0:T(8,128)S(1)}, f32[64,256]{1,0:T(8,128)S(1)}, u32[]{:S(2)}, u32[]{:S(2)}) collective-permute-start(f32[64,256]{1,0:T(8,128)S(1)} %fusion.34), channel_id=1, source_target_pairs={{0,16},{4,20},{8,24},{12,28},{16,0},{20,4},{24,8},{28,12},{1,17},{... | collective-permute-start | bytes 196616 | tf_op jit(solution)/shard_map/ppermute | solution.py:27
  104.4 4.3 %collective-permute-start.19 = (f32[64,256]{1,0:T(8,128)S(1)}, f32[64,256]{1,0:T(8,128)S(1)}, u32[]{:S(2)}, u32[]{:S(2)}) collective-permute-start(f32[64,256]{1,0:T(8,128)S(1)} %get-tuple-element.12), channel_id=1, source_target_pairs={{0,1},{1,0},{2,3},{3,2},{4,5},{5,4},{6,7},{7,6},{8,9},{9,8},{10,11... | collective-permute-start | bytes 196616 | tf_op jit(solution)/shard_map/ppermute | solution.py:43
  106.1 5.0 %collective-permute-start.20 = (f32[64,256]{1,0:T(8,128)S(1)}, f32[64,256]{1,0:T(8,128)S(1)}, u32[]{:S(2)}, u32[]{:S(2)}) collective-permute-start(f32[64,256]{1,0:T(8,128)S(1)} %get-tuple-element.12), channel_id=1, source_target_pairs={{0,2},{1,3},{2,0},{3,1},{4,6},{5,7},{6,4},{7,5},{8,10},{9,11},{10,... | collective-permute-start | bytes 196616 | tf_op jit(solution)/shard_map/ppermute | solution.py:43
  107.6 5.2 %collective-permute-start.21 = (f32[64,256]{1,0:T(8,128)S(1)}, f32[64,256]{1,0:T(8,128)S(1)}, u32[]{:S(2)}, u32[]{:S(2)}) collective-permute-start(f32[64,256]{1,0:T(8,128)S(1)} %get-tuple-element.12), channel_id=1, source_target_pairs={{0,3},{1,2},{2,1},{3,0},{4,7},{5,6},{6,5},{7,4},{8,11},{9,10},{10,... | collective-permute-start | bytes 196616 | tf_op jit(solution)/shard_map/ppermute | solution.py:43
  125.0 0.7 copy-start.3
  131.9 0.9 copy-start.4
  132.8 1.0 copy-start.5
  134.6 0.7 copy-start.6
  135.8 3.9 %collective-permute-start.23 = (f32[1,256]{1,0:T(1,128)}, f32[1,256]{1,0:T(1,128)}, u32[]{:S(2)}, u32[]{:S(2)}) collective-permute-start(f32[1,256]{1,0:T(1,128)} %slice.31), channel_id=1, source_target_pairs={{0,2},{1,3},{2,0},{3,1},{4,6},{5,7},{6,4},{7,5},{8,10},{9,11},{10,... | collective-permute-start | bytes 3080 | tf_op jit(solution)/shard_map/ppermute | solution.py:36
  137.3 4.8 %collective-permute-start.24 = (f32[1,256]{1,0:T(1,128)}, f32[1,256]{1,0:T(1,128)}, u32[]{:S(2)}, u32[]{:S(2)}) collective-permute-start(f32[1,256]{1,0:T(1,128)} %slice.31), channel_id=1, source_target_pairs={{0,3},{1,2},{2,1},{3,0},{4,7},{5,6},{6,5},{7,4},{8,11},{9,10},{10,... | collective-permute-start | bytes 3080 | tf_op jit(solution)/shard_map/ppermute | solution.py:36
  138.8 3.9 %collective-permute-start.22 = (f32[1,256]{1,0:T(1,128)}, f32[1,256]{1,0:T(1,128)}, u32[]{:S(2)}, u32[]{:S(2)}) collective-permute-start(f32[1,256]{1,0:T(1,128)} %slice.31), channel_id=1, source_target_pairs={{0,1},{1,0},{2,3},{3,2},{4,5},{5,4},{6,7},{7,6},{8,9},{9,8},{10,11... | collective-permute-start | bytes 3080 | tf_op jit(solution)/shard_map/ppermute | solution.py:36
  143.9 10.9 %collective-permute-start.27 = (f32[1,256]{1,0:T(1,128)}, f32[1,256]{1,0:T(1,128)S(1)}, u32[]{:S(2)}, u32[]{:S(2)}) collective-permute-start(f32[1,256]{1,0:T(1,128)} %add_add_fusion.1), channel_id=1, source_target_pairs={{0,24},{4,28},{8,16},{12,20},{16,8},{20,12},{24,0},{28,4},{1,25},{... | collective-permute-start | bytes 3080 | tf_op jit(solution)/shard_map/ppermute | solution.py:36
  145.7 9.1 %collective-permute-start.26 = (f32[1,256]{1,0:T(1,128)}, f32[1,256]{1,0:T(1,128)S(1)}, u32[]{:S(2)}, u32[]{:S(2)}) collective-permute-start(f32[1,256]{1,0:T(1,128)} %add_add_fusion.1), channel_id=1, source_target_pairs={{0,16},{4,20},{8,24},{12,28},{16,0},{20,4},{24,8},{28,12},{1,17},{... | collective-permute-start | bytes 3080 | tf_op jit(solution)/shard_map/ppermute | solution.py:36
  147.2 8.2 %collective-permute-start.25 = (f32[1,256]{1,0:T(1,128)}, f32[1,256]{1,0:T(1,128)}, u32[]{:S(2)}, u32[]{:S(2)}) collective-permute-start(f32[1,256]{1,0:T(1,128)} %add_add_fusion.1), channel_id=1, source_target_pairs={{0,8},{4,12},{8,0},{12,4},{16,24},{20,28},{24,16},{28,20},{1,9},{5... | collective-permute-start | bytes 3080 | tf_op jit(solution)/shard_map/ppermute | solution.py:36
  148.3 13.8 %collective-permute-start.30 = (s16[272,256]{1,0:T(8,128)(2,1)S(1)}, s16[272,256]{1,0:T(8,128)(2,1)}, u32[]{:S(2)}, u32[]{:S(2)}) collective-permute-start(s16[272,256]{1,0:T(8,128)(2,1)S(1)} %get-tuple-element.7), channel_id=1, source_target_pairs={{8,0},{12,4},{16,8},{20,12},{24,16},{28,20},{9,1},{13,5},{17,9},{2... | collective-permute-start | bytes 417800 | tf_op jit(solution)/shard_map/ppermute | solution.py:59
  149.6 13.9 %collective-permute-start.29 = (s16[272,256]{1,0:T(8,128)(2,1)S(1)}, s16[272,256]{1,0:T(8,128)(2,1)}, u32[]{:S(2)}, u32[]{:S(2)}) collective-permute-start(s16[272,256]{1,0:T(8,128)(2,1)S(1)} %get-tuple-element.7), channel_id=1, source_target_pairs={{0,8},{4,12},{8,16},{12,20},{16,24},{20,28},{1,9},{5,13},{9,17},{1... | collective-permute-start | bytes 417800 | tf_op jit(solution)/shard_map/ppermute | solution.py:59
  154.8 0.6 copy-start.12
  156.1 6.0 %collective-permute-start.28 = (f32[1,256]{1,0:T(1,128)S(1)}, f32[1,256]{1,0:T(1,128)}, u32[]{:S(2)}, u32[]{:S(2)}) collective-permute-start(f32[1,256]{1,0:T(1,128)S(1)} %add_add_fusion), channel_id=1, source_target_pairs={{0,4},{4,0},{8,12},{12,8},{16,20},{20,16},{24,28},{28,24},{1,5},{5... | collective-permute-start | bytes 3080 | tf_op jit(solution)/shard_map/ppermute | solution.py:284
  156.2 12.5 %collective-permute-start.34 = (s16[272,256]{1,0:T(8,128)(2,1)}, s16[272,256]{1,0:T(8,128)(2,1)S(1)}, u32[]{:S(2)}, u32[]{:S(2)}) collective-permute-start(s16[272,256]{1,0:T(8,128)(2,1)} %copy-done.6), channel_id=1, source_target_pairs={{8,0},{12,4},{16,8},{20,12},{24,16},{28,20},{9,1},{13,5},{17,9},{2... | collective-permute-start | bytes 417800 | tf_op jit(solution)/shard_map/ppermute | solution.py:59
  157.5 11.3 %collective-permute-start.33 = (s16[272,256]{1,0:T(8,128)(2,1)}, s16[272,256]{1,0:T(8,128)(2,1)S(1)}, u32[]{:S(2)}, u32[]{:S(2)}) collective-permute-start(s16[272,256]{1,0:T(8,128)(2,1)} %copy-done.6), channel_id=1, source_target_pairs={{0,8},{4,12},{8,16},{12,20},{16,24},{20,28},{1,9},{5,13},{9,17},{1... | collective-permute-start | bytes 417800 | tf_op jit(solution)/shard_map/ppermute | solution.py:59
  162.1 40.5 %collective-permute-start.42 = (s16[1,272,256]{2,1,0:T(8,128)(2,1)}, s16[1,272,256]{2,1,0:T(8,128)(2,1)S(1)}, u32[]{:S(2)}, u32[]{:S(2)}) collective-permute-start(s16[1,272,256]{2,1,0:T(8,128)(2,1)} %bitcast.41), channel_id=1, source_target_pairs={{0,4},{4,0},{8,12},{12,8},{16,20},{20,16},{24,28},{28,24},{1,5},{5... | collective-permute-start | bytes 417800 | tf_op jit(solution)/shard_map/ppermute | solution.py:284
  162.2 8.2 %collective-permute-start.31 = (s16[272,256]{1,0:T(8,128)(2,1)}, s16[272,256]{1,0:T(8,128)(2,1)S(1)}, u32[]{:S(2)}, u32[]{:S(2)}) collective-permute-start(s16[272,256]{1,0:T(8,128)(2,1)} %collective-permute-done.30), channel_id=1, source_target_pairs={{8,0},{12,4},{16,8},{20,12},{24,16},{28,20},{9,1},{13,5},{17,9},{2... | collective-permute-start | bytes 417800 | tf_op jit(solution)/shard_map/ppermute | solution.py:59
  163.5 11.2 %collective-permute-start.37 = (s16[272,256]{1,0:T(8,128)(2,1)}, s16[272,256]{1,0:T(8,128)(2,1)S(1)}, u32[]{:S(2)}, u32[]{:S(2)}) collective-permute-start(s16[272,256]{1,0:T(8,128)(2,1)} %collective-permute-done.29), channel_id=1, source_target_pairs={{0,8},{4,12},{8,16},{12,20},{16,24},{20,28},{1,9},{5,13},{9,17},{1... | collective-permute-start | bytes 417800 | tf_op jit(solution)/shard_map/ppermute | solution.py:59
  168.7 34.4 %collective-permute-start.41 = (s16[1,272,256]{2,1,0:T(8,128)(2,1)S(1)}, s16[1,272,256]{2,1,0:T(8,128)(2,1)S(1)}, u32[]{:S(2)}, u32[]{:S(2)}) collective-permute-start(s16[1,272,256]{2,1,0:T(8,128)(2,1)S(1)} %bitcast.39), channel_id=1, source_target_pairs={{0,4},{4,0},{8,12},{12,8},{16,20},{20,16},{24,28},{28,24},{1,5},{5... | collective-permute-start | bytes 417800 | tf_op jit(solution)/shard_map/ppermute | solution.py:284
  168.8 8.0 %collective-permute-start.35 = (s16[272,256]{1,0:T(8,128)(2,1)S(1)}, s16[272,256]{1,0:T(8,128)(2,1)S(1)}, u32[]{:S(2)}, u32[]{:S(2)}) collective-permute-start(s16[272,256]{1,0:T(8,128)(2,1)S(1)} %collective-permute-done.34), channel_id=1, source_target_pairs={{8,0},{12,4},{16,8},{20,12},{24,16},{28,20},{9,1},{13,5},{17,9},{2... | collective-permute-start | bytes 417800 | tf_op jit(solution)/shard_map/ppermute | solution.py:59
  170.3 7.7 %collective-permute-start.38 = (s16[272,256]{1,0:T(8,128)(2,1)S(1)}, s16[272,256]{1,0:T(8,128)(2,1)S(1)}, u32[]{:S(2)}, u32[]{:S(2)}) collective-permute-start(s16[272,256]{1,0:T(8,128)(2,1)S(1)} %collective-permute-done.33), channel_id=1, source_target_pairs={{0,8},{4,12},{8,16},{12,20},{16,24},{20,28},{1,9},{5,13},{9,17},{1... | collective-permute-start | bytes 417800 | tf_op jit(solution)/shard_map/ppermute | solution.py:59
  174.7 28.5 %collective-permute-start.45 = (s16[1,272,256]{2,1,0:T(8,128)(2,1)S(1)}, s16[1,272,256]{2,1,0:T(8,128)(2,1)S(1)}, u32[]{:S(2)}, u32[]{:S(2)}) collective-permute-start(s16[1,272,256]{2,1,0:T(8,128)(2,1)S(1)} %select_bitcast_fusion.4.refs_4_), channel_id=1, source_target_pairs={{0,4},{4,0},{8,12},{12,8},{16,20},{20,16},{24,28},{28,24},{1,5},{5... | collective-permute-start | bytes 417800 | tf_op jit(solution)/shard_map/ppermute | solution.py:284
  176.8 7.2 %collective-permute-start.32 = (s16[272,256]{1,0:T(8,128)(2,1)S(1)}, s16[272,256]{1,0:T(8,128)(2,1)S(1)}, u32[]{:S(2)}, u32[]{:S(2)}) collective-permute-start(s16[272,256]{1,0:T(8,128)(2,1)S(1)} %collective-permute-done.31), channel_id=1, source_target_pairs={{8,0},{12,4},{16,8},{20,12},{24,16},{28,20},{9,1},{13,5},{17,9},{2... | collective-permute-start | bytes 417800 | tf_op jit(solution)/shard_map/ppermute | solution.py:59
  178.1 27.0 %collective-permute-start.46 = (s16[1,272,256]{2,1,0:T(8,128)(2,1)S(1)}, s16[1,272,256]{2,1,0:T(8,128)(2,1)S(1)}, u32[]{:S(2)}, u32[]{:S(2)}) collective-permute-start(s16[1,272,256]{2,1,0:T(8,128)(2,1)S(1)} %select_bitcast_fusion.3.refs_5_), channel_id=1, source_target_pairs={{0,4},{4,0},{8,12},{12,8},{16,20},{20,16},{24,28},{28,24},{1,5},{5... | collective-permute-start | bytes 417800 | tf_op jit(solution)/shard_map/ppermute | solution.py:284
  183.9 4.7 %collective-permute-start.39 = (s16[272,256]{1,0:T(8,128)(2,1)S(1)}, s16[272,256]{1,0:T(8,128)(2,1)S(1)}, u32[]{:S(2)}, u32[]{:S(2)}) collective-permute-start(s16[272,256]{1,0:T(8,128)(2,1)S(1)} %collective-permute-done.37), channel_id=1, source_target_pairs={{0,8},{4,12},{8,16},{12,20},{16,24},{20,28},{1,9},{5,13},{9,17},{1... | collective-permute-start | bytes 417800 | tf_op jit(solution)/shard_map/ppermute | solution.py:59
  188.6 7.4 %collective-permute-start.36 = (s16[272,256]{1,0:T(8,128)(2,1)S(1)}, s16[272,256]{1,0:T(8,128)(2,1)S(1)}, u32[]{:S(2)}, u32[]{:S(2)}) collective-permute-start(s16[272,256]{1,0:T(8,128)(2,1)S(1)} %collective-permute-done.35), channel_id=1, source_target_pairs={{8,0},{12,4},{16,8},{20,12},{24,16},{28,20},{9,1},{13,5},{17,9},{2... | collective-permute-start | bytes 417800 | tf_op jit(solution)/shard_map/ppermute | solution.py:59
  196.0 6.5 %collective-permute-start.40 = (s16[272,256]{1,0:T(8,128)(2,1)S(1)}, s16[272,256]{1,0:T(8,128)(2,1)S(1)}, u32[]{:S(2)}, u32[]{:S(2)}) collective-permute-start(s16[272,256]{1,0:T(8,128)(2,1)S(1)} %collective-permute-done.38), channel_id=1, source_target_pairs={{0,8},{4,12},{8,16},{12,20},{16,24},{20,28},{1,9},{5,13},{9,17},{1... | collective-permute-start | bytes 417800 | tf_op jit(solution)/shard_map/ppermute | solution.py:59
  202.5 2.6 %collective-permute-start.43 = (s16[1,272,256]{2,1,0:T(8,128)(2,1)S(1)}, s16[1,272,256]{2,1,0:T(8,128)(2,1)S(1)}, u32[]{:S(2)}, u32[]{:S(2)}) collective-permute-start(s16[1,272,256]{2,1,0:T(8,128)(2,1)S(1)} %select_bitcast_fusion.6.refs_2_), channel_id=1, source_target_pairs={{0,4},{4,0},{8,12},{12,8},{16,20},{20,16},{24,28},{28,24},{1,5},{5... | collective-permute-start | bytes 417800 | tf_op jit(solution)/shard_map/ppermute | solution.py:284
  202.6 2.5 %collective-permute-start.47 = (s16[1,272,256]{2,1,0:T(8,128)(2,1)S(1)}, s16[1,272,256]{2,1,0:T(8,128)(2,1)S(1)}, u32[]{:S(2)}, u32[]{:S(2)}) collective-permute-start(s16[1,272,256]{2,1,0:T(8,128)(2,1)S(1)} %select_bitcast_fusion.2.refs_6_), channel_id=1, source_target_pairs={{0,4},{4,0},{8,12},{12,8},{16,20},{20,16},{24,28},{28,24},{1,5},{5... | collective-permute-start | bytes 417800 | tf_op jit(solution)/shard_map/ppermute | solution.py:284
  203.2 1.9 collective-permute-start.44
  203.2 1.9 collective-permute-start.48
  205.1 0.9 copy-start.7
Sparse Core Ops, SparseCore 0:
  84.4 47.4 reduce-scatter.1

commit v4 on v1

v4 whole, which is shorter than its diff:
```python
import functools
import math

import jax
import jax.numpy as jnp
from jax import lax
from jax.experimental import pallas as pl
from jax.experimental.pallas import tpu as pltpu
from jax.sharding import PartitionSpec as P

EPSILON = 1e-06
KEEP_SHARE = 0.5
HIGH = lax.Precision.HIGHEST
PANEL = 64
TILE = 8
HEAD = 16
TOP = 32766.0
PARAMS = pltpu.CompilerParams(vmem_limit_bytes=40 * 1024 * 1024)


def split_two(x):
    high = lax.reduce_precision(x, 8, 7)
    return high.astype(jnp.bfloat16), (x - high).astype(jnp.bfloat16)


def halves(x):
    high = x.astype(jnp.bfloat16)
    return high, (x - high.astype(jnp.float32)).astype(jnp.bfloat16)


def exchange(x, axis, k):
    return lax.ppermute(x, axis, [(i, i ^ k) for i in range(lax.axis_size(axis))])


def butterfly_sum(x, axis, step=1):
    while step < lax.axis_size(axis):
        x = x + exchange(x, axis, step)
        step *= 2
    return x


def quad_sum(x, axis, step=1):
    if lax.axis_size(axis) != 4 * step:
        return butterfly_sum(x, axis, step)
    near, far, across = [exchange(x, axis, k * step) for k in range(1, 4)]
    return (x + near) + (far + across)


def whole(x):
    return pl.BlockSpec(x.shape, lambda *_: (0,) * len(x.shape))


def dot_rows(a, b):
    return lax.dot_general(a, b, (((1,), (1,)), ((), ())), precision=HIGH, preferred_element_type=jnp.float32)


def gram_kernel(column_ref, near_ref, far_ref, order_ref, unit_ref, proj_ref, scaled_ref, piece_ref, gram_ref):
    proj = jnp.dot(near_ref[...] + far_ref[...], order_ref[...], precision=HIGH, preferred_element_type=jnp.float32)
    proj_ref[...] = proj
    scaled_ref[...] = proj * unit_ref[...]
    gram_ref[...] = lax.dot_general(
        proj, proj, (((0,), (0,)), ((), ())), precision=HIGH, preferred_element_type=jnp.float32
    )
    size = piece_ref.shape[0]
    piece_ref[...] = gram_ref[pl.ds(pl.multiple_of(column_ref[0] * size, size), size), :]


def gram_parts(column, near, far, order, unit, columns):
    rows, rank = near.shape
    operands = (near, far, order, unit)
    return pl.pallas_call(
        gram_kernel,
        grid_spec=pltpu.PrefetchScalarGridSpec(
            num_scalar_prefetch=1,
            grid=(1,),
            in_specs=[whole(x) for x in operands],
            out_specs=[whole(near), whole(near), pl.BlockSpec((rank // columns, rank), lambda *_: (0, 0))],
            scratch_shapes=[pltpu.VMEM((rank, rank), jnp.float32)],
        ),
        out_shape=[
            jax.ShapeDtypeStruct((rows, rank), jnp.float32),
            jax.ShapeDtypeStruct((rows, rank), jnp.float32),
            jax.ShapeDtypeStruct((rank // columns, rank), jnp.float32),
        ],
        compiler_params=PARAMS,
        cost_estimate=pl.CostEstimate(flops=24 * rows * rank * rank, bytes_accessed=rank * rank * 12, transcendentals=0),
    )(column, *operands)


def spread(row):
    return jnp.broadcast_to(row, (TILE, 2 * PANEL))


def panel_inverse(block):
    rows = lax.broadcasted_iota(jnp.int32, (PANEL, PANEL), 0)
    cols = lax.broadcasted_iota(jnp.int32, (PANEL, PANEL), 1)
    both = jnp.concatenate([block, (rows == cols).astype(jnp.float32)], axis=1)
    count = PANEL // TILE
    tiles = [both[TILE * i : TILE * (i + 1)] for i in range(count)]
    sub = lax.broadcasted_iota(jnp.int32, (TILE, 2 * PANEL), 0)
    done = []
    for k in range(count):
        columns = [
            [spread(tiles[i][:, TILE * k + j : TILE * k + j + 1]) for j in range(TILE)] for i in range(k, count)
        ]
        own, body = columns[0], tiles[k]
        final = jnp.zeros_like(body)
        for j in range(TILE):
            here = sub == j
            pivot = spread(own[j][j : j + 1])
            inverse = 1.0 / pivot
            final = jnp.where(here, body * lax.rsqrt(pivot), final)
            reduced = spread(body[j : j + 1]) * inverse
            body = jnp.where(here, reduced, body - own[j] * reduced)
            for other in range(j + 1, TILE):
                ratio = spread(own[other][j : j + 1]) * inverse
                own[other] = jnp.where(here, ratio, own[other] - own[j] * ratio)
        done.append(final)
        for i in range(k + 1, count):
            tile = tiles[i]
            for j in range(TILE):
                tile = tile - columns[i - k][j] * spread(body[j : j + 1])
            tiles[i] = tile
    return jnp.concatenate(done, axis=0)[:, PANEL:]


def factor_kernel(place_ref, *refs):
    piece_refs, (out_ref, work) = refs[:-2], refs[-2:]
    rank = out_ref.shape[0]
    for k, piece_ref in enumerate(piece_refs):
        size = piece_ref.shape[0]
        work[pl.ds(pl.multiple_of(place_ref[k] * size, size), size), :rank] = piece_ref[...]
    rows = lax.broadcasted_iota(jnp.int32, (rank, rank), 0)
    cols = lax.broadcasted_iota(jnp.int32, (rank, rank), 1)
    work[:, rank:] = (rows == cols).astype(jnp.float32)
    for start in range(0, rank, PANEL):
        end = start + PANEL
        inverse = panel_inverse(work[start:end, start:end])
        scaled = jnp.dot(inverse, work[start:end, :], precision=HIGH, preferred_element_type=jnp.float32)
        out_ref[start:end, :] = scaled[:, rank:]
        if end < rank:
            low = end // 128 * 128
            change = lax.dot_general(
                scaled[:, low:rank],
                scaled,
                (((0,), (0,)), ((), ())),
                precision=HIGH,
                preferred_element_type=jnp.float32,
            )
            work[end:, :] = work[end:, :] - change[end - low :, :]


def factor_inverse(places, pieces):
    rank = pieces[0].shape[1]
    return pl.pallas_call(
        factor_kernel,
        grid_spec=pltpu.PrefetchScalarGridSpec(
            num_scalar_prefetch=1,
            grid=(1,),
            in_specs=[whole(x) for x in pieces],
            out_specs=pl.BlockSpec((rank, rank), lambda *_: (0, 0)),
            scratch_shapes=[pltpu.VMEM((rank, 2 * rank), jnp.float32)],
        ),
        out_shape=jax.ShapeDtypeStruct((rank, rank), jnp.float32),
        compiler_params=PARAMS,
        cost_estimate=pl.CostEstimate(flops=6 * 2 * rank**3, bytes_accessed=2 * rank * rank * 4, transcendentals=rank),
    )(places, *pieces)


def mix_kernel(code_ref, proj_ref, out_ref):
    def times(a, b):
        return lax.dot_general(a, b, (((0,), (0,)), ((), ())), preferred_element_type=jnp.float32)

    code_high, code_low = halves(code_ref[...].astype(jnp.int32).astype(jnp.float32))
    proj_high, proj_low = halves(proj_ref[...])
    part = times(code_high, proj_high) + (times(code_low, proj_high) + times(code_high, proj_low))

    @pl.when(pl.program_id(0) == 0)
    def _():
        out_ref[...] = part

    @pl.when(pl.program_id(0) > 0)
    def _():
        out_ref[...] += part


def mix(codes, projected):
    rows, cols = codes.shape
    rank = projected.shape[1]
    block = min(512, rows)
    return pl.pallas_call(
        mix_kernel,
        grid=(rows // block,),
        in_specs=[pl.BlockSpec((block, cols), lambda i: (i, 0)), pl.BlockSpec((block, rank), lambda i: (i, 0))],
        out_specs=pl.BlockSpec((cols, rank), lambda i: (0, 0)),
        out_shape=jax.ShapeDtypeStruct((cols, rank), jnp.float32),
        compiler_params=PARAMS,
        cost_estimate=pl.CostEstimate(
            flops=6 * rows * cols * rank, bytes_accessed=rows * cols * 2 + rows * rank * 4, transcendentals=0
        ),
    )(codes, projected)


def unit_of(exponent, mantissa):
    return mantissa * jnp.exp2(exponent - 13.0)


def encode_kernel(share_ref, inverse_ref, proj_ref, code_ref, ortho_ref):
    inverse = inverse_ref[...]
    ortho_ref[...] = dot_rows(proj_ref[...], inverse)
    right = dot_rows(share_ref[...], inverse)
    rows, rank = right.shape
    square = jnp.maximum(jnp.sum(right * right, axis=0, keepdims=True), 1e-34)
    square_exponent = jnp.floor(jnp.log2(square))
    fine = square * jnp.exp2(13.0 - square_exponent)
    square_high = jnp.floor(fine)
    square_low = jnp.floor((fine - square_high) * 16384.0)
    top = jnp.maximum(jnp.max(jnp.abs(right), axis=0, keepdims=True), 1e-28) * (1.0 / TOP)
    exponent = jnp.floor(jnp.log2(top))
    mantissa = jnp.floor(top * jnp.exp2(13.0 - exponent)) + 1.0
    scaled = right * (1.0 / unit_of(exponent, mantissa))
    code_ref[:rows, :] = jnp.floor(scaled + 0.5).astype(jnp.int32).astype(jnp.int16)
    place = lax.broadcasted_iota(jnp.int32, (HEAD, rank), 0)
    head = jnp.zeros((HEAD, rank), jnp.float32)
    for k, row in enumerate((exponent, mantissa, square_exponent, square_high, square_low)):
        head = jnp.where(place == k, row, head)
    code_ref[rows:, :] = head.astype(jnp.int32).astype(jnp.int16)


def encode(share, inverse_low, projected):
    rows, rank = share.shape
    return pl.pallas_call(
        encode_kernel,
        out_shape=[
            jax.ShapeDtypeStruct((rows + HEAD, rank), jnp.int16),
            jax.ShapeDtypeStruct(projected.shape, jnp.float32),
        ],
        compiler_params=PARAMS,
        cost_estimate=pl.CostEstimate(flops=12 * rows * rank * rank, bytes_accessed=rows * rank * 6, transcendentals=0),
    )(share, inverse_low, projected)


def finish_kernel(
    gain, momentum_ref, grad_ref, code_ref, ortho_ref, scale_ref, next_ref, basis_ref, update_ref, high_ref, low_ref
):
    scale = scale_ref[...]
    rows = momentum_ref.shape[0]

    @pl.when(pl.program_id(0) == 0)
    def _():
        ortho = ortho_ref[...]
        for start, factor in ((0, -KEEP_SHARE * ortho), (rows, gain * ortho * scale)):
            high, low = halves(factor)
            high_ref[start : start + rows, :] = high
            low_ref[start : start + rows, :] = low

    code = code_ref[...].astype(jnp.int32).astype(jnp.float32)
    share = code.shape[1] - HEAD
    right = code[:, :share] * unit_of(code[:, share : share + 1], code[:, share + 1 : share + 2])
    right = right.reshape(basis_ref.shape)
    basis_ref[...] = right * scale
    right_high, right_low = halves(right)

    def times(a, b):
        return lax.dot_general(a, b, (((1,), (1,)), ((), ())), preferred_element_type=jnp.float32)

    high = high_ref[...]
    both = times(high, right_high) + (times(low_ref[...], right_high) + times(high, right_low))
    next_ref[...] = momentum_ref[...] + grad_ref[...].astype(jnp.float32) + both[:rows]
    update_ref[...] = both[rows:].astype(jnp.bfloat16)


def finish(momentum, grad, codes, orthonormal, scale, gain):
    rows, cols = momentum.shape
    shares, share, rank = codes.shape
    share -= HEAD
    group = max(1, min(512 // share, shares))
    block = group * share
    wide = pl.BlockSpec((rows, block), lambda i: (0, i))
    tall = pl.BlockSpec((block, rank), lambda i: (i, 0))
    return pl.pallas_call(
        functools.partial(finish_kernel, gain),
        grid=(cols // block,),
        in_specs=[
            wide,
            wide,
            pl.BlockSpec((group, share + HEAD, rank), lambda i: (i, 0, 0)),
            whole(orthonormal),
            whole(scale),
        ],
        out_specs=[wide, tall, wide],
        out_shape=[
            jax.ShapeDtypeStruct((rows, cols), jnp.float32),
            jax.ShapeDtypeStruct((cols, rank), jnp.float32),
            jax.ShapeDtypeStruct((rows, cols), jnp.bfloat16),
        ],
        scratch_shapes=[pltpu.VMEM((2 * rows, rank), jnp.bfloat16)] * 2,
        compiler_params=PARAMS,
        cost_estimate=pl.CostEstimate(
            flops=6 * 2 * rows * cols * rank, bytes_accessed=rows * cols * 12 + cols * rank * 6, transcendentals=0
        ),
    )(momentum, grad, codes, orthonormal, scale)


def on_device(momentum, grad, q_stored, perm):
    block_rows = q_stored.shape[0]
    num_blocks = lax.axis_size("fsdp")
    num_cols = lax.axis_size("tp")
    rank_total = block_rows * num_blocks
    rows, cols = momentum.shape
    row_total, col_total = rows * num_blocks, cols * num_cols
    column = lax.axis_index("tp")

    basis = lax.all_gather(q_stored, "fsdp", axis=0, tiled=True)

    combined = momentum + grad.astype(jnp.float32)
    unit = jnp.maximum(jnp.max(jnp.abs(combined), axis=1, keepdims=True), 1e-28) * (1.0 / TOP)
    codes = jnp.floor(combined * (1.0 / unit) + 0.5).astype(jnp.int16)
    codes = codes.reshape(rows, num_blocks, cols // num_blocks).transpose(1, 0, 2)
    codes = lax.all_to_all(codes, "fsdp", split_axis=0, concat_axis=0).reshape(row_total, cols // num_blocks)
    codes, combined = lax.optimization_barrier((codes, combined))

    stacked = lax.dot_general(
        jnp.concatenate(split_two(combined), axis=0),
        basis,
        (((1,), (1,)), ((), ())),
        preferred_element_type=jnp.float32,
    )
    near = stacked[:rows] + stacked[rows:]
    step = 1
    while 2 * step < num_cols:
        near = near + exchange(near, "tp", step)
        step *= 2
    far = exchange(near, "tp", step)
    blocks = jnp.arange(num_blocks, dtype=jnp.int32)
    inverse = jnp.sum(jnp.where(perm[:, None] == blocks[None, :], blocks[:, None], 0), axis=0)
    row_ids = jnp.arange(rank_total, dtype=jnp.int32)
    order_index = inverse[row_ids // block_rows] * block_rows + row_ids % block_rows
    order = (row_ids[:, None] == order_index[None, :]).astype(jnp.float32)
    projected, scaled, piece = gram_parts(column.reshape(1), near, far, order, unit, num_cols)

    all_scaled = lax.all_gather(scaled, "fsdp", axis=0, tiled=True)
    piece = quad_sum(piece, "fsdp", 2)
    piece = piece + exchange(piece, "fsdp", 1)
    pieces = [piece] + [exchange(piece, "tp", k) for k in range(1, num_cols)]
    places = jnp.stack([column ^ k for k in range(num_cols)]).astype(jnp.int32)
    inverse_low = factor_inverse(places, pieces)
    mixed = mix(codes, all_scaled)

    code, orthonormal = encode(mixed, inverse_low, projected)
    gathered = lax.all_gather(code, "fsdp", axis=0)
    share = mixed.shape[0]
    head = gathered[:, share : share + 5].astype(jnp.float32)
    parts = (head[:, 3] + head[:, 4] * (1.0 / 16384.0)) * jnp.exp2(head[:, 2] - 13.0)
    squares = quad_sum(jnp.sum(parts, axis=0, keepdims=True), "tp")
    scale = lax.rsqrt(squares / col_total + EPSILON)
    return tuple(finish(momentum, grad, gathered, orthonormal, scale, math.sqrt(row_total / rank_total)))


def solution(mesh):
    return jax.shard_map(
        on_device,
        mesh=mesh,
        in_specs=(P("fsdp", "tp"), P("fsdp", "tp"), P("fsdp", "tp"), P()),
        out_specs=(P("fsdp", "tp"), P("tp", None), P("fsdp", "tp")),
        check_vma=False,
    )
```

time: 175 us -> 150 us (0.86)
  waiting for transfers between devices: 103 us -> 56.2 us
  blocking collectives: 0 us -> 22.2 us
  matrix products: 10.7 us -> 2.97 us
  starting transfers between devices: 15.7 us -> 21.2 us
  Pallas kernels: 15.8 us -> 20.1 us
  local copies, waits for them, and re-layouts: 6.25 us -> 3.11 us
    all_to_all x0 -> x1, waiting for transfers between devices: none -> 38 us  [on_device(): lax.all_to_all(codes, 'fsdp', split_axis=0, concat_axis=0)]
    all_gather x1, waiting for transfers between devices: 29.2 us -> 0.02 us  [on_device(): all_scaled = lax.all_gather(scaled, 'fsdp', axis=0, tiled=True)]
    all_gather x1, waiting for transfers between devices: 24.5 us -> 0.01 us  [on_device(): basis = lax.all_gather(q_stored, 'fsdp', axis=0, tiled=True)]
    all_gather x0 -> x1, blocking collectives: none -> 22.2 us  [on_device(): gathered = lax.all_gather(code, 'fsdp', axis=0)]
    ppermute x13 -> x12, waiting for transfers between devices: 33.4 us -> 17.5 us  [exchange(): lax.ppermute(x, axis, [(i, i ^ k) for i in range(lax.axis_size(axis))])]
    reduce_scatter x1 -> x0, waiting for transfers between devices: 14.8 us -> none  [on_device(): lax.psum_scatter(mixed, 'fsdp', scatter_dimension=0, tiled=True)]
    dot_general x5 -> x1, matrix products: 10.7 us -> 2.97 us  [on_device(): lax.dot_general(jnp.concatenate(split_two(combined), axis=0), basis, (((1...]
    all_to_all x0 -> x1, starting transfers between devices: none -> 6.33 us  [on_device(): lax.all_to_all(codes, 'fsdp', split_axis=0, concat_axis=0)]
  transfers between devices with their start and end apart: 16 -> 15, of which waited for: 16 -> 12; matrix products, arithmetic and copies ran while one was open for 6% -> 8% of each run, Pallas kernels for 6% -> 7%
where the time goes in v4:
time: 150 us
  waiting for transfers between devices  56.2 us (37%)
  blocking collectives  22.2 us (15%)
  starting transfers between devices  21.2 us (14%)
  Pallas kernels  20.1 us (13%)
  between operations  14.2 us (9%)
  other arithmetic  9.81 us (7%)
  local copies, waits for them, and re-layouts  3.11 us (2%)
  matrix products  2.97 us (2%)
    all_to_all x1, waiting for transfers between devices, on_device(): lax.all_to_all(codes, 'fsdp', split_axis=0, concat_axis=0)  38 us
    all_gather x1, blocking collectives, on_device(): gathered = lax.all_gather(code, 'fsdp', axis=0)  22.2 us
    ppermute x12, waiting for transfers between devices, exchange(): lax.ppermute(x, axis, [(i, i ^ k) for i in range(lax.axis_size(axis))])  17.5 us
    ppermute x12, starting transfers between devices, exchange(): lax.ppermute(x, axis, [(i, i ^ k) for i in range(lax.axis_size(axis))])  14.8 us
    pallas_call x1, Pallas kernels, factor_inverse(): pl.pallas_call(factor_kernel, grid_spec=pltpu.PrefetchScalarGridSpec(num_...  11.2 us
    all_to_all x1, starting transfers between devices, on_device(): lax.all_to_all(codes, 'fsdp', split_axis=0, concat_axis=0)  6.33 us
    pallas_call x1, Pallas kernels, finish(): pl.pallas_call(functools.partial(finish_kernel, gain), grid=(cols // bloc...  5.4 us
    gather x2, other arithmetic, on_device(): inverse[row_ids // block_rows] * block_rows + row_ids % block_rows  4.48 us
  transfers between devices with their start and end apart: 15, of which 12 were waited for; matrix products, arithmetic and copies ran while one was open for 8% of the time, Pallas kernels for 7%

profile of v4, /device:TPU:0, one launch (start us, length us, event | category | flops | bytes accessed | tf_op | source)
XLA Modules:
  0.0 149.8 jit_solution(8440729689549109928)
XLA Ops:
  7.2 0.0 all-gather.5.cloned.1.call-start
  7.2 0.7 all-gather.5.cloned.1.call-update
  7.9 2.2 %abs_reduce_fusion = (f32[128]{0:T(128)S(1)}, f32[128,4096]{1,0:T(8,128)S(1)}) fusion(f32[128,4096]{1,0:T(8,128)} %momentum_ref.1, bf16[128,4096]{1,0:T(8,128)(2,1)} %grad_ref.1), kind=kLoop, calls=%fused_computation.8 | loop fusion | flops 2097024 | bytes 5243392 | tf_op jit(solution)/shard_map/reduce_max | solution.py:317
  10.1 0.6 floor_convert_fusion
  10.7 0.0 copy-start.3
  10.7 1.1 copy.18
  11.8 6.3 %all-to-all-start = ((s16[8,128,512]{2,1,0:T(8,128)(2,1)}), s16[8,128,512]{2,1,0:T(8,128)(2,1)S(1)}, u32[]{:S(2)}, u32[]{:S(2)}) async-start(s16[8,128,512]{2,1,0:T(8,128)(2,1)} %bitcast.29), calls=%async_computation | async-start | bytes 2097152 | tf_op jit(solution)/shard_map/all_to_all | solution.py:320
  18.1 0.0 all-gather.7.cloned.1.call-start
  18.1 0.1 copy.14.unit_ref
  18.3 0.0 copy-done.3
  18.3 0.1 select_reduce_fusion
  18.4 0.7 fusion.14
  19.1 4.4 %compare_select_fusion.1 = s32[256,1]{0,1:T(1,128)S(1)} fusion(s32[]{:T(128)} %bitcast.4, s32[]{:T(128)} %bitcast.5, s32[]{:T(128)} %bitcast.6, s32[]{:T(128)} %bitcast.7, s32[]{:T(128)} %bitcast.8, s32[]{:T(128)} %bitcast.10, s32[]{:T(128)} %bitcast.9), kind=kLoop, calls=%fused_computation.27 | loop fusion | flops 5888 | bytes 1052 | tf_op jit(solution)/shard_map/gather | solution.py:338
  23.5 38.0 %all-to-all-done = s16[8,128,512]{2,1,0:T(8,128)(2,1)S(1)} async-done(((s16[8,128,512]{2,1,0:T(8,128)(2,1)}), s16[8,128,512]{2,1,0:T(8,128)(2,1)S(1)}, u32[]{:S(2)}, u32[]{:S(2)}) %all-to-all-start) | async-done | bytes 1048608 | tf_op jit(solution)/shard_map/all_to_all | solution.py:320
  61.5 1.7 %reduce-precision_convert_fusion = (bf16[128,4096]{1,0:T(8,128)(2,1)}, bf16[128,4096]{1,0:T(8,128)(2,1)}) fusion(f32[128,4096]{1,0:T(8,128)S(1)} %get-tuple-element.11), kind=kLoop, calls=%fused_computation.1 | loop fusion | flops 2097152 | bytes 4194304 | tf_op jit(solution)/shard_map/convert_element_type | solution.py:23
  63.2 0.0 all-gather.5.cloned.1.call-done
  63.2 3.0 %fusion.1 = f32[256,256]{1,0:T(8,128)S(1)} fusion(bf16[256,4096]{1,0:T(8,128)(2,1)} %all-gather.5.cloned.1.call-done, bf16[128,4096]{1,0:T(8,128)(2,1)} %get-tuple-element.20, bf16[128,4096]{1,0:T(8,128)(2,1)} %get-tuple-element.19), kind=kOutput, calls=%fused_computation.3 | convolution fusion | flops 541065216 | bytes 4456448 | tf_op jit(solution)/shard_map/dot_general | solution.py:323
  66.2 1.6 %collective-permute-start = (f32[128,256]{1,0:T(8,128)S(1)}, f32[128,256]{1,0:T(8,128)S(1)}, u32[]{:S(2)}, u32[]{:S(2)}) collective-permute-start(f32[128,256]{1,0:T(8,128)S(1)} %slice_add_fusion), channel_id=1, source_target_pairs={{0,1},{1,0},{2,3},{3,2},{4,5},{5,4},{6,7},{7,6},{8,9},{9,8},{10,11... | collective-permute-start | bytes 393224 | tf_op jit(solution)/shard_map/ppermute | solution.py:32
  67.8 0.6 fusion.11
  68.3 3.0 %collective-permute-done = f32[128,256]{1,0:T(8,128)S(1)} collective-permute-done((f32[128,256]{1,0:T(8,128)S(1)}, f32[128,256]{1,0:T(8,128)S(1)}, u32[]{:S(2)}, u32[]{:S(2)}) %collective-permute-start) | collective-permute-done | bytes 131104 | tf_op jit(solution)/shard_map/ppermute | solution.py:32
  71.3 1.6 %collective-permute-start.1 = (f32[128,256]{1,0:T(8,128)S(1)}, f32[128,256]{1,0:T(8,128)S(1)}, u32[]{:S(2)}, u32[]{:S(2)}) collective-permute-start(f32[128,256]{1,0:T(8,128)S(1)} %fusion.16.near_ref), channel_id=1, source_target_pairs={{0,2},{1,3},{2,0},{3,1},{4,6},{5,7},{6,4},{7,5},{8,10},{9,11},{10,... | collective-permute-start | bytes 393224 | tf_op jit(solution)/shard_map/ppermute | solution.py:32
  73.0 3.4 %collective-permute-done.1.far_ref = f32[128,256]{1,0:T(8,128)S(1)} collective-permute-done((f32[128,256]{1,0:T(8,128)S(1)}, f32[128,256]{1,0:T(8,128)S(1)}, u32[]{:S(2)}, u32[]{:S(2)}) %collective-permute-start.1) | collective-permute-done | bytes 131104 | tf_op jit(solution)/shard_map/ppermute | solution.py:32
  76.4 1.1 shard_map.67
  77.5 0.0 all-gather.7.cloned.1.call-update
  77.5 1.8 %collective-permute-start.4 = (f32[64,256]{1,0:T(8,128)S(1)}, f32[64,256]{1,0:T(8,128)S(1)}, u32[]{:S(2)}, u32[]{:S(2)}) collective-permute-start(f32[64,256]{1,0:T(8,128)S(1)} %get-tuple-element.13), channel_id=1, source_target_pairs={{0,24},{4,28},{8,16},{12,20},{16,8},{20,12},{24,0},{28,4},{1,25},{... | collective-permute-start | bytes 196616 | tf_op jit(solution)/shard_map/ppermute | solution.py:32
  79.3 0.0 collective-permute-start.3
  79.3 2.7 %collective-permute-start.2 = (f32[64,256]{1,0:T(8,128)S(1)}, f32[64,256]{1,0:T(8,128)S(1)}, u32[]{:S(2)}, u32[]{:S(2)}) collective-permute-start(f32[64,256]{1,0:T(8,128)S(1)} %get-tuple-element.13), channel_id=1, source_target_pairs={{0,8},{4,12},{8,0},{12,4},{16,24},{20,28},{24,16},{28,20},{1,9},{5... | collective-permute-start | bytes 196616 | tf_op jit(solution)/shard_map/ppermute | solution.py:32
  82.0 1.7 %collective-permute-done.4 = f32[64,256]{1,0:T(8,128)S(1)} collective-permute-done((f32[64,256]{1,0:T(8,128)S(1)}, f32[64,256]{1,0:T(8,128)S(1)}, u32[]{:S(2)}, u32[]{:S(2)}) %collective-permute-start.4) | collective-permute-done | bytes 65568 | tf_op jit(solution)/shard_map/ppermute | solution.py:32
  83.7 1.4 collective-permute-done.3
  85.1 0.0 collective-permute-done.2
  85.1 0.1 collective-permute-start.5
  85.2 1.2 collective-permute-done.5
  86.4 2.5 %collective-permute-start.8 = (f32[64,256]{1,0:T(8,128)S(1)}, f32[64,256]{1,0:T(8,128)S(1)}, u32[]{:S(2)}, u32[]{:S(2)}) collective-permute-start(f32[64,256]{1,0:T(8,128)S(1)} %add.98.refs_0_), channel_id=1, source_target_pairs={{0,3},{1,2},{2,1},{3,0},{4,7},{5,6},{6,5},{7,4},{8,11},{9,10},{10,... | collective-permute-start | bytes 196616 | tf_op jit(solution)/shard_map/ppermute | solution.py:32
  88.9 0.5 collective-permute-start.7
  89.4 0.5 collective-permute-start.6
  90.0 0.1 pad_add_fusion.place_ref
  90.0 1.6 %collective-permute-done.8.refs_3_ = f32[64,256]{1,0:T(8,128)S(1)} collective-permute-done((f32[64,256]{1,0:T(8,128)S(1)}, f32[64,256]{1,0:T(8,128)S(1)}, u32[]{:S(2)}, u32[]{:S(2)}) %collective-permute-start.8) | collective-permute-done | bytes 65568 | tf_op jit(solution)/shard_map/ppermute | solution.py:32
  91.7 1.5 %collective-permute-done.7.refs_2_ = f32[64,256]{1,0:T(8,128)S(1)} collective-permute-done((f32[64,256]{1,0:T(8,128)S(1)}, f32[64,256]{1,0:T(8,128)S(1)}, u32[]{:S(2)}, u32[]{:S(2)}) %collective-permute-start.7) | collective-permute-done | bytes 65568 | tf_op jit(solution)/shard_map/ppermute | solution.py:32
  93.2 0.5 collective-permute-done.6.refs_1_
  93.7 11.2 %shard_map.69.inverse_ref = f32[256,256]{1,0:T(8,128)S(1)} custom-call(s32[4]{0:T(128)S(1)} %pad_add_fusion.place_ref, f32[64,256]{1,0:T(8,128)S(1)} %add.98.refs_0_, f32[64,256]{1,0:T(8,128)S(1)} %collective-permute-done.6.refs_1_, f32[64,256]{1,0:T(8,128)S(1)} %collective-permute-done.7.refs_2_, f32[64,256]{1,0:T(8,128)S(1)} %collective-permute-done.8.refs_3_), custom_call_target="tpu_custom_call" | custom-call | flops 201326592 | bytes 524288 | tf_op jit(solution)/shard_map/pallas_call | solution.py:155
  104.9 0.0 all-gather.7.cloned.1.call-done.proj_ref
  104.9 0.0 copy-start.2
  105.0 1.2 copy-done.2
  106.2 1.4 shard_map.68.share_ref
  107.6 0.0 copy-start
  107.6 0.0 copy-start.1
  107.6 1.0 shard_map.70
  108.6 22.2 %all-gather.8 = s16[4224,256]{1,0:T(8,128)(2,1)S(1)} all-gather(s16[528,256]{1,0:T(8,128)(2,1)S(1)} %get-tuple-element.15), channel_id=2, replica_groups=mesh['fsdp'=8,'tp'=4] {'fsdp'}, dimensions={0}, use_global_device_ids=true | all-gather | bytes 2433024 | tf_op jit(solution)/shard_map/all_gather | solution.py:351
  130.8 0.1 fusion.10
  130.9 1.6 %collective-permute-start.11 = (f32[1,256]{1,0:T(1,128)S(1)}, f32[1,256]{1,0:T(1,128)S(1)}, u32[]{:S(2)}, u32[]{:S(2)}) collective-permute-start(f32[1,256]{1,0:T(1,128)S(1)} %bitcast.31), channel_id=1, source_target_pairs={{0,3},{1,2},{2,1},{3,0},{4,7},{5,6},{6,5},{7,4},{8,11},{9,10},{10,... | collective-permute-start | bytes 3080 | tf_op jit(solution)/shard_map/ppermute | solution.py:32
  132.4 1.5 %collective-permute-start.10 = (f32[1,256]{1,0:T(1,128)S(1)}, f32[1,256]{1,0:T(1,128)S(1)}, u32[]{:S(2)}, u32[]{:S(2)}) collective-permute-start(f32[1,256]{1,0:T(1,128)S(1)} %bitcast.32), channel_id=1, source_target_pairs={{0,2},{1,3},{2,0},{3,1},{4,6},{5,7},{6,4},{7,5},{8,10},{9,11},{10,... | collective-permute-start | bytes 3080 | tf_op jit(solution)/shard_map/ppermute | solution.py:32
  134.0 0.4 collective-permute-start.9
  134.4 1.0 collective-permute-done.11
  135.4 0.6 collective-permute-done.10
  136.0 1.5 %collective-permute-done.9 = f32[1,256]{1,0:T(1,128)S(1)} collective-permute-done((f32[1,256]{1,0:T(1,128)S(1)}, f32[1,256]{1,0:T(1,128)S(1)}, u32[]{:S(2)}, u32[]{:S(2)}) %collective-permute-start.9) | collective-permute-done | bytes 1056 | tf_op jit(solution)/shard_map/ppermute | solution.py:32
  137.6 0.0 copy-done
  137.6 0.0 copy-done.1
  137.6 5.4 %shard_map.71 = (f32[128,4096]{1,0:T(8,128)}, f32[4096,256]{1,0:T(8,128)}, bf16[128,4096]{1,0:T(8,128)(2,1)}) custom-call(f32[128,4096]{1,0:T(8,128)S(1)} %copy-done, bf16[128,4096]{1,0:T(8,128)(2,1)S(1)} %copy-done.1, s16[8,528,256]{2,1,0:T(8,128)(2,1)S(1)} %bitcast.27, f32[128,256]{1,0:T(8,128)S(1)} %get-tuple-element.16.ortho_ref, ...), custom_call_target="tpu_custom_call" | custom-call | flops 1610612736 | bytes 12582912 | tf_op jit(solution)/shard_map/pallas_call | solution.py:281
  (9 shorter events, 0.2 us)
Async XLA Ops:
  7.2 56.0 %all-gather.5.cloned.1.call-start = ((), (), s32[]{:S(2)}) async-start(), calls=%async_computation.1 | async-start | bytes 2359296 | tf_op jit(solution)/shard_map/all_gather | solution.py:314
  10.7 7.6 %copy-start.3 = (s32[8]{0:T(128)S(1)}, s32[8]{0:T(128)}, u32[]{:S(2)}) copy-start(s32[8]{0:T(128)} %param.7) | copy-start | bytes 100
  11.8 49.8 %all-to-all-start = ((s16[8,128,512]{2,1,0:T(8,128)(2,1)}), s16[8,128,512]{2,1,0:T(8,128)(2,1)S(1)}, u32[]{:S(2)}, u32[]{:S(2)}) async-start(s16[8,128,512]{2,1,0:T(8,128)(2,1)} %bitcast.29), calls=%async_computation | async-start | bytes 2097152 | tf_op jit(solution)/shard_map/all_to_all | solution.py:320
  18.1 86.8 %all-gather.7.cloned.1.call-start = ((), (), s32[]{:S(2)}) async-start(), calls=%async_computation.2 | async-start | bytes 1179648 | tf_op jit(solution)/shard_map/all_gather | solution.py:342
  66.2 5.1 %collective-permute-start = (f32[128,256]{1,0:T(8,128)S(1)}, f32[128,256]{1,0:T(8,128)S(1)}, u32[]{:S(2)}, u32[]{:S(2)}) collective-permute-start(f32[128,256]{1,0:T(8,128)S(1)} %slice_add_fusion), channel_id=1, source_target_pairs={{0,1},{1,0},{2,3},{3,2},{4,5},{5,4},{6,7},{7,6},{8,9},{9,8},{10,11... | collective-permute-start | bytes 393224 | tf_op jit(solution)/shard_map/ppermute | solution.py:32
  71.3 5.0 %collective-permute-start.1 = (f32[128,256]{1,0:T(8,128)S(1)}, f32[128,256]{1,0:T(8,128)S(1)}, u32[]{:S(2)}, u32[]{:S(2)}) collective-permute-start(f32[128,256]{1,0:T(8,128)S(1)} %fusion.16.near_ref), channel_id=1, source_target_pairs={{0,2},{1,3},{2,0},{3,1},{4,6},{5,7},{6,4},{7,5},{8,10},{9,11},{10,... | collective-permute-start | bytes 393224 | tf_op jit(solution)/shard_map/ppermute | solution.py:32
  77.5 6.1 %collective-permute-start.4 = (f32[64,256]{1,0:T(8,128)S(1)}, f32[64,256]{1,0:T(8,128)S(1)}, u32[]{:S(2)}, u32[]{:S(2)}) collective-permute-start(f32[64,256]{1,0:T(8,128)S(1)} %get-tuple-element.13), channel_id=1, source_target_pairs={{0,24},{4,28},{8,16},{12,20},{16,8},{20,12},{24,0},{28,4},{1,25},{... | collective-permute-start | bytes 196616 | tf_op jit(solution)/shard_map/ppermute | solution.py:32
  79.3 5.8 %collective-permute-start.3 = (f32[64,256]{1,0:T(8,128)S(1)}, f32[64,256]{1,0:T(8,128)S(1)}, u32[]{:S(2)}, u32[]{:S(2)}) collective-permute-start(f32[64,256]{1,0:T(8,128)S(1)} %get-tuple-element.13), channel_id=1, source_target_pairs={{0,16},{4,20},{8,24},{12,28},{16,0},{20,4},{24,8},{28,12},{1,17},{... | collective-permute-start | bytes 196616 | tf_op jit(solution)/shard_map/ppermute | solution.py:32
  79.3 5.8 %collective-permute-start.2 = (f32[64,256]{1,0:T(8,128)S(1)}, f32[64,256]{1,0:T(8,128)S(1)}, u32[]{:S(2)}, u32[]{:S(2)}) collective-permute-start(f32[64,256]{1,0:T(8,128)S(1)} %get-tuple-element.13), channel_id=1, source_target_pairs={{0,8},{4,12},{8,0},{12,4},{16,24},{20,28},{24,16},{28,20},{1,9},{5... | collective-permute-start | bytes 196616 | tf_op jit(solution)/shard_map/ppermute | solution.py:32
  85.1 1.3 collective-permute-start.5
  86.4 5.3 %collective-permute-start.8 = (f32[64,256]{1,0:T(8,128)S(1)}, f32[64,256]{1,0:T(8,128)S(1)}, u32[]{:S(2)}, u32[]{:S(2)}) collective-permute-start(f32[64,256]{1,0:T(8,128)S(1)} %add.98.refs_0_), channel_id=1, source_target_pairs={{0,3},{1,2},{2,1},{3,0},{4,7},{5,6},{6,5},{7,4},{8,11},{9,10},{10,... | collective-permute-start | bytes 196616 | tf_op jit(solution)/shard_map/ppermute | solution.py:32
  88.9 4.3 %collective-permute-start.7 = (f32[64,256]{1,0:T(8,128)S(1)}, f32[64,256]{1,0:T(8,128)S(1)}, u32[]{:S(2)}, u32[]{:S(2)}) collective-permute-start(f32[64,256]{1,0:T(8,128)S(1)} %add.98.refs_0_), channel_id=1, source_target_pairs={{0,2},{1,3},{2,0},{3,1},{4,6},{5,7},{6,4},{7,5},{8,10},{9,11},{10,... | collective-permute-start | bytes 196616 | tf_op jit(solution)/shard_map/ppermute | solution.py:32
  89.4 4.3 %collective-permute-start.6 = (f32[64,256]{1,0:T(8,128)S(1)}, f32[64,256]{1,0:T(8,128)S(1)}, u32[]{:S(2)}, u32[]{:S(2)}) collective-permute-start(f32[64,256]{1,0:T(8,128)S(1)} %add.98.refs_0_), channel_id=1, source_target_pairs={{0,1},{1,0},{2,3},{3,2},{4,5},{5,4},{6,7},{7,6},{8,9},{9,8},{10,11... | collective-permute-start | bytes 196616 | tf_op jit(solution)/shard_map/ppermute | solution.py:32
  104.9 1.2 copy-start.2
  107.6 30.0 %copy-start = (f32[128,4096]{1,0:T(8,128)S(1)}, f32[128,4096]{1,0:T(8,128)}, u32[]{:S(2)}) copy-start(f32[128,4096]{1,0:T(8,128)} %momentum_ref.1) | copy-start | bytes 6291460
  107.6 30.0 %copy-start.1 = (bf16[128,4096]{1,0:T(8,128)(2,1)S(1)}, bf16[128,4096]{1,0:T(8,128)(2,1)}, u32[]{:S(2)}) copy-start(bf16[128,4096]{1,0:T(8,128)(2,1)} %grad_ref.1) | copy-start | bytes 3145732
  130.9 4.5 %collective-permute-start.11 = (f32[1,256]{1,0:T(1,128)S(1)}, f32[1,256]{1,0:T(1,128)S(1)}, u32[]{:S(2)}, u32[]{:S(2)}) collective-permute-start(f32[1,256]{1,0:T(1,128)S(1)} %bitcast.31), channel_id=1, source_target_pairs={{0,3},{1,2},{2,1},{3,0},{4,7},{5,6},{6,5},{7,4},{8,11},{9,10},{10,... | collective-permute-start | bytes 3080 | tf_op jit(solution)/shard_map/ppermute | solution.py:32
  132.4 3.6 %collective-permute-start.10 = (f32[1,256]{1,0:T(1,128)S(1)}, f32[1,256]{1,0:T(1,128)S(1)}, u32[]{:S(2)}, u32[]{:S(2)}) collective-permute-start(f32[1,256]{1,0:T(1,128)S(1)} %bitcast.32), channel_id=1, source_target_pairs={{0,2},{1,3},{2,0},{3,1},{4,6},{5,7},{6,4},{7,5},{8,10},{9,11},{10,... | collective-permute-start | bytes 3080 | tf_op jit(solution)/shard_map/ppermute | solution.py:32
  134.0 3.6 %collective-permute-start.9 = (f32[1,256]{1,0:T(1,128)S(1)}, f32[1,256]{1,0:T(1,128)S(1)}, u32[]{:S(2)}, u32[]{:S(2)}) collective-permute-start(f32[1,256]{1,0:T(1,128)S(1)} %bitcast.33), channel_id=1, source_target_pairs={{0,1},{1,0},{2,3},{3,2},{4,5},{5,4},{6,7},{7,6},{8,9},{9,8},{10,11... | collective-permute-start | bytes 3080 | tf_op jit(solution)/shard_map/ppermute | solution.py:32
Sparse Core Ops, SparseCore 0:
  9.6 51.6 all-gather.4
  77.6 21.4 all-gather.6

commit v5 on v4

--- a/solution.py
+++ b/solution.py
@@ -18,11 +18,6 @@
 PARAMS = pltpu.CompilerParams(vmem_limit_bytes=40 * 1024 * 1024)
 
 
-def split_two(x):
-    high = lax.reduce_precision(x, 8, 7)
-    return high.astype(jnp.bfloat16), (x - high).astype(jnp.bfloat16)
-
-
 def halves(x):
     high = x.astype(jnp.bfloat16)
     return high, (x - high.astype(jnp.float32)).astype(jnp.bfloat16)
@@ -52,6 +47,54 @@
 
 def dot_rows(a, b):
     return lax.dot_general(a, b, (((1,), (1,)), ((), ())), precision=HIGH, preferred_element_type=jnp.float32)
+
+
+def code_basis(basis):
+    value = basis.astype(jnp.float32)
+    size = jnp.abs(value)
+    normal = size >= 2.0**-126
+    exponent = jnp.floor(jnp.log2(jnp.where(normal, size, 1.0)))
+    code = 128.0 * (exponent + 126.0) + jnp.floor(128.0 * (size * jnp.exp2(-exponent)) + 0.5)
+    return jnp.where(normal, jnp.where(value < 0.0, -code, code), 0.0).astype(jnp.int16)
+
+
+def project_kernel(momentum_ref, grad_ref, code_ref, out_ref):
+    code = code_ref[...].astype(jnp.int32)
+    size = jnp.abs(code)
+    value = ((size & 127) + 128).astype(jnp.float32) * jnp.exp2(((size >> 7) - 134).astype(jnp.float32))
+    basis = jnp.where(code == 0, 0.0, jnp.where(code < 0, -value, value)).astype(jnp.bfloat16)
+    high, low = halves(momentum_ref[...] + grad_ref[...].astype(jnp.float32))
+
+    def times(a, b):
+        return lax.dot_general(a, b, (((1,), (1,)), ((), ())), preferred_element_type=jnp.float32)
+
+    part = times(high, basis) + times(low, basis)
+
+    @pl.when(pl.program_id(0) == 0)
+    def _():
+        out_ref[...] = part
+
+    @pl.when(pl.program_id(0) > 0)
+    def _():
+        out_ref[...] += part
+
+
+def project(momentum, grad, codes):
+    rows, cols = momentum.shape
+    rank = codes.shape[0]
+    block = min(1024, cols)
+    wide = pl.BlockSpec((rows, block), lambda i: (0, i))
+    return pl.pallas_call(
+        project_kernel,
+        grid=(cols // block,),
+        in_specs=[wide, wide, pl.BlockSpec((rank, block), lambda i: (0, i))],
+        out_specs=pl.BlockSpec((rows, rank), lambda i: (0, 0)),
+        out_shape=jax.ShapeDtypeStruct((rows, rank), jnp.float32),
+        compiler_params=PARAMS,
+        cost_estimate=pl.CostEstimate(
+            flops=4 * rows * cols * rank, bytes_accessed=rows * cols * 6 + rank * cols * 2, transcendentals=rank * cols
+        ),
+    )(momentum, grad, codes)
 
 
 def gram_kernel(column_ref, near_ref, far_ref, order_ref, unit_ref, proj_ref, scaled_ref, piece_ref, gram_ref):
@@ -167,107 +210,111 @@
     )(places, *pieces)
 
 
-def mix_kernel(code_ref, proj_ref, out_ref):
+def unit_of(exponent, mantissa):
+    return mantissa * jnp.exp2(exponent - 13.0)
+
+
+def encode_kernel(source_ref, scaled_ref, inverse_ref, proj_ref, code_ref, ortho_ref, mixed_ref):
     def times(a, b):
         return lax.dot_general(a, b, (((0,), (0,)), ((), ())), preferred_element_type=jnp.float32)
 
-    code_high, code_low = halves(code_ref[...].astype(jnp.int32).astype(jnp.float32))
-    proj_high, proj_low = halves(proj_ref[...])
-    part = times(code_high, proj_high) + (times(code_low, proj_high) + times(code_high, proj_low))
-
-    @pl.when(pl.program_id(0) == 0)
-    def _():
-        out_ref[...] = part
-
-    @pl.when(pl.program_id(0) > 0)
-    def _():
-        out_ref[...] += part
-
-
-def mix(codes, projected):
-    rows, cols = codes.shape
-    rank = projected.shape[1]
-    block = min(512, rows)
-    return pl.pallas_call(
-        mix_kernel,
-        grid=(rows // block,),
-        in_specs=[pl.BlockSpec((block, cols), lambda i: (i, 0)), pl.BlockSpec((block, rank), lambda i: (i, 0))],
-        out_specs=pl.BlockSpec((cols, rank), lambda i: (0, 0)),
-        out_shape=jax.ShapeDtypeStruct((cols, rank), jnp.float32),
-        compiler_params=PARAMS,
-        cost_estimate=pl.CostEstimate(
-            flops=6 * rows * cols * rank, bytes_accessed=rows * cols * 2 + rows * rank * 4, transcendentals=0
-        ),
-    )(codes, projected)
-
-
-def unit_of(exponent, mantissa):
-    return mantissa * jnp.exp2(exponent - 13.0)
-
-
-def encode_kernel(share_ref, inverse_ref, proj_ref, code_ref, ortho_ref):
-    inverse = inverse_ref[...]
-    ortho_ref[...] = dot_rows(proj_ref[...], inverse)
-    right = dot_rows(share_ref[...], inverse)
-    rows, rank = right.shape
-    square = jnp.maximum(jnp.sum(right * right, axis=0, keepdims=True), 1e-34)
-    square_exponent = jnp.floor(jnp.log2(square))
-    fine = square * jnp.exp2(13.0 - square_exponent)
-    square_high = jnp.floor(fine)
-    square_low = jnp.floor((fine - square_high) * 16384.0)
-    top = jnp.maximum(jnp.max(jnp.abs(right), axis=0, keepdims=True), 1e-28) * (1.0 / TOP)
-    exponent = jnp.floor(jnp.log2(top))
-    mantissa = jnp.floor(top * jnp.exp2(13.0 - exponent)) + 1.0
-    scaled = right * (1.0 / unit_of(exponent, mantissa))
-    code_ref[:rows, :] = jnp.floor(scaled + 0.5).astype(jnp.int32).astype(jnp.int16)
-    place = lax.broadcasted_iota(jnp.int32, (HEAD, rank), 0)
-    head = jnp.zeros((HEAD, rank), jnp.float32)
-    for k, row in enumerate((exponent, mantissa, square_exponent, square_high, square_low)):
-        head = jnp.where(place == k, row, head)
-    code_ref[rows:, :] = head.astype(jnp.int32).astype(jnp.int16)
-
-
-def encode(share, inverse_low, projected):
-    rows, rank = share.shape
+    source_high, source_low = halves(source_ref[...].astype(jnp.int32).astype(jnp.float32))
+    scaled_high, scaled_low = halves(scaled_ref[...])
+    part = times(source_high, scaled_high) + (times(source_low, scaled_high) + times(source_high, scaled_low))
+    first, last = pl.program_id(0) == 0, pl.program_id(0) == pl.num_programs(0) - 1
+
+    @pl.when(first)
+    def _():
+        mixed_ref[...] = part
+
+    @pl.when(jnp.logical_not(first))
+    def _():
+        mixed_ref[...] += part
+
+    @pl.when(last)
+    def _():
+        inverse = inverse_ref[...]
+        ortho_ref[...] = dot_rows(proj_ref[...], inverse)
+        right = dot_rows(mixed_ref[...], inverse)
+        rows, rank = right.shape
+        square = jnp.maximum(jnp.sum(right * right, axis=0, keepdims=True), 1e-34)
+        square_exponent = jnp.floor(jnp.log2(square))
+        fine = square * jnp.exp2(13.0 - square_exponent)
+        square_high = jnp.floor(fine)
+        square_low = jnp.floor((fine - square_high) * 16384.0)
+        top = jnp.maximum(jnp.max(jnp.abs(right), axis=0, keepdims=True), 1e-28) * (1.0 / TOP)
+        exponent = jnp.floor(jnp.log2(top))
+        mantissa = jnp.floor(top * jnp.exp2(13.0 - exponent)) + 1.0
+        scaled = right * (1.0 / unit_of(exponent, mantissa))
+        code_ref[:rows, :] = jnp.floor(scaled + 0.5).astype(jnp.int32).astype(jnp.int16)
+        place = lax.broadcasted_iota(jnp.int32, (HEAD, rank), 0)
+        head = jnp.zeros((HEAD, rank), jnp.float32)
+        for k, row in enumerate((exponent, mantissa, square_exponent, square_high, square_low)):
+            head = jnp.where(place == k, row, head)
+        code_ref[rows:, :] = head.astype(jnp.int32).astype(jnp.int16)
+
+
+def encode(source, scaled, inverse_low, projected):
+    total, share = source.shape
+    rank = scaled.shape[1]
+    block = min(512, total)
     return pl.pallas_call(
         encode_kernel,
+        grid=(total // block,),
+        in_specs=[
+            pl.BlockSpec((block, share), lambda i: (i, 0)),
+            pl.BlockSpec((block, rank), lambda i: (i, 0)),
+            whole(inverse_low),
+            whole(projected),
+        ],
+        out_specs=[pl.BlockSpec((share + HEAD, rank), lambda i: (0, 0)), whole(projected)],
         out_shape=[
-            jax.ShapeDtypeStruct((rows + HEAD, rank), jnp.int16),
+            jax.ShapeDtypeStruct((share + HEAD, rank), jnp.int16),
             jax.ShapeDtypeStruct(projected.shape, jnp.float32),
         ],
-        compiler_params=PARAMS,
-        cost_estimate=pl.CostEstimate(flops=12 * rows * rank * rank, bytes_accessed=rows * rank * 6, transcendentals=0),
-    )(share, inverse_low, projected)
-
-
-def finish_kernel(
-    gain, momentum_ref, grad_ref, code_ref, ortho_ref, scale_ref, next_ref, basis_ref, update_ref, high_ref, low_ref
-):
-    scale = scale_ref[...]
-    rows = momentum_ref.shape[0]
-
-    @pl.when(pl.program_id(0) == 0)
-    def _():
-        ortho = ortho_ref[...]
-        for start, factor in ((0, -KEEP_SHARE * ortho), (rows, gain * ortho * scale)):
-            high, low = halves(factor)
-            high_ref[start : start + rows, :] = high
-            low_ref[start : start + rows, :] = low
-
+        scratch_shapes=[pltpu.VMEM((share, rank), jnp.float32)],
+        compiler_params=PARAMS,
+        cost_estimate=pl.CostEstimate(
+            flops=6 * total * share * rank, bytes_accessed=total * (share * 2 + rank * 4), transcendentals=0
+        ),
+    )(source, scaled, inverse_low, projected)
+
+
+def decode(code_ref):
     code = code_ref[...].astype(jnp.int32).astype(jnp.float32)
     share = code.shape[1] - HEAD
     right = code[:, :share] * unit_of(code[:, share : share + 1], code[:, share + 1 : share + 2])
-    right = right.reshape(basis_ref.shape)
-    basis_ref[...] = right * scale
-    right_high, right_low = halves(right)
-
+    return right.reshape(code.shape[0] * share, code.shape[2])
+
+
+def times_rows(high_ref, low_ref, right):
     def times(a, b):
         return lax.dot_general(a, b, (((1,), (1,)), ((), ())), preferred_element_type=jnp.float32)
 
+    right_high, right_low = halves(right)
     high = high_ref[...]
-    both = times(high, right_high) + (times(low_ref[...], right_high) + times(high, right_low))
-    next_ref[...] = momentum_ref[...] + grad_ref[...].astype(jnp.float32) + both[:rows]
-    update_ref[...] = both[rows:].astype(jnp.bfloat16)
+    return times(high, right_high) + (times(low_ref[...], right_high) + times(high, right_low))
+
+
+def momentum_kernel(momentum_ref, grad_ref, code_ref, ortho_ref, next_ref, high_ref, low_ref):
+    @pl.when(pl.program_id(0) == 0)
+    def _():
+        high_ref[...], low_ref[...] = halves(-KEEP_SHARE * ortho_ref[...])
+
+    change = times_rows(high_ref, low_ref, decode(code_ref))
+    next_ref[...] = momentum_ref[...] + grad_ref[...].astype(jnp.float32) + change
+
+
+def update_kernel(gain, code_ref, ortho_ref, scale_ref, basis_ref, update_ref, high_ref, low_ref):
+    scale = scale_ref[...]
+
+    @pl.when(pl.program_id(0) == 0)
+    def _():
+        high_ref[...], low_ref[...] = halves(gain * ortho_ref[...])
+
+    basis = decode(code_ref) * scale
+    basis_ref[...] = basis
+    update_ref[...] = times_rows(high_ref, low_ref, basis).astype(jnp.bfloat16)
 
 
 def finish(momentum, grad, codes, orthonormal, scale, gain):
@@ -278,28 +325,35 @@
     block = group * share
     wide = pl.BlockSpec((rows, block), lambda i: (0, i))
     tall = pl.BlockSpec((block, rank), lambda i: (i, 0))
-    return pl.pallas_call(
-        functools.partial(finish_kernel, gain),
+    coded = pl.BlockSpec((group, share + HEAD, rank), lambda i: (i, 0, 0))
+    split = [pltpu.VMEM((rows, rank), jnp.bfloat16)] * 2
+    flops = 6 * rows * cols * rank
+    momentum_next = pl.pallas_call(
+        momentum_kernel,
         grid=(cols // block,),
-        in_specs=[
-            wide,
-            wide,
-            pl.BlockSpec((group, share + HEAD, rank), lambda i: (i, 0, 0)),
-            whole(orthonormal),
-            whole(scale),
-        ],
-        out_specs=[wide, tall, wide],
+        in_specs=[wide, wide, coded, whole(orthonormal)],
+        out_specs=wide,
+        out_shape=jax.ShapeDtypeStruct((rows, cols), jnp.float32),
+        scratch_shapes=split,
+        compiler_params=PARAMS,
+        cost_estimate=pl.CostEstimate(
+            flops=flops, bytes_accessed=rows * cols * 10 + cols * rank * 2, transcendentals=0
+        ),
+    )(momentum, grad, codes, orthonormal)
+    q_next, update = pl.pallas_call(
+        functools.partial(update_kernel, gain),
+        grid=(cols // block,),
+        in_specs=[coded, whole(orthonormal), whole(scale)],
+        out_specs=[tall, wide],
         out_shape=[
-            jax.ShapeDtypeStruct((rows, cols), jnp.float32),
             jax.ShapeDtypeStruct((cols, rank), jnp.float32),
             jax.ShapeDtypeStruct((rows, cols), jnp.bfloat16),
         ],
-        scratch_shapes=[pltpu.VMEM((2 * rows, rank), jnp.bfloat16)] * 2,
-        compiler_params=PARAMS,
-        cost_estimate=pl.CostEstimate(
-            flops=6 * 2 * rows * cols * rank, bytes_accessed=rows * cols * 12 + cols * rank * 6, transcendentals=0
-        ),
-    )(momentum, grad, codes, orthonormal, scale)
+        scratch_shapes=split,
+        compiler_params=PARAMS,
+        cost_estimate=pl.CostEstimate(flops=flops, bytes_accessed=rows * cols * 2 + cols * rank * 6, transcendentals=0),
+    )(codes, orthonormal, scale)
+    return momentum_next, q_next, update
 
 
 def on_device(momentum, grad, q_stored, perm):
@@ -311,22 +365,17 @@
     row_total, col_total = rows * num_blocks, cols * num_cols
     column = lax.axis_index("tp")
 
-    basis = lax.all_gather(q_stored, "fsdp", axis=0, tiled=True)
-
-    combined = momentum + grad.astype(jnp.float32)
+    basis = lax.all_gather(code_basis(q_stored), "fsdp", axis=0, tiled=True)
+
+    near = project(momentum, grad, basis)
+
+    momentum_again, near = lax.optimization_barrier((momentum, near))
+    combined = momentum_again + grad.astype(jnp.float32)
     unit = jnp.maximum(jnp.max(jnp.abs(combined), axis=1, keepdims=True), 1e-28) * (1.0 / TOP)
     codes = jnp.floor(combined * (1.0 / unit) + 0.5).astype(jnp.int16)
     codes = codes.reshape(rows, num_blocks, cols // num_blocks).transpose(1, 0, 2)
     codes = lax.all_to_all(codes, "fsdp", split_axis=0, concat_axis=0).reshape(row_total, cols // num_blocks)
-    codes, combined = lax.optimization_barrier((codes, combined))
-
-    stacked = lax.dot_general(
-        jnp.concatenate(split_two(combined), axis=0),
-        basis,
-        (((1,), (1,)), ((), ())),
-        preferred_element_type=jnp.float32,
-    )
-    near = stacked[:rows] + stacked[rows:]
+
     step = 1
     while 2 * step < num_cols:
         near = near + exchange(near, "tp", step)
@@ -345,11 +394,9 @@
     pieces = [piece] + [exchange(piece, "tp", k) for k in range(1, num_cols)]
     places = jnp.stack([column ^ k for k in range(num_cols)]).astype(jnp.int32)
     inverse_low = factor_inverse(places, pieces)
-    mixed = mix(codes, all_scaled)
-
-    code, orthonormal = encode(mixed, inverse_low, projected)
+    code, orthonormal = encode(codes, all_scaled, inverse_low, projected)
     gathered = lax.all_gather(code, "fsdp", axis=0)
-    share = mixed.shape[0]
+    share = codes.shape[1]
     head = gathered[:, share : share + 5].astype(jnp.float32)
     parts = (head[:, 3] + head[:, 4] * (1.0 / 16384.0)) * jnp.exp2(head[:, 2] - 13.0)
     squares = quad_sum(jnp.sum(parts, axis=0, keepdims=True), "tp")

time: 150 us -> 154 us (1.027)
  waiting for transfers between devices: 56.2 us -> 31.2 us
  blocking collectives: 22.2 us -> 47.1 us
  Pallas kernels: 20.1 us -> 28.4 us
  matrix products: 2.97 us -> 0 us
  local copies, waits for them, and re-layouts: 3.11 us -> 5.98 us
  starting transfers between devices: 21.2 us -> 18.8 us
  other arithmetic: 9.81 us -> 7.95 us
    all_to_all x1, waiting for transfers between devices: 38 us -> 0.01 us  [on_device(): lax.all_to_all(codes, 'fsdp', split_axis=0, concat_axis=0)]
    all_gather x0 -> x1, blocking collectives: none -> 25.1 us  [on_device(): basis = lax.all_gather(code_basis(q_stored), 'fsdp', axis=0, tiled=True)]
    ppermute x12, waiting for transfers between devices: 17.5 us -> 31.2 us  [exchange(): lax.ppermute(x, axis, [(i, i ^ k) for i in range(lax.axis_size(axis))])]
    pallas_call x3 -> x4, Pallas kernels: 7.8 us -> 16 us  [the longest x1 5.22 us: finish(): pl.pallas_call(momentum_kernel, grid=(cols // block,), in_specs=[wide, wi...]
    dot_general x1 -> x0, matrix products: 2.97 us -> none  [on_device(): lax.dot_general(jnp.concatenate(split_two(combined), axis=0), basis, (((1...]
    unnamed x8 -> x14, local copies, waits for them, and re-layouts: 1.24 us -> 4.11 us
    all_to_all x1, starting transfers between devices: 6.33 us -> 3.84 us  [on_device(): lax.all_to_all(codes, 'fsdp', split_axis=0, concat_axis=0)]
    reduce_max x1, other arithmetic: 2.18 us -> 0.33 us  [on_device(): jnp.max(jnp.abs(combined), axis=1, keepdims=True)]
  transfers between devices with their start and end apart: 15 -> 14, of which waited for: 12 -> 7; matrix products, arithmetic and copies ran while one was open for 8% -> 5% of each run, Pallas kernels for 7% -> 11%
where the time goes in v5:
time: 154 us
  blocking collectives  47.1 us (31%)
  waiting for transfers between devices  31.2 us (20%)
  Pallas kernels  28.4 us (18%)
  starting transfers between devices  18.8 us (12%)
  between operations  14.2 us (9%)
  other arithmetic  7.95 us (5%)
  local copies, waits for them, and re-layouts  5.98 us (4%)
    ppermute x12, waiting for transfers between devices, exchange(): lax.ppermute(x, axis, [(i, i ^ k) for i in range(lax.axis_size(axis))])  31.2 us
    all_gather x1, blocking collectives, on_device(): basis = lax.all_gather(code_basis(q_stored), 'fsdp', axis=0, tiled=True)  25.1 us
    all_gather x1, blocking collectives, on_device(): gathered = lax.all_gather(code, 'fsdp', axis=0)  22 us
    ppermute x12, starting transfers between devices, exchange(): lax.ppermute(x, axis, [(i, i ^ k) for i in range(lax.axis_size(axis))])  14.8 us
    pallas_call x1, Pallas kernels, factor_inverse(): pl.pallas_call(factor_kernel, grid_spec=pltpu.PrefetchScalarGridSpec(num_...  11.2 us
    pallas_call x1, Pallas kernels, finish(): pl.pallas_call(momentum_kernel, grid=(cols // block,), in_specs=[wide, wi...  5.22 us
    pallas_call x1, Pallas kernels, finish(): pl.pallas_call(functools.partial(update_kernel, gain), grid=(cols // bloc...  4.97 us
    gather x2, other arithmetic, on_device(): inverse[row_ids // block_rows] * block_rows + row_ids % block_rows  4.4 us
  transfers between devices with their start and end apart: 14, of which 7 were waited for; matrix products, arithmetic and copies ran while one was open for 5% of the time, Pallas kernels for 11%

profile of v5, /device:TPU:0, one launch (start us, length us, event | category | flops | bytes accessed | tf_op | source)
XLA Modules:
  0.0 153.6 jit_solution(9942426024719510744)
XLA Ops:
  7.2 0.0 copy-start
  7.2 1.6 %fusion.8 = s16[32,4096]{1,0:T(8,128)(2,1)S(1)} fusion(bf16[32,4096]{1,0:T(8,128)(2,1)} %param.6), kind=kLoop, calls=%fused_computation.17 | loop fusion | flops 2621440 | bytes 524288 | tf_op jit(solution)/shard_map/convert_element_type | solution.py:58
  8.7 25.1 %all-gather.6.code_ref = s16[256,4096]{1,0:T(8,128)(2,1)S(1)} all-gather(s16[32,4096]{1,0:T(8,128)(2,1)S(1)} %fusion.8), channel_id=1, replica_groups=mesh['fsdp'=8,'tp'=4] {'fsdp'}, dimensions={0}, use_global_device_ids=true | all-gather | bytes 2359296 | tf_op jit(solution)/shard_map/all_gather | solution.py:368
  33.9 0.0 copy-done
  33.9 0.0 copy-start.1
  33.9 1.2 copy-done.1
  35.1 3.5 %shard_map.67 = f32[128,256]{1,0:T(8,128)S(1)} custom-call(f32[128,4096]{1,0:T(8,128)S(1)} %copy-done, bf16[128,4096]{1,0:T(8,128)(2,1)S(1)} %copy-done.1, s16[256,4096]{1,0:T(8,128)(2,1)S(1)} %all-gather.6.code_ref), custom_call_target="tpu_custom_call" | custom-call | flops 536870912 | bytes 5242880 | tf_op jit(solution)/shard_map/pallas_call | solution.py:87
  38.6 1.6 %collective-permute-start = (f32[128,256]{1,0:T(8,128)S(1)}, f32[128,256]{1,0:T(8,128)S(1)}, u32[]{:S(2)}, u32[]{:S(2)}) collective-permute-start(f32[128,256]{1,0:T(8,128)S(1)} %shard_map.67), channel_id=1, source_target_pairs={{0,1},{1,0},{2,3},{3,2},{4,5},{5,4},{6,7},{7,6},{8,9},{9,8},{10,11... | collective-permute-start | bytes 393224 | tf_op jit(solution)/shard_map/ppermute | solution.py:27
  40.1 0.3 abs_reduce_fusion
  40.5 0.7 floor_convert_fusion
  41.2 0.0 copy-start.6
  41.2 1.1 copy.18
  42.2 3.8 %all-to-all-start = ((s16[8,128,512]{2,1,0:T(8,128)(2,1)}), s16[8,128,512]{2,1,0:T(8,128)(2,1)S(1)}, u32[]{:S(2)}, u32[]{:S(2)}) async-start(s16[8,128,512]{2,1,0:T(8,128)(2,1)} %bitcast.30), calls=%async_computation | async-start | bytes 2097152 | tf_op jit(solution)/shard_map/all_to_all | solution.py:377
  46.1 0.2 all-gather.5.cloned.1.call-start
  46.3 0.0 copy-done.6
  46.4 0.1 select_reduce_fusion
  46.4 0.7 fusion.17
  47.1 0.1 copy.14.unit_ref
  47.2 4.4 %compare_select_fusion.3 = s32[256,1]{0,1:T(1,128)S(1)} fusion(s32[]{:T(128)} %bitcast.4, s32[]{:T(128)} %bitcast.5, s32[]{:T(128)} %bitcast.6, s32[]{:T(128)} %bitcast.7, s32[]{:T(128)} %bitcast.8, s32[]{:T(128)} %bitcast.10, s32[]{:T(128)} %bitcast.9), kind=kLoop, calls=%fused_computation.33 | loop fusion | flops 5888 | bytes 1052 | tf_op jit(solution)/shard_map/gather | solution.py:387
  51.6 0.7 fusion.15
  52.3 0.0 collective-permute-done
  52.3 1.6 %collective-permute-start.1 = (f32[128,256]{1,0:T(8,128)S(1)}, f32[128,256]{1,0:T(8,128)S(1)}, u32[]{:S(2)}, u32[]{:S(2)}) collective-permute-start(f32[128,256]{1,0:T(8,128)S(1)} %add.106.near_ref), channel_id=1, source_target_pairs={{0,2},{1,3},{2,0},{3,1},{4,6},{5,7},{6,4},{7,5},{8,10},{9,11},{10,... | collective-permute-start | bytes 393224 | tf_op jit(solution)/shard_map/ppermute | solution.py:27
  53.9 4.1 %collective-permute-done.1.far_ref = f32[128,256]{1,0:T(8,128)S(1)} collective-permute-done((f32[128,256]{1,0:T(8,128)S(1)}, f32[128,256]{1,0:T(8,128)S(1)}, u32[]{:S(2)}, u32[]{:S(2)}) %collective-permute-start.1) | collective-permute-done | bytes 131104 | tf_op jit(solution)/shard_map/ppermute | solution.py:27
  58.1 1.1 shard_map.68
  59.2 0.0 all-gather.5.cloned.1.call-update
  59.2 1.7 %collective-permute-start.2 = (f32[64,256]{1,0:T(8,128)S(1)}, f32[64,256]{1,0:T(8,128)S(1)}, u32[]{:S(2)}, u32[]{:S(2)}) collective-permute-start(f32[64,256]{1,0:T(8,128)S(1)} %get-tuple-element.15), channel_id=1, source_target_pairs={{0,8},{4,12},{8,0},{12,4},{16,24},{20,28},{24,16},{28,20},{1,9},{5... | collective-permute-start | bytes 196616 | tf_op jit(solution)/shard_map/ppermute | solution.py:27
  60.9 2.4 %collective-permute-start.3 = (f32[64,256]{1,0:T(8,128)S(1)}, f32[64,256]{1,0:T(8,128)S(1)}, u32[]{:S(2)}, u32[]{:S(2)}) collective-permute-start(f32[64,256]{1,0:T(8,128)S(1)} %get-tuple-element.15), channel_id=1, source_target_pairs={{0,16},{4,20},{8,24},{12,28},{16,0},{20,4},{24,8},{28,12},{1,17},{... | collective-permute-start | bytes 196616 | tf_op jit(solution)/shard_map/ppermute | solution.py:27
  63.3 0.4 collective-permute-start.4
  63.7 2.0 %collective-permute-done.2 = f32[64,256]{1,0:T(8,128)S(1)} collective-permute-done((f32[64,256]{1,0:T(8,128)S(1)}, f32[64,256]{1,0:T(8,128)S(1)}, u32[]{:S(2)}, u32[]{:S(2)}) %collective-permute-start.2) | collective-permute-done | bytes 65568 | tf_op jit(solution)/shard_map/ppermute | solution.py:27
  65.7 20.1 %collective-permute-done.3 = f32[64,256]{1,0:T(8,128)S(1)} collective-permute-done((f32[64,256]{1,0:T(8,128)S(1)}, f32[64,256]{1,0:T(8,128)S(1)}, u32[]{:S(2)}, u32[]{:S(2)}) %collective-permute-start.3) | collective-permute-done | bytes 65568 | tf_op jit(solution)/shard_map/ppermute | solution.py:27
  85.8 0.0 collective-permute-done.4
  85.8 0.1 collective-permute-start.5
  85.9 1.2 collective-permute-done.5
  87.2 0.6 collective-permute-start.6
  87.8 1.5 collective-permute-start.7
  89.3 1.4 collective-permute-start.8
  90.7 0.1 pad_add_fusion.place_ref
  90.8 0.8 collective-permute-done.6.refs_1_
  91.6 0.5 collective-permute-done.7.refs_2_
  92.0 2.4 %collective-permute-done.8.refs_3_ = f32[64,256]{1,0:T(8,128)S(1)} collective-permute-done((f32[64,256]{1,0:T(8,128)S(1)}, f32[64,256]{1,0:T(8,128)S(1)}, u32[]{:S(2)}, u32[]{:S(2)}) %collective-permute-start.8) | collective-permute-done | bytes 65568 | tf_op jit(solution)/shard_map/ppermute | solution.py:27
  94.4 11.2 %shard_map.69.inverse_ref = f32[256,256]{1,0:T(8,128)S(1)} custom-call(s32[4]{0:T(128)S(1)} %pad_add_fusion.place_ref, f32[64,256]{1,0:T(8,128)S(1)} %add.114.refs_0_, f32[64,256]{1,0:T(8,128)S(1)} %collective-permute-done.6.refs_1_, f32[64,256]{1,0:T(8,128)S(1)} %collective-permute-done.7.refs_2_, f32[64,256]{1,0:T(8,128)S(1)} %collective-permute-done.8.refs_3_), custom_call_target="tpu_custom_call" | custom-call | flops 201326592 | bytes 524288 | tf_op jit(solution)/shard_map/pallas_call | solution.py:198
  105.7 0.0 copy-start.4
  105.7 0.7 copy-done.4
  106.4 0.0 all-to-all-done
  106.4 0.0 all-gather.5.cloned.1.call-done.scaled_ref
  106.4 0.0 copy-start.3
  106.4 1.2 copy-done.3
  107.6 0.0 copy-start.5
  107.6 0.9 copy-done.5
  108.5 0.0 copy-start.2
  108.5 2.4 %shard_map.70 = (s16[528,256]{1,0:T(8,128)(2,1)S(1)}, f32[128,256]{1,0:T(8,128)S(1)}) custom-call(s16[1024,512]{1,0:T(8,128)(2,1)S(1)} %bitcast.28, f32[1024,256]{1,0:T(8,128)S(1)} %copy-done.3, f32[256,256]{1,0:T(8,128)S(1)} %copy-done.5, f32[128,256]{1,0:T(8,128)S(1)} %get-tuple-element.16.proj_ref), custom_call_target="tpu_custom_call" | custom-call | flops 805306368 | bytes 2097152 | tf_op jit(solution)/shard_map/pallas_call | solution.py:261
  110.9 22.0 %all-gather.7 = s16[4224,256]{1,0:T(8,128)(2,1)S(1)} all-gather(s16[528,256]{1,0:T(8,128)(2,1)S(1)} %get-tuple-element.17), channel_id=2, replica_groups=mesh['fsdp'=8,'tp'=4] {'fsdp'}, dimensions={0}, use_global_device_ids=true | all-gather | bytes 2433024 | tf_op jit(solution)/shard_map/all_gather | solution.py:398
  132.9 0.1 fusion.14
  133.0 0.6 collective-permute-start.10
  133.6 2.4 %collective-permute-start.11 = (f32[1,256]{1,0:T(1,128)S(1)}, f32[1,256]{1,0:T(1,128)S(1)}, u32[]{:S(2)}, u32[]{:S(2)}) collective-permute-start(f32[1,256]{1,0:T(1,128)S(1)} %bitcast.32), channel_id=1, source_target_pairs={{0,3},{1,2},{2,1},{3,0},{4,7},{5,6},{6,5},{7,4},{8,11},{9,10},{10,... | collective-permute-start | bytes 3080 | tf_op jit(solution)/shard_map/ppermute | solution.py:27
  136.0 0.5 collective-permute-start.9
  136.5 0.0 copy-done.2
  136.5 5.2 %shard_map.71 = f32[128,4096]{1,0:T(8,128)} custom-call(f32[128,4096]{1,0:T(8,128)S(1)} %copy-done, bf16[128,4096]{1,0:T(8,128)(2,1)S(1)} %copy-done.2, s16[8,528,256]{2,1,0:T(8,128)(2,1)S(1)} %bitcast.26, f32[128,256]{1,0:T(8,128)S(1)} %get-tuple-element.18.ortho_ref), custom_call_target="tpu_custom_call" | custom-call | flops 805306368 | bytes 7340032 | tf_op jit(solution)/shard_map/pallas_call | solution.py:331
  141.8 0.0 collective-permute-done.10
  141.8 0.0 collective-permute-done.11
  141.8 0.0 collective-permute-done.9
  141.8 5.0 %shard_map.72 = (f32[4096,256]{1,0:T(8,128)}, bf16[128,4096]{1,0:T(8,128)(2,1)}) custom-call(s16[8,528,256]{2,1,0:T(8,128)(2,1)S(1)} %bitcast.27, f32[128,256]{1,0:T(8,128)S(1)} %get-tuple-element.18.ortho_ref, f32[1,256]{1,0:T(1,128)S(1)} %add_rsqrt_fusion.scale_ref), custom_call_target="tpu_custom_call" | custom-call | flops 805306368 | bytes 7340032 | tf_op jit(solution)/shard_map/pallas_call | solution.py:343
  (8 shorter events, 0.1 us)
Async XLA Ops:
  7.2 26.7 %copy-start = (f32[128,4096]{1,0:T(8,128)S(1)}, f32[128,4096]{1,0:T(8,128)}, u32[]{:S(2)}) copy-start(f32[128,4096]{1,0:T(8,128)} %momentum_ref.3) | copy-start | bytes 6291460
  33.9 1.2 copy-start.1
  38.6 13.7 %collective-permute-start = (f32[128,256]{1,0:T(8,128)S(1)}, f32[128,256]{1,0:T(8,128)S(1)}, u32[]{:S(2)}, u32[]{:S(2)}) collective-permute-start(f32[128,256]{1,0:T(8,128)S(1)} %shard_map.67), channel_id=1, source_target_pairs={{0,1},{1,0},{2,3},{3,2},{4,5},{5,4},{6,7},{7,6},{8,9},{9,8},{10,11... | collective-permute-start | bytes 393224 | tf_op jit(solution)/shard_map/ppermute | solution.py:27
  41.2 5.2 %copy-start.6 = (s32[8]{0:T(128)S(1)}, s32[8]{0:T(128)}, u32[]{:S(2)}) copy-start(s32[8]{0:T(128)} %param.7) | copy-start | bytes 100
  42.2 64.1 %all-to-all-start = ((s16[8,128,512]{2,1,0:T(8,128)(2,1)}), s16[8,128,512]{2,1,0:T(8,128)(2,1)S(1)}, u32[]{:S(2)}, u32[]{:S(2)}) async-start(s16[8,128,512]{2,1,0:T(8,128)(2,1)} %bitcast.30), calls=%async_computation | async-start | bytes 2097152 | tf_op jit(solution)/shard_map/all_to_all | solution.py:377
  46.1 60.3 %all-gather.5.cloned.1.call-start = ((), (), s32[]{:S(2)}) async-start(), calls=%async_computation.1 | async-start | bytes 1179648 | tf_op jit(solution)/shard_map/all_gather | solution.py:391
  52.3 5.7 %collective-permute-start.1 = (f32[128,256]{1,0:T(8,128)S(1)}, f32[128,256]{1,0:T(8,128)S(1)}, u32[]{:S(2)}, u32[]{:S(2)}) collective-permute-start(f32[128,256]{1,0:T(8,128)S(1)} %add.106.near_ref), channel_id=1, source_target_pairs={{0,2},{1,3},{2,0},{3,1},{4,6},{5,7},{6,4},{7,5},{8,10},{9,11},{10,... | collective-permute-start | bytes 393224 | tf_op jit(solution)/shard_map/ppermute | solution.py:27
  59.2 6.5 %collective-permute-start.2 = (f32[64,256]{1,0:T(8,128)S(1)}, f32[64,256]{1,0:T(8,128)S(1)}, u32[]{:S(2)}, u32[]{:S(2)}) collective-permute-start(f32[64,256]{1,0:T(8,128)S(1)} %get-tuple-element.15), channel_id=1, source_target_pairs={{0,8},{4,12},{8,0},{12,4},{16,24},{20,28},{24,16},{28,20},{1,9},{5... | collective-permute-start | bytes 196616 | tf_op jit(solution)/shard_map/ppermute | solution.py:27
  60.9 24.9 %collective-permute-start.3 = (f32[64,256]{1,0:T(8,128)S(1)}, f32[64,256]{1,0:T(8,128)S(1)}, u32[]{:S(2)}, u32[]{:S(2)}) collective-permute-start(f32[64,256]{1,0:T(8,128)S(1)} %get-tuple-element.15), channel_id=1, source_target_pairs={{0,16},{4,20},{8,24},{12,28},{16,0},{20,4},{24,8},{28,12},{1,17},{... | collective-permute-start | bytes 196616 | tf_op jit(solution)/shard_map/ppermute | solution.py:27
  63.3 22.5 %collective-permute-start.4 = (f32[64,256]{1,0:T(8,128)S(1)}, f32[64,256]{1,0:T(8,128)S(1)}, u32[]{:S(2)}, u32[]{:S(2)}) collective-permute-start(f32[64,256]{1,0:T(8,128)S(1)} %get-tuple-element.15), channel_id=1, source_target_pairs={{0,24},{4,28},{8,16},{12,20},{16,8},{20,12},{24,0},{28,4},{1,25},{... | collective-permute-start | bytes 196616 | tf_op jit(solution)/shard_map/ppermute | solution.py:27
  85.8 1.3 collective-permute-start.5
  87.2 4.4 %collective-permute-start.6 = (f32[64,256]{1,0:T(8,128)S(1)}, f32[64,256]{1,0:T(8,128)S(1)}, u32[]{:S(2)}, u32[]{:S(2)}) collective-permute-start(f32[64,256]{1,0:T(8,128)S(1)} %add.114.refs_0_), channel_id=1, source_target_pairs={{0,1},{1,0},{2,3},{3,2},{4,5},{5,4},{6,7},{7,6},{8,9},{9,8},{10,11... | collective-permute-start | bytes 196616 | tf_op jit(solution)/shard_map/ppermute | solution.py:27
  87.8 4.3 %collective-permute-start.7 = (f32[64,256]{1,0:T(8,128)S(1)}, f32[64,256]{1,0:T(8,128)S(1)}, u32[]{:S(2)}, u32[]{:S(2)}) collective-permute-start(f32[64,256]{1,0:T(8,128)S(1)} %add.114.refs_0_), channel_id=1, source_target_pairs={{0,2},{1,3},{2,0},{3,1},{4,6},{5,7},{6,4},{7,5},{8,10},{9,11},{10,... | collective-permute-start | bytes 196616 | tf_op jit(solution)/shard_map/ppermute | solution.py:27
  89.3 5.2 %collective-permute-start.8 = (f32[64,256]{1,0:T(8,128)S(1)}, f32[64,256]{1,0:T(8,128)S(1)}, u32[]{:S(2)}, u32[]{:S(2)}) collective-permute-start(f32[64,256]{1,0:T(8,128)S(1)} %add.114.refs_0_), channel_id=1, source_target_pairs={{0,3},{1,2},{2,1},{3,0},{4,7},{5,6},{6,5},{7,4},{8,11},{9,10},{10,... | collective-permute-start | bytes 196616 | tf_op jit(solution)/shard_map/ppermute | solution.py:27
  105.7 0.7 copy-start.4
  106.4 1.2 copy-start.3
  107.6 0.9 copy-start.5
  108.5 28.0 %copy-start.2 = (bf16[128,4096]{1,0:T(8,128)(2,1)S(1)}, bf16[128,4096]{1,0:T(8,128)(2,1)}, u32[]{:S(2)}) copy-start(bf16[128,4096]{1,0:T(8,128)(2,1)} %grad_ref.3) | copy-start | bytes 3145732
  133.0 8.8 %collective-permute-start.10 = (f32[1,256]{1,0:T(1,128)S(1)}, f32[1,256]{1,0:T(1,128)S(1)}, u32[]{:S(2)}, u32[]{:S(2)}) collective-permute-start(f32[1,256]{1,0:T(1,128)S(1)} %bitcast.31), channel_id=1, source_target_pairs={{0,2},{1,3},{2,0},{3,1},{4,6},{5,7},{6,4},{7,5},{8,10},{9,11},{10,... | collective-permute-start | bytes 3080 | tf_op jit(solution)/shard_map/ppermute | solution.py:27
  133.6 8.2 %collective-permute-start.11 = (f32[1,256]{1,0:T(1,128)S(1)}, f32[1,256]{1,0:T(1,128)S(1)}, u32[]{:S(2)}, u32[]{:S(2)}) collective-permute-start(f32[1,256]{1,0:T(1,128)S(1)} %bitcast.32), channel_id=1, source_target_pairs={{0,3},{1,2},{2,1},{3,0},{4,7},{5,6},{6,5},{7,4},{8,11},{9,10},{10,... | collective-permute-start | bytes 3080 | tf_op jit(solution)/shard_map/ppermute | solution.py:27
  136.0 5.8 %collective-permute-start.9 = (f32[1,256]{1,0:T(1,128)S(1)}, f32[1,256]{1,0:T(1,128)S(1)}, u32[]{:S(2)}, u32[]{:S(2)}) collective-permute-start(f32[1,256]{1,0:T(1,128)S(1)} %bitcast.33), channel_id=1, source_target_pairs={{0,1},{1,0},{2,3},{3,2},{4,5},{5,4},{6,7},{7,6},{8,9},{9,8},{10,11... | collective-permute-start | bytes 3080 | tf_op jit(solution)/shard_map/ppermute | solution.py:27
Sparse Core Ops, SparseCore 0:
  59.3 27.2 all-gather.4

commit v6 on v5

--- a/solution.py
+++ b/solution.py
@@ -97,24 +97,32 @@
     )(momentum, grad, codes)
 
 
-def gram_kernel(column_ref, near_ref, far_ref, order_ref, unit_ref, proj_ref, scaled_ref, piece_ref, gram_ref):
-    proj = jnp.dot(near_ref[...] + far_ref[...], order_ref[...], precision=HIGH, preferred_element_type=jnp.float32)
+def gram_kernel(column_ref, perm_ref, near_ref, far_ref, unit_ref, proj_ref, scaled_ref, piece_ref, gram_ref):
+    rank = gram_ref.shape[0]
+    blocks = perm_ref.shape[0]
+    size = rank // blocks
+    stored = lax.broadcasted_iota(jnp.int32, (rank, rank), 0)
+    target = jnp.zeros((rank, rank), jnp.int32)
+    for s in range(blocks):
+        target = jnp.where(stored // size == s, perm_ref[s] * size + stored % size, target)
+    order = (target == lax.broadcasted_iota(jnp.int32, (rank, rank), 1)).astype(jnp.float32)
+    proj = jnp.dot(near_ref[...] + far_ref[...], order, precision=HIGH, preferred_element_type=jnp.float32)
     proj_ref[...] = proj
     scaled_ref[...] = proj * unit_ref[...]
     gram_ref[...] = lax.dot_general(
         proj, proj, (((0,), (0,)), ((), ())), precision=HIGH, preferred_element_type=jnp.float32
     )
-    size = piece_ref.shape[0]
-    piece_ref[...] = gram_ref[pl.ds(pl.multiple_of(column_ref[0] * size, size), size), :]
-
-
-def gram_parts(column, near, far, order, unit, columns):
+    rows = piece_ref.shape[0]
+    piece_ref[...] = gram_ref[pl.ds(pl.multiple_of(column_ref[0] * rows, rows), rows), :]
+
+
+def gram_parts(column, perm, near, far, unit, columns):
     rows, rank = near.shape
-    operands = (near, far, order, unit)
+    operands = (near, far, unit)
     return pl.pallas_call(
         gram_kernel,
         grid_spec=pltpu.PrefetchScalarGridSpec(
-            num_scalar_prefetch=1,
+            num_scalar_prefetch=2,
             grid=(1,),
             in_specs=[whole(x) for x in operands],
             out_specs=[whole(near), whole(near), pl.BlockSpec((rank // columns, rank), lambda *_: (0, 0))],
@@ -127,7 +135,7 @@
         ],
         compiler_params=PARAMS,
         cost_estimate=pl.CostEstimate(flops=24 * rows * rank * rank, bytes_accessed=rank * rank * 12, transcendentals=0),
-    )(column, *operands)
+    )(column, perm, *operands)
 
 
 def spread(row):
@@ -287,46 +295,48 @@
     return right.reshape(code.shape[0] * share, code.shape[2])
 
 
-def times_rows(high_ref, low_ref, right):
+def times_rows(split_ref, right):
     def times(a, b):
         return lax.dot_general(a, b, (((1,), (1,)), ((), ())), preferred_element_type=jnp.float32)
 
     right_high, right_low = halves(right)
-    high = high_ref[...]
-    return times(high, right_high) + (times(low_ref[...], right_high) + times(high, right_low))
-
-
-def momentum_kernel(momentum_ref, grad_ref, code_ref, ortho_ref, next_ref, high_ref, low_ref):
+    split = split_ref[...]
+    rows = split.shape[0] // 2
+    most = times(split, right_high)
+    return most[:rows] + (most[rows:] + times(split[:rows], right_low))
+
+
+def set_split(split_ref, x):
+    rows = x.shape[0]
+
     @pl.when(pl.program_id(0) == 0)
     def _():
-        high_ref[...], low_ref[...] = halves(-KEEP_SHARE * ortho_ref[...])
-
-    change = times_rows(high_ref, low_ref, decode(code_ref))
+        split_ref[:rows], split_ref[rows:] = halves(x)
+
+
+def momentum_kernel(momentum_ref, grad_ref, code_ref, ortho_ref, next_ref, split_ref):
+    set_split(split_ref, -KEEP_SHARE * ortho_ref[...])
+    change = times_rows(split_ref, decode(code_ref))
     next_ref[...] = momentum_ref[...] + grad_ref[...].astype(jnp.float32) + change
 
 
-def update_kernel(gain, code_ref, ortho_ref, scale_ref, basis_ref, update_ref, high_ref, low_ref):
-    scale = scale_ref[...]
-
-    @pl.when(pl.program_id(0) == 0)
-    def _():
-        high_ref[...], low_ref[...] = halves(gain * ortho_ref[...])
-
-    basis = decode(code_ref) * scale
+def update_kernel(gain, code_ref, ortho_ref, scale_ref, basis_ref, update_ref, split_ref):
+    set_split(split_ref, gain * ortho_ref[...])
+    basis = decode(code_ref) * scale_ref[...]
     basis_ref[...] = basis
-    update_ref[...] = times_rows(high_ref, low_ref, basis).astype(jnp.bfloat16)
+    update_ref[...] = times_rows(split_ref, basis).astype(jnp.bfloat16)
 
 
 def finish(momentum, grad, codes, orthonormal, scale, gain):
     rows, cols = momentum.shape
     shares, share, rank = codes.shape
     share -= HEAD
-    group = max(1, min(512 // share, shares))
+    group = max(1, min(1024 // share, shares))
     block = group * share
     wide = pl.BlockSpec((rows, block), lambda i: (0, i))
     tall = pl.BlockSpec((block, rank), lambda i: (i, 0))
     coded = pl.BlockSpec((group, share + HEAD, rank), lambda i: (i, 0, 0))
-    split = [pltpu.VMEM((rows, rank), jnp.bfloat16)] * 2
+    split = [pltpu.VMEM((2 * rows, rank), jnp.bfloat16)]
     flops = 6 * rows * cols * rank
     momentum_next = pl.pallas_call(
         momentum_kernel,
@@ -365,28 +375,23 @@
     row_total, col_total = rows * num_blocks, cols * num_cols
     column = lax.axis_index("tp")
 
-    basis = lax.all_gather(code_basis(q_stored), "fsdp", axis=0, tiled=True)
-
-    near = project(momentum, grad, basis)
-
-    momentum_again, near = lax.optimization_barrier((momentum, near))
-    combined = momentum_again + grad.astype(jnp.float32)
+    combined = momentum + grad.astype(jnp.float32)
     unit = jnp.maximum(jnp.max(jnp.abs(combined), axis=1, keepdims=True), 1e-28) * (1.0 / TOP)
     codes = jnp.floor(combined * (1.0 / unit) + 0.5).astype(jnp.int16)
     codes = codes.reshape(rows, num_blocks, cols // num_blocks).transpose(1, 0, 2)
+
+    basis, codes = lax.optimization_barrier((code_basis(q_stored), codes))
+    basis = lax.all_gather(basis, "fsdp", axis=0, tiled=True)
+    codes, basis = lax.optimization_barrier((codes, basis))
     codes = lax.all_to_all(codes, "fsdp", split_axis=0, concat_axis=0).reshape(row_total, cols // num_blocks)
 
+    near = project(momentum, grad, basis)
     step = 1
     while 2 * step < num_cols:
         near = near + exchange(near, "tp", step)
         step *= 2
     far = exchange(near, "tp", step)
-    blocks = jnp.arange(num_blocks, dtype=jnp.int32)
-    inverse = jnp.sum(jnp.where(perm[:, None] == blocks[None, :], blocks[:, None], 0), axis=0)
-    row_ids = jnp.arange(rank_total, dtype=jnp.int32)
-    order_index = inverse[row_ids // block_rows] * block_rows + row_ids % block_rows
-    order = (row_ids[:, None] == order_index[None, :]).astype(jnp.float32)
-    projected, scaled, piece = gram_parts(column.reshape(1), near, far, order, unit, num_cols)
+    projected, scaled, piece = gram_parts(column.reshape(1), perm, near, far, unit, num_cols)
 
     all_scaled = lax.all_gather(scaled, "fsdp", axis=0, tiled=True)
     piece = quad_sum(piece, "fsdp", 2)

time: 154 us -> 157 us (1.019)
  waiting for transfers between devices: 31.2 us -> 41.7 us
  other arithmetic: 7.95 us -> 3.69 us
  Pallas kernels: 28.4 us -> 26.2 us
    ppermute x12, waiting for transfers between devices: 31.2 us -> 41.7 us  [exchange(): lax.ppermute(x, axis, [(i, i ^ k) for i in range(lax.axis_size(axis))])]
    gather x2 -> x0, other arithmetic: 4.4 us -> none  [on_device(): inverse[row_ids // block_rows] * block_rows + row_ids % block_rows]
    reduce_max x1, other arithmetic: 0.33 us -> 2.33 us  [on_device(): jnp.max(jnp.abs(combined), axis=1, keepdims=True)]
    pallas_call x1, Pallas kernels: 5.22 us -> 3.3 us  [finish(): pl.pallas_call(momentum_kernel, grid=(cols // block,), in_specs=[wide, wi...]
    pallas_call x1, Pallas kernels: 4.97 us -> 3.06 us  [finish(): pl.pallas_call(functools.partial(update_kernel, gain), grid=(cols // bloc...]
  transfers between devices with their start and end apart: 14 -> 14, of which waited for: 7 -> 7; matrix products, arithmetic and copies ran while one was open for 5% -> 0% of each run, Pallas kernels for 11% -> 10%
where the time goes in v6:
time: 157 us; the launch traced here: 156 us
  blocking collectives  47.1 us (30%)
  waiting for transfers between devices  41.7 us (27%)
  Pallas kernels  26.2 us (17%)
  starting transfers between devices  19.1 us (12%)
  between operations  14.2 us (9%)
  local copies, waits for them, and re-layouts  4.42 us (3%)
  other arithmetic  3.69 us (2%)
    ppermute x12, waiting for transfers between devices, exchange(): lax.ppermute(x, axis, [(i, i ^ k) for i in range(lax.axis_size(axis))])  41.7 us
    all_gather x1, blocking collectives, on_device(): basis = lax.all_gather(basis, 'fsdp', axis=0, tiled=True)  25.1 us
    all_gather x1, blocking collectives, on_device(): gathered = lax.all_gather(code, 'fsdp', axis=0)  22 us
    ppermute x12, starting transfers between devices, exchange(): lax.ppermute(x, axis, [(i, i ^ k) for i in range(lax.axis_size(axis))])  14.8 us
    pallas_call x1, Pallas kernels, factor_inverse(): pl.pallas_call(factor_kernel, grid_spec=pltpu.PrefetchScalarGridSpec(num_...  11.2 us
    all_to_all x1, starting transfers between devices, on_device(): lax.all_to_all(codes, 'fsdp', split_axis=0, concat_axis=0)  4.24 us
    pallas_call x1, Pallas kernels, project(): pl.pallas_call(project_kernel, grid=(cols // block,), in_specs=[wide, wid...  3.48 us
    pallas_call x1, Pallas kernels, encode(): pl.pallas_call(encode_kernel, grid=(total // block,), in_specs=[pl.BlockS...  3.44 us
  transfers between devices with their start and end apart: 14, of which 7 were waited for; matrix products, arithmetic and copies ran while one was open for 0% of the time, Pallas kernels for 10%

profile of v6, /device:TPU:0, one launch (start us, length us, event | category | flops | bytes accessed | tf_op | source)
XLA Modules:
  0.0 156.3 jit_solution(16087960312625144638)
XLA Ops:
  7.2 0.0 copy-start
  7.2 0.0 copy-start.1
  7.2 2.3 %abs_reduce_fusion = f32[128]{0:T(128)S(1)} fusion(f32[128,4096]{1,0:T(8,128)} %momentum_ref.3, bf16[128,4096]{1,0:T(8,128)(2,1)} %grad_ref.3), kind=kLoop, calls=%fused_computation.1 | loop fusion | flops 2097024 | bytes 3146240 | tf_op jit(solution)/shard_map/reduce_max | solution.py:379
  9.5 0.2 copy-done
  9.7 0.3 copy-done.1
  10.0 0.7 floor_convert_fusion
  10.7 0.0 copy-start.6
  10.7 1.1 copy.14
  11.7 0.0 copy-done.6
  11.7 0.5 fusion.8
  12.2 25.1 %all-gather.6.code_ref = s16[256,4096]{1,0:T(8,128)(2,1)S(1)} all-gather(s16[32,4096]{1,0:T(8,128)(2,1)S(1)} %fusion.8), channel_id=1, replica_groups=mesh['fsdp'=8,'tp'=4] {'fsdp'}, dimensions={0}, use_global_device_ids=true | all-gather | bytes 2359296 | tf_op jit(solution)/shard_map/all_gather | solution.py:384
  37.3 3.5 %shard_map.67 = f32[128,256]{1,0:T(8,128)S(1)} custom-call(f32[128,4096]{1,0:T(8,128)S(1)} %copy-done, bf16[128,4096]{1,0:T(8,128)(2,1)S(1)} %copy-done.1, s16[256,4096]{1,0:T(8,128)(2,1)S(1)} %all-gather.6.code_ref), custom_call_target="tpu_custom_call" | custom-call | flops 536870912 | bytes 5242880 | tf_op jit(solution)/shard_map/pallas_call | solution.py:87
  40.8 0.0 copy-start.3
  40.8 1.6 collective-permute-start
  42.4 4.3 %collective-permute-done = f32[128,256]{1,0:T(8,128)S(1)} collective-permute-done((f32[128,256]{1,0:T(8,128)S(1)}, f32[128,256]{1,0:T(8,128)S(1)}, u32[]{:S(2)}, u32[]{:S(2)}) %collective-permute-start) | collective-permute-done | bytes 131104 | tf_op jit(solution)/shard_map/ppermute | solution.py:27
  46.7 1.6 %collective-permute-start.1 = (f32[128,256]{1,0:T(8,128)S(1)}, f32[128,256]{1,0:T(8,128)S(1)}, u32[]{:S(2)}, u32[]{:S(2)}) collective-permute-start(f32[128,256]{1,0:T(8,128)S(1)} %add.68.near_ref), channel_id=1, source_target_pairs={{0,2},{1,3},{2,0},{3,1},{4,6},{5,7},{6,4},{7,5},{8,10},{9,11},{10,... | collective-permute-start | bytes 393224 | tf_op jit(solution)/shard_map/ppermute | solution.py:27
  48.3 4.2 %all-to-all-start = ((s16[8,128,512]{2,1,0:T(8,128)(2,1)}), s16[8,128,512]{2,1,0:T(8,128)(2,1)}, u32[]{:S(2)}, u32[]{:S(2)}) async-start(s16[8,128,512]{2,1,0:T(8,128)(2,1)} %bitcast.20), calls=%async_computation | async-start | bytes 2097152 | tf_op jit(solution)/shard_map/all_to_all | solution.py:386
  52.5 0.0 all-gather.5.cloned.1.call-start
  52.6 0.1 copy.10.unit_ref
  52.7 0.0 collective-permute-done.1.far_ref
  52.7 0.0 copy-done.3
  52.7 1.7 %shard_map.68 = (f32[128,256]{1,0:T(8,128)S(1)}, f32[128,256]{1,0:T(8,128)}, f32[64,256]{1,0:T(8,128)S(1)}) custom-call(s32[1]{0:T(128)} %bitcast.2.column_ref, s32[8]{0:T(128)S(1)} %copy-done.3, f32[128,256]{1,0:T(8,128)S(1)} %add.68.near_ref, f32[128,256]{1,0:T(8,128)S(1)} %collective-permute-done.1.far_ref, f32[128,1]{1,0:T(8,128)S(1)} %copy.10.unit_ref), custom_call_target="tpu_custom_call" | custom-call | flops 201326592 | bytes 786432 | tf_op jit(solution)/shard_map/pallas_call | solution.py:122
  54.4 0.0 copy-start.4
  54.4 0.7 copy-done.4
  55.0 0.0 all-gather.5.cloned.1.call-update
  55.1 1.9 %collective-permute-start.2 = (f32[64,256]{1,0:T(8,128)S(1)}, f32[64,256]{1,0:T(8,128)S(1)}, u32[]{:S(2)}, u32[]{:S(2)}) collective-permute-start(f32[64,256]{1,0:T(8,128)S(1)} %get-tuple-element.19), channel_id=1, source_target_pairs={{0,8},{4,12},{8,0},{12,4},{16,24},{20,28},{24,16},{28,20},{1,9},{5... | collective-permute-start | bytes 196616 | tf_op jit(solution)/shard_map/ppermute | solution.py:27
  57.0 2.4 %collective-permute-start.3 = (f32[64,256]{1,0:T(8,128)S(1)}, f32[64,256]{1,0:T(8,128)S(1)}, u32[]{:S(2)}, u32[]{:S(2)}) collective-permute-start(f32[64,256]{1,0:T(8,128)S(1)} %get-tuple-element.19), channel_id=1, source_target_pairs={{0,16},{4,20},{8,24},{12,28},{16,0},{20,4},{24,8},{28,12},{1,17},{... | collective-permute-start | bytes 196616 | tf_op jit(solution)/shard_map/ppermute | solution.py:27
  59.4 0.2 collective-permute-start.4
  59.5 17.8 %collective-permute-done.2 = f32[64,256]{1,0:T(8,128)S(1)} collective-permute-done((f32[64,256]{1,0:T(8,128)S(1)}, f32[64,256]{1,0:T(8,128)S(1)}, u32[]{:S(2)}, u32[]{:S(2)}) %collective-permute-start.2) | collective-permute-done | bytes 65568 | tf_op jit(solution)/shard_map/ppermute | solution.py:27
  77.3 14.8 %collective-permute-done.3 = f32[64,256]{1,0:T(8,128)S(1)} collective-permute-done((f32[64,256]{1,0:T(8,128)S(1)}, f32[64,256]{1,0:T(8,128)S(1)}, u32[]{:S(2)}, u32[]{:S(2)}) %collective-permute-start.3) | collective-permute-done | bytes 65568 | tf_op jit(solution)/shard_map/ppermute | solution.py:27
  92.1 0.0 collective-permute-done.4
  92.1 0.1 collective-permute-start.5
  92.2 1.2 collective-permute-done.5
  93.5 1.6 collective-permute-start.6
  95.0 0.5 collective-permute-start.7
  95.5 1.5 collective-permute-start.8
  97.0 0.1 pad_add_fusion.place_ref
  97.1 0.7 collective-permute-done.6.refs_1_
  97.8 2.2 %collective-permute-done.7.refs_2_ = f32[64,256]{1,0:T(8,128)S(1)} collective-permute-done((f32[64,256]{1,0:T(8,128)S(1)}, f32[64,256]{1,0:T(8,128)S(1)}, u32[]{:S(2)}, u32[]{:S(2)}) %collective-permute-start.7) | collective-permute-done | bytes 65568 | tf_op jit(solution)/shard_map/ppermute | solution.py:27
  100.0 0.7 collective-permute-done.8.refs_3_
  100.7 11.2 %shard_map.69.inverse_ref = f32[256,256]{1,0:T(8,128)S(1)} custom-call(s32[4]{0:T(128)S(1)} %pad_add_fusion.place_ref, f32[64,256]{1,0:T(8,128)S(1)} %add.72.refs_0_, f32[64,256]{1,0:T(8,128)S(1)} %collective-permute-done.6.refs_1_, f32[64,256]{1,0:T(8,128)S(1)} %collective-permute-done.7.refs_2_, f32[64,256]{1,0:T(8,128)S(1)} %collective-permute-done.8.refs_3_), custom_call_target="tpu_custom_call" | custom-call | flops 201326592 | bytes 524288 | tf_op jit(solution)/shard_map/pallas_call | solution.py:206
  111.9 0.0 all-to-all-done
  111.9 0.0 all-gather.5.cloned.1.call-done.scaled_ref
  111.9 0.0 copy-start.2
  112.0 1.2 copy-done.2
  113.2 0.0 copy-start.5
  113.2 0.9 copy-done.5
  114.1 3.4 %shard_map.70 = (s16[528,256]{1,0:T(8,128)(2,1)S(1)}, f32[128,256]{1,0:T(8,128)S(1)}) custom-call(s16[1024,512]{1,0:T(8,128)(2,1)} %bitcast.1.source_ref, f32[1024,256]{1,0:T(8,128)S(1)} %copy-done.2, f32[256,256]{1,0:T(8,128)S(1)} %shard_map.69.inverse_ref, f32[128,256]{1,0:T(8,128)S(1)} %copy-done.5), custom_call_target="tpu_custom_call" | custom-call | flops 805306368 | bytes 2097152 | tf_op jit(solution)/shard_map/pallas_call | solution.py:269
  117.5 22.0 %all-gather.7 = s16[4224,256]{1,0:T(8,128)(2,1)S(1)} all-gather(s16[528,256]{1,0:T(8,128)(2,1)S(1)} %get-tuple-element.21), channel_id=2, replica_groups=mesh['fsdp'=8,'tp'=4] {'fsdp'}, dimensions={0}, use_global_device_ids=true | all-gather | bytes 2433024 | tf_op jit(solution)/shard_map/all_gather | solution.py:403
  139.5 0.1 fusion.13
  139.6 1.6 %collective-permute-start.10 = (f32[1,256]{1,0:T(1,128)S(1)}, f32[1,256]{1,0:T(1,128)S(1)}, u32[]{:S(2)}, u32[]{:S(2)}) collective-permute-start(f32[1,256]{1,0:T(1,128)S(1)} %bitcast.21), channel_id=1, source_target_pairs={{0,2},{1,3},{2,0},{3,1},{4,6},{5,7},{6,4},{7,5},{8,10},{9,11},{10,... | collective-permute-start | bytes 3080 | tf_op jit(solution)/shard_map/ppermute | solution.py:27
  141.1 0.5 collective-permute-start.11
  141.6 1.5 collective-permute-start.9
  143.1 3.3 %shard_map.71 = f32[128,4096]{1,0:T(8,128)} custom-call(f32[128,4096]{1,0:T(8,128)S(1)} %copy-done, bf16[128,4096]{1,0:T(8,128)(2,1)S(1)} %copy-done.1, s16[8,528,256]{2,1,0:T(8,128)(2,1)S(1)} %bitcast.17, f32[128,256]{1,0:T(8,128)S(1)} %get-tuple-element.22.ortho_ref), custom_call_target="tpu_custom_call" | custom-call | flops 805306368 | bytes 7340032 | tf_op jit(solution)/shard_map/pallas_call | solution.py:341
  146.4 0.0 collective-permute-done.10
  146.4 0.0 collective-permute-done.11
  146.4 0.0 collective-permute-done.9
  146.4 3.1 %shard_map.72 = (f32[4096,256]{1,0:T(8,128)}, bf16[128,4096]{1,0:T(8,128)(2,1)}) custom-call(s16[8,528,256]{2,1,0:T(8,128)(2,1)S(1)} %bitcast.18, f32[128,256]{1,0:T(8,128)S(1)} %get-tuple-element.22.ortho_ref, f32[1,256]{1,0:T(1,128)S(1)} %add_rsqrt_fusion.scale_ref), custom_call_target="tpu_custom_call" | custom-call | flops 805306368 | bytes 7340032 | tf_op jit(solution)/shard_map/pallas_call | solution.py:353
  (6 shorter events, 0.1 us)
Async XLA Ops:
  7.2 2.5 %copy-start = (f32[128,4096]{1,0:T(8,128)S(1)}, f32[128,4096]{1,0:T(8,128)}, u32[]{:S(2)}) copy-start(f32[128,4096]{1,0:T(8,128)} %momentum_ref.3) | copy-start | bytes 6291460
  7.2 2.8 %copy-start.1 = (bf16[128,4096]{1,0:T(8,128)(2,1)S(1)}, bf16[128,4096]{1,0:T(8,128)(2,1)}, u32[]{:S(2)}) copy-start(bf16[128,4096]{1,0:T(8,128)(2,1)} %grad_ref.3) | copy-start | bytes 3145732
  10.7 1.1 copy-start.6
  40.8 11.9 %copy-start.3 = (s32[8]{0:T(128)S(1)}, s32[8]{0:T(128)}, u32[]{:S(2)}) copy-start(s32[8]{0:T(128)} %perm_ref.1) | copy-start | bytes 100
  40.8 5.8 %collective-permute-start = (f32[128,256]{1,0:T(8,128)S(1)}, f32[128,256]{1,0:T(8,128)S(1)}, u32[]{:S(2)}, u32[]{:S(2)}) collective-permute-start(f32[128,256]{1,0:T(8,128)S(1)} %shard_map.67), channel_id=1, source_target_pairs={{0,1},{1,0},{2,3},{3,2},{4,5},{5,4},{6,7},{7,6},{8,9},{9,8},{10,11... | collective-permute-start | bytes 393224 | tf_op jit(solution)/shard_map/ppermute | solution.py:27
  46.7 6.0 %collective-permute-start.1 = (f32[128,256]{1,0:T(8,128)S(1)}, f32[128,256]{1,0:T(8,128)S(1)}, u32[]{:S(2)}, u32[]{:S(2)}) collective-permute-start(f32[128,256]{1,0:T(8,128)S(1)} %add.68.near_ref), channel_id=1, source_target_pairs={{0,2},{1,3},{2,0},{3,1},{4,6},{5,7},{6,4},{7,5},{8,10},{9,11},{10,... | collective-permute-start | bytes 393224 | tf_op jit(solution)/shard_map/ppermute | solution.py:27
  48.3 63.7 %all-to-all-start = ((s16[8,128,512]{2,1,0:T(8,128)(2,1)}), s16[8,128,512]{2,1,0:T(8,128)(2,1)}, u32[]{:S(2)}, u32[]{:S(2)}) async-start(s16[8,128,512]{2,1,0:T(8,128)(2,1)} %bitcast.20), calls=%async_computation | async-start | bytes 2097152 | tf_op jit(solution)/shard_map/all_to_all | solution.py:386
  52.5 59.4 %all-gather.5.cloned.1.call-start = ((), (), s32[]{:S(2)}) async-start(), calls=%async_computation.1 | async-start | bytes 1179648 | tf_op jit(solution)/shard_map/all_gather | solution.py:396
  54.4 0.7 copy-start.4
  55.1 22.2 %collective-permute-start.2 = (f32[64,256]{1,0:T(8,128)S(1)}, f32[64,256]{1,0:T(8,128)S(1)}, u32[]{:S(2)}, u32[]{:S(2)}) collective-permute-start(f32[64,256]{1,0:T(8,128)S(1)} %get-tuple-element.19), channel_id=1, source_target_pairs={{0,8},{4,12},{8,0},{12,4},{16,24},{20,28},{24,16},{28,20},{1,9},{5... | collective-permute-start | bytes 196616 | tf_op jit(solution)/shard_map/ppermute | solution.py:27
  57.0 35.1 %collective-permute-start.3 = (f32[64,256]{1,0:T(8,128)S(1)}, f32[64,256]{1,0:T(8,128)S(1)}, u32[]{:S(2)}, u32[]{:S(2)}) collective-permute-start(f32[64,256]{1,0:T(8,128)S(1)} %get-tuple-element.19), channel_id=1, source_target_pairs={{0,16},{4,20},{8,24},{12,28},{16,0},{20,4},{24,8},{28,12},{1,17},{... | collective-permute-start | bytes 196616 | tf_op jit(solution)/shard_map/ppermute | solution.py:27
  59.4 32.7 %collective-permute-start.4 = (f32[64,256]{1,0:T(8,128)S(1)}, f32[64,256]{1,0:T(8,128)S(1)}, u32[]{:S(2)}, u32[]{:S(2)}) collective-permute-start(f32[64,256]{1,0:T(8,128)S(1)} %get-tuple-element.19), channel_id=1, source_target_pairs={{0,24},{4,28},{8,16},{12,20},{16,8},{20,12},{24,0},{28,4},{1,25},{... | collective-permute-start | bytes 196616 | tf_op jit(solution)/shard_map/ppermute | solution.py:27
  92.1 1.3 collective-permute-start.5
  93.5 4.3 %collective-permute-start.6 = (f32[64,256]{1,0:T(8,128)S(1)}, f32[64,256]{1,0:T(8,128)S(1)}, u32[]{:S(2)}, u32[]{:S(2)}) collective-permute-start(f32[64,256]{1,0:T(8,128)S(1)} %add.72.refs_0_), channel_id=1, source_target_pairs={{0,1},{1,0},{2,3},{3,2},{4,5},{5,4},{6,7},{7,6},{8,9},{9,8},{10,11... | collective-permute-start | bytes 196616 | tf_op jit(solution)/shard_map/ppermute | solution.py:27
  95.0 5.0 %collective-permute-start.7 = (f32[64,256]{1,0:T(8,128)S(1)}, f32[64,256]{1,0:T(8,128)S(1)}, u32[]{:S(2)}, u32[]{:S(2)}) collective-permute-start(f32[64,256]{1,0:T(8,128)S(1)} %add.72.refs_0_), channel_id=1, source_target_pairs={{0,2},{1,3},{2,0},{3,1},{4,6},{5,7},{6,4},{7,5},{8,10},{9,11},{10,... | collective-permute-start | bytes 196616 | tf_op jit(solution)/shard_map/ppermute | solution.py:27
  95.5 5.2 %collective-permute-start.8 = (f32[64,256]{1,0:T(8,128)S(1)}, f32[64,256]{1,0:T(8,128)S(1)}, u32[]{:S(2)}, u32[]{:S(2)}) collective-permute-start(f32[64,256]{1,0:T(8,128)S(1)} %add.72.refs_0_), channel_id=1, source_target_pairs={{0,3},{1,2},{2,1},{3,0},{4,7},{5,6},{6,5},{7,4},{8,11},{9,10},{10,... | collective-permute-start | bytes 196616 | tf_op jit(solution)/shard_map/ppermute | solution.py:27
  111.9 1.2 copy-start.2
  113.2 0.9 copy-start.5
  139.6 6.9 %collective-permute-start.10 = (f32[1,256]{1,0:T(1,128)S(1)}, f32[1,256]{1,0:T(1,128)S(1)}, u32[]{:S(2)}, u32[]{:S(2)}) collective-permute-start(f32[1,256]{1,0:T(1,128)S(1)} %bitcast.21), channel_id=1, source_target_pairs={{0,2},{1,3},{2,0},{3,1},{4,6},{5,7},{6,4},{7,5},{8,10},{9,11},{10,... | collective-permute-start | bytes 3080 | tf_op jit(solution)/shard_map/ppermute | solution.py:27
  141.1 5.3 %collective-permute-start.11 = (f32[1,256]{1,0:T(1,128)S(1)}, f32[1,256]{1,0:T(1,128)S(1)}, u32[]{:S(2)}, u32[]{:S(2)}) collective-permute-start(f32[1,256]{1,0:T(1,128)S(1)} %bitcast.22), channel_id=1, source_target_pairs={{0,3},{1,2},{2,1},{3,0},{4,7},{5,6},{6,5},{7,4},{8,11},{9,10},{10,... | collective-permute-start | bytes 3080 | tf_op jit(solution)/shard_map/ppermute | solution.py:27
  141.6 4.8 %collective-permute-start.9 = (f32[1,256]{1,0:T(1,128)S(1)}, f32[1,256]{1,0:T(1,128)S(1)}, u32[]{:S(2)}, u32[]{:S(2)}) collective-permute-start(f32[1,256]{1,0:T(1,128)S(1)} %bitcast.23), channel_id=1, source_target_pairs={{0,1},{1,0},{2,3},{3,2},{4,5},{5,4},{6,7},{7,6},{8,9},{9,8},{10,11... | collective-permute-start | bytes 3080 | tf_op jit(solution)/shard_map/ppermute | solution.py:27
Sparse Core Ops, SparseCore 0:
  55.5 35.2 all-gather.4

commit v7 on v6

--- a/solution.py
+++ b/solution.py
@@ -16,6 +16,7 @@
 HEAD = 16
 TOP = 32766.0
 PARAMS = pltpu.CompilerParams(vmem_limit_bytes=40 * 1024 * 1024)
+STREAM = pltpu.CompilerParams(vmem_limit_bytes=54 * 1024 * 1024)
 
 
 def halves(x):
@@ -281,7 +282,7 @@
             jax.ShapeDtypeStruct(projected.shape, jnp.float32),
         ],
         scratch_shapes=[pltpu.VMEM((share, rank), jnp.float32)],
-        compiler_params=PARAMS,
+        compiler_params=STREAM,
         cost_estimate=pl.CostEstimate(
             flops=6 * total * share * rank, bytes_accessed=total * (share * 2 + rank * 4), transcendentals=0
         ),
@@ -393,8 +394,9 @@
     far = exchange(near, "tp", step)
     projected, scaled, piece = gram_parts(column.reshape(1), perm, near, far, unit, num_cols)
 
+    piece = quad_sum(piece, "fsdp", 2)
+    piece, scaled, codes = lax.optimization_barrier((piece, scaled, codes))
     all_scaled = lax.all_gather(scaled, "fsdp", axis=0, tiled=True)
-    piece = quad_sum(piece, "fsdp", 2)
     piece = piece + exchange(piece, "fsdp", 1)
     pieces = [piece] + [exchange(piece, "tp", k) for k in range(1, num_cols)]
     places = jnp.stack([column ^ k for k in range(num_cols)]).astype(jnp.int32)

time: 157 us -> 140 us (0.89)
  waiting for transfers between devices: 41.7 us -> 21.9 us
  blocking collectives: 47.1 us -> 49.3 us
    ppermute x12, waiting for transfers between devices: 41.7 us -> 21.9 us  [exchange(): lax.ppermute(x, axis, [(i, i ^ k) for i in range(lax.axis_size(axis))])]
    unnamed x14 -> x16, local copies, waits for them, and re-layouts: 3.23 us -> 3.39 us
  transfers between devices with their start and end apart: 14 -> 14, of which waited for: 7 -> 8; matrix products, arithmetic and copies ran while one was open for 0% -> 0% of each run, Pallas kernels for 10% -> 14%
where the time goes in v7:
time: 140 us
  blocking collectives  49.3 us (35%)
  Pallas kernels  27.2 us (19%)
  waiting for transfers between devices  21.9 us (16%)
  starting transfers between devices  19 us (14%)
  between operations  14.2 us (10%)
  local copies, waits for them, and re-layouts  4.57 us (3%)
  other arithmetic  3.69 us (3%)
    all_gather x1, blocking collectives, on_device(): basis = lax.all_gather(basis, 'fsdp', axis=0, tiled=True)  25.9 us
    all_gather x1, blocking collectives, on_device(): gathered = lax.all_gather(code, 'fsdp', axis=0)  23.5 us
    ppermute x12, waiting for transfers between devices, exchange(): lax.ppermute(x, axis, [(i, i ^ k) for i in range(lax.axis_size(axis))])  21.9 us
    ppermute x12, starting transfers between devices, exchange(): lax.ppermute(x, axis, [(i, i ^ k) for i in range(lax.axis_size(axis))])  14.7 us
    pallas_call x1, Pallas kernels, factor_inverse(): pl.pallas_call(factor_kernel, grid_spec=pltpu.PrefetchScalarGridSpec(num_...  11.2 us
    pallas_call x1, Pallas kernels, encode(): pl.pallas_call(encode_kernel, grid=(total // block,), in_specs=[pl.BlockS...  4.44 us
    all_to_all x1, starting transfers between devices, on_device(): lax.all_to_all(codes, 'fsdp', split_axis=0, concat_axis=0)  4.25 us
    pallas_call x1, Pallas kernels, project(): pl.pallas_call(project_kernel, grid=(cols // block,), in_specs=[wide, wid...  3.48 us
  transfers between devices with their start and end apart: 14, of which 8 were waited for; matrix products, arithmetic and copies ran while one was open for 0% of the time, Pallas kernels for 14%

profile of v7, /device:TPU:0, one launch (start us, length us, event | category | flops | bytes accessed | tf_op | source)
XLA Modules:
  0.0 139.8 jit_solution(9096869216329667891)
XLA Ops:
  7.2 0.0 copy-start
  7.2 0.0 copy-start.1
  7.2 2.3 %abs_reduce_fusion = f32[128]{0:T(128)S(1)} fusion(f32[128,4096]{1,0:T(8,128)} %momentum_ref.3, bf16[128,4096]{1,0:T(8,128)(2,1)} %grad_ref.3), kind=kLoop, calls=%fused_computation.1 | loop fusion | flops 2097024 | bytes 3146240 | tf_op jit(solution)/shard_map/reduce_max | solution.py:380
  9.5 0.2 copy-done
  9.7 0.3 copy-done.1
  10.0 0.7 floor_convert_fusion
  10.7 0.0 copy-start.7
  10.7 1.1 copy.14
  11.7 0.0 copy-done.7
  11.7 0.5 fusion.8
  12.2 25.9 %all-gather.6.code_ref = s16[256,4096]{1,0:T(8,128)(2,1)} all-gather(s16[32,4096]{1,0:T(8,128)(2,1)S(1)} %fusion.8), channel_id=1, replica_groups=mesh['fsdp'=8,'tp'=4] {'fsdp'}, dimensions={0}, use_global_device_ids=true | all-gather | bytes 2359296 | tf_op jit(solution)/shard_map/all_gather | solution.py:385
  38.1 4.2 %all-to-all-start = ((s16[8,128,512]{2,1,0:T(8,128)(2,1)}), s16[8,128,512]{2,1,0:T(8,128)(2,1)}, u32[]{:S(2)}, u32[]{:S(2)}) async-start(s16[8,128,512]{2,1,0:T(8,128)(2,1)} %bitcast.20), calls=%async_computation | async-start | bytes 2097152 | tf_op jit(solution)/shard_map/all_to_all | solution.py:387
  42.4 0.0 all-gather.5.cloned.1.call-start
  42.4 0.0 copy-start.2
  42.4 1.6 %copy-done.2 = s16[256,4096]{1,0:T(8,128)(2,1)S(1)} copy-done((s16[256,4096]{1,0:T(8,128)(2,1)S(1)}, s16[256,4096]{1,0:T(8,128)(2,1)}, u32[]{:S(2)}) %copy-start.2) | copy-done | bytes 2097176
  44.0 0.0 copy-start.4
  44.0 3.5 %shard_map.67 = f32[128,256]{1,0:T(8,128)S(1)} custom-call(f32[128,4096]{1,0:T(8,128)S(1)} %copy-done, bf16[128,4096]{1,0:T(8,128)(2,1)S(1)} %copy-done.1, s16[256,4096]{1,0:T(8,128)(2,1)S(1)} %copy-done.2), custom_call_target="tpu_custom_call" | custom-call | flops 536870912 | bytes 5242880 | tf_op jit(solution)/shard_map/pallas_call | solution.py:88
  47.5 1.6 %collective-permute-start = (f32[128,256]{1,0:T(8,128)S(1)}, f32[128,256]{1,0:T(8,128)S(1)}, u32[]{:S(2)}, u32[]{:S(2)}) collective-permute-start(f32[128,256]{1,0:T(8,128)S(1)} %shard_map.67), channel_id=1, source_target_pairs={{0,1},{1,0},{2,3},{3,2},{4,5},{5,4},{6,7},{7,6},{8,9},{9,8},{10,11... | collective-permute-start | bytes 393224 | tf_op jit(solution)/shard_map/ppermute | solution.py:28
  49.0 4.2 %collective-permute-done = f32[128,256]{1,0:T(8,128)S(1)} collective-permute-done((f32[128,256]{1,0:T(8,128)S(1)}, f32[128,256]{1,0:T(8,128)S(1)}, u32[]{:S(2)}, u32[]{:S(2)}) %collective-permute-start) | collective-permute-done | bytes 131104 | tf_op jit(solution)/shard_map/ppermute | solution.py:28
  53.3 1.6 %collective-permute-start.1 = (f32[128,256]{1,0:T(8,128)S(1)}, f32[128,256]{1,0:T(8,128)S(1)}, u32[]{:S(2)}, u32[]{:S(2)}) collective-permute-start(f32[128,256]{1,0:T(8,128)S(1)} %add.68.near_ref), channel_id=1, source_target_pairs={{0,2},{1,3},{2,0},{3,1},{4,6},{5,7},{6,4},{7,5},{8,10},{9,11},{10,... | collective-permute-start | bytes 393224 | tf_op jit(solution)/shard_map/ppermute | solution.py:28
  54.9 0.1 copy.10.unit_ref
  55.0 3.4 %collective-permute-done.1.far_ref = f32[128,256]{1,0:T(8,128)S(1)} collective-permute-done((f32[128,256]{1,0:T(8,128)S(1)}, f32[128,256]{1,0:T(8,128)S(1)}, u32[]{:S(2)}, u32[]{:S(2)}) %collective-permute-start.1) | collective-permute-done | bytes 131104 | tf_op jit(solution)/shard_map/ppermute | solution.py:28
  58.4 0.0 copy-done.4
  58.4 1.7 %shard_map.68 = (f32[128,256]{1,0:T(8,128)S(1)}, f32[128,256]{1,0:T(8,128)}, f32[64,256]{1,0:T(8,128)S(1)}) custom-call(s32[1]{0:T(128)} %bitcast.column_ref, s32[8]{0:T(128)S(1)} %copy-done.4, f32[128,256]{1,0:T(8,128)S(1)} %add.68.near_ref, f32[128,256]{1,0:T(8,128)S(1)} %collective-permute-done.1.far_ref, f32[128,1]{1,0:T(8,128)S(1)} %copy.10.unit_ref), custom_call_target="tpu_custom_call" | custom-call | flops 201326592 | bytes 786432 | tf_op jit(solution)/shard_map/pallas_call | solution.py:123
  60.1 0.0 copy-start.6
  60.1 0.7 copy-done.6
  60.7 1.6 %collective-permute-start.2 = (f32[64,256]{1,0:T(8,128)S(1)}, f32[64,256]{1,0:T(8,128)S(1)}, u32[]{:S(2)}, u32[]{:S(2)}) collective-permute-start(f32[64,256]{1,0:T(8,128)S(1)} %get-tuple-element.20), channel_id=1, source_target_pairs={{0,8},{4,12},{8,0},{12,4},{16,24},{20,28},{24,16},{28,20},{1,9},{5... | collective-permute-start | bytes 196616 | tf_op jit(solution)/shard_map/ppermute | solution.py:28
  62.4 2.4 %collective-permute-start.3 = (f32[64,256]{1,0:T(8,128)S(1)}, f32[64,256]{1,0:T(8,128)S(1)}, u32[]{:S(2)}, u32[]{:S(2)}) collective-permute-start(f32[64,256]{1,0:T(8,128)S(1)} %get-tuple-element.20), channel_id=1, source_target_pairs={{0,16},{4,20},{8,24},{12,28},{16,0},{20,4},{24,8},{28,12},{1,17},{... | collective-permute-start | bytes 196616 | tf_op jit(solution)/shard_map/ppermute | solution.py:28
  64.7 0.4 collective-permute-start.4
  65.1 0.2 collective-permute-done.2
  65.3 8.2 %collective-permute-done.3 = f32[64,256]{1,0:T(8,128)S(1)} collective-permute-done((f32[64,256]{1,0:T(8,128)S(1)}, f32[64,256]{1,0:T(8,128)S(1)}, u32[]{:S(2)}, u32[]{:S(2)}) %collective-permute-start.3) | collective-permute-done | bytes 65568 | tf_op jit(solution)/shard_map/ppermute | solution.py:28
  73.5 0.0 collective-permute-done.4
  73.5 0.0 all-to-all-done
  73.6 0.0 all-gather.5.cloned.1.call-update
  73.6 0.1 collective-permute-start.5
  73.7 1.2 collective-permute-done.5
  74.9 1.6 %collective-permute-start.6 = (f32[64,256]{1,0:T(8,128)S(1)}, f32[64,256]{1,0:T(8,128)S(1)}, u32[]{:S(2)}, u32[]{:S(2)}) collective-permute-start(f32[64,256]{1,0:T(8,128)S(1)} %add.72.refs_0_), channel_id=1, source_target_pairs={{0,1},{1,0},{2,3},{3,2},{4,5},{5,4},{6,7},{7,6},{8,9},{9,8},{10,11... | collective-permute-start | bytes 196616 | tf_op jit(solution)/shard_map/ppermute | solution.py:28
  76.5 1.5 %collective-permute-start.7 = (f32[64,256]{1,0:T(8,128)S(1)}, f32[64,256]{1,0:T(8,128)S(1)}, u32[]{:S(2)}, u32[]{:S(2)}) collective-permute-start(f32[64,256]{1,0:T(8,128)S(1)} %add.72.refs_0_), channel_id=1, source_target_pairs={{0,2},{1,3},{2,0},{3,1},{4,6},{5,7},{6,4},{7,5},{8,10},{9,11},{10,... | collective-permute-start | bytes 196616 | tf_op jit(solution)/shard_map/ppermute | solution.py:28
  78.0 0.5 collective-permute-start.8
  78.5 0.1 pad_add_fusion.place_ref
  78.5 0.7 collective-permute-done.6.refs_1_
  79.2 1.5 %collective-permute-done.7.refs_2_ = f32[64,256]{1,0:T(8,128)S(1)} collective-permute-done((f32[64,256]{1,0:T(8,128)S(1)}, f32[64,256]{1,0:T(8,128)S(1)}, u32[]{:S(2)}, u32[]{:S(2)}) %collective-permute-start.7) | collective-permute-done | bytes 65568 | tf_op jit(solution)/shard_map/ppermute | solution.py:28
  80.7 2.4 %collective-permute-done.8.refs_3_ = f32[64,256]{1,0:T(8,128)S(1)} collective-permute-done((f32[64,256]{1,0:T(8,128)S(1)}, f32[64,256]{1,0:T(8,128)S(1)}, u32[]{:S(2)}, u32[]{:S(2)}) %collective-permute-start.8) | collective-permute-done | bytes 65568 | tf_op jit(solution)/shard_map/ppermute | solution.py:28
  83.2 11.2 %shard_map.69.inverse_ref = f32[256,256]{1,0:T(8,128)S(1)} custom-call(s32[4]{0:T(128)S(1)} %pad_add_fusion.place_ref, f32[64,256]{1,0:T(8,128)S(1)} %add.72.refs_0_, f32[64,256]{1,0:T(8,128)S(1)} %collective-permute-done.6.refs_1_, f32[64,256]{1,0:T(8,128)S(1)} %collective-permute-done.7.refs_2_, f32[64,256]{1,0:T(8,128)S(1)} %collective-permute-done.8.refs_3_), custom_call_target="tpu_custom_call" | custom-call | flops 201326592 | bytes 524288 | tf_op jit(solution)/shard_map/pallas_call | solution.py:207
  94.4 0.0 copy-start.5
  94.4 0.7 copy-done.5
  95.1 0.0 all-gather.5.cloned.1.call-done.scaled_ref
  95.1 4.4 %shard_map.70 = (s16[528,256]{1,0:T(8,128)(2,1)}, f32[128,256]{1,0:T(8,128)}) custom-call(s16[1024,512]{1,0:T(8,128)(2,1)} %bitcast.3.source_ref, f32[1024,256]{1,0:T(8,128)} %all-gather.5.cloned.1.call-done.scaled_ref, f32[256,256]{1,0:T(8,128)} %copy-done.5, f32[128,256]{1,0:T(8,128)} %copy-done.6), custom_call_target="tpu_custom_call" | custom-call | flops 805306368 | bytes 2097152 | tf_op jit(solution)/shard_map/pallas_call | solution.py:270
  99.5 0.0 copy-start.3
  99.5 23.5 %all-gather.7 = s16[4224,256]{1,0:T(8,128)(2,1)S(1)} all-gather(s16[528,256]{1,0:T(8,128)(2,1)} %get-tuple-element.27), channel_id=2, replica_groups=mesh['fsdp'=8,'tp'=4] {'fsdp'}, dimensions={0}, use_global_device_ids=true | all-gather | bytes 2433024 | tf_op jit(solution)/shard_map/all_gather | solution.py:405
  123.0 0.1 fusion.13
  123.0 1.6 %collective-permute-start.10 = (f32[1,256]{1,0:T(1,128)S(1)}, f32[1,256]{1,0:T(1,128)S(1)}, u32[]{:S(2)}, u32[]{:S(2)}) collective-permute-start(f32[1,256]{1,0:T(1,128)S(1)} %bitcast.21), channel_id=1, source_target_pairs={{0,2},{1,3},{2,0},{3,1},{4,6},{5,7},{6,4},{7,5},{8,10},{9,11},{10,... | collective-permute-start | bytes 3080 | tf_op jit(solution)/shard_map/ppermute | solution.py:28
  124.6 1.3 collective-permute-start.11
  125.9 0.7 collective-permute-start.9
  126.6 0.0 copy-done.3
  126.6 3.3 %shard_map.71 = f32[128,4096]{1,0:T(8,128)} custom-call(f32[128,4096]{1,0:T(8,128)S(1)} %copy-done, bf16[128,4096]{1,0:T(8,128)(2,1)S(1)} %copy-done.1, s16[8,528,256]{2,1,0:T(8,128)(2,1)S(1)} %bitcast.17, f32[128,256]{1,0:T(8,128)S(1)} %copy-done.3), custom_call_target="tpu_custom_call" | custom-call | flops 805306368 | bytes 7340032 | tf_op jit(solution)/shard_map/pallas_call | solution.py:342
  129.9 0.0 collective-permute-done.10
  129.9 0.0 collective-permute-done.11
  129.9 0.0 collective-permute-done.9
  129.9 3.1 %shard_map.72 = (f32[4096,256]{1,0:T(8,128)}, bf16[128,4096]{1,0:T(8,128)(2,1)}) custom-call(s16[8,528,256]{2,1,0:T(8,128)(2,1)S(1)} %bitcast.18, f32[128,256]{1,0:T(8,128)S(1)} %copy-done.3, f32[1,256]{1,0:T(1,128)S(1)} %add_rsqrt_fusion.scale_ref), custom_call_target="tpu_custom_call" | custom-call | flops 805306368 | bytes 7340032 | tf_op jit(solution)/shard_map/pallas_call | solution.py:354
  (6 shorter events, 0.1 us)
Async XLA Ops:
  7.2 2.5 %copy-start = (f32[128,4096]{1,0:T(8,128)S(1)}, f32[128,4096]{1,0:T(8,128)}, u32[]{:S(2)}) copy-start(f32[128,4096]{1,0:T(8,128)} %momentum_ref.3) | copy-start | bytes 6291460
  7.2 2.8 %copy-start.1 = (bf16[128,4096]{1,0:T(8,128)(2,1)S(1)}, bf16[128,4096]{1,0:T(8,128)(2,1)}, u32[]{:S(2)}) copy-start(bf16[128,4096]{1,0:T(8,128)(2,1)} %grad_ref.3) | copy-start | bytes 3145732
  10.7 1.1 copy-start.7
  38.1 35.5 %all-to-all-start = ((s16[8,128,512]{2,1,0:T(8,128)(2,1)}), s16[8,128,512]{2,1,0:T(8,128)(2,1)}, u32[]{:S(2)}, u32[]{:S(2)}) async-start(s16[8,128,512]{2,1,0:T(8,128)(2,1)} %bitcast.20), calls=%async_computation | async-start | bytes 2097152 | tf_op jit(solution)/shard_map/all_to_all | solution.py:387
  42.4 52.7 %all-gather.5.cloned.1.call-start = ((), (), s32[]{:S(2)}) async-start(), calls=%async_computation.1 | async-start | bytes 1179648 | tf_op jit(solution)/shard_map/all_gather | solution.py:399
  42.4 1.6 %copy-start.2 = (s16[256,4096]{1,0:T(8,128)(2,1)S(1)}, s16[256,4096]{1,0:T(8,128)(2,1)}, u32[]{:S(2)}) copy-start(s16[256,4096]{1,0:T(8,128)(2,1)} %all-gather.6.code_ref) | copy-start | bytes 6291460
  44.0 14.4 %copy-start.4 = (s32[8]{0:T(128)S(1)}, s32[8]{0:T(128)}, u32[]{:S(2)}) copy-start(s32[8]{0:T(128)} %perm_ref.1) | copy-start | bytes 100
  47.5 5.8 %collective-permute-start = (f32[128,256]{1,0:T(8,128)S(1)}, f32[128,256]{1,0:T(8,128)S(1)}, u32[]{:S(2)}, u32[]{:S(2)}) collective-permute-start(f32[128,256]{1,0:T(8,128)S(1)} %shard_map.67), channel_id=1, source_target_pairs={{0,1},{1,0},{2,3},{3,2},{4,5},{5,4},{6,7},{7,6},{8,9},{9,8},{10,11... | collective-permute-start | bytes 393224 | tf_op jit(solution)/shard_map/ppermute | solution.py:28
  53.3 5.1 %collective-permute-start.1 = (f32[128,256]{1,0:T(8,128)S(1)}, f32[128,256]{1,0:T(8,128)S(1)}, u32[]{:S(2)}, u32[]{:S(2)}) collective-permute-start(f32[128,256]{1,0:T(8,128)S(1)} %add.68.near_ref), channel_id=1, source_target_pairs={{0,2},{1,3},{2,0},{3,1},{4,6},{5,7},{6,4},{7,5},{8,10},{9,11},{10,... | collective-permute-start | bytes 393224 | tf_op jit(solution)/shard_map/ppermute | solution.py:28
  60.1 0.7 copy-start.6
  60.7 4.6 %collective-permute-start.2 = (f32[64,256]{1,0:T(8,128)S(1)}, f32[64,256]{1,0:T(8,128)S(1)}, u32[]{:S(2)}, u32[]{:S(2)}) collective-permute-start(f32[64,256]{1,0:T(8,128)S(1)} %get-tuple-element.20), channel_id=1, source_target_pairs={{0,8},{4,12},{8,0},{12,4},{16,24},{20,28},{24,16},{28,20},{1,9},{5... | collective-permute-start | bytes 196616 | tf_op jit(solution)/shard_map/ppermute | solution.py:28
  62.4 11.2 %collective-permute-start.3 = (f32[64,256]{1,0:T(8,128)S(1)}, f32[64,256]{1,0:T(8,128)S(1)}, u32[]{:S(2)}, u32[]{:S(2)}) collective-permute-start(f32[64,256]{1,0:T(8,128)S(1)} %get-tuple-element.20), channel_id=1, source_target_pairs={{0,16},{4,20},{8,24},{12,28},{16,0},{20,4},{24,8},{28,12},{1,17},{... | collective-permute-start | bytes 196616 | tf_op jit(solution)/shard_map/ppermute | solution.py:28
  64.7 8.8 %collective-permute-start.4 = (f32[64,256]{1,0:T(8,128)S(1)}, f32[64,256]{1,0:T(8,128)S(1)}, u32[]{:S(2)}, u32[]{:S(2)}) collective-permute-start(f32[64,256]{1,0:T(8,128)S(1)} %get-tuple-element.20), channel_id=1, source_target_pairs={{0,24},{4,28},{8,16},{12,20},{16,8},{20,12},{24,0},{28,4},{1,25},{... | collective-permute-start | bytes 196616 | tf_op jit(solution)/shard_map/ppermute | solution.py:28
  73.6 1.3 collective-permute-start.5
  74.9 4.3 %collective-permute-start.6 = (f32[64,256]{1,0:T(8,128)S(1)}, f32[64,256]{1,0:T(8,128)S(1)}, u32[]{:S(2)}, u32[]{:S(2)}) collective-permute-start(f32[64,256]{1,0:T(8,128)S(1)} %add.72.refs_0_), channel_id=1, source_target_pairs={{0,1},{1,0},{2,3},{3,2},{4,5},{5,4},{6,7},{7,6},{8,9},{9,8},{10,11... | collective-permute-start | bytes 196616 | tf_op jit(solution)/shard_map/ppermute | solution.py:28
  76.5 4.3 %collective-permute-start.7 = (f32[64,256]{1,0:T(8,128)S(1)}, f32[64,256]{1,0:T(8,128)S(1)}, u32[]{:S(2)}, u32[]{:S(2)}) collective-permute-start(f32[64,256]{1,0:T(8,128)S(1)} %add.72.refs_0_), channel_id=1, source_target_pairs={{0,2},{1,3},{2,0},{3,1},{4,6},{5,7},{6,4},{7,5},{8,10},{9,11},{10,... | collective-permute-start | bytes 196616 | tf_op jit(solution)/shard_map/ppermute | solution.py:28
  78.0 5.2 %collective-permute-start.8 = (f32[64,256]{1,0:T(8,128)S(1)}, f32[64,256]{1,0:T(8,128)S(1)}, u32[]{:S(2)}, u32[]{:S(2)}) collective-permute-start(f32[64,256]{1,0:T(8,128)S(1)} %add.72.refs_0_), channel_id=1, source_target_pairs={{0,3},{1,2},{2,1},{3,0},{4,7},{5,6},{6,5},{7,4},{8,11},{9,10},{10,... | collective-permute-start | bytes 196616 | tf_op jit(solution)/shard_map/ppermute | solution.py:28
  94.4 0.7 copy-start.5
  99.5 27.1 %copy-start.3 = (f32[128,256]{1,0:T(8,128)S(1)}, f32[128,256]{1,0:T(8,128)}, u32[]{:S(2)}) copy-start(f32[128,256]{1,0:T(8,128)} %get-tuple-element.28.ortho_ref) | copy-start | bytes 393220
  123.0 6.9 %collective-permute-start.10 = (f32[1,256]{1,0:T(1,128)S(1)}, f32[1,256]{1,0:T(1,128)S(1)}, u32[]{:S(2)}, u32[]{:S(2)}) collective-permute-start(f32[1,256]{1,0:T(1,128)S(1)} %bitcast.21), channel_id=1, source_target_pairs={{0,2},{1,3},{2,0},{3,1},{4,6},{5,7},{6,4},{7,5},{8,10},{9,11},{10,... | collective-permute-start | bytes 3080 | tf_op jit(solution)/shard_map/ppermute | solution.py:28
  124.6 5.3 %collective-permute-start.11 = (f32[1,256]{1,0:T(1,128)S(1)}, f32[1,256]{1,0:T(1,128)S(1)}, u32[]{:S(2)}, u32[]{:S(2)}) collective-permute-start(f32[1,256]{1,0:T(1,128)S(1)} %bitcast.22), channel_id=1, source_target_pairs={{0,3},{1,2},{2,1},{3,0},{4,7},{5,6},{6,5},{7,4},{8,11},{9,10},{10,... | collective-permute-start | bytes 3080 | tf_op jit(solution)/shard_map/ppermute | solution.py:28
  125.9 4.0 %collective-permute-start.9 = (f32[1,256]{1,0:T(1,128)S(1)}, f32[1,256]{1,0:T(1,128)S(1)}, u32[]{:S(2)}, u32[]{:S(2)}) collective-permute-start(f32[1,256]{1,0:T(1,128)S(1)} %bitcast.23), channel_id=1, source_target_pairs={{0,1},{1,0},{2,3},{3,2},{4,5},{5,4},{6,7},{7,6},{8,9},{9,8},{10,11... | collective-permute-start | bytes 3080 | tf_op jit(solution)/shard_map/ppermute | solution.py:28
Sparse Core Ops, SparseCore 0:
  73.7 21.2 all-gather.4

commit v8 on v6

v8 whole, which is shorter than its diff:
```python
import functools
import math

import jax
import jax.numpy as jnp
from jax import lax
from jax.experimental import pallas as pl
from jax.experimental.pallas import tpu as pltpu
from jax.sharding import PartitionSpec as P

EPSILON = 1e-06
KEEP_SHARE = 0.5
HIGH = lax.Precision.HIGHEST
PANEL = 64
TILE = 8
HEAD = 16
TOP = 32766.0
PARAMS = pltpu.CompilerParams(vmem_limit_bytes=40 * 1024 * 1024)


def halves(x):
    high = x.astype(jnp.bfloat16)
    return high, (x - high.astype(jnp.float32)).astype(jnp.bfloat16)


def exchange(x, axis, k):
    return lax.ppermute(x, axis, [(i, i ^ k) for i in range(lax.axis_size(axis))])


def butterfly_sum(x, axis, step=1):
    while step < lax.axis_size(axis):
        x = x + exchange(x, axis, step)
        step *= 2
    return x


def quad_sum(x, axis, step=1):
    if lax.axis_size(axis) != 4 * step:
        return butterfly_sum(x, axis, step)
    near, far, across = [exchange(x, axis, k * step) for k in range(1, 4)]
    return (x + near) + (far + across)


def whole(x):
    return pl.BlockSpec(x.shape, lambda *_: (0,) * len(x.shape))


def dot_rows(a, b):
    return lax.dot_general(a, b, (((1,), (1,)), ((), ())), precision=HIGH, preferred_element_type=jnp.float32)


def unit_of(exponent, mantissa):
    return mantissa * jnp.exp2(exponent - 13.0)


def code_unit(top):
    top = jnp.maximum(top, 1e-28) * (1.0 / TOP)
    exponent = jnp.floor(jnp.log2(top))
    return exponent, jnp.floor(top * jnp.exp2(13.0 - exponent)) + 1.0


def whole_number(x):
    return x.astype(jnp.int32).astype(jnp.int16)


def set_head(head_ref, *rows):
    place = lax.broadcasted_iota(jnp.int32, head_ref.shape, 0)
    head = jnp.zeros(head_ref.shape, jnp.float32)
    for k, row in enumerate(rows):
        head = jnp.where(place == k, row, head)
    head_ref[...] = whole_number(head)


def code_basis(basis):
    value = basis.astype(jnp.float32)
    size = jnp.abs(value)
    normal = size >= 2.0**-126
    exponent = jnp.floor(jnp.log2(jnp.where(normal, size, 1.0)))
    code = 128.0 * (exponent + 126.0) + jnp.floor(128.0 * (size * jnp.exp2(-exponent)) + 0.5)
    return whole_number(jnp.where(normal, jnp.where(value < 0.0, -code, code), 0.0))


def prepare_kernel(momentum_ref, grad_ref, basis_ref, pack_ref, code_ref):
    rows, cols = momentum_ref.shape
    width = code_ref.shape[-1]
    spans = [slice(i, i + width) for i in range(0, cols, width)]
    combined = lambda span: momentum_ref[:, span] + grad_ref[:, span].astype(jnp.float32)
    top = functools.reduce(jnp.maximum, [jnp.abs(combined(span)) for span in spans])
    exponent, mantissa = code_unit(jnp.max(top, axis=1, keepdims=True))
    inverse = 1.0 / unit_of(exponent, mantissa)
    for k, span in enumerate(spans):
        code_ref[k] = whole_number(jnp.floor(combined(span) * inverse + 0.5))
        pack_ref[:, span] = code_basis(basis_ref[:, span])
    across = lax.broadcasted_iota(jnp.int32, (rows, rows), 0) == lax.broadcasted_iota(jnp.int32, (rows, rows), 1)
    turn = lambda x: jnp.sum(jnp.where(across, x, 0.0), axis=0, keepdims=True)
    set_head(pack_ref.at[:, cols:], turn(exponent), turn(mantissa))


def prepare(momentum, grad, basis, share):
    rows, cols = momentum.shape
    width = share if share % 128 == 0 else cols
    return pl.pallas_call(
        prepare_kernel,
        out_shape=[
            jax.ShapeDtypeStruct((basis.shape[0], cols + rows), jnp.int16),
            jax.ShapeDtypeStruct((cols // width, rows, width), jnp.int16),
        ],
        compiler_params=PARAMS,
        cost_estimate=pl.CostEstimate(flops=10 * rows * cols, bytes_accessed=rows * cols * 8, transcendentals=0),
    )(momentum, grad, basis)


def project_kernel(column_ref, momentum_ref, grad_ref, code_ref, *refs):
    out_refs, total_ref = refs[:-1], refs[-1]
    code = code_ref[...].astype(jnp.int32)
    size = jnp.abs(code)
    value = ((size & 127) + 128).astype(jnp.float32) * jnp.exp2(((size >> 7) - 134).astype(jnp.float32))
    basis = jnp.where(code == 0, 0.0, jnp.where(code < 0, -value, value)).astype(jnp.bfloat16)
    combined = momentum_ref[...] + grad_ref[...].astype(jnp.float32)
    rows = combined.shape[0]
    part = lax.dot_general(
        jnp.concatenate(halves(combined), axis=0),
        basis,
        (((1,), (1,)), ((), ())),
        preferred_element_type=jnp.float32,
    )
    part = part[:rows] + part[rows:]

    @pl.when(pl.program_id(0) == 0)
    def _():
        total_ref[...] = part

    @pl.when(pl.program_id(0) > 0)
    def _():
        total_ref[...] += part

    @pl.when(pl.program_id(0) == pl.num_programs(0) - 1)
    def _():
        for k, out_ref in enumerate(out_refs):
            piece = out_ref.shape[0]
            out_ref[...] = total_ref[pl.ds(pl.multiple_of((column_ref[0] ^ k) * piece, piece), piece), :]


def project(column, momentum, grad, codes, columns):
    rows, cols = momentum.shape
    rank = codes.shape[0]
    block = min(1024, cols)
    wide = pl.BlockSpec((rows, block), lambda i, column: (0, i))
    return pl.pallas_call(
        project_kernel,
        grid_spec=pltpu.PrefetchScalarGridSpec(
            num_scalar_prefetch=1,
            grid=(cols // block,),
            in_specs=[wide, wide, pl.BlockSpec((rank, block), lambda i, column: (0, i))],
            out_specs=[pl.BlockSpec((rows // columns, rank), lambda i, column: (0, 0))] * columns,
            scratch_shapes=[pltpu.VMEM((rows, rank), jnp.float32)],
        ),
        out_shape=[jax.ShapeDtypeStruct((rows // columns, rank), jnp.float32)] * columns,
        compiler_params=PARAMS,
        cost_estimate=pl.CostEstimate(
            flops=4 * rows * cols * rank, bytes_accessed=rows * cols * 6 + rank * cols * 2, transcendentals=rank * cols
        ),
    )(column, momentum, grad, codes)


def pack_kernel(perm_ref, *refs):
    part_refs, out_ref = refs[:-1], refs[-1]
    rows, rank = part_refs[0].shape
    blocks = perm_ref.shape[0]
    size = rank // blocks
    stored = lax.broadcasted_iota(jnp.int32, (rank, rank), 0)
    target = jnp.zeros((rank, rank), jnp.int32)
    for s in range(blocks):
        target = jnp.where(stored // size == s, perm_ref[s] * size + stored % size, target)
    order = (target == lax.broadcasted_iota(jnp.int32, (rank, rank), 1)).astype(jnp.float32)
    total = functools.reduce(jnp.add, [ref[...] for ref in part_refs])
    total = jnp.dot(total, order, precision=HIGH, preferred_element_type=jnp.float32)
    exponent, mantissa = code_unit(jnp.max(jnp.abs(total), axis=0, keepdims=True))
    value = total * (1.0 / unit_of(exponent, mantissa))
    high = jnp.floor(value + 0.5)
    out_ref[:rows] = whole_number(high)
    out_ref[rows : 2 * rows] = whole_number(jnp.floor((value - high) * 32768.0 + 0.5))
    set_head(out_ref.at[2 * rows :], exponent, mantissa)


def pack(perm, parts):
    rows, rank = parts[0].shape
    return pl.pallas_call(
        pack_kernel,
        grid_spec=pltpu.PrefetchScalarGridSpec(
            num_scalar_prefetch=1,
            grid=(1,),
            in_specs=[whole(x) for x in parts],
            out_specs=pl.BlockSpec((2 * rows + HEAD, rank), lambda *_: (0, 0)),
        ),
        out_shape=jax.ShapeDtypeStruct((2 * rows + HEAD, rank), jnp.int16),
        compiler_params=PARAMS,
        cost_estimate=pl.CostEstimate(flops=12 * rows * rank * rank, bytes_accessed=rank * rank * 4, transcendentals=0),
    )(perm, *parts)


def spread(row):
    return jnp.broadcast_to(row, (TILE, 2 * PANEL))


def panel_inverse(block):
    rows = lax.broadcasted_iota(jnp.int32, (PANEL, PANEL), 0)
    cols = lax.broadcasted_iota(jnp.int32, (PANEL, PANEL), 1)
    both = jnp.concatenate([block, (rows == cols).astype(jnp.float32)], axis=1)
    count = PANEL // TILE
    tiles = [both[TILE * i : TILE * (i + 1)] for i in range(count)]
    sub = lax.broadcasted_iota(jnp.int32, (TILE, 2 * PANEL), 0)
    done = []
    for k in range(count):
        columns = [
            [spread(tiles[i][:, TILE * k + j : TILE * k + j + 1]) for j in range(TILE)] for i in range(k, count)
        ]
        own, body = list(columns[0]), tiles[k]
        final = jnp.zeros_like(body)
        for j in range(0, TILE, 2):
            first, second = sub == j, sub == j + 1
            a, b, c = spread(own[j][j : j + 1]), spread(own[j + 1][j : j + 1]), spread(own[j + 1][j + 1 : j + 2])
            minor = a * c - b * b
            inverse = 1.0 / minor

            def solve(x):
                upper, lower = spread(x[j : j + 1]), spread(x[j + 1 : j + 2])
                return (c * upper - b * lower) * inverse, (a * lower - b * upper) * inverse

            def reduce_rows(x):
                upper, lower = solve(x)
                rest = x - own[j] * upper - own[j + 1] * lower
                return jnp.where(first, upper, jnp.where(second, lower, rest))

            ratio = 1.0 / a
            below = (body - b * ratio * spread(body[j : j + 1])) * lax.rsqrt(minor * ratio)
            final = jnp.where(first, body * lax.rsqrt(a), jnp.where(second, below, final))
            body = reduce_rows(body)
            later = {other: reduce_rows(own[other]) for other in range(j + 2, TILE)}
            for other, column in later.items():
                own[other] = column
        done.append(final)
        for i in range(k + 1, count):
            tile = tiles[i]
            for j in range(TILE):
                tile = tile - columns[i - k][j] * spread(body[j : j + 1])
            tiles[i] = tile
    return jnp.concatenate(done, axis=0)[:, PANEL:]


def lanes_up(x):
    return (x + 127) // 128 * 128


def inverse_factor(gram, out_ref, work):
    rank = gram.shape[0]
    rows = lax.broadcasted_iota(jnp.int32, (rank, rank), 0)
    cols = lax.broadcasted_iota(jnp.int32, (rank, rank), 1)
    diagonal = jnp.where(rows == cols, gram, 0.0)
    scale = lax.rsqrt(jnp.sum(diagonal, axis=0, keepdims=True))
    work[:, :rank] = gram * scale * lax.rsqrt(jnp.sum(diagonal, axis=1, keepdims=True))
    work[:, rank:] = (rows == cols).astype(jnp.float32)
    for start in range(0, rank, PANEL):
        end = start + PANEL
        left, right = start // 128 * 128, rank + lanes_up(end)
        inverse = panel_inverse(work[start:end, start:end])
        scaled = jnp.dot(inverse, work[start:end, left:right], precision=HIGH, preferred_element_type=jnp.float32)
        out_ref[start:end, : lanes_up(end)] = scaled[:, rank - left :] * scale[:, : lanes_up(end)]
        if lanes_up(end) < rank:
            out_ref[start:end, lanes_up(end) :] = jnp.zeros((PANEL, rank - lanes_up(end)), jnp.float32)
        if end < rank:
            low = end // 128 * 128
            change = lax.dot_general(
                scaled[:, low - left : rank - left],
                scaled[:, low - left :],
                (((0,), (0,)), ((), ())),
                precision=HIGH,
                preferred_element_type=jnp.float32,
            )
            work[end:, low:right] = work[end:, low:right] - change[end - low :, :]


def factor_kernel(code_ref, turned_ref, out_ref, gram_ref, work):
    count, size, rank = code_ref.shape
    size = (size - HEAD) // 2
    code = code_ref[...].astype(jnp.int32).astype(jnp.float32)
    unit = unit_of(code[:, 2 * size : 2 * size + 1], code[:, 2 * size + 1 : 2 * size + 2])
    part = (code[:, :size] + code[:, size : 2 * size] * (1.0 / 32768.0)) * unit
    turned = part.reshape(count * size, rank).T
    turned_ref[...] = turned
    gram = dot_rows(turned, turned)

    @pl.when(pl.program_id(0) == 0)
    def _():
        gram_ref[...] = gram

    @pl.when(pl.program_id(0) > 0)
    def _():
        gram_ref[...] += gram

    @pl.when(pl.program_id(0) == pl.num_programs(0) - 1)
    def _():
        inverse_factor(gram_ref[...], out_ref, work)


def factor(codes):
    devices, size, rank = codes.shape
    rows = (size - HEAD) // 2
    group = 256 // rows
    return pl.pallas_call(
        factor_kernel,
        grid=(devices // group,),
        in_specs=[pl.BlockSpec((group, size, rank), lambda i: (i, 0, 0))],
        out_specs=[pl.BlockSpec((rank, group * rows), lambda i: (0, i)), pl.BlockSpec((rank, rank), lambda i: (0, 0))],
        out_shape=[
            jax.ShapeDtypeStruct((rank, devices * rows), jnp.float32),
            jax.ShapeDtypeStruct((rank, rank), jnp.float32),
        ],
        scratch_shapes=[pltpu.VMEM((rank, rank), jnp.float32), pltpu.VMEM((rank, 2 * rank), jnp.float32)],
        compiler_params=PARAMS,
        cost_estimate=pl.CostEstimate(
            flops=12 * devices * rows * rank * rank, bytes_accessed=devices * size * rank * 4, transcendentals=rank
        ),
    )(codes)


def encode_kernel(place_ref, source_ref, turned_ref, unit_ref, inverse_ref, own_ref, code_ref, ortho_ref, mixed_ref):
    def times(a, b):
        return jnp.dot(a, b, preferred_element_type=jnp.float32)

    def turned_dot(a, b):
        return lax.dot_general(a, b, (((0,), (1,)), ((), ())), precision=HIGH, preferred_element_type=jnp.float32)

    rank = turned_ref.shape[0]
    source_high, source_low = halves(source_ref[...].astype(jnp.int32).astype(jnp.float32))
    scaled_high, scaled_low = halves(turned_ref[...] * unit_ref[...])
    most = times(jnp.concatenate([scaled_high, scaled_low], axis=0), source_high)
    part = most[:rank] + (most[rank:] + times(scaled_high, source_low))
    first, last = pl.program_id(0) == 0, pl.program_id(0) == pl.num_programs(0) - 1

    @pl.when(first)
    def _():
        mixed_ref[...] = part

    @pl.when(jnp.logical_not(first))
    def _():
        mixed_ref[...] += part

    @pl.when(last)
    def _():
        inverse = inverse_ref[...]
        ortho_ref[...] = turned_dot(own_ref[...], inverse)
        right = turned_dot(mixed_ref[...], inverse)
        rows = right.shape[0]
        square = jnp.maximum(jnp.sum(right * right, axis=0, keepdims=True), 1e-34)
        square_exponent = jnp.floor(jnp.log2(square))
        fine = square * jnp.exp2(13.0 - square_exponent)
        square_high = jnp.floor(fine)
        square_low = jnp.floor((fine - square_high) * 16384.0)
        exponent, mantissa = code_unit(jnp.max(jnp.abs(right), axis=0, keepdims=True))
        code_ref[:rows] = whole_number(jnp.floor(right * (1.0 / unit_of(exponent, mantissa)) + 0.5))
        set_head(code_ref.at[rows:], exponent, mantissa, square_exponent, square_high, square_low)


def encode(place, source, turned, unit, inverse_low, rows):
    total, share = source.shape
    rank = turned.shape[0]
    block = min(512, total)
    return pl.pallas_call(
        encode_kernel,
        grid_spec=pltpu.PrefetchScalarGridSpec(
            num_scalar_prefetch=1,
            grid=(total // block,),
            in_specs=[
                pl.BlockSpec((block, share), lambda i, place: (i, 0)),
                pl.BlockSpec((rank, block), lambda i, place: (0, i)),
                pl.BlockSpec((1, block), lambda i, place: (0, i)),
                whole(inverse_low),
                pl.BlockSpec((rank, rows), lambda i, place: (0, place[0])),
            ],
            out_specs=[
                pl.BlockSpec((share + HEAD, rank), lambda i, place: (0, 0)),
                pl.BlockSpec((rows, rank), lambda i, place: (0, 0)),
            ],
            scratch_shapes=[pltpu.VMEM((rank, share), jnp.float32)],
        ),
        out_shape=[
            jax.ShapeDtypeStruct((share + HEAD, rank), jnp.int16),
            jax.ShapeDtypeStruct((rows, rank), jnp.float32),
        ],
        compiler_params=PARAMS,
        cost_estimate=pl.CostEstimate(
            flops=6 * total * share * rank, bytes_accessed=total * (share * 2 + rank * 4), transcendentals=0
        ),
    )(place, source, turned, unit, inverse_low, turned)


def decode(code_ref):
    code = code_ref[...].astype(jnp.int32).astype(jnp.float32)
    share = code.shape[1] - HEAD
    right = code[:, :share] * unit_of(code[:, share : share + 1], code[:, share + 1 : share + 2])
    return right.reshape(code.shape[0] * share, code.shape[2])


def times_rows(split_ref, right):
    def times(a, b):
        return lax.dot_general(a, b, (((1,), (1,)), ((), ())), preferred_element_type=jnp.float32)

    right_high, right_low = halves(right)
    split = split_ref[...]
    rows = split.shape[0] // 2
    most = times(split, right_high)
    return most[:rows] + (most[rows:] + times(split[:rows], right_low))


def set_split(split_ref, x):
    rows = x.shape[0]

    @pl.when(pl.program_id(0) == 0)
    def _():
        split_ref[:rows], split_ref[rows:] = halves(x)


def momentum_kernel(momentum_ref, grad_ref, code_ref, ortho_ref, next_ref, split_ref):
    set_split(split_ref, -KEEP_SHARE * ortho_ref[...])
    change = times_rows(split_ref, decode(code_ref))
    next_ref[...] = momentum_ref[...] + grad_ref[...].astype(jnp.float32) + change


def update_kernel(gain, code_ref, ortho_ref, scale_ref, basis_ref, update_ref, split_ref):
    set_split(split_ref, gain * ortho_ref[...])
    basis = decode(code_ref) * scale_ref[...]
    basis_ref[...] = basis
    update_ref[...] = times_rows(split_ref, basis).astype(jnp.bfloat16)


def finish(momentum, grad, codes, orthonormal, scale, gain):
    rows, cols = momentum.shape
    shares, share, rank = codes.shape
    share -= HEAD
    group = max(1, min(1024 // share, shares))
    block = group * share
    wide = pl.BlockSpec((rows, block), lambda i: (0, i))
    tall = pl.BlockSpec((block, rank), lambda i: (i, 0))
    coded = pl.BlockSpec((group, share + HEAD, rank), lambda i: (i, 0, 0))
    split = [pltpu.VMEM((2 * rows, rank), jnp.bfloat16)]
    flops = 6 * rows * cols * rank
    momentum_next = pl.pallas_call(
        momentum_kernel,
        grid=(cols // block,),
        in_specs=[wide, wide, coded, whole(orthonormal)],
        out_specs=wide,
        out_shape=jax.ShapeDtypeStruct((rows, cols), jnp.float32),
        scratch_shapes=split,
        compiler_params=PARAMS,
        cost_estimate=pl.CostEstimate(
            flops=flops, bytes_accessed=rows * cols * 10 + cols * rank * 2, transcendentals=0
        ),
    )(momentum, grad, codes, orthonormal)
    q_next, update = pl.pallas_call(
        functools.partial(update_kernel, gain),
        grid=(cols // block,),
        in_specs=[coded, whole(orthonormal), whole(scale)],
        out_specs=[tall, wide],
        out_shape=[
            jax.ShapeDtypeStruct((cols, rank), jnp.float32),
            jax.ShapeDtypeStruct((rows, cols), jnp.bfloat16),
        ],
        scratch_shapes=split,
        compiler_params=PARAMS,
        cost_estimate=pl.CostEstimate(flops=flops, bytes_accessed=rows * cols * 2 + cols * rank * 6, transcendentals=0),
    )(codes, orthonormal, scale)
    return momentum_next, q_next, update


def on_device(momentum, grad, q_stored, perm):
    block_rows = q_stored.shape[0]
    num_blocks = lax.axis_size("fsdp")
    num_cols = lax.axis_size("tp")
    rank_total = block_rows * num_blocks
    rows, cols = momentum.shape
    row_total, col_total = rows * num_blocks, cols * num_cols
    column = lax.axis_index("tp")
    share = cols // num_blocks

    basis, codes = prepare(momentum, grad, q_stored, share)
    codes = codes.reshape(-1, rows, codes.shape[2] // share, share).swapaxes(1, 2).reshape(num_blocks, rows, share)
    basis = lax.all_gather(basis, "fsdp", axis=0, tiled=True)
    codes, basis = lax.optimization_barrier((codes, basis))
    codes = lax.all_to_all(codes, "fsdp", split_axis=0, concat_axis=0).reshape(row_total, share)
    head = basis.reshape(num_blocks, block_rows, cols + rows)[:, :2, cols:].astype(jnp.float32)
    unit = unit_of(head[:, 0], head[:, 1]).reshape(1, row_total)

    parts = project(column.reshape(1), momentum, grad, basis, num_cols)
    parts = [parts[0]] + [exchange(parts[k], "tp", k) for k in range(1, num_cols)]
    packed = pack(perm, parts)
    if num_blocks * num_cols <= 64:
        packed = lax.all_gather(packed, ("fsdp", "tp"), axis=0)
    else:
        packed = lax.all_gather(lax.all_gather(packed, "tp", axis=0), "fsdp", axis=0, tiled=True)
    packed, codes = lax.optimization_barrier((packed, codes))
    turned, inverse_low = factor(packed)
    code, orthonormal = encode(lax.axis_index("fsdp").reshape(1), codes, turned, unit, inverse_low, rows)
    gathered = lax.all_gather(code, "fsdp", axis=0)
    head = gathered[:, share : share + 5].astype(jnp.float32)
    parts = (head[:, 3] + head[:, 4] * (1.0 / 16384.0)) * jnp.exp2(head[:, 2] - 13.0)
    squares = quad_sum(jnp.sum(parts, axis=0, keepdims=True), "tp")
    scale = lax.rsqrt(squares / col_total + EPSILON)
    return tuple(finish(momentum, grad, gathered, orthonormal, scale, math.sqrt(row_total / rank_total)))


def solution(mesh):
    return jax.shard_map(
        on_device,
        mesh=mesh,
        in_specs=(P("fsdp", "tp"), P("fsdp", "tp"), P("fsdp", "tp"), P()),
        out_specs=(P("fsdp", "tp"), P("tp", None), P("fsdp", "tp")),
        check_vma=False,
    )
```

time: 157 us -> 178 us (1.13)
  blocking collectives: 47.1 us -> 125 us
  waiting for transfers between devices: 41.7 us -> 4.31 us
  between operations: 14.2 us -> 0.76 us
  starting transfers between devices: 19.1 us -> 11.8 us
  other arithmetic: 3.69 us -> 0.1 us
  Pallas kernels: 26.2 us -> 28.7 us
  local copies, waits for them, and re-layouts: 4.42 us -> 6.71 us
    all_gather x0 -> x1, blocking collectives: none -> 77.8 us  [on_device(): packed = lax.all_gather(packed, ('fsdp', 'tp'), axis=0)]
    ppermute x12 -> x6, waiting for transfers between devices: 41.7 us -> 4.3 us  [exchange(): lax.ppermute(x, axis, [(i, i ^ k) for i in range(lax.axis_size(axis))])]
    ppermute x12 -> x6, starting transfers between devices: 14.8 us -> 7.51 us  [exchange(): lax.ppermute(x, axis, [(i, i ^ k) for i in range(lax.axis_size(axis))])]
    unnamed x14 -> x18, local copies, waits for them, and re-layouts: 3.23 us -> 6.7 us
    pallas_call x4 -> x5, Pallas kernels: 19.8 us -> 22.4 us  [the longest x1 13.1 us: factor(): pl.pallas_call(factor_kernel, grid=(devices // group,), in_specs=[pl.Bloc...]
    reduce_max x1 -> x0, other arithmetic: 2.33 us -> none  [on_device(): jnp.max(jnp.abs(combined), axis=1, keepdims=True)]
  transfers between devices with their start and end apart: 14 -> 7, of which waited for: 7 -> 3; matrix products, arithmetic and copies ran while one was open for 0% -> 0% of each run, Pallas kernels for 10% -> 4%
where the time goes in v8:
time: 178 us
  blocking collectives  125 us (70%)
  Pallas kernels  28.7 us (16%)
  starting transfers between devices  11.8 us (7%)
  local copies, waits for them, and re-layouts  6.71 us (4%)
  waiting for transfers between devices  4.31 us (2%)
    all_gather x1, blocking collectives, on_device(): packed = lax.all_gather(packed, ('fsdp', 'tp'), axis=0)  77.8 us
    all_gather x1, blocking collectives, on_device(): basis = lax.all_gather(basis, 'fsdp', axis=0, tiled=True)  26.4 us
    all_gather x1, blocking collectives, on_device(): gathered = lax.all_gather(code, 'fsdp', axis=0)  21 us
    pallas_call x1, Pallas kernels, factor(): pl.pallas_call(factor_kernel, grid=(devices // group,), in_specs=[pl.Bloc...  13.1 us
    ppermute x6, starting transfers between devices, exchange(): lax.ppermute(x, axis, [(i, i ^ k) for i in range(lax.axis_size(axis))])  7.51 us
    unnamed x18, local copies, waits for them, and re-layouts  6.7 us
    ppermute x6, waiting for transfers between devices, exchange(): lax.ppermute(x, axis, [(i, i ^ k) for i in range(lax.axis_size(axis))])  4.3 us
    all_to_all x1, starting transfers between devices, on_device(): lax.all_to_all(codes, 'fsdp', split_axis=0, concat_axis=0)  4.25 us
  transfers between devices with their start and end apart: 7, of which 3 were waited for; matrix products, arithmetic and copies ran while one was open for 0% of the time, Pallas kernels for 4%

profile of v8, /device:TPU:0, one launch (start us, length us, event | category | flops | bytes accessed | tf_op | source)
XLA Modules:
  0.0 177.6 jit_solution(18132977699789340758)
XLA Ops:
  0.6 0.0 copy-start
  0.6 1.6 copy-done
  2.2 0.0 copy-start.2
  2.2 1.2 copy-done.2
  3.4 0.0 copy-start.7
  3.5 0.9 copy-done.7
  4.4 1.4 shard_map.67
  5.8 0.0 copy-start.6
  5.8 0.0 copy-start.1
  5.8 0.0 copy-start.3
  5.8 26.4 %all-gather.5.code_ref = s16[256,4224]{1,0:T(8,128)(2,1)} all-gather(s16[32,4224]{1,0:T(8,128)(2,1)S(1)} %get-tuple-element.20), channel_id=1, replica_groups=mesh['fsdp'=8,'tp'=4] {'fsdp'}, dimensions={0}, use_global_device_ids=true | all-gather | bytes 2433024 | tf_op jit(solution)/shard_map/all_gather | solution.py:488
  32.2 0.0 copy-done.6
  32.2 4.2 %all-to-all-start = ((s16[8,128,512]{2,1,0:T(8,128)(2,1)}), s16[8,128,512]{2,1,0:T(8,128)(2,1)}, u32[]{:S(2)}, u32[]{:S(2)}) async-start(s16[8,128,512]{2,1,0:T(8,128)(2,1)} %copy-done.6), calls=%async_computation | async-start | bytes 2097152 | tf_op jit(solution)/shard_map/all_to_all | solution.py:490
  36.4 0.0 copy-done.1
  36.5 0.0 copy-done.3
  36.5 0.0 copy-start.4
  36.5 1.6 copy-done.4
  38.1 0.0 copy-start.8
  38.1 3.7 %shard_map.68 = (f32[32,256]{1,0:T(8,128)S(1)}, f32[32,256]{1,0:T(8,128)S(1)}, f32[32,256]{1,0:T(8,128)S(1)}, f32[32,256]{1,0:T(8,128)S(1)}) custom-call(s32[1]{0:T(128)} %bitcast.1.column_ref, f32[128,4096]{1,0:T(8,128)S(1)} %copy-done.1, bf16[128,4096]{1,0:T(8,128)(2,1)S(1)} %copy-done.3, s16[256,4224]{1,0:T(8,128)(2,1)S(1)} %copy-done.4), custom_call_target="tpu_custom_call" | custom-call | flops 536870912 | bytes 5242880 | tf_op jit(solution)/shard_map/pallas_call | solution.py:149
  41.8 1.6 collective-permute-start
  43.3 1.5 collective-permute-start.1
  44.9 0.5 collective-permute-start.2
  45.4 0.4 collective-permute-done.refs_1_
  45.8 1.5 collective-permute-done.1.refs_2_
  47.3 2.4 %collective-permute-done.2.refs_3_ = f32[32,256]{1,0:T(8,128)S(1)} collective-permute-done((f32[32,256]{1,0:T(8,128)S(1)}, f32[32,256]{1,0:T(8,128)S(1)}, u32[]{:S(2)}, u32[]{:S(2)}) %collective-permute-start.2) | collective-permute-done | bytes 32800 | tf_op jit(solution)/shard_map/ppermute | solution.py:27
  49.7 0.0 copy-done.8
  49.7 0.9 shard_map.69
  50.5 77.8 %all-gather.6 = s16[2560,256]{1,0:T(8,128)(2,1)} all-gather(s16[80,256]{1,0:T(8,128)(2,1)S(1)} %shard_map.69), channel_id=2, replica_groups=mesh['fsdp'=8,'tp'=4] {'fsdp','tp'}, dimensions={0}, use_global_device_ids=true | all-gather | bytes 1351680 | tf_op jit(solution)/shard_map/all_gather | solution.py:498
  128.3 0.0 all-to-all-done
  128.3 0.0 copy-start.5
  128.3 1.3 copy-done.5
  129.7 13.1 %shard_map.70 = (f32[256,1024]{1,0:T(8,128)S(1)}, f32[256,256]{1,0:T(8,128)S(1)}) custom-call(s16[32,80,256]{2,1,0:T(8,128)(2,1)S(1)} %bitcast.12), custom_call_target="tpu_custom_call" | custom-call | flops 805306368 | bytes 2621440 | tf_op jit(solution)/shard_map/pallas_call | solution.py:310
  142.7 3.4 %shard_map.71 = (s16[528,256]{1,0:T(8,128)(2,1)S(1)}, f32[128,256]{1,0:T(8,128)S(1)}) custom-call(s32[1]{0:T(128)} %bitcast.place_ref, s16[1024,512]{1,0:T(8,128)(2,1)} %bitcast.3.source_ref, f32[256,1024]{1,0:T(8,128)S(1)} %get-tuple-element.29.turned_ref.own_ref, f32[1,1024]{1,0:T(1,128)S(1)} %bitcast.13, f32[256,256]{1,0:T(8,128)S(1)} %get-tuple-element.30.inverse_ref, ...), custom_call_target="tpu_custom_call" | custom-call | flops 805306368 | bytes 2097152 | tf_op jit(solution)/shard_map/pallas_call | solution.py:369
  146.1 21.0 %all-gather.7 = s16[4224,256]{1,0:T(8,128)(2,1)S(1)} all-gather(s16[528,256]{1,0:T(8,128)(2,1)S(1)} %get-tuple-element.31), channel_id=3, replica_groups=mesh['fsdp'=8,'tp'=4] {'fsdp'}, dimensions={0}, use_global_device_ids=true | all-gather | bytes 2433024 | tf_op jit(solution)/shard_map/all_gather | solution.py:504
  167.2 0.1 fusion.4
  167.2 2.4 %collective-permute-start.3 = (f32[1,256]{1,0:T(1,128)S(1)}, f32[1,256]{1,0:T(1,128)S(1)}, u32[]{:S(2)}, u32[]{:S(2)}) collective-permute-start(f32[1,256]{1,0:T(1,128)S(1)} %bitcast.14), channel_id=1, source_target_pairs={{0,1},{1,0},{2,3},{3,2},{4,5},{5,4},{6,7},{7,6},{8,9},{9,8},{10,11... | collective-permute-start | bytes 3080 | tf_op jit(solution)/shard_map/ppermute | solution.py:27
  169.6 0.0 collective-permute-start.4
  169.6 1.5 collective-permute-start.5
  171.2 3.3 %shard_map.72 = f32[128,4096]{1,0:T(8,128)} custom-call(f32[128,4096]{1,0:T(8,128)S(1)} %copy-done.1, bf16[128,4096]{1,0:T(8,128)(2,1)S(1)} %copy-done.3, s16[8,528,256]{2,1,0:T(8,128)(2,1)S(1)} %bitcast.9, f32[128,256]{1,0:T(8,128)S(1)} %get-tuple-element.32.ortho_ref), custom_call_target="tpu_custom_call" | custom-call | flops 805306368 | bytes 7340032 | tf_op jit(solution)/shard_map/pallas_call | solution.py:448
  174.5 0.0 collective-permute-done.3
  174.5 0.0 collective-permute-done.4
  174.5 0.0 collective-permute-done.5
  174.5 3.1 %shard_map.73 = (f32[4096,256]{1,0:T(8,128)}, bf16[128,4096]{1,0:T(8,128)(2,1)}) custom-call(s16[8,528,256]{2,1,0:T(8,128)(2,1)S(1)} %bitcast.10, f32[128,256]{1,0:T(8,128)S(1)} %get-tuple-element.32.ortho_ref, f32[1,256]{1,0:T(1,128)S(1)} %add_rsqrt_fusion.scale_ref), custom_call_target="tpu_custom_call" | custom-call | flops 805306368 | bytes 7340032 | tf_op jit(solution)/shard_map/pallas_call | solution.py:460
  (5 shorter events, 0.0 us)
Async XLA Ops:
  0.6 1.6 copy-start
  2.2 1.2 copy-start.2
  3.4 0.9 copy-start.7
  5.8 26.4 %copy-start.6 = (s16[8,128,512]{2,1,0:T(8,128)(2,1)}, s16[8,128,512]{2,1,0:T(8,128)(2,1)S(1)}, u32[]{:S(2)}) copy-start(s16[8,128,512]{2,1,0:T(8,128)(2,1)S(1)} %get-tuple-element.26) | copy-start | bytes 3145732
  5.8 30.7 %copy-start.1 = (f32[128,4096]{1,0:T(8,128)S(1)}, f32[128,4096]{1,0:T(8,128)}, u32[]{:S(2)}) copy-start(f32[128,4096]{1,0:T(8,128)} %momentum_ref.5) | copy-start | bytes 6291460
  5.8 30.7 %copy-start.3 = (bf16[128,4096]{1,0:T(8,128)(2,1)S(1)}, bf16[128,4096]{1,0:T(8,128)(2,1)}, u32[]{:S(2)}) copy-start(bf16[128,4096]{1,0:T(8,128)(2,1)} %grad_ref.5) | copy-start | bytes 3145732
  32.2 96.2 %all-to-all-start = ((s16[8,128,512]{2,1,0:T(8,128)(2,1)}), s16[8,128,512]{2,1,0:T(8,128)(2,1)}, u32[]{:S(2)}, u32[]{:S(2)}) async-start(s16[8,128,512]{2,1,0:T(8,128)(2,1)} %copy-done.6), calls=%async_computation | async-start | bytes 2097152 | tf_op jit(solution)/shard_map/all_to_all | solution.py:490
  36.5 1.6 copy-start.4
  38.1 11.6 %copy-start.8 = (s32[8]{0:T(128)S(1)}, s32[8]{0:T(128)}, u32[]{:S(2)}) copy-start(s32[8]{0:T(128)} %perm_ref.1) | copy-start | bytes 100
  41.8 4.0 %collective-permute-start = (f32[32,256]{1,0:T(8,128)S(1)}, f32[32,256]{1,0:T(8,128)S(1)}, u32[]{:S(2)}, u32[]{:S(2)}) collective-permute-start(f32[32,256]{1,0:T(8,128)S(1)} %get-tuple-element.23), channel_id=1, source_target_pairs={{0,1},{1,0},{2,3},{3,2},{4,5},{5,4},{6,7},{7,6},{8,9},{9,8},{10,11... | collective-permute-start | bytes 98312 | tf_op jit(solution)/shard_map/ppermute | solution.py:27
  43.3 3.9 %collective-permute-start.1 = (f32[32,256]{1,0:T(8,128)S(1)}, f32[32,256]{1,0:T(8,128)S(1)}, u32[]{:S(2)}, u32[]{:S(2)}) collective-permute-start(f32[32,256]{1,0:T(8,128)S(1)} %get-tuple-element.24), channel_id=1, source_target_pairs={{0,2},{1,3},{2,0},{3,1},{4,6},{5,7},{6,4},{7,5},{8,10},{9,11},{10,... | collective-permute-start | bytes 98312 | tf_op jit(solution)/shard_map/ppermute | solution.py:27
  44.9 4.8 %collective-permute-start.2 = (f32[32,256]{1,0:T(8,128)S(1)}, f32[32,256]{1,0:T(8,128)S(1)}, u32[]{:S(2)}, u32[]{:S(2)}) collective-permute-start(f32[32,256]{1,0:T(8,128)S(1)} %get-tuple-element.25), channel_id=1, source_target_pairs={{0,3},{1,2},{2,1},{3,0},{4,7},{5,6},{6,5},{7,4},{8,11},{9,10},{10,... | collective-permute-start | bytes 98312 | tf_op jit(solution)/shard_map/ppermute | solution.py:27
  128.3 1.3 copy-start.5
  167.2 7.3 %collective-permute-start.3 = (f32[1,256]{1,0:T(1,128)S(1)}, f32[1,256]{1,0:T(1,128)S(1)}, u32[]{:S(2)}, u32[]{:S(2)}) collective-permute-start(f32[1,256]{1,0:T(1,128)S(1)} %bitcast.14), channel_id=1, source_target_pairs={{0,1},{1,0},{2,3},{3,2},{4,5},{5,4},{6,7},{7,6},{8,9},{9,8},{10,11... | collective-permute-start | bytes 3080 | tf_op jit(solution)/shard_map/ppermute | solution.py:27
  169.6 4.9 %collective-permute-start.4 = (f32[1,256]{1,0:T(1,128)S(1)}, f32[1,256]{1,0:T(1,128)S(1)}, u32[]{:S(2)}, u32[]{:S(2)}) collective-permute-start(f32[1,256]{1,0:T(1,128)S(1)} %bitcast.15), channel_id=1, source_target_pairs={{0,2},{1,3},{2,0},{3,1},{4,6},{5,7},{6,4},{7,5},{8,10},{9,11},{10,... | collective-permute-start | bytes 3080 | tf_op jit(solution)/shard_map/ppermute | solution.py:27
  169.6 4.9 %collective-permute-start.5 = (f32[1,256]{1,0:T(1,128)S(1)}, f32[1,256]{1,0:T(1,128)S(1)}, u32[]{:S(2)}, u32[]{:S(2)}) collective-permute-start(f32[1,256]{1,0:T(1,128)S(1)} %bitcast.16), channel_id=1, source_target_pairs={{0,3},{1,2},{2,1},{3,0},{4,7},{5,6},{6,5},{7,4},{8,11},{9,10},{10,... | collective-permute-start | bytes 3080 | tf_op jit(solution)/shard_map/ppermute | solution.py:27

commit v9 on v8

--- a/solution.py
+++ b/solution.py
@@ -16,6 +16,7 @@
 HEAD = 16
 TOP = 32766.0
 PARAMS = pltpu.CompilerParams(vmem_limit_bytes=40 * 1024 * 1024)
+STREAM = pltpu.CompilerParams(vmem_limit_bytes=54 * 1024 * 1024)
 
 
 def halves(x):
@@ -105,13 +106,12 @@
             jax.ShapeDtypeStruct((basis.shape[0], cols + rows), jnp.int16),
             jax.ShapeDtypeStruct((cols // width, rows, width), jnp.int16),
         ],
-        compiler_params=PARAMS,
+        compiler_params=STREAM,
         cost_estimate=pl.CostEstimate(flops=10 * rows * cols, bytes_accessed=rows * cols * 8, transcendentals=0),
     )(momentum, grad, basis)
 
 
-def project_kernel(column_ref, momentum_ref, grad_ref, code_ref, *refs):
-    out_refs, total_ref = refs[:-1], refs[-1]
+def project_kernel(momentum_ref, grad_ref, code_ref, out_ref):
     code = code_ref[...].astype(jnp.int32)
     size = jnp.abs(code)
     value = ((size & 127) + 128).astype(jnp.float32) * jnp.exp2(((size >> 7) - 134).astype(jnp.float32))
@@ -128,39 +128,29 @@
 
     @pl.when(pl.program_id(0) == 0)
     def _():
-        total_ref[...] = part
+        out_ref[...] = part
 
     @pl.when(pl.program_id(0) > 0)
     def _():
-        total_ref[...] += part
-
-    @pl.when(pl.program_id(0) == pl.num_programs(0) - 1)
-    def _():
-        for k, out_ref in enumerate(out_refs):
-            piece = out_ref.shape[0]
-            out_ref[...] = total_ref[pl.ds(pl.multiple_of((column_ref[0] ^ k) * piece, piece), piece), :]
-
-
-def project(column, momentum, grad, codes, columns):
+        out_ref[...] += part
+
+
+def project(momentum, grad, codes):
     rows, cols = momentum.shape
     rank = codes.shape[0]
     block = min(1024, cols)
-    wide = pl.BlockSpec((rows, block), lambda i, column: (0, i))
+    wide = pl.BlockSpec((rows, block), lambda i: (0, i))
     return pl.pallas_call(
         project_kernel,
-        grid_spec=pltpu.PrefetchScalarGridSpec(
-            num_scalar_prefetch=1,
-            grid=(cols // block,),
-            in_specs=[wide, wide, pl.BlockSpec((rank, block), lambda i, column: (0, i))],
-            out_specs=[pl.BlockSpec((rows // columns, rank), lambda i, column: (0, 0))] * columns,
-            scratch_shapes=[pltpu.VMEM((rows, rank), jnp.float32)],
-        ),
-        out_shape=[jax.ShapeDtypeStruct((rows // columns, rank), jnp.float32)] * columns,
-        compiler_params=PARAMS,
+        grid=(cols // block,),
+        in_specs=[wide, wide, pl.BlockSpec((rank, block), lambda i: (0, i))],
+        out_specs=pl.BlockSpec((rows, rank), lambda i: (0, 0)),
+        out_shape=jax.ShapeDtypeStruct((rows, rank), jnp.float32),
+        compiler_params=STREAM,
         cost_estimate=pl.CostEstimate(
             flops=4 * rows * cols * rank, bytes_accessed=rows * cols * 6 + rank * cols * 2, transcendentals=rank * cols
         ),
-    )(column, momentum, grad, codes)
+    )(momentum, grad, codes)
 
 
 def pack_kernel(perm_ref, *refs):
@@ -203,47 +193,45 @@
     return jnp.broadcast_to(row, (TILE, 2 * PANEL))
 
 
-def panel_inverse(block):
+def panel_inverse(block, band):
     rows = lax.broadcasted_iota(jnp.int32, (PANEL, PANEL), 0)
     cols = lax.broadcasted_iota(jnp.int32, (PANEL, PANEL), 1)
     both = jnp.concatenate([block, (rows == cols).astype(jnp.float32)], axis=1)
     count = PANEL // TILE
     tiles = [both[TILE * i : TILE * (i + 1)] for i in range(count)]
     sub = lax.broadcasted_iota(jnp.int32, (TILE, 2 * PANEL), 0)
+    row = lambda k, j: band[k, pl.ds(j, TILE, stride=0), :]
     done = []
     for k in range(count):
         columns = [
             [spread(tiles[i][:, TILE * k + j : TILE * k + j + 1]) for j in range(TILE)] for i in range(k, count)
         ]
-        own, body = list(columns[0]), tiles[k]
-        final = jnp.zeros_like(body)
+        state = list(columns[0]) + [tiles[k]]
+        for m, x in enumerate(state):
+            band[m] = x
+        final = jnp.zeros_like(tiles[k])
         for j in range(0, TILE, 2):
             first, second = sub == j, sub == j + 1
-            a, b, c = spread(own[j][j : j + 1]), spread(own[j + 1][j : j + 1]), spread(own[j + 1][j + 1 : j + 2])
+            a, b, c = row(j, j), row(j + 1, j), row(j + 1, j + 1)
             minor = a * c - b * b
             inverse = 1.0 / minor
-
-            def solve(x):
-                upper, lower = spread(x[j : j + 1]), spread(x[j + 1 : j + 2])
-                return (c * upper - b * lower) * inverse, (a * lower - b * upper) * inverse
-
-            def reduce_rows(x):
-                upper, lower = solve(x)
-                rest = x - own[j] * upper - own[j + 1] * lower
-                return jnp.where(first, upper, jnp.where(second, lower, rest))
-
+            left, right = state[j], state[j + 1]
             ratio = 1.0 / a
-            below = (body - b * ratio * spread(body[j : j + 1])) * lax.rsqrt(minor * ratio)
-            final = jnp.where(first, body * lax.rsqrt(a), jnp.where(second, below, final))
-            body = reduce_rows(body)
-            later = {other: reduce_rows(own[other]) for other in range(j + 2, TILE)}
-            for other, column in later.items():
-                own[other] = column
+            below = (state[TILE] - b * ratio * row(TILE, j)) * lax.rsqrt(minor * ratio)
+            final = jnp.where(first, state[TILE] * lax.rsqrt(a), jnp.where(second, below, final))
+            for m in range(j + 2, TILE + 1):
+                upper, lower = row(m, j), row(m, j + 1)
+                upper, lower = (c * upper - b * lower) * inverse, (a * lower - b * upper) * inverse
+                rest = state[m] - left * upper - right * lower
+                state[m] = jnp.where(first, upper, jnp.where(second, lower, rest))
+            for m in range(j + 2, TILE + 1):
+                band[m] = state[m]
         done.append(final)
+        reduced = [row(TILE, j) for j in range(TILE)]
         for i in range(k + 1, count):
             tile = tiles[i]
             for j in range(TILE):
-                tile = tile - columns[i - k][j] * spread(body[j : j + 1])
+                tile = tile - columns[i - k][j] * reduced[j]
             tiles[i] = tile
     return jnp.concatenate(done, axis=0)[:, PANEL:]
 
@@ -252,7 +240,7 @@
     return (x + 127) // 128 * 128
 
 
-def inverse_factor(gram, out_ref, work):
+def inverse_factor(gram, out_ref, work, band):
     rank = gram.shape[0]
     rows = lax.broadcasted_iota(jnp.int32, (rank, rank), 0)
     cols = lax.broadcasted_iota(jnp.int32, (rank, rank), 1)
@@ -263,7 +251,7 @@
     for start in range(0, rank, PANEL):
         end = start + PANEL
         left, right = start // 128 * 128, rank + lanes_up(end)
-        inverse = panel_inverse(work[start:end, start:end])
+        inverse = panel_inverse(work[start:end, start:end], band)
         scaled = jnp.dot(inverse, work[start:end, left:right], precision=HIGH, preferred_element_type=jnp.float32)
         out_ref[start:end, : lanes_up(end)] = scaled[:, rank - left :] * scale[:, : lanes_up(end)]
         if lanes_up(end) < rank:
@@ -280,7 +268,7 @@
             work[end:, low:right] = work[end:, low:right] - change[end - low :, :]
 
 
-def factor_kernel(code_ref, turned_ref, out_ref, gram_ref, work):
+def factor_kernel(code_ref, turned_ref, out_ref, gram_ref, work, band):
     count, size, rank = code_ref.shape
     size = (size - HEAD) // 2
     code = code_ref[...].astype(jnp.int32).astype(jnp.float32)
@@ -300,7 +288,7 @@
 
     @pl.when(pl.program_id(0) == pl.num_programs(0) - 1)
     def _():
-        inverse_factor(gram_ref[...], out_ref, work)
+        inverse_factor(gram_ref[...], out_ref, work, band)
 
 
 def factor(codes):
@@ -316,7 +304,11 @@
             jax.ShapeDtypeStruct((rank, devices * rows), jnp.float32),
             jax.ShapeDtypeStruct((rank, rank), jnp.float32),
         ],
-        scratch_shapes=[pltpu.VMEM((rank, rank), jnp.float32), pltpu.VMEM((rank, 2 * rank), jnp.float32)],
+        scratch_shapes=[
+            pltpu.VMEM((rank, rank), jnp.float32),
+            pltpu.VMEM((rank, 2 * rank), jnp.float32),
+            pltpu.VMEM((TILE + 1, TILE, 2 * PANEL), jnp.float32),
+        ],
         compiler_params=PARAMS,
         cost_estimate=pl.CostEstimate(
             flops=12 * devices * rows * rank * rank, bytes_accessed=devices * size * rank * 4, transcendentals=rank
@@ -480,7 +472,6 @@
     rank_total = block_rows * num_blocks
     rows, cols = momentum.shape
     row_total, col_total = rows * num_blocks, cols * num_cols
-    column = lax.axis_index("tp")
     share = cols // num_blocks
 
     basis, codes = prepare(momentum, grad, q_stored, share)
@@ -491,13 +482,12 @@
     head = basis.reshape(num_blocks, block_rows, cols + rows)[:, :2, cols:].astype(jnp.float32)
     unit = unit_of(head[:, 0], head[:, 1]).reshape(1, row_total)
 
-    parts = project(column.reshape(1), momentum, grad, basis, num_cols)
-    parts = [parts[0]] + [exchange(parts[k], "tp", k) for k in range(1, num_cols)]
-    packed = pack(perm, parts)
-    if num_blocks * num_cols <= 64:
-        packed = lax.all_gather(packed, ("fsdp", "tp"), axis=0)
-    else:
-        packed = lax.all_gather(lax.all_gather(packed, "tp", axis=0), "fsdp", axis=0, tiled=True)
+    near = project(momentum, grad, basis)
+    step = 1
+    while 2 * step < num_cols:
+        near = near + exchange(near, "tp", step)
+        step *= 2
+    packed = lax.all_gather(pack(perm, [near, exchange(near, "tp", step)]), "fsdp", axis=0)
     packed, codes = lax.optimization_barrier((packed, codes))
     turned, inverse_low = factor(packed)
     code, orthonormal = encode(lax.axis_index("fsdp").reshape(1), codes, turned, unit, inverse_low, rows)

time: 178 us -> 123 us (0.69)
  blocking collectives: 125 us -> 69.8 us
  local copies, waits for them, and re-layouts: 6.71 us -> 0.74 us
  waiting for transfers between devices: 4.31 us -> 8.18 us
  Pallas kernels: 28.7 us -> 31.6 us
    all_gather x1, blocking collectives: 77.8 us -> 20.1 us  [on_device(): lax.all_gather(pack(perm, [near, exchange(near, 'tp', step)]), 'fsdp', ax...]
    unnamed x18 -> x6, local copies, waits for them, and re-layouts: 6.7 us -> 0.02 us
    ppermute x6 -> x5, waiting for transfers between devices: 4.3 us -> 8.17 us  [exchange(): lax.ppermute(x, axis, [(i, i ^ k) for i in range(lax.axis_size(axis))])]
    pallas_call x1, Pallas kernels: 1.37 us -> 4.25 us  [prepare(): pl.pallas_call(prepare_kernel, out_shape=[jax.ShapeDtypeStruct((basis.sha...]
    all_gather x1, blocking collectives: 21 us -> 23.3 us  [on_device(): gathered = lax.all_gather(code, 'fsdp', axis=0)]
    pallas_call x1, Pallas kernels: 3.7 us -> 5.72 us  [project(): pl.pallas_call(project_kernel, grid=(cols // block,), in_specs=[wide, wid...]
    ppermute x6 -> x5, starting transfers between devices: 7.51 us -> 6.61 us  [exchange(): lax.ppermute(x, axis, [(i, i ^ k) for i in range(lax.axis_size(axis))])]
  transfers between devices with their start and end apart: 7 -> 6, of which waited for: 3 -> 3; matrix products, arithmetic and copies ran while one was open for 0% -> 1% of each run, Pallas kernels for 4% -> 8%
where the time goes in v9:
time: 123 us; the launch traced here: 122 us
  blocking collectives  69.8 us (57%)
  Pallas kernels  31.6 us (26%)
  starting transfers between devices  10.3 us (8%)
  waiting for transfers between devices  8.18 us (7%)
    all_gather x1, blocking collectives, on_device(): basis = lax.all_gather(basis, 'fsdp', axis=0, tiled=True)  26.4 us
    all_gather x1, blocking collectives, on_device(): gathered = lax.all_gather(code, 'fsdp', axis=0)  23.3 us
    all_gather x1, blocking collectives, on_device(): lax.all_gather(pack(perm, [near, exchange(near, 'tp', step)]), 'fsdp', ax...  20.1 us
    pallas_call x1, Pallas kernels, factor(): pl.pallas_call(factor_kernel, grid=(devices // group,), in_specs=[pl.Bloc...  11.9 us
    ppermute x5, waiting for transfers between devices, exchange(): lax.ppermute(x, axis, [(i, i ^ k) for i in range(lax.axis_size(axis))])  8.17 us
    ppermute x5, starting transfers between devices, exchange(): lax.ppermute(x, axis, [(i, i ^ k) for i in range(lax.axis_size(axis))])  6.61 us
    pallas_call x1, Pallas kernels, project(): pl.pallas_call(project_kernel, grid=(cols // block,), in_specs=[wide, wid...  5.72 us
    pallas_call x1, Pallas kernels, prepare(): pl.pallas_call(prepare_kernel, out_shape=[jax.ShapeDtypeStruct((basis.sha...  4.25 us
  transfers between devices with their start and end apart: 6, of which 3 were waited for; matrix products, arithmetic and copies ran while one was open for 1% of the time, Pallas kernels for 8%

profile of v9, /device:TPU:0, one launch (start us, length us, event | category | flops | bytes accessed | tf_op | source)
XLA Modules:
  0.0 122.4 jit_solution(6803554725779200778)
XLA Ops:
  0.6 4.3 %shard_map.67 = (s16[32,4224]{1,0:T(8,128)(2,1)}, s16[8,128,512]{2,1,0:T(8,128)(2,1)}) custom-call(f32[128,4096]{1,0:T(8,128)} %momentum_ref.5, bf16[128,4096]{1,0:T(8,128)(2,1)} %grad_ref.5, bf16[32,4096]{1,0:T(8,128)(2,1)} %basis_ref.1), custom_call_target="tpu_custom_call" | custom-call | flops 5242880 | bytes 4194304 | tf_op jit(solution)/shard_map/pallas_call | solution.py:103
  4.9 26.4 %all-gather.5.code_ref = s16[256,4224]{1,0:T(8,128)(2,1)} all-gather(s16[32,4224]{1,0:T(8,128)(2,1)} %get-tuple-element.16), channel_id=1, replica_groups=mesh['fsdp'=8,'tp'=4] {'fsdp'}, dimensions={0}, use_global_device_ids=true | all-gather | bytes 2433024 | tf_op jit(solution)/shard_map/all_gather | solution.py:479
  31.3 3.7 %all-to-all-start = ((s16[8,128,512]{2,1,0:T(8,128)(2,1)}), s16[8,128,512]{2,1,0:T(8,128)(2,1)S(1)}, u32[]{:S(2)}, u32[]{:S(2)}) async-start(s16[8,128,512]{2,1,0:T(8,128)(2,1)} %get-tuple-element.18), calls=%async_computation | async-start | bytes 2097152 | tf_op jit(solution)/shard_map/all_to_all | solution.py:481
  35.0 0.0 copy-start.2
  35.0 5.7 %shard_map.68 = f32[128,256]{1,0:T(8,128)} custom-call(f32[128,4096]{1,0:T(8,128)} %momentum_ref.5, bf16[128,4096]{1,0:T(8,128)(2,1)} %grad_ref.5, s16[256,4224]{1,0:T(8,128)(2,1)} %all-gather.5.code_ref), custom_call_target="tpu_custom_call" | custom-call | flops 536870912 | bytes 5242880 | tf_op jit(solution)/shard_map/pallas_call | solution.py:143
  40.7 1.5 %collective-permute-start = (f32[128,256]{1,0:T(8,128)}, f32[128,256]{1,0:T(8,128)S(1)}, u32[]{:S(2)}, u32[]{:S(2)}) collective-permute-start(f32[128,256]{1,0:T(8,128)} %shard_map.68), channel_id=1, source_target_pairs={{0,1},{1,0},{2,3},{3,2},{4,5},{5,4},{6,7},{7,6},{8,9},{9,8},{10,11... | collective-permute-start | bytes 393224 | tf_op jit(solution)/shard_map/ppermute | solution.py:28
  42.2 0.7 slice.28
  43.0 3.9 %collective-permute-done = f32[128,256]{1,0:T(8,128)S(1)} collective-permute-done((f32[128,256]{1,0:T(8,128)}, f32[128,256]{1,0:T(8,128)S(1)}, u32[]{:S(2)}, u32[]{:S(2)}) %collective-permute-start) | collective-permute-done | bytes 131104 | tf_op jit(solution)/shard_map/ppermute | solution.py:28
  46.8 0.9 add.33.refs_0_
  47.8 1.6 %collective-permute-start.1 = (f32[128,256]{1,0:T(8,128)S(1)}, f32[128,256]{1,0:T(8,128)S(1)}, u32[]{:S(2)}, u32[]{:S(2)}) collective-permute-start(f32[128,256]{1,0:T(8,128)S(1)} %add.33.refs_0_), channel_id=1, source_target_pairs={{0,2},{1,3},{2,0},{3,1},{4,6},{5,7},{6,4},{7,5},{8,10},{9,11},{10,... | collective-permute-start | bytes 393224 | tf_op jit(solution)/shard_map/ppermute | solution.py:28
  49.4 3.6 %collective-permute-done.1.refs_1_ = f32[128,256]{1,0:T(8,128)S(1)} collective-permute-done((f32[128,256]{1,0:T(8,128)S(1)}, f32[128,256]{1,0:T(8,128)S(1)}, u32[]{:S(2)}, u32[]{:S(2)}) %collective-permute-start.1) | collective-permute-done | bytes 131104 | tf_op jit(solution)/shard_map/ppermute | solution.py:28
  52.9 0.0 copy-done.2
  52.9 0.9 shard_map.69
  53.9 20.1 %all-gather.6 = s16[2176,256]{1,0:T(8,128)(2,1)S(1)} all-gather(s16[272,256]{1,0:T(8,128)(2,1)S(1)} %shard_map.69), channel_id=2, replica_groups=mesh['fsdp'=8,'tp'=4] {'fsdp'}, dimensions={0}, use_global_device_ids=true | all-gather | bytes 1253376 | tf_op jit(solution)/shard_map/all_gather | solution.py:490
  74.0 0.0 all-to-all-done
  74.0 11.9 %shard_map.70 = (f32[256,1024]{1,0:T(8,128)S(1)}, f32[256,256]{1,0:T(8,128)S(1)}) custom-call(s16[8,272,256]{2,1,0:T(8,128)(2,1)S(1)} %bitcast.11), custom_call_target="tpu_custom_call" | custom-call | flops 805306368 | bytes 2228224 | tf_op jit(solution)/shard_map/pallas_call | solution.py:298
  85.9 0.0 copy-start
  85.9 0.0 copy-start.1
  85.9 2.4 %shard_map.71 = (s16[528,256]{1,0:T(8,128)(2,1)S(1)}, f32[128,256]{1,0:T(8,128)S(1)}) custom-call(s32[1]{0:T(128)} %bitcast.place_ref, s16[1024,512]{1,0:T(8,128)(2,1)S(1)} %bitcast.10, f32[256,1024]{1,0:T(8,128)S(1)} %get-tuple-element.21.turned_ref.own_ref, f32[1,1024]{1,0:T(1,128)S(1)} %bitcast.12, f32[256,256]{1,0:T(8,128)S(1)} %get-tuple-element.22.inverse_ref, ...), custom_call_target="tpu_custom_call" | custom-call | flops 805306368 | bytes 2097152 | tf_op jit(solution)/shard_map/pallas_call | solution.py:361
  88.3 23.3 %all-gather.7 = s16[4224,256]{1,0:T(8,128)(2,1)S(1)} all-gather(s16[528,256]{1,0:T(8,128)(2,1)S(1)} %get-tuple-element.23), channel_id=3, replica_groups=mesh['fsdp'=8,'tp'=4] {'fsdp'}, dimensions={0}, use_global_device_ids=true | all-gather | bytes 2433024 | tf_op jit(solution)/shard_map/all_gather | solution.py:494
  111.7 0.1 fusion.4
  111.7 1.6 %collective-permute-start.2 = (f32[1,256]{1,0:T(1,128)S(1)}, f32[1,256]{1,0:T(1,128)S(1)}, u32[]{:S(2)}, u32[]{:S(2)}) collective-permute-start(f32[1,256]{1,0:T(1,128)S(1)} %bitcast.14), channel_id=1, source_target_pairs={{0,1},{1,0},{2,3},{3,2},{4,5},{5,4},{6,7},{7,6},{8,9},{9,8},{10,11... | collective-permute-start | bytes 3080 | tf_op jit(solution)/shard_map/ppermute | solution.py:28
  113.3 1.5 %collective-permute-start.3 = (f32[1,256]{1,0:T(1,128)S(1)}, f32[1,256]{1,0:T(1,128)S(1)}, u32[]{:S(2)}, u32[]{:S(2)}) collective-permute-start(f32[1,256]{1,0:T(1,128)S(1)} %bitcast.15), channel_id=1, source_target_pairs={{0,2},{1,3},{2,0},{3,1},{4,6},{5,7},{6,4},{7,5},{8,10},{9,11},{10,... | collective-permute-start | bytes 3080 | tf_op jit(solution)/shard_map/ppermute | solution.py:28
  114.8 0.5 collective-permute-start.4
  115.3 0.0 copy-done
  115.3 0.0 copy-done.1
  115.3 3.3 %shard_map.72 = f32[128,4096]{1,0:T(8,128)} custom-call(f32[128,4096]{1,0:T(8,128)S(1)} %copy-done, bf16[128,4096]{1,0:T(8,128)(2,1)S(1)} %copy-done.1, s16[8,528,256]{2,1,0:T(8,128)(2,1)S(1)} %bitcast.8, f32[128,256]{1,0:T(8,128)S(1)} %get-tuple-element.24.ortho_ref), custom_call_target="tpu_custom_call" | custom-call | flops 805306368 | bytes 7340032 | tf_op jit(solution)/shard_map/pallas_call | solution.py:440
  118.6 0.0 collective-permute-done.2
  118.6 0.0 collective-permute-done.3
  118.6 0.7 collective-permute-done.4
  119.3 3.1 %shard_map.73 = (f32[4096,256]{1,0:T(8,128)}, bf16[128,4096]{1,0:T(8,128)(2,1)}) custom-call(s16[8,528,256]{2,1,0:T(8,128)(2,1)S(1)} %bitcast.9, f32[128,256]{1,0:T(8,128)S(1)} %get-tuple-element.24.ortho_ref, f32[1,256]{1,0:T(1,128)S(1)} %add_rsqrt_fusion.scale_ref), custom_call_target="tpu_custom_call" | custom-call | flops 805306368 | bytes 7340032 | tf_op jit(solution)/shard_map/pallas_call | solution.py:452
  (4 shorter events, 0.0 us)
Async XLA Ops:
  31.3 42.6 %all-to-all-start = ((s16[8,128,512]{2,1,0:T(8,128)(2,1)}), s16[8,128,512]{2,1,0:T(8,128)(2,1)S(1)}, u32[]{:S(2)}, u32[]{:S(2)}) async-start(s16[8,128,512]{2,1,0:T(8,128)(2,1)} %get-tuple-element.18), calls=%async_computation | async-start | bytes 2097152 | tf_op jit(solution)/shard_map/all_to_all | solution.py:481
  35.0 17.9 %copy-start.2 = (s32[8]{0:T(128)S(1)}, s32[8]{0:T(128)}, u32[]{:S(2)}) copy-start(s32[8]{0:T(128)} %perm_ref.1) | copy-start | bytes 100
  40.7 6.1 %collective-permute-start = (f32[128,256]{1,0:T(8,128)}, f32[128,256]{1,0:T(8,128)S(1)}, u32[]{:S(2)}, u32[]{:S(2)}) collective-permute-start(f32[128,256]{1,0:T(8,128)} %shard_map.68), channel_id=1, source_target_pairs={{0,1},{1,0},{2,3},{3,2},{4,5},{5,4},{6,7},{7,6},{8,9},{9,8},{10,11... | collective-permute-start | bytes 393224 | tf_op jit(solution)/shard_map/ppermute | solution.py:28
  47.8 5.2 %collective-permute-start.1 = (f32[128,256]{1,0:T(8,128)S(1)}, f32[128,256]{1,0:T(8,128)S(1)}, u32[]{:S(2)}, u32[]{:S(2)}) collective-permute-start(f32[128,256]{1,0:T(8,128)S(1)} %add.33.refs_0_), channel_id=1, source_target_pairs={{0,2},{1,3},{2,0},{3,1},{4,6},{5,7},{6,4},{7,5},{8,10},{9,11},{10,... | collective-permute-start | bytes 393224 | tf_op jit(solution)/shard_map/ppermute | solution.py:28
  85.9 29.4 %copy-start = (f32[128,4096]{1,0:T(8,128)S(1)}, f32[128,4096]{1,0:T(8,128)}, u32[]{:S(2)}) copy-start(f32[128,4096]{1,0:T(8,128)} %momentum_ref.5) | copy-start | bytes 6291460
  85.9 29.4 %copy-start.1 = (bf16[128,4096]{1,0:T(8,128)(2,1)S(1)}, bf16[128,4096]{1,0:T(8,128)(2,1)}, u32[]{:S(2)}) copy-start(bf16[128,4096]{1,0:T(8,128)(2,1)} %grad_ref.5) | copy-start | bytes 3145732
  111.7 6.9 %collective-permute-start.2 = (f32[1,256]{1,0:T(1,128)S(1)}, f32[1,256]{1,0:T(1,128)S(1)}, u32[]{:S(2)}, u32[]{:S(2)}) collective-permute-start(f32[1,256]{1,0:T(1,128)S(1)} %bitcast.14), channel_id=1, source_target_pairs={{0,1},{1,0},{2,3},{3,2},{4,5},{5,4},{6,7},{7,6},{8,9},{9,8},{10,11... | collective-permute-start | bytes 3080 | tf_op jit(solution)/shard_map/ppermute | solution.py:28
  113.3 5.3 %collective-permute-start.3 = (f32[1,256]{1,0:T(1,128)S(1)}, f32[1,256]{1,0:T(1,128)S(1)}, u32[]{:S(2)}, u32[]{:S(2)}) collective-permute-start(f32[1,256]{1,0:T(1,128)S(1)} %bitcast.15), channel_id=1, source_target_pairs={{0,2},{1,3},{2,0},{3,1},{4,6},{5,7},{6,4},{7,5},{8,10},{9,11},{10,... | collective-permute-start | bytes 3080 | tf_op jit(solution)/shard_map/ppermute | solution.py:28
  114.8 4.5 %collective-permute-start.4 = (f32[1,256]{1,0:T(1,128)S(1)}, f32[1,256]{1,0:T(1,128)S(1)}, u32[]{:S(2)}, u32[]{:S(2)}) collective-permute-start(f32[1,256]{1,0:T(1,128)S(1)} %bitcast.16), channel_id=1, source_target_pairs={{0,3},{1,2},{2,1},{3,0},{4,7},{5,6},{6,5},{7,4},{8,11},{9,10},{10,... | collective-permute-start | bytes 3080 | tf_op jit(solution)/shard_map/ppermute | solution.py:28

commit v10 on v9

--- a/solution.py
+++ b/solution.py
@@ -78,10 +78,10 @@
     normal = size >= 2.0**-126
     exponent = jnp.floor(jnp.log2(jnp.where(normal, size, 1.0)))
     code = 128.0 * (exponent + 126.0) + jnp.floor(128.0 * (size * jnp.exp2(-exponent)) + 0.5)
-    return whole_number(jnp.where(normal, jnp.where(value < 0.0, -code, code), 0.0))
-
-
-def prepare_kernel(momentum_ref, grad_ref, basis_ref, pack_ref, code_ref):
+    return whole_number(jnp.where(normal, jnp.where(value < 0.0, code - 32768.0, code), 0.0))
+
+
+def prepare_kernel(momentum_ref, grad_ref, basis_ref, pack_ref, code_ref, head_ref):
     rows, cols = momentum_ref.shape
     width = code_ref.shape[-1]
     spans = [slice(i, i + width) for i in range(0, cols, width)]
@@ -92,20 +92,40 @@
     for k, span in enumerate(spans):
         code_ref[k] = whole_number(jnp.floor(combined(span) * inverse + 0.5))
         pack_ref[:, span] = code_basis(basis_ref[:, span])
-    across = lax.broadcasted_iota(jnp.int32, (rows, rows), 0) == lax.broadcasted_iota(jnp.int32, (rows, rows), 1)
-    turn = lambda x: jnp.sum(jnp.where(across, x, 0.0), axis=0, keepdims=True)
-    set_head(pack_ref.at[:, cols:], turn(exponent), turn(mantissa))
+    step = pl.program_id(0)
+    here = pl.ds(pl.multiple_of(step * rows, rows), rows)
+    for k, column in enumerate((exponent, mantissa)):
+        head_ref[k, here, :] = jnp.broadcast_to(column, (rows, head_ref.shape[2]))
+    pack_ref[:, cols:] = jnp.zeros((pack_ref.shape[0], pack_ref.shape[1] - cols), jnp.int16)
+
+    @pl.when(step == pl.num_programs(0) - 1)
+    def _():
+        place = lax.broadcasted_iota(jnp.int32, (pack_ref.shape[0], head_ref.shape[1]), 0)
+        first, second = head_ref[0].T[:1], head_ref[1].T[:1]
+        last = pack_ref.shape[0] - 1
+        head = jnp.where(place == last - 1, first, jnp.where(place == last, second, 0.0))
+        pack_ref[:, cols:] = whole_number(head)
 
 
 def prepare(momentum, grad, basis, share):
     rows, cols = momentum.shape
     width = share if share % 128 == 0 else cols
+    steps = 2 if basis.shape[0] % 32 == 0 else 1
+    wide = pl.BlockSpec((rows // steps, cols), lambda i: (i, 0))
+    ranks = basis.shape[0] // steps
     return pl.pallas_call(
         prepare_kernel,
+        grid=(steps,),
+        in_specs=[wide, wide, pl.BlockSpec((ranks, cols), lambda i: (i, 0))],
+        out_specs=[
+            pl.BlockSpec((ranks, cols + rows), lambda i: (i, 0)),
+            pl.BlockSpec((cols // width, rows // steps, width), lambda i: (0, i, 0)),
+        ],
         out_shape=[
             jax.ShapeDtypeStruct((basis.shape[0], cols + rows), jnp.int16),
             jax.ShapeDtypeStruct((cols // width, rows, width), jnp.int16),
         ],
+        scratch_shapes=[pltpu.VMEM((2, rows, 128), jnp.float32)],
         compiler_params=STREAM,
         cost_estimate=pl.CostEstimate(flops=10 * rows * cols, bytes_accessed=rows * cols * 8, transcendentals=0),
     )(momentum, grad, basis)
@@ -113,9 +133,9 @@
 
 def project_kernel(momentum_ref, grad_ref, code_ref, out_ref):
     code = code_ref[...].astype(jnp.int32)
-    size = jnp.abs(code)
-    value = ((size & 127) + 128).astype(jnp.float32) * jnp.exp2(((size >> 7) - 134).astype(jnp.float32))
-    basis = jnp.where(code == 0, 0.0, jnp.where(code < 0, -value, value)).astype(jnp.bfloat16)
+    power = jnp.exp2(((code >> 7) & 255).astype(jnp.float32) - 134.0)
+    value = ((code & 127) | 128).astype(jnp.float32) * power
+    basis = jnp.where(code < 0, -value, value).astype(jnp.bfloat16)
     combined = momentum_ref[...] + grad_ref[...].astype(jnp.float32)
     rows = combined.shape[0]
     part = lax.dot_general(
@@ -163,14 +183,18 @@
     for s in range(blocks):
         target = jnp.where(stored // size == s, perm_ref[s] * size + stored % size, target)
     order = (target == lax.broadcasted_iota(jnp.int32, (rank, rank), 1)).astype(jnp.float32)
-    total = functools.reduce(jnp.add, [ref[...] for ref in part_refs])
-    total = jnp.dot(total, order, precision=HIGH, preferred_element_type=jnp.float32)
+    parts = [ref[...] for ref in part_refs]
+    while len(parts) > 1:
+        parts = [parts[k] + parts[k + 1] for k in range(0, len(parts), 2)]
+    total = jnp.dot(parts[0], order, precision=HIGH, preferred_element_type=jnp.float32)
     exponent, mantissa = code_unit(jnp.max(jnp.abs(total), axis=0, keepdims=True))
     value = total * (1.0 / unit_of(exponent, mantissa))
     high = jnp.floor(value + 0.5)
     out_ref[:rows] = whole_number(high)
-    out_ref[rows : 2 * rows] = whole_number(jnp.floor((value - high) * 32768.0 + 0.5))
-    set_head(out_ref.at[2 * rows :], exponent, mantissa)
+    low = jnp.minimum(jnp.floor((value - high) * 256.0 + 0.5), 127.0)
+    half = rows // 2
+    out_ref[rows : rows + half] = whole_number(low[:half] * 256.0 + (low[half:] + 128.0))
+    set_head(out_ref.at[rows + half :], exponent, mantissa)
 
 
 def pack(perm, parts):
@@ -181,12 +205,17 @@
             num_scalar_prefetch=1,
             grid=(1,),
             in_specs=[whole(x) for x in parts],
-            out_specs=pl.BlockSpec((2 * rows + HEAD, rank), lambda *_: (0, 0)),
+            out_specs=pl.BlockSpec((rows + rows // 2 + HEAD, rank), lambda *_: (0, 0)),
         ),
-        out_shape=jax.ShapeDtypeStruct((2 * rows + HEAD, rank), jnp.int16),
+        out_shape=jax.ShapeDtypeStruct((rows + rows // 2 + HEAD, rank), jnp.int16),
         compiler_params=PARAMS,
         cost_estimate=pl.CostEstimate(flops=12 * rows * rank * rank, bytes_accessed=rank * rank * 4, transcendentals=0),
     )(perm, *parts)
+
+
+def reciprocal(x):
+    guess = pl.reciprocal(x, approx=True)
+    return guess * (2.0 - x * guess)
 
 
 def spread(row):
@@ -214,9 +243,9 @@
             first, second = sub == j, sub == j + 1
             a, b, c = row(j, j), row(j + 1, j), row(j + 1, j + 1)
             minor = a * c - b * b
-            inverse = 1.0 / minor
+            inverse = reciprocal(minor)
             left, right = state[j], state[j + 1]
-            ratio = 1.0 / a
+            ratio = reciprocal(a)
             below = (state[TILE] - b * ratio * row(TILE, j)) * lax.rsqrt(minor * ratio)
             final = jnp.where(first, state[TILE] * lax.rsqrt(a), jnp.where(second, below, final))
             for m in range(j + 2, TILE + 1):
@@ -270,10 +299,12 @@
 
 def factor_kernel(code_ref, turned_ref, out_ref, gram_ref, work, band):
     count, size, rank = code_ref.shape
-    size = (size - HEAD) // 2
-    code = code_ref[...].astype(jnp.int32).astype(jnp.float32)
-    unit = unit_of(code[:, 2 * size : 2 * size + 1], code[:, 2 * size + 1 : 2 * size + 2])
-    part = (code[:, :size] + code[:, size : 2 * size] * (1.0 / 32768.0)) * unit
+    size = (size - HEAD) * 2 // 3
+    code = code_ref[...].astype(jnp.int32)
+    low = code[:, size : size + size // 2]
+    low = jnp.concatenate([low >> 8, (low & 255) - 128], axis=1).astype(jnp.float32)
+    head = code[:, size + size // 2 :].astype(jnp.float32)
+    part = (code[:, :size].astype(jnp.float32) + low * (1.0 / 256.0)) * unit_of(head[:, :1], head[:, 1:2])
     turned = part.reshape(count * size, rank).T
     turned_ref[...] = turned
     gram = dot_rows(turned, turned)
@@ -293,7 +324,7 @@
 
 def factor(codes):
     devices, size, rank = codes.shape
-    rows = (size - HEAD) // 2
+    rows = (size - HEAD) * 2 // 3
     group = 256 // rows
     return pl.pallas_call(
         factor_kernel,
@@ -479,15 +510,15 @@
     basis = lax.all_gather(basis, "fsdp", axis=0, tiled=True)
     codes, basis = lax.optimization_barrier((codes, basis))
     codes = lax.all_to_all(codes, "fsdp", split_axis=0, concat_axis=0).reshape(row_total, share)
-    head = basis.reshape(num_blocks, block_rows, cols + rows)[:, :2, cols:].astype(jnp.float32)
+    head = basis.reshape(num_blocks, block_rows, cols + rows)[:, -2:, cols:].astype(jnp.float32)
     unit = unit_of(head[:, 0], head[:, 1]).reshape(1, row_total)
 
-    near = project(momentum, grad, basis)
-    step = 1
-    while 2 * step < num_cols:
+    near, step = project(momentum, grad, basis), 1
+    while 4 * step < num_cols:
         near = near + exchange(near, "tp", step)
         step *= 2
-    packed = lax.all_gather(pack(perm, [near, exchange(near, "tp", step)]), "fsdp", axis=0)
+    parts = [near] + [exchange(near, "tp", k) for k in range(step, num_cols, step)]
+    packed = lax.all_gather(pack(perm, parts), "fsdp", axis=0)
     packed, codes = lax.optimization_barrier((packed, codes))
     turned, inverse_low = factor(packed)
     code, orthonormal = encode(lax.axis_index("fsdp").reshape(1), codes, turned, unit, inverse_low, rows)

time: 123 us -> 121 us (0.984)
  waiting for transfers between devices: 8.18 us -> 5.91 us
    ppermute x5 -> x6, waiting for transfers between devices: 8.17 us -> 5.91 us  [exchange(): lax.ppermute(x, axis, [(i, i ^ k) for i in range(lax.axis_size(axis))])]
    pallas_call x1, Pallas kernels: 11.9 us -> 13.3 us  [factor(): pl.pallas_call(factor_kernel, grid=(devices // group,), in_specs=[pl.Bloc...]
    ppermute x5 -> x6, starting transfers between devices: 6.61 us -> 7.04 us  [exchange(): lax.ppermute(x, axis, [(i, i ^ k) for i in range(lax.axis_size(axis))])]
  transfers between devices with their start and end apart: 6 -> 7, of which waited for: 3 -> 2; matrix products, arithmetic and copies ran while one was open for 1% -> 1% of each run, Pallas kernels for 8% -> 8%
where the time goes in v10:
time: 121 us; the launch traced here: 120 us
  blocking collectives  69.2 us (57%)
  Pallas kernels  32.1 us (27%)
  starting transfers between devices  10.7 us (9%)
  waiting for transfers between devices  5.91 us (5%)
  local copies, waits for them, and re-layouts  1.64 us (1%)
    all_gather x1, blocking collectives, on_device(): basis = lax.all_gather(basis, 'fsdp', axis=0, tiled=True)  26.4 us
    all_gather x1, blocking collectives, on_device(): gathered = lax.all_gather(code, 'fsdp', axis=0)  23.3 us
    all_gather x1, blocking collectives, on_device(): packed = lax.all_gather(pack(perm, parts), 'fsdp', axis=0)  19.4 us
    pallas_call x1, Pallas kernels, factor(): pl.pallas_call(factor_kernel, grid=(devices // group,), in_specs=[pl.Bloc...  13.3 us
    ppermute x6, starting transfers between devices, exchange(): lax.ppermute(x, axis, [(i, i ^ k) for i in range(lax.axis_size(axis))])  7.04 us
    ppermute x6, waiting for transfers between devices, exchange(): lax.ppermute(x, axis, [(i, i ^ k) for i in range(lax.axis_size(axis))])  5.91 us
    pallas_call x1, Pallas kernels, project(): pl.pallas_call(project_kernel, grid=(cols // block,), in_specs=[wide, wid...  5.5 us
    all_to_all x1, starting transfers between devices, on_device(): lax.all_to_all(codes, 'fsdp', split_axis=0, concat_axis=0)  3.69 us
  transfers between devices with their start and end apart: 7, of which 2 were waited for; matrix products, arithmetic and copies ran while one was open for 1% of the time, Pallas kernels for 8%

profile of v10, /device:TPU:0, one launch (start us, length us, event | category | flops | bytes accessed | tf_op | source)
XLA Modules:
  0.0 120.3 jit_solution(4252918800591877347)
XLA Ops:
  0.6 3.5 %shard_map.67 = (s16[32,4224]{1,0:T(8,128)(2,1)}, s16[8,128,512]{2,1,0:T(8,128)(2,1)}) custom-call(f32[128,4096]{1,0:T(8,128)} %momentum_ref.5, bf16[128,4096]{1,0:T(8,128)(2,1)} %grad_ref.5, bf16[32,4096]{1,0:T(8,128)(2,1)} %basis_ref.1), custom_call_target="tpu_custom_call" | custom-call | flops 5242880 | bytes 4194304 | tf_op jit(solution)/shard_map/pallas_call | solution.py:116
  4.2 26.4 %all-gather.4.code_ref = s16[256,4224]{1,0:T(8,128)(2,1)} all-gather(s16[32,4224]{1,0:T(8,128)(2,1)} %get-tuple-element.16), channel_id=1, replica_groups=mesh['fsdp'=8,'tp'=4] {'fsdp'}, dimensions={0}, use_global_device_ids=true | all-gather | bytes 2433024 | tf_op jit(solution)/shard_map/all_gather | solution.py:510
  30.6 3.7 %all-to-all-start = ((s16[8,128,512]{2,1,0:T(8,128)(2,1)}), s16[8,128,512]{2,1,0:T(8,128)(2,1)S(1)}, u32[]{:S(2)}, u32[]{:S(2)}) async-start(s16[8,128,512]{2,1,0:T(8,128)(2,1)} %get-tuple-element.18), calls=%async_computation | async-start | bytes 2097152 | tf_op jit(solution)/shard_map/all_to_all | solution.py:512
  34.3 0.0 copy-start.3
  34.3 5.5 %shard_map.68.refs_0_ = f32[128,256]{1,0:T(8,128)} custom-call(f32[128,4096]{1,0:T(8,128)} %momentum_ref.5, bf16[128,4096]{1,0:T(8,128)(2,1)} %grad_ref.5, s16[256,4224]{1,0:T(8,128)(2,1)} %all-gather.4.code_ref), custom_call_target="tpu_custom_call" | custom-call | flops 536870912 | bytes 5242880 | tf_op jit(solution)/shard_map/pallas_call | solution.py:163
  39.8 1.5 %collective-permute-start = (f32[128,256]{1,0:T(8,128)}, f32[128,256]{1,0:T(8,128)S(1)}, u32[]{:S(2)}, u32[]{:S(2)}) collective-permute-start(f32[128,256]{1,0:T(8,128)} %shard_map.68.refs_0_), channel_id=1, source_target_pairs={{0,1},{1,0},{2,3},{3,2},{4,5},{5,4},{6,7},{7,6},{8,9},{9,8},{10,11... | collective-permute-start | bytes 393224 | tf_op jit(solution)/shard_map/ppermute | solution.py:28
  41.3 1.5 %collective-permute-start.1 = (f32[128,256]{1,0:T(8,128)}, f32[128,256]{1,0:T(8,128)S(1)}, u32[]{:S(2)}, u32[]{:S(2)}) collective-permute-start(f32[128,256]{1,0:T(8,128)} %shard_map.68.refs_0_), channel_id=1, source_target_pairs={{0,2},{1,3},{2,0},{3,1},{4,6},{5,7},{6,4},{7,5},{8,10},{9,11},{10,... | collective-permute-start | bytes 393224 | tf_op jit(solution)/shard_map/ppermute | solution.py:28
  42.8 0.5 collective-permute-start.2
  43.3 0.7 slice.28
  44.0 2.3 %collective-permute-done.refs_1_ = f32[128,256]{1,0:T(8,128)S(1)} collective-permute-done((f32[128,256]{1,0:T(8,128)}, f32[128,256]{1,0:T(8,128)S(1)}, u32[]{:S(2)}, u32[]{:S(2)}) %collective-permute-start) | collective-permute-done | bytes 131104 | tf_op jit(solution)/shard_map/ppermute | solution.py:28
  46.3 3.6 %collective-permute-done.1.refs_2_ = f32[128,256]{1,0:T(8,128)S(1)} collective-permute-done((f32[128,256]{1,0:T(8,128)}, f32[128,256]{1,0:T(8,128)S(1)}, u32[]{:S(2)}, u32[]{:S(2)}) %collective-permute-start.1) | collective-permute-done | bytes 131104 | tf_op jit(solution)/shard_map/ppermute | solution.py:28
  49.9 0.0 collective-permute-done.2.refs_3_
  49.9 0.0 copy-done.3
  49.9 0.0 copy-start.2
  49.9 0.9 copy-done.2
  50.8 0.9 shard_map.69
  51.8 19.4 %all-gather = s16[1664,256]{1,0:T(8,128)(2,1)S(1)} all-gather(s16[208,256]{1,0:T(8,128)(2,1)S(1)} %shard_map.69), channel_id=2, replica_groups=mesh['fsdp'=8,'tp'=4] {'fsdp'}, dimensions={0}, use_global_device_ids=true | all-gather | bytes 958464 | tf_op jit(solution)/shard_map/all_gather | solution.py:521
  71.2 0.0 all-to-all-done
  71.2 13.3 %shard_map.70 = (f32[256,1024]{1,0:T(8,128)S(1)}, f32[256,256]{1,0:T(8,128)S(1)}) custom-call(s16[8,208,256]{2,1,0:T(8,128)(2,1)S(1)} %bitcast.11), custom_call_target="tpu_custom_call" | custom-call | flops 805306368 | bytes 1703936 | tf_op jit(solution)/shard_map/pallas_call | solution.py:329
  84.5 0.0 copy-start
  84.5 0.0 copy-start.1
  84.5 2.5 %shard_map.71 = (s16[528,256]{1,0:T(8,128)(2,1)S(1)}, f32[128,256]{1,0:T(8,128)S(1)}) custom-call(s32[1]{0:T(128)} %bitcast.place_ref, s16[1024,512]{1,0:T(8,128)(2,1)S(1)} %bitcast.10, f32[256,1024]{1,0:T(8,128)S(1)} %get-tuple-element.21.turned_ref.own_ref, f32[1,1024]{1,0:T(1,128)S(1)} %bitcast.12, f32[256,256]{1,0:T(8,128)S(1)} %get-tuple-element.22.inverse_ref, ...), custom_call_target="tpu_custom_call" | custom-call | flops 805306368 | bytes 2097152 | tf_op jit(solution)/shard_map/pallas_call | solution.py:392
  87.0 23.3 %all-gather.5 = s16[4224,256]{1,0:T(8,128)(2,1)S(1)} all-gather(s16[528,256]{1,0:T(8,128)(2,1)S(1)} %get-tuple-element.23), channel_id=3, replica_groups=mesh['fsdp'=8,'tp'=4] {'fsdp'}, dimensions={0}, use_global_device_ids=true | all-gather | bytes 2433024 | tf_op jit(solution)/shard_map/all_gather | solution.py:525
  110.3 0.1 fusion.4
  110.4 1.2 collective-permute-start.3
  111.5 1.2 collective-permute-start.4
  112.7 1.2 %collective-permute-start.5 = (f32[1,256]{1,0:T(1,128)S(1)}, f32[1,256]{1,0:T(1,128)S(1)}, u32[]{:S(2)}, u32[]{:S(2)}) collective-permute-start(f32[1,256]{1,0:T(1,128)S(1)} %bitcast.16), channel_id=1, source_target_pairs={{0,3},{1,2},{2,1},{3,0},{4,7},{5,6},{6,5},{7,4},{8,11},{9,10},{10,... | collective-permute-start | bytes 3080 | tf_op jit(solution)/shard_map/ppermute | solution.py:28
  113.9 0.0 copy-done
  113.9 0.0 copy-done.1
  113.9 3.3 %shard_map.72 = f32[128,4096]{1,0:T(8,128)} custom-call(f32[128,4096]{1,0:T(8,128)S(1)} %copy-done, bf16[128,4096]{1,0:T(8,128)(2,1)S(1)} %copy-done.1, s16[8,528,256]{2,1,0:T(8,128)(2,1)S(1)} %bitcast.8, f32[128,256]{1,0:T(8,128)S(1)} %get-tuple-element.24.ortho_ref), custom_call_target="tpu_custom_call" | custom-call | flops 805306368 | bytes 7340032 | tf_op jit(solution)/shard_map/pallas_call | solution.py:471
  117.2 0.0 collective-permute-done.3
  117.2 0.0 collective-permute-done.4
  117.2 0.0 collective-permute-done.5
  117.3 3.1 %shard_map.73 = (f32[4096,256]{1,0:T(8,128)}, bf16[128,4096]{1,0:T(8,128)(2,1)}) custom-call(s16[8,528,256]{2,1,0:T(8,128)(2,1)S(1)} %bitcast.9, f32[128,256]{1,0:T(8,128)S(1)} %get-tuple-element.24.ortho_ref, f32[1,256]{1,0:T(1,128)S(1)} %add_rsqrt_fusion.scale_ref), custom_call_target="tpu_custom_call" | custom-call | flops 805306368 | bytes 7340032 | tf_op jit(solution)/shard_map/pallas_call | solution.py:483
  (4 shorter events, 0.0 us)
Async XLA Ops:
  30.6 40.6 %all-to-all-start = ((s16[8,128,512]{2,1,0:T(8,128)(2,1)}), s16[8,128,512]{2,1,0:T(8,128)(2,1)S(1)}, u32[]{:S(2)}, u32[]{:S(2)}) async-start(s16[8,128,512]{2,1,0:T(8,128)(2,1)} %get-tuple-element.18), calls=%async_computation | async-start | bytes 2097152 | tf_op jit(solution)/shard_map/all_to_all | solution.py:512
  34.3 15.6 %copy-start.3 = (s32[8]{0:T(128)S(1)}, s32[8]{0:T(128)}, u32[]{:S(2)}) copy-start(s32[8]{0:T(128)} %perm_ref.1) | copy-start | bytes 100
  39.8 6.5 %collective-permute-start = (f32[128,256]{1,0:T(8,128)}, f32[128,256]{1,0:T(8,128)S(1)}, u32[]{:S(2)}, u32[]{:S(2)}) collective-permute-start(f32[128,256]{1,0:T(8,128)} %shard_map.68.refs_0_), channel_id=1, source_target_pairs={{0,1},{1,0},{2,3},{3,2},{4,5},{5,4},{6,7},{7,6},{8,9},{9,8},{10,11... | collective-permute-start | bytes 393224 | tf_op jit(solution)/shard_map/ppermute | solution.py:28
  41.3 8.6 %collective-permute-start.1 = (f32[128,256]{1,0:T(8,128)}, f32[128,256]{1,0:T(8,128)S(1)}, u32[]{:S(2)}, u32[]{:S(2)}) collective-permute-start(f32[128,256]{1,0:T(8,128)} %shard_map.68.refs_0_), channel_id=1, source_target_pairs={{0,2},{1,3},{2,0},{3,1},{4,6},{5,7},{6,4},{7,5},{8,10},{9,11},{10,... | collective-permute-start | bytes 393224 | tf_op jit(solution)/shard_map/ppermute | solution.py:28
  42.8 7.1 %collective-permute-start.2 = (f32[128,256]{1,0:T(8,128)}, f32[128,256]{1,0:T(8,128)S(1)}, u32[]{:S(2)}, u32[]{:S(2)}) collective-permute-start(f32[128,256]{1,0:T(8,128)} %shard_map.68.refs_0_), channel_id=1, source_target_pairs={{0,3},{1,2},{2,1},{3,0},{4,7},{5,6},{6,5},{7,4},{8,11},{9,10},{10,... | collective-permute-start | bytes 393224 | tf_op jit(solution)/shard_map/ppermute | solution.py:28
  49.9 0.9 copy-start.2
  84.5 29.4 %copy-start = (f32[128,4096]{1,0:T(8,128)S(1)}, f32[128,4096]{1,0:T(8,128)}, u32[]{:S(2)}) copy-start(f32[128,4096]{1,0:T(8,128)} %momentum_ref.5) | copy-start | bytes 6291460
  84.5 29.4 %copy-start.1 = (bf16[128,4096]{1,0:T(8,128)(2,1)S(1)}, bf16[128,4096]{1,0:T(8,128)(2,1)}, u32[]{:S(2)}) copy-start(bf16[128,4096]{1,0:T(8,128)(2,1)} %grad_ref.5) | copy-start | bytes 3145732
  110.4 6.9 %collective-permute-start.3 = (f32[1,256]{1,0:T(1,128)S(1)}, f32[1,256]{1,0:T(1,128)S(1)}, u32[]{:S(2)}, u32[]{:S(2)}) collective-permute-start(f32[1,256]{1,0:T(1,128)S(1)} %bitcast.14), channel_id=1, source_target_pairs={{0,1},{1,0},{2,3},{3,2},{4,5},{5,4},{6,7},{7,6},{8,9},{9,8},{10,11... | collective-permute-start | bytes 3080 | tf_op jit(solution)/shard_map/ppermute | solution.py:28
  111.5 5.7 %collective-permute-start.4 = (f32[1,256]{1,0:T(1,128)S(1)}, f32[1,256]{1,0:T(1,128)S(1)}, u32[]{:S(2)}, u32[]{:S(2)}) collective-permute-start(f32[1,256]{1,0:T(1,128)S(1)} %bitcast.15), channel_id=1, source_target_pairs={{0,2},{1,3},{2,0},{3,1},{4,6},{5,7},{6,4},{7,5},{8,10},{9,11},{10,... | collective-permute-start | bytes 3080 | tf_op jit(solution)/shard_map/ppermute | solution.py:28
  112.7 4.5 %collective-permute-start.5 = (f32[1,256]{1,0:T(1,128)S(1)}, f32[1,256]{1,0:T(1,128)S(1)}, u32[]{:S(2)}, u32[]{:S(2)}) collective-permute-start(f32[1,256]{1,0:T(1,128)S(1)} %bitcast.16), channel_id=1, source_target_pairs={{0,3},{1,2},{2,1},{3,0},{4,7},{5,6},{6,5},{7,4},{8,11},{9,10},{10,... | collective-permute-start | bytes 3080 | tf_op jit(solution)/shard_map/ppermute | solution.py:28

commit v11 on v10

--- a/solution.py
+++ b/solution.py
@@ -16,6 +16,7 @@
 HEAD = 16
 TOP = 32766.0
 PARAMS = pltpu.CompilerParams(vmem_limit_bytes=40 * 1024 * 1024)
+FLOW = pltpu.CompilerParams(vmem_limit_bytes=53 * 1024 * 1024)
 STREAM = pltpu.CompilerParams(vmem_limit_bytes=54 * 1024 * 1024)
 
 
@@ -166,7 +167,7 @@
         in_specs=[wide, wide, pl.BlockSpec((rank, block), lambda i: (0, i))],
         out_specs=pl.BlockSpec((rows, rank), lambda i: (0, 0)),
         out_shape=jax.ShapeDtypeStruct((rows, rank), jnp.float32),
-        compiler_params=STREAM,
+        compiler_params=FLOW,
         cost_estimate=pl.CostEstimate(
             flops=4 * rows * cols * rank, bytes_accessed=rows * cols * 6 + rank * cols * 2, transcendentals=rank * cols
         ),
@@ -213,11 +214,6 @@
     )(perm, *parts)
 
 
-def reciprocal(x):
-    guess = pl.reciprocal(x, approx=True)
-    return guess * (2.0 - x * guess)
-
-
 def spread(row):
     return jnp.broadcast_to(row, (TILE, 2 * PANEL))
 
@@ -243,26 +239,43 @@
             first, second = sub == j, sub == j + 1
             a, b, c = row(j, j), row(j + 1, j), row(j + 1, j + 1)
             minor = a * c - b * b
-            inverse = reciprocal(minor)
-            left, right = state[j], state[j + 1]
-            ratio = reciprocal(a)
-            below = (state[TILE] - b * ratio * row(TILE, j)) * lax.rsqrt(minor * ratio)
-            final = jnp.where(first, state[TILE] * lax.rsqrt(a), jnp.where(second, below, final))
+            inverse = 1.0 / minor
+            left, right, body = state[j], state[j + 1], state[TILE]
+            ratio = 1.0 / a
+            below = (body - b * ratio * row(TILE, j)) * lax.rsqrt(minor * ratio)
+            final = jnp.where(first, body * lax.rsqrt(a), jnp.where(second, below, final))
+            rests = {}
             for m in range(j + 2, TILE + 1):
                 upper, lower = row(m, j), row(m, j + 1)
-                upper, lower = (c * upper - b * lower) * inverse, (a * lower - b * upper) * inverse
-                rest = state[m] - left * upper - right * lower
-                state[m] = jnp.where(first, upper, jnp.where(second, lower, rest))
-            for m in range(j + 2, TILE + 1):
-                band[m] = state[m]
+                upper, lower = c * upper - b * lower, a * lower - b * upper
+                rests[m] = state[m] - (left * upper + right * lower) * inverse
+                state[m] = jnp.where(first, upper * inverse, jnp.where(second, lower * inverse, rests[m]))
+            for m, rest in rests.items():
+                band[m] = rest
         done.append(final)
+        band[TILE] = state[TILE]
         reduced = [row(TILE, j) for j in range(TILE)]
         for i in range(k + 1, count):
-            tile = tiles[i]
-            for j in range(TILE):
-                tile = tile - columns[i - k][j] * reduced[j]
-            tiles[i] = tile
+            terms = [columns[i - k][j] * reduced[j] for j in range(TILE)]
+            while len(terms) > 1:
+                terms = [terms[j] + terms[j + 1] for j in range(0, len(terms), 2)]
+            tiles[i] = tiles[i] - terms[0]
     return jnp.concatenate(done, axis=0)[:, PANEL:]
+
+
+def split_three(x):
+    high, rest = x.astype(jnp.bfloat16), x
+    rest = rest - high.astype(jnp.float32)
+    middle = rest.astype(jnp.bfloat16)
+    return high, middle, (rest - middle.astype(jnp.float32)).astype(jnp.bfloat16)
+
+
+def short_dot(a, b):
+    a1, a2, a3 = split_three(a)
+    b1, b2, b3 = split_three(b)
+    a = jnp.concatenate([a1, a1, a2, a2, a1, a3], axis=1)
+    b = jnp.concatenate([b1, b2, b1, b2, b3, b1], axis=0)
+    return jnp.dot(a, b, preferred_element_type=jnp.float32)
 
 
 def lanes_up(x):
@@ -281,19 +294,13 @@
         end = start + PANEL
         left, right = start // 128 * 128, rank + lanes_up(end)
         inverse = panel_inverse(work[start:end, start:end], band)
-        scaled = jnp.dot(inverse, work[start:end, left:right], precision=HIGH, preferred_element_type=jnp.float32)
+        scaled = short_dot(inverse, work[start:end, left:right])
         out_ref[start:end, : lanes_up(end)] = scaled[:, rank - left :] * scale[:, : lanes_up(end)]
         if lanes_up(end) < rank:
             out_ref[start:end, lanes_up(end) :] = jnp.zeros((PANEL, rank - lanes_up(end)), jnp.float32)
         if end < rank:
             low = end // 128 * 128
-            change = lax.dot_general(
-                scaled[:, low - left : rank - left],
-                scaled[:, low - left :],
-                (((0,), (0,)), ((), ())),
-                precision=HIGH,
-                preferred_element_type=jnp.float32,
-            )
+            change = short_dot(scaled[:, low - left : rank - left].T, scaled[:, low - left :])
             work[end:, low:right] = work[end:, low:right] - change[end - low :, :]
 
 

time: 121 us -> 119 us (0.983)
  Pallas kernels: 32.1 us -> 29.6 us
    pallas_call x1, Pallas kernels: 13.3 us -> 11.4 us  [factor(): pl.pallas_call(factor_kernel, grid=(devices // group,), in_specs=[pl.Bloc...]
  transfers between devices with their start and end apart: 7 -> 7, of which waited for: 2 -> 3; matrix products, arithmetic and copies ran while one was open for 1% -> 1% of each run, Pallas kernels for 8% -> 8%
where the time goes in v11:
time: 119 us
  blocking collectives  70.2 us (59%)
  Pallas kernels  29.6 us (25%)
  starting transfers between devices  10.8 us (9%)
  waiting for transfers between devices  6.42 us (5%)
    all_gather x1, blocking collectives, on_device(): basis = lax.all_gather(basis, 'fsdp', axis=0, tiled=True)  26.4 us
    all_gather x1, blocking collectives, on_device(): gathered = lax.all_gather(code, 'fsdp', axis=0)  23.4 us
    all_gather x1, blocking collectives, on_device(): packed = lax.all_gather(pack(perm, parts), 'fsdp', axis=0)  20.4 us
    pallas_call x1, Pallas kernels, factor(): pl.pallas_call(factor_kernel, grid=(devices // group,), in_specs=[pl.Bloc...  11.4 us
    ppermute x6, starting transfers between devices, exchange(): lax.ppermute(x, axis, [(i, i ^ k) for i in range(lax.axis_size(axis))])  7.1 us
    ppermute x6, waiting for transfers between devices, exchange(): lax.ppermute(x, axis, [(i, i ^ k) for i in range(lax.axis_size(axis))])  6.42 us
    pallas_call x1, Pallas kernels, project(): pl.pallas_call(project_kernel, grid=(cols // block,), in_specs=[wide, wid...  4.86 us
    all_to_all x1, starting transfers between devices, on_device(): lax.all_to_all(codes, 'fsdp', split_axis=0, concat_axis=0)  3.69 us
  transfers between devices with their start and end apart: 7, of which 3 were waited for; matrix products, arithmetic and copies ran while one was open for 1% of the time, Pallas kernels for 8%

profile of v11, /device:TPU:0, one launch (start us, length us, event | category | flops | bytes accessed | tf_op | source)
XLA Modules:
  0.0 118.6 jit_solution(12338758774158434332)
XLA Ops:
  0.6 3.5 %shard_map.67 = (s16[32,4224]{1,0:T(8,128)(2,1)}, s16[8,128,512]{2,1,0:T(8,128)(2,1)}) custom-call(f32[128,4096]{1,0:T(8,128)} %momentum_ref.5, bf16[128,4096]{1,0:T(8,128)(2,1)} %grad_ref.5, bf16[32,4096]{1,0:T(8,128)(2,1)} %basis_ref.1), custom_call_target="tpu_custom_call" | custom-call | flops 5242880 | bytes 4194304 | tf_op jit(solution)/shard_map/pallas_call | solution.py:117
  4.2 26.4 %all-gather.4.code_ref = s16[256,4224]{1,0:T(8,128)(2,1)} all-gather(s16[32,4224]{1,0:T(8,128)(2,1)} %get-tuple-element.16), channel_id=1, replica_groups=mesh['fsdp'=8,'tp'=4] {'fsdp'}, dimensions={0}, use_global_device_ids=true | all-gather | bytes 2433024 | tf_op jit(solution)/shard_map/all_gather | solution.py:517
  30.6 3.7 %all-to-all-start = ((s16[8,128,512]{2,1,0:T(8,128)(2,1)}), s16[8,128,512]{2,1,0:T(8,128)(2,1)S(1)}, u32[]{:S(2)}, u32[]{:S(2)}) async-start(s16[8,128,512]{2,1,0:T(8,128)(2,1)} %get-tuple-element.18), calls=%async_computation | async-start | bytes 2097152 | tf_op jit(solution)/shard_map/all_to_all | solution.py:519
  34.3 0.0 copy-start.2
  34.3 4.9 %shard_map.68.refs_0_ = f32[128,256]{1,0:T(8,128)S(1)} custom-call(f32[128,4096]{1,0:T(8,128)} %momentum_ref.5, bf16[128,4096]{1,0:T(8,128)(2,1)} %grad_ref.5, s16[256,4224]{1,0:T(8,128)(2,1)} %all-gather.4.code_ref), custom_call_target="tpu_custom_call" | custom-call | flops 536870912 | bytes 5242880 | tf_op jit(solution)/shard_map/pallas_call | solution.py:164
  39.2 1.6 %collective-permute-start = (f32[128,256]{1,0:T(8,128)S(1)}, f32[128,256]{1,0:T(8,128)S(1)}, u32[]{:S(2)}, u32[]{:S(2)}) collective-permute-start(f32[128,256]{1,0:T(8,128)S(1)} %shard_map.68.refs_0_), channel_id=1, source_target_pairs={{0,1},{1,0},{2,3},{3,2},{4,5},{5,4},{6,7},{7,6},{8,9},{9,8},{10,11... | collective-permute-start | bytes 393224 | tf_op jit(solution)/shard_map/ppermute | solution.py:29
  40.7 1.5 %collective-permute-start.1 = (f32[128,256]{1,0:T(8,128)S(1)}, f32[128,256]{1,0:T(8,128)S(1)}, u32[]{:S(2)}, u32[]{:S(2)}) collective-permute-start(f32[128,256]{1,0:T(8,128)S(1)} %shard_map.68.refs_0_), channel_id=1, source_target_pairs={{0,2},{1,3},{2,0},{3,1},{4,6},{5,7},{6,4},{7,5},{8,10},{9,11},{10,... | collective-permute-start | bytes 393224 | tf_op jit(solution)/shard_map/ppermute | solution.py:29
  42.2 0.5 collective-permute-start.2
  42.7 0.7 slice.28
  43.5 2.1 %collective-permute-done.refs_1_ = f32[128,256]{1,0:T(8,128)S(1)} collective-permute-done((f32[128,256]{1,0:T(8,128)S(1)}, f32[128,256]{1,0:T(8,128)S(1)}, u32[]{:S(2)}, u32[]{:S(2)}) %collective-permute-start) | collective-permute-done | bytes 131104 | tf_op jit(solution)/shard_map/ppermute | solution.py:29
  45.5 3.6 %collective-permute-done.1.refs_2_ = f32[128,256]{1,0:T(8,128)S(1)} collective-permute-done((f32[128,256]{1,0:T(8,128)S(1)}, f32[128,256]{1,0:T(8,128)S(1)}, u32[]{:S(2)}, u32[]{:S(2)}) %collective-permute-start.1) | collective-permute-done | bytes 131104 | tf_op jit(solution)/shard_map/ppermute | solution.py:29
  49.1 0.0 collective-permute-done.2.refs_3_
  49.2 0.0 copy-done.2
  49.2 0.9 shard_map.69
  50.1 20.4 %all-gather = s16[1664,256]{1,0:T(8,128)(2,1)S(1)} all-gather(s16[208,256]{1,0:T(8,128)(2,1)S(1)} %shard_map.69), channel_id=2, replica_groups=mesh['fsdp'=8,'tp'=4] {'fsdp'}, dimensions={0}, use_global_device_ids=true | all-gather | bytes 958464 | tf_op jit(solution)/shard_map/all_gather | solution.py:528
  70.5 0.0 all-to-all-done
  70.5 11.4 %shard_map.70 = (f32[256,1024]{1,0:T(8,128)S(1)}, f32[256,256]{1,0:T(8,128)S(1)}) custom-call(s16[8,208,256]{2,1,0:T(8,128)(2,1)S(1)} %bitcast.11), custom_call_target="tpu_custom_call" | custom-call | flops 805306368 | bytes 1703936 | tf_op jit(solution)/shard_map/pallas_call | solution.py:336
  81.9 0.0 copy-start
  81.9 0.0 copy-start.1
  81.9 2.5 %shard_map.71 = (s16[528,256]{1,0:T(8,128)(2,1)S(1)}, f32[128,256]{1,0:T(8,128)S(1)}) custom-call(s32[1]{0:T(128)} %bitcast.place_ref, s16[1024,512]{1,0:T(8,128)(2,1)S(1)} %bitcast.10, f32[256,1024]{1,0:T(8,128)S(1)} %get-tuple-element.21.turned_ref.own_ref, f32[1,1024]{1,0:T(1,128)S(1)} %bitcast.12, f32[256,256]{1,0:T(8,128)S(1)} %get-tuple-element.22.inverse_ref, ...), custom_call_target="tpu_custom_call" | custom-call | flops 805306368 | bytes 2097152 | tf_op jit(solution)/shard_map/pallas_call | solution.py:399
  84.4 23.4 %all-gather.5 = s16[4224,256]{1,0:T(8,128)(2,1)S(1)} all-gather(s16[528,256]{1,0:T(8,128)(2,1)S(1)} %get-tuple-element.23), channel_id=3, replica_groups=mesh['fsdp'=8,'tp'=4] {'fsdp'}, dimensions={0}, use_global_device_ids=true | all-gather | bytes 2433024 | tf_op jit(solution)/shard_map/all_gather | solution.py:532
  107.9 0.1 fusion.4
  107.9 1.6 %collective-permute-start.3 = (f32[1,256]{1,0:T(1,128)S(1)}, f32[1,256]{1,0:T(1,128)S(1)}, u32[]{:S(2)}, u32[]{:S(2)}) collective-permute-start(f32[1,256]{1,0:T(1,128)S(1)} %bitcast.14), channel_id=1, source_target_pairs={{0,1},{1,0},{2,3},{3,2},{4,5},{5,4},{6,7},{7,6},{8,9},{9,8},{10,11... | collective-permute-start | bytes 3080 | tf_op jit(solution)/shard_map/ppermute | solution.py:29
  109.5 1.5 %collective-permute-start.4 = (f32[1,256]{1,0:T(1,128)S(1)}, f32[1,256]{1,0:T(1,128)S(1)}, u32[]{:S(2)}, u32[]{:S(2)}) collective-permute-start(f32[1,256]{1,0:T(1,128)S(1)} %bitcast.15), channel_id=1, source_target_pairs={{0,2},{1,3},{2,0},{3,1},{4,6},{5,7},{6,4},{7,5},{8,10},{9,11},{10,... | collective-permute-start | bytes 3080 | tf_op jit(solution)/shard_map/ppermute | solution.py:29
  111.0 0.4 collective-permute-start.5
  111.5 0.0 copy-done
  111.5 0.0 copy-done.1
  111.5 3.3 %shard_map.72 = f32[128,4096]{1,0:T(8,128)} custom-call(f32[128,4096]{1,0:T(8,128)S(1)} %copy-done, bf16[128,4096]{1,0:T(8,128)(2,1)S(1)} %copy-done.1, s16[8,528,256]{2,1,0:T(8,128)(2,1)S(1)} %bitcast.8, f32[128,256]{1,0:T(8,128)S(1)} %get-tuple-element.24.ortho_ref), custom_call_target="tpu_custom_call" | custom-call | flops 805306368 | bytes 7340032 | tf_op jit(solution)/shard_map/pallas_call | solution.py:478
  114.8 0.0 collective-permute-done.3
  114.8 0.0 collective-permute-done.4
  114.8 0.7 collective-permute-done.5
  115.5 3.1 %shard_map.73 = (f32[4096,256]{1,0:T(8,128)}, bf16[128,4096]{1,0:T(8,128)(2,1)}) custom-call(s16[8,528,256]{2,1,0:T(8,128)(2,1)S(1)} %bitcast.9, f32[128,256]{1,0:T(8,128)S(1)} %get-tuple-element.24.ortho_ref, f32[1,256]{1,0:T(1,128)S(1)} %add_rsqrt_fusion.scale_ref), custom_call_target="tpu_custom_call" | custom-call | flops 805306368 | bytes 7340032 | tf_op jit(solution)/shard_map/pallas_call | solution.py:490
  (4 shorter events, 0.0 us)
Async XLA Ops:
  30.6 39.9 %all-to-all-start = ((s16[8,128,512]{2,1,0:T(8,128)(2,1)}), s16[8,128,512]{2,1,0:T(8,128)(2,1)S(1)}, u32[]{:S(2)}, u32[]{:S(2)}) async-start(s16[8,128,512]{2,1,0:T(8,128)(2,1)} %get-tuple-element.18), calls=%async_computation | async-start | bytes 2097152 | tf_op jit(solution)/shard_map/all_to_all | solution.py:519
  34.3 14.9 %copy-start.2 = (s32[8]{0:T(128)S(1)}, s32[8]{0:T(128)}, u32[]{:S(2)}) copy-start(s32[8]{0:T(128)} %perm_ref.1) | copy-start | bytes 100
  39.2 6.4 %collective-permute-start = (f32[128,256]{1,0:T(8,128)S(1)}, f32[128,256]{1,0:T(8,128)S(1)}, u32[]{:S(2)}, u32[]{:S(2)}) collective-permute-start(f32[128,256]{1,0:T(8,128)S(1)} %shard_map.68.refs_0_), channel_id=1, source_target_pairs={{0,1},{1,0},{2,3},{3,2},{4,5},{5,4},{6,7},{7,6},{8,9},{9,8},{10,11... | collective-permute-start | bytes 393224 | tf_op jit(solution)/shard_map/ppermute | solution.py:29
  40.7 8.4 %collective-permute-start.1 = (f32[128,256]{1,0:T(8,128)S(1)}, f32[128,256]{1,0:T(8,128)S(1)}, u32[]{:S(2)}, u32[]{:S(2)}) collective-permute-start(f32[128,256]{1,0:T(8,128)S(1)} %shard_map.68.refs_0_), channel_id=1, source_target_pairs={{0,2},{1,3},{2,0},{3,1},{4,6},{5,7},{6,4},{7,5},{8,10},{9,11},{10,... | collective-permute-start | bytes 393224 | tf_op jit(solution)/shard_map/ppermute | solution.py:29
  42.2 6.9 %collective-permute-start.2 = (f32[128,256]{1,0:T(8,128)S(1)}, f32[128,256]{1,0:T(8,128)S(1)}, u32[]{:S(2)}, u32[]{:S(2)}) collective-permute-start(f32[128,256]{1,0:T(8,128)S(1)} %shard_map.68.refs_0_), channel_id=1, source_target_pairs={{0,3},{1,2},{2,1},{3,0},{4,7},{5,6},{6,5},{7,4},{8,11},{9,10},{10,... | collective-permute-start | bytes 393224 | tf_op jit(solution)/shard_map/ppermute | solution.py:29
  81.9 29.6 %copy-start = (f32[128,4096]{1,0:T(8,128)S(1)}, f32[128,4096]{1,0:T(8,128)}, u32[]{:S(2)}) copy-start(f32[128,4096]{1,0:T(8,128)} %momentum_ref.5) | copy-start | bytes 6291460
  81.9 29.6 %copy-start.1 = (bf16[128,4096]{1,0:T(8,128)(2,1)S(1)}, bf16[128,4096]{1,0:T(8,128)(2,1)}, u32[]{:S(2)}) copy-start(bf16[128,4096]{1,0:T(8,128)(2,1)} %grad_ref.5) | copy-start | bytes 3145732
  107.9 6.9 %collective-permute-start.3 = (f32[1,256]{1,0:T(1,128)S(1)}, f32[1,256]{1,0:T(1,128)S(1)}, u32[]{:S(2)}, u32[]{:S(2)}) collective-permute-start(f32[1,256]{1,0:T(1,128)S(1)} %bitcast.14), channel_id=1, source_target_pairs={{0,1},{1,0},{2,3},{3,2},{4,5},{5,4},{6,7},{7,6},{8,9},{9,8},{10,11... | collective-permute-start | bytes 3080 | tf_op jit(solution)/shard_map/ppermute | solution.py:29
  109.5 5.3 %collective-permute-start.4 = (f32[1,256]{1,0:T(1,128)S(1)}, f32[1,256]{1,0:T(1,128)S(1)}, u32[]{:S(2)}, u32[]{:S(2)}) collective-permute-start(f32[1,256]{1,0:T(1,128)S(1)} %bitcast.15), channel_id=1, source_target_pairs={{0,2},{1,3},{2,0},{3,1},{4,6},{5,7},{6,4},{7,5},{8,10},{9,11},{10,... | collective-permute-start | bytes 3080 | tf_op jit(solution)/shard_map/ppermute | solution.py:29
  111.0 4.5 %collective-permute-start.5 = (f32[1,256]{1,0:T(1,128)S(1)}, f32[1,256]{1,0:T(1,128)S(1)}, u32[]{:S(2)}, u32[]{:S(2)}) collective-permute-start(f32[1,256]{1,0:T(1,128)S(1)} %bitcast.16), channel_id=1, source_target_pairs={{0,3},{1,2},{2,1},{3,0},{4,7},{5,6},{6,5},{7,4},{8,11},{9,10},{10,... | collective-permute-start | bytes 3080 | tf_op jit(solution)/shard_map/ppermute | solution.py:29

commit v12 on v11

--- a/solution.py
+++ b/solution.py
@@ -12,7 +12,7 @@
 KEEP_SHARE = 0.5
 HIGH = lax.Precision.HIGHEST
 PANEL = 64
-TILE = 8
+TILE = 16
 HEAD = 16
 TOP = 32766.0
 PARAMS = pltpu.CompilerParams(vmem_limit_bytes=40 * 1024 * 1024)
@@ -304,7 +304,7 @@
             work[end:, low:right] = work[end:, low:right] - change[end - low :, :]
 
 
-def factor_kernel(code_ref, turned_ref, out_ref, gram_ref, work, band):
+def factor_kernel(code_ref, turned_ref, out_ref, gram_ref, mixed_ref, work, band):
     count, size, rank = code_ref.shape
     size = (size - HEAD) * 2 // 3
     code = code_ref[...].astype(jnp.int32)
@@ -314,19 +314,28 @@
     part = (code[:, :size].astype(jnp.float32) + low * (1.0 / 256.0)) * unit_of(head[:, :1], head[:, 1:2])
     turned = part.reshape(count * size, rank).T
     turned_ref[...] = turned
-    gram = dot_rows(turned, turned)
+
+    def times(a, b):
+        a, b = jnp.concatenate(a, axis=1), jnp.concatenate(b, axis=1)
+        return lax.dot_general(a, b, (((1,), (1,)), ((), ())), preferred_element_type=jnp.float32)
+
+    high, middle, small = split_three(turned)
+    even, mixed = times((high, middle), (high, middle)), times((high, high), (middle, small))
 
     @pl.when(pl.program_id(0) == 0)
     def _():
-        gram_ref[...] = gram
+        gram_ref[...] = even
+        mixed_ref[...] = mixed
 
     @pl.when(pl.program_id(0) > 0)
     def _():
-        gram_ref[...] += gram
+        gram_ref[...] += even
+        mixed_ref[...] += mixed
 
     @pl.when(pl.program_id(0) == pl.num_programs(0) - 1)
     def _():
-        inverse_factor(gram_ref[...], out_ref, work, band)
+        mixed = mixed_ref[...]
+        inverse_factor(gram_ref[...] + (mixed + mixed.T), out_ref, work, band)
 
 
 def factor(codes):
@@ -343,6 +352,7 @@
             jax.ShapeDtypeStruct((rank, rank), jnp.float32),
         ],
         scratch_shapes=[
+            pltpu.VMEM((rank, rank), jnp.float32),
             pltpu.VMEM((rank, rank), jnp.float32),
             pltpu.VMEM((rank, 2 * rank), jnp.float32),
             pltpu.VMEM((TILE + 1, TILE, 2 * PANEL), jnp.float32),

time: 119 us -> 118 us (level)
  no operation moved by 1% of the time
where the time goes in v12:
time: 118 us
  blocking collectives  70.2 us (59%)
  Pallas kernels  28.7 us (24%)
  starting transfers between devices  10.8 us (9%)
  waiting for transfers between devices  6.38 us (5%)
    all_gather x1, blocking collectives, on_device(): basis = lax.all_gather(basis, 'fsdp', axis=0, tiled=True)  26.4 us
    all_gather x1, blocking collectives, on_device(): gathered = lax.all_gather(code, 'fsdp', axis=0)  23.4 us
    all_gather x1, blocking collectives, on_device(): packed = lax.all_gather(pack(perm, parts), 'fsdp', axis=0)  20.4 us
    pallas_call x1, Pallas kernels, factor(): pl.pallas_call(factor_kernel, grid=(devices // group,), in_specs=[pl.Bloc...  10.5 us
    ppermute x6, starting transfers between devices, exchange(): lax.ppermute(x, axis, [(i, i ^ k) for i in range(lax.axis_size(axis))])  7.1 us
    ppermute x6, waiting for transfers between devices, exchange(): lax.ppermute(x, axis, [(i, i ^ k) for i in range(lax.axis_size(axis))])  6.37 us
    pallas_call x1, Pallas kernels, project(): pl.pallas_call(project_kernel, grid=(cols // block,), in_specs=[wide, wid...  4.86 us
    all_to_all x1, starting transfers between devices, on_device(): lax.all_to_all(codes, 'fsdp', split_axis=0, concat_axis=0)  3.69 us
  transfers between devices with their start and end apart: 7, of which 3 were waited for; matrix products, arithmetic and copies ran while one was open for 1% of the time, Pallas kernels for 8%

profile of v12, /device:TPU:0, one launch (start us, length us, event | category | flops | bytes accessed | tf_op | source)
XLA Modules:
  0.0 117.6 jit_solution(9699832815470273544)
XLA Ops:
  0.6 3.5 %shard_map.67 = (s16[32,4224]{1,0:T(8,128)(2,1)}, s16[8,128,512]{2,1,0:T(8,128)(2,1)}) custom-call(f32[128,4096]{1,0:T(8,128)} %momentum_ref.5, bf16[128,4096]{1,0:T(8,128)(2,1)} %grad_ref.5, bf16[32,4096]{1,0:T(8,128)(2,1)} %basis_ref.1), custom_call_target="tpu_custom_call" | custom-call | flops 5242880 | bytes 4194304 | tf_op jit(solution)/shard_map/pallas_call | solution.py:117
  4.2 26.4 %all-gather.4.code_ref = s16[256,4224]{1,0:T(8,128)(2,1)} all-gather(s16[32,4224]{1,0:T(8,128)(2,1)} %get-tuple-element.16), channel_id=1, replica_groups=mesh['fsdp'=8,'tp'=4] {'fsdp'}, dimensions={0}, use_global_device_ids=true | all-gather | bytes 2433024 | tf_op jit(solution)/shard_map/all_gather | solution.py:527
  30.6 3.7 %all-to-all-start = ((s16[8,128,512]{2,1,0:T(8,128)(2,1)}), s16[8,128,512]{2,1,0:T(8,128)(2,1)S(1)}, u32[]{:S(2)}, u32[]{:S(2)}) async-start(s16[8,128,512]{2,1,0:T(8,128)(2,1)} %get-tuple-element.18), calls=%async_computation | async-start | bytes 2097152 | tf_op jit(solution)/shard_map/all_to_all | solution.py:529
  34.3 0.0 copy-start.2
  34.3 4.9 %shard_map.68.refs_0_ = f32[128,256]{1,0:T(8,128)S(1)} custom-call(f32[128,4096]{1,0:T(8,128)} %momentum_ref.5, bf16[128,4096]{1,0:T(8,128)(2,1)} %grad_ref.5, s16[256,4224]{1,0:T(8,128)(2,1)} %all-gather.4.code_ref), custom_call_target="tpu_custom_call" | custom-call | flops 536870912 | bytes 5242880 | tf_op jit(solution)/shard_map/pallas_call | solution.py:164
  39.2 1.6 %collective-permute-start = (f32[128,256]{1,0:T(8,128)S(1)}, f32[128,256]{1,0:T(8,128)S(1)}, u32[]{:S(2)}, u32[]{:S(2)}) collective-permute-start(f32[128,256]{1,0:T(8,128)S(1)} %shard_map.68.refs_0_), channel_id=1, source_target_pairs={{0,1},{1,0},{2,3},{3,2},{4,5},{5,4},{6,7},{7,6},{8,9},{9,8},{10,11... | collective-permute-start | bytes 393224 | tf_op jit(solution)/shard_map/ppermute | solution.py:29
  40.7 1.5 %collective-permute-start.1 = (f32[128,256]{1,0:T(8,128)S(1)}, f32[128,256]{1,0:T(8,128)S(1)}, u32[]{:S(2)}, u32[]{:S(2)}) collective-permute-start(f32[128,256]{1,0:T(8,128)S(1)} %shard_map.68.refs_0_), channel_id=1, source_target_pairs={{0,2},{1,3},{2,0},{3,1},{4,6},{5,7},{6,4},{7,5},{8,10},{9,11},{10,... | collective-permute-start | bytes 393224 | tf_op jit(solution)/shard_map/ppermute | solution.py:29
  42.2 0.5 collective-permute-start.2
  42.7 0.7 slice.28
  43.5 2.1 %collective-permute-done.refs_1_ = f32[128,256]{1,0:T(8,128)S(1)} collective-permute-done((f32[128,256]{1,0:T(8,128)S(1)}, f32[128,256]{1,0:T(8,128)S(1)}, u32[]{:S(2)}, u32[]{:S(2)}) %collective-permute-start) | collective-permute-done | bytes 131104 | tf_op jit(solution)/shard_map/ppermute | solution.py:29
  45.5 3.6 %collective-permute-done.1.refs_2_ = f32[128,256]{1,0:T(8,128)S(1)} collective-permute-done((f32[128,256]{1,0:T(8,128)S(1)}, f32[128,256]{1,0:T(8,128)S(1)}, u32[]{:S(2)}, u32[]{:S(2)}) %collective-permute-start.1) | collective-permute-done | bytes 131104 | tf_op jit(solution)/shard_map/ppermute | solution.py:29
  49.1 0.0 collective-permute-done.2.refs_3_
  49.2 0.0 copy-done.2
  49.2 0.9 shard_map.69
  50.1 20.4 %all-gather = s16[1664,256]{1,0:T(8,128)(2,1)S(1)} all-gather(s16[208,256]{1,0:T(8,128)(2,1)S(1)} %shard_map.69), channel_id=2, replica_groups=mesh['fsdp'=8,'tp'=4] {'fsdp'}, dimensions={0}, use_global_device_ids=true | all-gather | bytes 958464 | tf_op jit(solution)/shard_map/all_gather | solution.py:538
  70.5 0.0 all-to-all-done
  70.5 10.5 %shard_map.70 = (f32[256,1024]{1,0:T(8,128)S(1)}, f32[256,256]{1,0:T(8,128)S(1)}) custom-call(s16[8,208,256]{2,1,0:T(8,128)(2,1)S(1)} %bitcast.11), custom_call_target="tpu_custom_call" | custom-call | flops 805306368 | bytes 1703936 | tf_op jit(solution)/shard_map/pallas_call | solution.py:345
  81.0 0.0 copy-start
  81.0 0.0 copy-start.1
  81.0 2.5 %shard_map.71 = (s16[528,256]{1,0:T(8,128)(2,1)S(1)}, f32[128,256]{1,0:T(8,128)S(1)}) custom-call(s32[1]{0:T(128)} %bitcast.place_ref, s16[1024,512]{1,0:T(8,128)(2,1)S(1)} %bitcast.10, f32[256,1024]{1,0:T(8,128)S(1)} %get-tuple-element.21.turned_ref.own_ref, f32[1,1024]{1,0:T(1,128)S(1)} %bitcast.12, f32[256,256]{1,0:T(8,128)S(1)} %get-tuple-element.22.inverse_ref, ...), custom_call_target="tpu_custom_call" | custom-call | flops 805306368 | bytes 2097152 | tf_op jit(solution)/shard_map/pallas_call | solution.py:409
  83.5 23.4 %all-gather.5 = s16[4224,256]{1,0:T(8,128)(2,1)S(1)} all-gather(s16[528,256]{1,0:T(8,128)(2,1)S(1)} %get-tuple-element.23), channel_id=3, replica_groups=mesh['fsdp'=8,'tp'=4] {'fsdp'}, dimensions={0}, use_global_device_ids=true | all-gather | bytes 2433024 | tf_op jit(solution)/shard_map/all_gather | solution.py:542
  107.0 0.1 fusion.4
  107.0 1.6 %collective-permute-start.3 = (f32[1,256]{1,0:T(1,128)S(1)}, f32[1,256]{1,0:T(1,128)S(1)}, u32[]{:S(2)}, u32[]{:S(2)}) collective-permute-start(f32[1,256]{1,0:T(1,128)S(1)} %bitcast.14), channel_id=1, source_target_pairs={{0,1},{1,0},{2,3},{3,2},{4,5},{5,4},{6,7},{7,6},{8,9},{9,8},{10,11... | collective-permute-start | bytes 3080 | tf_op jit(solution)/shard_map/ppermute | solution.py:29
  108.6 1.5 %collective-permute-start.4 = (f32[1,256]{1,0:T(1,128)S(1)}, f32[1,256]{1,0:T(1,128)S(1)}, u32[]{:S(2)}, u32[]{:S(2)}) collective-permute-start(f32[1,256]{1,0:T(1,128)S(1)} %bitcast.15), channel_id=1, source_target_pairs={{0,2},{1,3},{2,0},{3,1},{4,6},{5,7},{6,4},{7,5},{8,10},{9,11},{10,... | collective-permute-start | bytes 3080 | tf_op jit(solution)/shard_map/ppermute | solution.py:29
  110.1 0.5 collective-permute-start.5
  110.6 0.0 copy-done
  110.6 0.0 copy-done.1
  110.6 3.3 %shard_map.72 = f32[128,4096]{1,0:T(8,128)} custom-call(f32[128,4096]{1,0:T(8,128)S(1)} %copy-done, bf16[128,4096]{1,0:T(8,128)(2,1)S(1)} %copy-done.1, s16[8,528,256]{2,1,0:T(8,128)(2,1)S(1)} %bitcast.8, f32[128,256]{1,0:T(8,128)S(1)} %get-tuple-element.24.ortho_ref), custom_call_target="tpu_custom_call" | custom-call | flops 805306368 | bytes 7340032 | tf_op jit(solution)/shard_map/pallas_call | solution.py:488
  113.9 0.0 collective-permute-done.3
  113.9 0.0 collective-permute-done.4
  113.9 0.7 collective-permute-done.5
  114.6 3.1 %shard_map.73 = (f32[4096,256]{1,0:T(8,128)}, bf16[128,4096]{1,0:T(8,128)(2,1)}) custom-call(s16[8,528,256]{2,1,0:T(8,128)(2,1)S(1)} %bitcast.9, f32[128,256]{1,0:T(8,128)S(1)} %get-tuple-element.24.ortho_ref, f32[1,256]{1,0:T(1,128)S(1)} %add_rsqrt_fusion.scale_ref), custom_call_target="tpu_custom_call" | custom-call | flops 805306368 | bytes 7340032 | tf_op jit(solution)/shard_map/pallas_call | solution.py:500
  (4 shorter events, 0.0 us)
Async XLA Ops:
  30.6 39.9 %all-to-all-start = ((s16[8,128,512]{2,1,0:T(8,128)(2,1)}), s16[8,128,512]{2,1,0:T(8,128)(2,1)S(1)}, u32[]{:S(2)}, u32[]{:S(2)}) async-start(s16[8,128,512]{2,1,0:T(8,128)(2,1)} %get-tuple-element.18), calls=%async_computation | async-start | bytes 2097152 | tf_op jit(solution)/shard_map/all_to_all | solution.py:529
  34.3 14.9 %copy-start.2 = (s32[8]{0:T(128)S(1)}, s32[8]{0:T(128)}, u32[]{:S(2)}) copy-start(s32[8]{0:T(128)} %perm_ref.1) | copy-start | bytes 100
  39.2 6.4 %collective-permute-start = (f32[128,256]{1,0:T(8,128)S(1)}, f32[128,256]{1,0:T(8,128)S(1)}, u32[]{:S(2)}, u32[]{:S(2)}) collective-permute-start(f32[128,256]{1,0:T(8,128)S(1)} %shard_map.68.refs_0_), channel_id=1, source_target_pairs={{0,1},{1,0},{2,3},{3,2},{4,5},{5,4},{6,7},{7,6},{8,9},{9,8},{10,11... | collective-permute-start | bytes 393224 | tf_op jit(solution)/shard_map/ppermute | solution.py:29
  40.7 8.4 %collective-permute-start.1 = (f32[128,256]{1,0:T(8,128)S(1)}, f32[128,256]{1,0:T(8,128)S(1)}, u32[]{:S(2)}, u32[]{:S(2)}) collective-permute-start(f32[128,256]{1,0:T(8,128)S(1)} %shard_map.68.refs_0_), channel_id=1, source_target_pairs={{0,2},{1,3},{2,0},{3,1},{4,6},{5,7},{6,4},{7,5},{8,10},{9,11},{10,... | collective-permute-start | bytes 393224 | tf_op jit(solution)/shard_map/ppermute | solution.py:29
  42.2 6.9 %collective-permute-start.2 = (f32[128,256]{1,0:T(8,128)S(1)}, f32[128,256]{1,0:T(8,128)S(1)}, u32[]{:S(2)}, u32[]{:S(2)}) collective-permute-start(f32[128,256]{1,0:T(8,128)S(1)} %shard_map.68.refs_0_), channel_id=1, source_target_pairs={{0,3},{1,2},{2,1},{3,0},{4,7},{5,6},{6,5},{7,4},{8,11},{9,10},{10,... | collective-permute-start | bytes 393224 | tf_op jit(solution)/shard_map/ppermute | solution.py:29
  81.0 29.6 %copy-start = (f32[128,4096]{1,0:T(8,128)S(1)}, f32[128,4096]{1,0:T(8,128)}, u32[]{:S(2)}) copy-start(f32[128,4096]{1,0:T(8,128)} %momentum_ref.5) | copy-start | bytes 6291460
  81.0 29.6 %copy-start.1 = (bf16[128,4096]{1,0:T(8,128)(2,1)S(1)}, bf16[128,4096]{1,0:T(8,128)(2,1)}, u32[]{:S(2)}) copy-start(bf16[128,4096]{1,0:T(8,128)(2,1)} %grad_ref.5) | copy-start | bytes 3145732
  107.0 6.9 %collective-permute-start.3 = (f32[1,256]{1,0:T(1,128)S(1)}, f32[1,256]{1,0:T(1,128)S(1)}, u32[]{:S(2)}, u32[]{:S(2)}) collective-permute-start(f32[1,256]{1,0:T(1,128)S(1)} %bitcast.14), channel_id=1, source_target_pairs={{0,1},{1,0},{2,3},{3,2},{4,5},{5,4},{6,7},{7,6},{8,9},{9,8},{10,11... | collective-permute-start | bytes 3080 | tf_op jit(solution)/shard_map/ppermute | solution.py:29
  108.6 5.3 %collective-permute-start.4 = (f32[1,256]{1,0:T(1,128)S(1)}, f32[1,256]{1,0:T(1,128)S(1)}, u32[]{:S(2)}, u32[]{:S(2)}) collective-permute-start(f32[1,256]{1,0:T(1,128)S(1)} %bitcast.15), channel_id=1, source_target_pairs={{0,2},{1,3},{2,0},{3,1},{4,6},{5,7},{6,4},{7,5},{8,10},{9,11},{10,... | collective-permute-start | bytes 3080 | tf_op jit(solution)/shard_map/ppermute | solution.py:29
  110.1 4.5 %collective-permute-start.5 = (f32[1,256]{1,0:T(1,128)S(1)}, f32[1,256]{1,0:T(1,128)S(1)}, u32[]{:S(2)}, u32[]{:S(2)}) collective-permute-start(f32[1,256]{1,0:T(1,128)S(1)} %bitcast.16), channel_id=1, source_target_pairs={{0,3},{1,2},{2,1},{3,0},{4,7},{5,6},{6,5},{7,4},{8,11},{9,10},{10,... | collective-permute-start | bytes 3080 | tf_op jit(solution)/shard_map/ppermute | solution.py:29

commit v13 on v12

--- a/solution.py
+++ b/solution.py
@@ -368,9 +368,6 @@
     def times(a, b):
         return jnp.dot(a, b, preferred_element_type=jnp.float32)
 
-    def turned_dot(a, b):
-        return lax.dot_general(a, b, (((0,), (1,)), ((), ())), precision=HIGH, preferred_element_type=jnp.float32)
-
     rank = turned_ref.shape[0]
     source_high, source_low = halves(source_ref[...].astype(jnp.int32).astype(jnp.float32))
     scaled_high, scaled_low = halves(turned_ref[...] * unit_ref[...])
@@ -389,17 +386,28 @@
     @pl.when(last)
     def _():
         inverse = inverse_ref[...]
-        ortho_ref[...] = turned_dot(own_ref[...], inverse)
-        right = turned_dot(mixed_ref[...], inverse)
-        rows = right.shape[0]
-        square = jnp.maximum(jnp.sum(right * right, axis=0, keepdims=True), 1e-34)
+        ortho_ref[...] = lax.dot_general(
+            own_ref[...], inverse, (((0,), (1,)), ((), ())), precision=HIGH, preferred_element_type=jnp.float32
+        )
+        right = jnp.dot(inverse, mixed_ref[...], precision=HIGH, preferred_element_type=jnp.float32)
+        share = right.shape[1]
+        width = code_ref.shape[1]
+        square = jnp.maximum(jnp.sum(right * right, axis=1, keepdims=True), 1e-34)
         square_exponent = jnp.floor(jnp.log2(square))
         fine = square * jnp.exp2(13.0 - square_exponent)
         square_high = jnp.floor(fine)
         square_low = jnp.floor((fine - square_high) * 16384.0)
-        exponent, mantissa = code_unit(jnp.max(jnp.abs(right), axis=0, keepdims=True))
-        code_ref[:rows] = whole_number(jnp.floor(right * (1.0 / unit_of(exponent, mantissa)) + 0.5))
-        set_head(code_ref.at[rows:], exponent, mantissa, square_exponent, square_high, square_low)
+        exponent, mantissa = code_unit(jnp.max(jnp.abs(right), axis=1, keepdims=True))
+        code_ref[:rank, :share] = whole_number(jnp.floor(right * (1.0 / unit_of(exponent, mantissa)) + 0.5))
+        lane = lax.broadcasted_iota(jnp.int32, (rank, 128), 1)
+        head = jnp.zeros((rank, 128), jnp.float32)
+        for k, column in enumerate((exponent, mantissa, square_exponent, square_high, square_low)):
+            head = jnp.where(lane == k, column, head)
+        code_ref[rank:, :rank] = whole_number(head.T[:HEAD])
+        if width > rank:
+            code_ref[rank:, rank:] = jnp.zeros((HEAD, width - rank), jnp.int16)
+        if width > share:
+            code_ref[:rank, share:] = jnp.zeros((rank, width - share), jnp.int16)
 
 
 def encode(place, source, turned, unit, inverse_low, rows):
@@ -419,13 +427,13 @@
                 pl.BlockSpec((rank, rows), lambda i, place: (0, place[0])),
             ],
             out_specs=[
-                pl.BlockSpec((share + HEAD, rank), lambda i, place: (0, 0)),
+                pl.BlockSpec((rank + HEAD, max(share, rank)), lambda i, place: (0, 0)),
                 pl.BlockSpec((rows, rank), lambda i, place: (0, 0)),
             ],
             scratch_shapes=[pltpu.VMEM((rank, share), jnp.float32)],
         ),
         out_shape=[
-            jax.ShapeDtypeStruct((share + HEAD, rank), jnp.int16),
+            jax.ShapeDtypeStruct((rank + HEAD, max(share, rank)), jnp.int16),
             jax.ShapeDtypeStruct((rows, rank), jnp.float32),
         ],
         compiler_params=PARAMS,
@@ -435,81 +443,70 @@
     )(place, source, turned, unit, inverse_low, turned)
 
 
-def decode(code_ref):
-    code = code_ref[...].astype(jnp.int32).astype(jnp.float32)
-    share = code.shape[1] - HEAD
-    right = code[:, :share] * unit_of(code[:, share : share + 1], code[:, share + 1 : share + 2])
-    return right.reshape(code.shape[0] * share, code.shape[2])
-
-
-def times_rows(split_ref, right):
-    def times(a, b):
-        return lax.dot_general(a, b, (((1,), (1,)), ((), ())), preferred_element_type=jnp.float32)
-
-    right_high, right_low = halves(right)
-    split = split_ref[...]
-    rows = split.shape[0] // 2
-    most = times(split, right_high)
-    return most[:rows] + (most[rows:] + times(split[:rows], right_low))
-
-
-def set_split(split_ref, x):
-    rows = x.shape[0]
-
-    @pl.when(pl.program_id(0) == 0)
-    def _():
-        split_ref[:rows], split_ref[rows:] = halves(x)
-
-
-def momentum_kernel(momentum_ref, grad_ref, code_ref, ortho_ref, next_ref, split_ref):
-    set_split(split_ref, -KEEP_SHARE * ortho_ref[...])
-    change = times_rows(split_ref, decode(code_ref))
-    next_ref[...] = momentum_ref[...] + grad_ref[...].astype(jnp.float32) + change
-
-
-def update_kernel(gain, code_ref, ortho_ref, scale_ref, basis_ref, update_ref, split_ref):
-    set_split(split_ref, gain * ortho_ref[...])
-    basis = decode(code_ref) * scale_ref[...]
-    basis_ref[...] = basis
-    update_ref[...] = times_rows(split_ref, basis).astype(jnp.bfloat16)
-
-
-def finish(momentum, grad, codes, orthonormal, scale, gain):
+def float_of(code):
+    return code if code.dtype == jnp.float32 else code.astype(jnp.int32).astype(jnp.float32)
+
+
+def split_dot(left, code):
+    rows = left.shape[0]
+    left_high, left_low = halves(left)
+    code_high, code_low = halves(code)
+    most = jnp.dot(jnp.concatenate([left_high, left_low], axis=0), code_high, preferred_element_type=jnp.float32)
+    return most[:rows] + (most[rows:] + jnp.dot(left_high, code_low, preferred_element_type=jnp.float32))
+
+
+def momentum_kernel(momentum_ref, grad_ref, code_ref, unit_ref, ortho_ref, next_ref):
+    group, _, width = code_ref.shape
+    for k in range(group):
+        span = slice(width * k, width * (k + 1))
+        change = split_dot(-KEEP_SHARE * ortho_ref[...] * unit_ref[k], float_of(code_ref[k]))
+        next_ref[:, span] = momentum_ref[:, span] + grad_ref[:, span].astype(jnp.float32) + change
+
+
+def update_kernel(gain, code_ref, unit_ref, ortho_ref, scale_ref, basis_ref, update_ref):
+    group, _, width = code_ref.shape
+    for k in range(group):
+        span = slice(width * k, width * (k + 1))
+        code = float_of(code_ref[k])
+        factor = unit_ref[k] * scale_ref[...]
+        basis_ref[span, :] = code.T * factor
+        update_ref[:, span] = split_dot(gain * ortho_ref[...] * factor, code).astype(jnp.bfloat16)
+
+
+def finish(momentum, grad, codes, units, orthonormal, scale, gain):
     rows, cols = momentum.shape
-    shares, share, rank = codes.shape
-    share -= HEAD
-    group = max(1, min(1024 // share, shares))
-    block = group * share
+    shares, _, width = codes.shape
+    rank = orthonormal.shape[1]
+    group = 2 if shares % 2 == 0 else 1
+    block = group * width
     wide = pl.BlockSpec((rows, block), lambda i: (0, i))
     tall = pl.BlockSpec((block, rank), lambda i: (i, 0))
-    coded = pl.BlockSpec((group, share + HEAD, rank), lambda i: (i, 0, 0))
-    split = [pltpu.VMEM((2 * rows, rank), jnp.bfloat16)]
+    coded = pl.BlockSpec((group, rank, width), lambda i: (i, 0, 0))
+    unit = pl.BlockSpec((group, 1, rank), lambda i: (i, 0, 0))
     flops = 6 * rows * cols * rank
     momentum_next = pl.pallas_call(
         momentum_kernel,
         grid=(cols // block,),
-        in_specs=[wide, wide, coded, whole(orthonormal)],
+        in_specs=[wide, wide, coded, unit, whole(orthonormal)],
         out_specs=wide,
         out_shape=jax.ShapeDtypeStruct((rows, cols), jnp.float32),
-        scratch_shapes=split,
         compiler_params=PARAMS,
         cost_estimate=pl.CostEstimate(
             flops=flops, bytes_accessed=rows * cols * 10 + cols * rank * 2, transcendentals=0
         ),
-    )(momentum, grad, codes, orthonormal)
+    )(momentum, grad, codes, units, orthonormal)
     q_next, update = pl.pallas_call(
         functools.partial(update_kernel, gain),
         grid=(cols // block,),
-        in_specs=[coded, whole(orthonormal), whole(scale)],
+        in_specs=[coded, unit, whole(orthonormal), whole(scale)],
         out_specs=[tall, wide],
         out_shape=[
             jax.ShapeDtypeStruct((cols, rank), jnp.float32),
             jax.ShapeDtypeStruct((rows, cols), jnp.bfloat16),
         ],
-        scratch_shapes=split,
         compiler_params=PARAMS,
         cost_estimate=pl.CostEstimate(flops=flops, bytes_accessed=rows * cols * 2 + cols * rank * 6, transcendentals=0),
-    )(codes, orthonormal, scale)
+    )(codes, units, orthonormal, scale)
     return momentum_next, q_next, update
 
 
@@ -540,11 +537,16 @@
     turned, inverse_low = factor(packed)
     code, orthonormal = encode(lax.axis_index("fsdp").reshape(1), codes, turned, unit, inverse_low, rows)
     gathered = lax.all_gather(code, "fsdp", axis=0)
-    head = gathered[:, share : share + 5].astype(jnp.float32)
+    head = gathered[:, rank_total : rank_total + 5, :rank_total].astype(jnp.float32)
+    units = unit_of(head[:, :1], head[:, 1:2])
     parts = (head[:, 3] + head[:, 4] * (1.0 / 16384.0)) * jnp.exp2(head[:, 2] - 13.0)
     squares = quad_sum(jnp.sum(parts, axis=0, keepdims=True), "tp")
     scale = lax.rsqrt(squares / col_total + EPSILON)
-    return tuple(finish(momentum, grad, gathered, orthonormal, scale, math.sqrt(row_total / rank_total)))
+    if share % 128 != 0:
+        gathered = gathered[:, :rank_total, :share].astype(jnp.float32) * units.swapaxes(1, 2)
+        gathered = gathered.swapaxes(0, 1).reshape(1, rank_total, cols)
+        units = jnp.ones((1, 1, rank_total), jnp.float32)
+    return tuple(finish(momentum, grad, gathered, units, orthonormal, scale, math.sqrt(row_total / rank_total)))
 
 
 def solution(mesh):

time: 118 us -> 119 us (level)
  no operation moved by 1% of the time
where the time goes in v13:
time: 119 us
  blocking collectives  70.7 us (59%)
  Pallas kernels  29.1 us (24%)
  starting transfers between devices  10.8 us (9%)
  waiting for transfers between devices  6.53 us (5%)
    all_gather x1, blocking collectives, on_device(): basis = lax.all_gather(basis, 'fsdp', axis=0, tiled=True)  26.4 us
    all_gather x1, blocking collectives, on_device(): gathered = lax.all_gather(code, 'fsdp', axis=0)  23.9 us
    all_gather x1, blocking collectives, on_device(): packed = lax.all_gather(pack(perm, parts), 'fsdp', axis=0)  20.4 us
    pallas_call x1, Pallas kernels, factor(): pl.pallas_call(factor_kernel, grid=(devices // group,), in_specs=[pl.Bloc...  10.5 us
    ppermute x6, starting transfers between devices, exchange(): lax.ppermute(x, axis, [(i, i ^ k) for i in range(lax.axis_size(axis))])  7.1 us
    ppermute x6, waiting for transfers between devices, exchange(): lax.ppermute(x, axis, [(i, i ^ k) for i in range(lax.axis_size(axis))])  6.52 us
    pallas_call x1, Pallas kernels, project(): pl.pallas_call(project_kernel, grid=(cols // block,), in_specs=[wide, wid...  4.86 us
    all_to_all x1, starting transfers between devices, on_device(): lax.all_to_all(codes, 'fsdp', split_axis=0, concat_axis=0)  3.69 us
  transfers between devices with their start and end apart: 7, of which 3 were waited for; matrix products, arithmetic and copies ran while one was open for 1% of the time, Pallas kernels for 8%

profile of v13, /device:TPU:0, one launch (start us, length us, event | category | flops | bytes accessed | tf_op | source)
XLA Modules:
  0.0 118.7 jit_solution(4547615572436772849)
XLA Ops:
  0.6 3.5 %shard_map.67 = (s16[32,4224]{1,0:T(8,128)(2,1)}, s16[8,128,512]{2,1,0:T(8,128)(2,1)}) custom-call(f32[128,4096]{1,0:T(8,128)} %momentum_ref.5, bf16[128,4096]{1,0:T(8,128)(2,1)} %grad_ref.5, bf16[32,4096]{1,0:T(8,128)(2,1)} %basis_ref.1), custom_call_target="tpu_custom_call" | custom-call | flops 5242880 | bytes 4194304 | tf_op jit(solution)/shard_map/pallas_call | solution.py:117
  4.2 26.4 %all-gather.4.code_ref = s16[256,4224]{1,0:T(8,128)(2,1)} all-gather(s16[32,4224]{1,0:T(8,128)(2,1)} %get-tuple-element.16), channel_id=1, replica_groups=mesh['fsdp'=8,'tp'=4] {'fsdp'}, dimensions={0}, use_global_device_ids=true | all-gather | bytes 2433024 | tf_op jit(solution)/shard_map/all_gather | solution.py:524
  30.6 3.7 %all-to-all-start = ((s16[8,128,512]{2,1,0:T(8,128)(2,1)}), s16[8,128,512]{2,1,0:T(8,128)(2,1)S(1)}, u32[]{:S(2)}, u32[]{:S(2)}) async-start(s16[8,128,512]{2,1,0:T(8,128)(2,1)} %get-tuple-element.18), calls=%async_computation | async-start | bytes 2097152 | tf_op jit(solution)/shard_map/all_to_all | solution.py:526
  34.3 0.0 copy-start.2
  34.3 4.9 %shard_map.68.refs_0_ = f32[128,256]{1,0:T(8,128)S(1)} custom-call(f32[128,4096]{1,0:T(8,128)} %momentum_ref.5, bf16[128,4096]{1,0:T(8,128)(2,1)} %grad_ref.5, s16[256,4224]{1,0:T(8,128)(2,1)} %all-gather.4.code_ref), custom_call_target="tpu_custom_call" | custom-call | flops 536870912 | bytes 5242880 | tf_op jit(solution)/shard_map/pallas_call | solution.py:164
  39.2 1.6 %collective-permute-start = (f32[128,256]{1,0:T(8,128)S(1)}, f32[128,256]{1,0:T(8,128)S(1)}, u32[]{:S(2)}, u32[]{:S(2)}) collective-permute-start(f32[128,256]{1,0:T(8,128)S(1)} %shard_map.68.refs_0_), channel_id=1, source_target_pairs={{0,1},{1,0},{2,3},{3,2},{4,5},{5,4},{6,7},{7,6},{8,9},{9,8},{10,11... | collective-permute-start | bytes 393224 | tf_op jit(solution)/shard_map/ppermute | solution.py:29
  40.7 1.5 %collective-permute-start.1 = (f32[128,256]{1,0:T(8,128)S(1)}, f32[128,256]{1,0:T(8,128)S(1)}, u32[]{:S(2)}, u32[]{:S(2)}) collective-permute-start(f32[128,256]{1,0:T(8,128)S(1)} %shard_map.68.refs_0_), channel_id=1, source_target_pairs={{0,2},{1,3},{2,0},{3,1},{4,6},{5,7},{6,4},{7,5},{8,10},{9,11},{10,... | collective-permute-start | bytes 393224 | tf_op jit(solution)/shard_map/ppermute | solution.py:29
  42.2 0.5 collective-permute-start.2
  42.7 0.7 slice.36
  43.5 2.1 %collective-permute-done.refs_1_ = f32[128,256]{1,0:T(8,128)S(1)} collective-permute-done((f32[128,256]{1,0:T(8,128)S(1)}, f32[128,256]{1,0:T(8,128)S(1)}, u32[]{:S(2)}, u32[]{:S(2)}) %collective-permute-start) | collective-permute-done | bytes 131104 | tf_op jit(solution)/shard_map/ppermute | solution.py:29
  45.5 3.6 %collective-permute-done.1.refs_2_ = f32[128,256]{1,0:T(8,128)S(1)} collective-permute-done((f32[128,256]{1,0:T(8,128)S(1)}, f32[128,256]{1,0:T(8,128)S(1)}, u32[]{:S(2)}, u32[]{:S(2)}) %collective-permute-start.1) | collective-permute-done | bytes 131104 | tf_op jit(solution)/shard_map/ppermute | solution.py:29
  49.1 0.0 collective-permute-done.2.refs_3_
  49.2 0.0 copy-done.2
  49.2 0.9 shard_map.69
  50.1 20.4 %all-gather = s16[1664,256]{1,0:T(8,128)(2,1)S(1)} all-gather(s16[208,256]{1,0:T(8,128)(2,1)S(1)} %shard_map.69), channel_id=2, replica_groups=mesh['fsdp'=8,'tp'=4] {'fsdp'}, dimensions={0}, use_global_device_ids=true | all-gather | bytes 958464 | tf_op jit(solution)/shard_map/all_gather | solution.py:535
  70.5 0.0 all-to-all-done
  70.5 10.5 %shard_map.70 = (f32[256,1024]{1,0:T(8,128)S(1)}, f32[256,256]{1,0:T(8,128)S(1)}) custom-call(s16[8,208,256]{2,1,0:T(8,128)(2,1)S(1)} %bitcast.11), custom_call_target="tpu_custom_call" | custom-call | flops 805306368 | bytes 1703936 | tf_op jit(solution)/shard_map/pallas_call | solution.py:345
  81.0 0.0 copy-start
  81.0 0.0 copy-start.1
  81.0 2.5 %shard_map.71 = (s16[272,512]{1,0:T(8,128)(2,1)S(1)}, f32[128,256]{1,0:T(8,128)S(1)}) custom-call(s32[1]{0:T(128)} %bitcast.place_ref, s16[1024,512]{1,0:T(8,128)(2,1)S(1)} %bitcast.10, f32[256,1024]{1,0:T(8,128)S(1)} %get-tuple-element.21.turned_ref.own_ref, f32[1,1024]{1,0:T(1,128)S(1)} %bitcast.12, f32[256,256]{1,0:T(8,128)S(1)} %get-tuple-element.22.inverse_ref, ...), custom_call_target="tpu_custom_call" | custom-call | flops 805306368 | bytes 2097152 | tf_op jit(solution)/shard_map/pallas_call | solution.py:417
  83.6 23.9 %all-gather.5 = s16[2176,512]{1,0:T(8,128)(2,1)S(1)} all-gather(s16[272,512]{1,0:T(8,128)(2,1)S(1)} %get-tuple-element.23), channel_id=3, replica_groups=mesh['fsdp'=8,'tp'=4] {'fsdp'}, dimensions={0}, use_global_device_ids=true | all-gather | bytes 2506752 | tf_op jit(solution)/shard_map/all_gather | solution.py:539
  107.5 0.1 fusion.7
  107.6 1.6 %collective-permute-start.3 = (f32[1,256]{1,0:T(1,128)S(1)}, f32[1,256]{1,0:T(1,128)S(1)}, u32[]{:S(2)}, u32[]{:S(2)}) collective-permute-start(f32[1,256]{1,0:T(1,128)S(1)} %bitcast.14), channel_id=1, source_target_pairs={{0,1},{1,0},{2,3},{3,2},{4,5},{5,4},{6,7},{7,6},{8,9},{9,8},{10,11... | collective-permute-start | bytes 3080 | tf_op jit(solution)/shard_map/ppermute | solution.py:29
  109.2 1.5 %collective-permute-start.4 = (f32[1,256]{1,0:T(1,128)S(1)}, f32[1,256]{1,0:T(1,128)S(1)}, u32[]{:S(2)}, u32[]{:S(2)}) collective-permute-start(f32[1,256]{1,0:T(1,128)S(1)} %bitcast.15), channel_id=1, source_target_pairs={{0,2},{1,3},{2,0},{3,1},{4,6},{5,7},{6,4},{7,5},{8,10},{9,11},{10,... | collective-permute-start | bytes 3080 | tf_op jit(solution)/shard_map/ppermute | solution.py:29
  110.7 0.5 collective-permute-start.5
  111.2 0.0 copy-done
  111.2 0.0 copy-done.1
  111.2 3.1 %shard_map.72 = f32[128,4096]{1,0:T(8,128)} custom-call(f32[128,4096]{1,0:T(8,128)S(1)} %copy-done, bf16[128,4096]{1,0:T(8,128)(2,1)S(1)} %copy-done.1, s16[8,272,512]{2,1,0:T(8,128)(2,1)S(1)} %bitcast.8, f32[8,1,256]{2,1,0:T(1,128)S(1)} %get-tuple-element.28.unit_ref, f32[128,256]{1,0:T(8,128)S(1)} %get-tuple-element.24.ortho_ref), custom_call_target="tpu_custom_call" | custom-call | flops 805306368 | bytes 7340032 | tf_op jit(solution)/shard_map/pallas_call | solution.py:487
  114.3 0.0 collective-permute-done.3
  114.3 0.0 collective-permute-done.4
  114.3 0.8 collective-permute-done.5
  115.2 3.6 %shard_map.73 = (f32[4096,256]{1,0:T(8,128)}, bf16[128,4096]{1,0:T(8,128)(2,1)}) custom-call(s16[8,272,512]{2,1,0:T(8,128)(2,1)S(1)} %bitcast.9, f32[8,1,256]{2,1,0:T(1,128)S(1)} %get-tuple-element.28.unit_ref, f32[128,256]{1,0:T(8,128)S(1)} %get-tuple-element.24.ortho_ref, f32[1,256]{1,0:T(1,128)S(1)} %add_rsqrt_fusion.scale_ref), custom_call_target="tpu_custom_call" | custom-call | flops 805306368 | bytes 7340032 | tf_op jit(solution)/shard_map/pallas_call | solution.py:498
  (4 shorter events, 0.0 us)
Async XLA Ops:
  30.6 39.9 %all-to-all-start = ((s16[8,128,512]{2,1,0:T(8,128)(2,1)}), s16[8,128,512]{2,1,0:T(8,128)(2,1)S(1)}, u32[]{:S(2)}, u32[]{:S(2)}) async-start(s16[8,128,512]{2,1,0:T(8,128)(2,1)} %get-tuple-element.18), calls=%async_computation | async-start | bytes 2097152 | tf_op jit(solution)/shard_map/all_to_all | solution.py:526
  34.3 14.9 %copy-start.2 = (s32[8]{0:T(128)S(1)}, s32[8]{0:T(128)}, u32[]{:S(2)}) copy-start(s32[8]{0:T(128)} %perm_ref.1) | copy-start | bytes 100
  39.2 6.4 %collective-permute-start = (f32[128,256]{1,0:T(8,128)S(1)}, f32[128,256]{1,0:T(8,128)S(1)}, u32[]{:S(2)}, u32[]{:S(2)}) collective-permute-start(f32[128,256]{1,0:T(8,128)S(1)} %shard_map.68.refs_0_), channel_id=1, source_target_pairs={{0,1},{1,0},{2,3},{3,2},{4,5},{5,4},{6,7},{7,6},{8,9},{9,8},{10,11... | collective-permute-start | bytes 393224 | tf_op jit(solution)/shard_map/ppermute | solution.py:29
  40.7 8.4 %collective-permute-start.1 = (f32[128,256]{1,0:T(8,128)S(1)}, f32[128,256]{1,0:T(8,128)S(1)}, u32[]{:S(2)}, u32[]{:S(2)}) collective-permute-start(f32[128,256]{1,0:T(8,128)S(1)} %shard_map.68.refs_0_), channel_id=1, source_target_pairs={{0,2},{1,3},{2,0},{3,1},{4,6},{5,7},{6,4},{7,5},{8,10},{9,11},{10,... | collective-permute-start | bytes 393224 | tf_op jit(solution)/shard_map/ppermute | solution.py:29
  42.2 6.9 %collective-permute-start.2 = (f32[128,256]{1,0:T(8,128)S(1)}, f32[128,256]{1,0:T(8,128)S(1)}, u32[]{:S(2)}, u32[]{:S(2)}) collective-permute-start(f32[128,256]{1,0:T(8,128)S(1)} %shard_map.68.refs_0_), channel_id=1, source_target_pairs={{0,3},{1,2},{2,1},{3,0},{4,7},{5,6},{6,5},{7,4},{8,11},{9,10},{10,... | collective-permute-start | bytes 393224 | tf_op jit(solution)/shard_map/ppermute | solution.py:29
  81.0 30.2 %copy-start = (f32[128,4096]{1,0:T(8,128)S(1)}, f32[128,4096]{1,0:T(8,128)}, u32[]{:S(2)}) copy-start(f32[128,4096]{1,0:T(8,128)} %momentum_ref.5) | copy-start | bytes 6291460
  81.0 30.1 %copy-start.1 = (bf16[128,4096]{1,0:T(8,128)(2,1)S(1)}, bf16[128,4096]{1,0:T(8,128)(2,1)}, u32[]{:S(2)}) copy-start(bf16[128,4096]{1,0:T(8,128)(2,1)} %grad_ref.5) | copy-start | bytes 3145732
  107.6 6.7 %collective-permute-start.3 = (f32[1,256]{1,0:T(1,128)S(1)}, f32[1,256]{1,0:T(1,128)S(1)}, u32[]{:S(2)}, u32[]{:S(2)}) collective-permute-start(f32[1,256]{1,0:T(1,128)S(1)} %bitcast.14), channel_id=1, source_target_pairs={{0,1},{1,0},{2,3},{3,2},{4,5},{5,4},{6,7},{7,6},{8,9},{9,8},{10,11... | collective-permute-start | bytes 3080 | tf_op jit(solution)/shard_map/ppermute | solution.py:29
  109.2 5.2 %collective-permute-start.4 = (f32[1,256]{1,0:T(1,128)S(1)}, f32[1,256]{1,0:T(1,128)S(1)}, u32[]{:S(2)}, u32[]{:S(2)}) collective-permute-start(f32[1,256]{1,0:T(1,128)S(1)} %bitcast.15), channel_id=1, source_target_pairs={{0,2},{1,3},{2,0},{3,1},{4,6},{5,7},{6,4},{7,5},{8,10},{9,11},{10,... | collective-permute-start | bytes 3080 | tf_op jit(solution)/shard_map/ppermute | solution.py:29
  110.7 4.5 %collective-permute-start.5 = (f32[1,256]{1,0:T(1,128)S(1)}, f32[1,256]{1,0:T(1,128)S(1)}, u32[]{:S(2)}, u32[]{:S(2)}) collective-permute-start(f32[1,256]{1,0:T(1,128)S(1)} %bitcast.16), channel_id=1, source_target_pairs={{0,3},{1,2},{2,1},{3,0},{4,7},{5,6},{6,5},{7,4},{8,11},{9,10},{10,... | collective-permute-start | bytes 3080 | tf_op jit(solution)/shard_map/ppermute | solution.py:29

commit v14 on v12

--- a/solution.py
+++ b/solution.py
@@ -82,7 +82,7 @@
     return whole_number(jnp.where(normal, jnp.where(value < 0.0, code - 32768.0, code), 0.0))
 
 
-def prepare_kernel(momentum_ref, grad_ref, basis_ref, pack_ref, code_ref, head_ref):
+def prepare_kernel(momentum_ref, grad_ref, basis_ref, basis_code_ref, code_ref, unit_ref, column_ref):
     rows, cols = momentum_ref.shape
     width = code_ref.shape[-1]
     spans = [slice(i, i + width) for i in range(0, cols, width)]
@@ -92,20 +92,16 @@
     inverse = 1.0 / unit_of(exponent, mantissa)
     for k, span in enumerate(spans):
         code_ref[k] = whole_number(jnp.floor(combined(span) * inverse + 0.5))
-        pack_ref[:, span] = code_basis(basis_ref[:, span])
+        basis_code_ref[:, span] = code_basis(basis_ref[:, span])
     step = pl.program_id(0)
     here = pl.ds(pl.multiple_of(step * rows, rows), rows)
     for k, column in enumerate((exponent, mantissa)):
-        head_ref[k, here, :] = jnp.broadcast_to(column, (rows, head_ref.shape[2]))
-    pack_ref[:, cols:] = jnp.zeros((pack_ref.shape[0], pack_ref.shape[1] - cols), jnp.int16)
+        column_ref[k, here, :] = jnp.broadcast_to(column, (rows, column_ref.shape[2]))
 
     @pl.when(step == pl.num_programs(0) - 1)
     def _():
-        place = lax.broadcasted_iota(jnp.int32, (pack_ref.shape[0], head_ref.shape[1]), 0)
-        first, second = head_ref[0].T[:1], head_ref[1].T[:1]
-        last = pack_ref.shape[0] - 1
-        head = jnp.where(place == last - 1, first, jnp.where(place == last, second, 0.0))
-        pack_ref[:, cols:] = whole_number(head)
+        for k in range(2):
+            unit_ref[k : k + 1, :] = column_ref[k].T[:1]
 
 
 def prepare(momentum, grad, basis, share):
@@ -113,18 +109,20 @@
     width = share if share % 128 == 0 else cols
     steps = 2 if basis.shape[0] % 32 == 0 else 1
     wide = pl.BlockSpec((rows // steps, cols), lambda i: (i, 0))
-    ranks = basis.shape[0] // steps
+    narrow = pl.BlockSpec((basis.shape[0] // steps, cols), lambda i: (i, 0))
     return pl.pallas_call(
         prepare_kernel,
         grid=(steps,),
-        in_specs=[wide, wide, pl.BlockSpec((ranks, cols), lambda i: (i, 0))],
+        in_specs=[wide, wide, narrow],
         out_specs=[
-            pl.BlockSpec((ranks, cols + rows), lambda i: (i, 0)),
+            narrow,
             pl.BlockSpec((cols // width, rows // steps, width), lambda i: (0, i, 0)),
+            pl.BlockSpec((2, rows), lambda i: (0, 0)),
         ],
         out_shape=[
-            jax.ShapeDtypeStruct((basis.shape[0], cols + rows), jnp.int16),
+            jax.ShapeDtypeStruct(basis.shape, jnp.int16),
             jax.ShapeDtypeStruct((cols // width, rows, width), jnp.int16),
+            jax.ShapeDtypeStruct((2, rows), jnp.float32),
         ],
         scratch_shapes=[pltpu.VMEM((2, rows, 128), jnp.float32)],
         compiler_params=STREAM,
@@ -174,7 +172,7 @@
     )(momentum, grad, codes)
 
 
-def pack_kernel(perm_ref, *refs):
+def pack_kernel(perm_ref, unit_ref, *refs):
     part_refs, out_ref = refs[:-1], refs[-1]
     rows, rank = part_refs[0].shape
     blocks = perm_ref.shape[0]
@@ -195,23 +193,24 @@
     low = jnp.minimum(jnp.floor((value - high) * 256.0 + 0.5), 127.0)
     half = rows // 2
     out_ref[rows : rows + half] = whole_number(low[:half] * 256.0 + (low[half:] + 128.0))
-    set_head(out_ref.at[rows + half :], exponent, mantissa)
-
-
-def pack(perm, parts):
+    units = jnp.concatenate([unit_ref[...], jnp.zeros((2, rank - rows), jnp.float32)], axis=1)
+    set_head(out_ref.at[rows + half :], exponent, mantissa, units[:1], units[1:])
+
+
+def pack(perm, units, parts):
     rows, rank = parts[0].shape
     return pl.pallas_call(
         pack_kernel,
         grid_spec=pltpu.PrefetchScalarGridSpec(
             num_scalar_prefetch=1,
             grid=(1,),
-            in_specs=[whole(x) for x in parts],
+            in_specs=[whole(x) for x in (units, *parts)],
             out_specs=pl.BlockSpec((rows + rows // 2 + HEAD, rank), lambda *_: (0, 0)),
         ),
         out_shape=jax.ShapeDtypeStruct((rows + rows // 2 + HEAD, rank), jnp.int16),
         compiler_params=PARAMS,
         cost_estimate=pl.CostEstimate(flops=12 * rows * rank * rank, bytes_accessed=rank * rank * 4, transcendentals=0),
-    )(perm, *parts)
+    )(perm, units, *parts)
 
 
 def spread(row):
@@ -341,7 +340,7 @@
 def factor(codes):
     devices, size, rank = codes.shape
     rows = (size - HEAD) * 2 // 3
-    group = 256 // rows
+    group = min(devices, max(1, 1024 // rows))
     return pl.pallas_call(
         factor_kernel,
         grid=(devices // group,),
@@ -364,7 +363,7 @@
     )(codes)
 
 
-def encode_kernel(place_ref, source_ref, turned_ref, unit_ref, inverse_ref, own_ref, code_ref, ortho_ref, mixed_ref):
+def encode_kernel(place_ref, source_ref, turned_ref, head_ref, inverse_ref, own_ref, code_ref, ortho_ref, mixed_ref):
     def times(a, b):
         return jnp.dot(a, b, preferred_element_type=jnp.float32)
 
@@ -373,7 +372,11 @@
 
     rank = turned_ref.shape[0]
     source_high, source_low = halves(source_ref[...].astype(jnp.int32).astype(jnp.float32))
-    scaled_high, scaled_low = halves(turned_ref[...] * unit_ref[...])
+    head = head_ref[...].astype(jnp.int32).astype(jnp.float32)
+    devices = head.shape[0]
+    rows = turned_ref.shape[1] // devices
+    unit = jnp.concatenate([unit_of(head[k, 2:3, :rows], head[k, 3:4, :rows]) for k in range(devices)], axis=1)
+    scaled_high, scaled_low = halves(turned_ref[...] * unit)
     most = times(jnp.concatenate([scaled_high, scaled_low], axis=0), source_high)
     part = most[:rank] + (most[rank:] + times(scaled_high, source_low))
     first, last = pl.program_id(0) == 0, pl.program_id(0) == pl.num_programs(0) - 1
@@ -402,10 +405,11 @@
         set_head(code_ref.at[rows:], exponent, mantissa, square_exponent, square_high, square_low)
 
 
-def encode(place, source, turned, unit, inverse_low, rows):
+def encode(place, source, turned, packed, inverse_low, rows):
     total, share = source.shape
     rank = turned.shape[0]
-    block = min(512, total)
+    block = min(1024, total)
+    size = packed.shape[1]
     return pl.pallas_call(
         encode_kernel,
         grid_spec=pltpu.PrefetchScalarGridSpec(
@@ -414,7 +418,7 @@
             in_specs=[
                 pl.BlockSpec((block, share), lambda i, place: (i, 0)),
                 pl.BlockSpec((rank, block), lambda i, place: (0, i)),
-                pl.BlockSpec((1, block), lambda i, place: (0, i)),
+                pl.BlockSpec((block // rows, HEAD, rank), lambda i, place: (i, size // HEAD - 1, 0)),
                 whole(inverse_low),
                 pl.BlockSpec((rank, rows), lambda i, place: (0, place[0])),
             ],
@@ -432,7 +436,7 @@
         cost_estimate=pl.CostEstimate(
             flops=6 * total * share * rank, bytes_accessed=total * (share * 2 + rank * 4), transcendentals=0
         ),
-    )(place, source, turned, unit, inverse_low, turned)
+    )(place, source, turned, packed, inverse_low, turned)
 
 
 def decode(code_ref):
@@ -478,7 +482,7 @@
     rows, cols = momentum.shape
     shares, share, rank = codes.shape
     share -= HEAD
-    group = max(1, min(1024 // share, shares))
+    group = max(1, min(2048 // share, shares))
     block = group * share
     wide = pl.BlockSpec((rows, block), lambda i: (0, i))
     tall = pl.BlockSpec((block, rank), lambda i: (i, 0))
@@ -522,23 +526,21 @@
     row_total, col_total = rows * num_blocks, cols * num_cols
     share = cols // num_blocks
 
-    basis, codes = prepare(momentum, grad, q_stored, share)
+    basis, codes, units = prepare(momentum, grad, q_stored, share)
     codes = codes.reshape(-1, rows, codes.shape[2] // share, share).swapaxes(1, 2).reshape(num_blocks, rows, share)
     basis = lax.all_gather(basis, "fsdp", axis=0, tiled=True)
     codes, basis = lax.optimization_barrier((codes, basis))
     codes = lax.all_to_all(codes, "fsdp", split_axis=0, concat_axis=0).reshape(row_total, share)
-    head = basis.reshape(num_blocks, block_rows, cols + rows)[:, -2:, cols:].astype(jnp.float32)
-    unit = unit_of(head[:, 0], head[:, 1]).reshape(1, row_total)
 
     near, step = project(momentum, grad, basis), 1
     while 4 * step < num_cols:
         near = near + exchange(near, "tp", step)
         step *= 2
     parts = [near] + [exchange(near, "tp", k) for k in range(step, num_cols, step)]
-    packed = lax.all_gather(pack(perm, parts), "fsdp", axis=0)
+    packed = lax.all_gather(pack(perm, units, parts), "fsdp", axis=0)
     packed, codes = lax.optimization_barrier((packed, codes))
     turned, inverse_low = factor(packed)
-    code, orthonormal = encode(lax.axis_index("fsdp").reshape(1), codes, turned, unit, inverse_low, rows)
+    code, orthonormal = encode(lax.axis_index("fsdp").reshape(1), codes, turned, packed, inverse_low, rows)
     gathered = lax.all_gather(code, "fsdp", axis=0)
     head = gathered[:, share : share + 5].astype(jnp.float32)
     parts = (head[:, 3] + head[:, 4] * (1.0 / 16384.0)) * jnp.exp2(head[:, 2] - 13.0)

time: 118 us -> 116 us (0.983)
  Pallas kernels: 28.7 us -> 27 us
  transfers between devices with their start and end apart: 7 -> 7, of which waited for: 3 -> 3; matrix products, arithmetic and copies ran while one was open for 1% -> 0% of each run, Pallas kernels for 8% -> 7%
where the time goes in v14:
time: 116 us
  blocking collectives  70.2 us (61%)
  Pallas kernels  27 us (23%)
  starting transfers between devices  10.7 us (9%)
  waiting for transfers between devices  7.52 us (6%)
    all_gather x1, blocking collectives, on_device(): basis = lax.all_gather(basis, 'fsdp', axis=0, tiled=True)  26.1 us
    all_gather x1, blocking collectives, on_device(): gathered = lax.all_gather(code, 'fsdp', axis=0)  23.8 us
    all_gather x1, blocking collectives, on_device(): packed = lax.all_gather(pack(perm, units, parts), 'fsdp', axis=0)  20.3 us
    pallas_call x1, Pallas kernels, factor(): pl.pallas_call(factor_kernel, grid=(devices // group,), in_specs=[pl.Bloc...  9.57 us
    ppermute x6, waiting for transfers between devices, exchange(): lax.ppermute(x, axis, [(i, i ^ k) for i in range(lax.axis_size(axis))])  7.51 us
    ppermute x6, starting transfers between devices, exchange(): lax.ppermute(x, axis, [(i, i ^ k) for i in range(lax.axis_size(axis))])  7.1 us
    pallas_call x1, Pallas kernels, project(): pl.pallas_call(project_kernel, grid=(cols // block,), in_specs=[wide, wid...  4.86 us
    all_to_all x1, starting transfers between devices, on_device(): lax.all_to_all(codes, 'fsdp', split_axis=0, concat_axis=0)  3.56 us
  transfers between devices with their start and end apart: 7, of which 3 were waited for; matrix products, arithmetic and copies ran while one was open for 0% of the time, Pallas kernels for 7%

profile of v14, /device:TPU:0, one launch (start us, length us, event | category | flops | bytes accessed | tf_op | source)
XLA Modules:
  0.0 116.1 jit_solution(10206146955178581938)
XLA Ops:
  0.6 3.5 %shard_map.67 = (s16[32,4096]{1,0:T(8,128)(2,1)}, s16[8,128,512]{2,1,0:T(8,128)(2,1)}, f32[2,128]{1,0:T(2,128)}) custom-call(f32[128,4096]{1,0:T(8,128)} %momentum_ref.5, bf16[128,4096]{1,0:T(8,128)(2,1)} %grad_ref.5, bf16[32,4096]{1,0:T(8,128)(2,1)} %basis_ref.1), custom_call_target="tpu_custom_call" | custom-call | flops 5242880 | bytes 4194304 | tf_op jit(solution)/shard_map/pallas_call | solution.py:113
  4.2 26.1 %all-gather.4.code_ref = s16[256,4096]{1,0:T(8,128)(2,1)} all-gather(s16[32,4096]{1,0:T(8,128)(2,1)} %get-tuple-element.18), channel_id=1, replica_groups=mesh['fsdp'=8,'tp'=4] {'fsdp'}, dimensions={0}, use_global_device_ids=true | all-gather | bytes 2359296 | tf_op jit(solution)/shard_map/all_gather | solution.py:531
  30.2 3.6 %all-to-all-start = ((s16[8,128,512]{2,1,0:T(8,128)(2,1)}), s16[8,128,512]{2,1,0:T(8,128)(2,1)S(1)}, u32[]{:S(2)}, u32[]{:S(2)}) async-start(s16[8,128,512]{2,1,0:T(8,128)(2,1)} %get-tuple-element.20), calls=%async_computation | async-start | bytes 2097152 | tf_op jit(solution)/shard_map/all_to_all | solution.py:533
  33.8 0.0 copy-start.2
  33.8 0.0 copy-start.3
  33.8 4.9 %shard_map.68.refs_0_ = f32[128,256]{1,0:T(8,128)S(1)} custom-call(f32[128,4096]{1,0:T(8,128)} %momentum_ref.5, bf16[128,4096]{1,0:T(8,128)(2,1)} %grad_ref.5, s16[256,4096]{1,0:T(8,128)(2,1)} %all-gather.4.code_ref), custom_call_target="tpu_custom_call" | custom-call | flops 536870912 | bytes 5242880 | tf_op jit(solution)/shard_map/pallas_call | solution.py:162
  38.7 1.6 %collective-permute-start = (f32[128,256]{1,0:T(8,128)S(1)}, f32[128,256]{1,0:T(8,128)S(1)}, u32[]{:S(2)}, u32[]{:S(2)}) collective-permute-start(f32[128,256]{1,0:T(8,128)S(1)} %shard_map.68.refs_0_), channel_id=1, source_target_pairs={{0,1},{1,0},{2,3},{3,2},{4,5},{5,4},{6,7},{7,6},{8,9},{9,8},{10,11... | collective-permute-start | bytes 393224 | tf_op jit(solution)/shard_map/ppermute | solution.py:29
  40.2 1.5 %collective-permute-start.1 = (f32[128,256]{1,0:T(8,128)S(1)}, f32[128,256]{1,0:T(8,128)S(1)}, u32[]{:S(2)}, u32[]{:S(2)}) collective-permute-start(f32[128,256]{1,0:T(8,128)S(1)} %shard_map.68.refs_0_), channel_id=1, source_target_pairs={{0,2},{1,3},{2,0},{3,1},{4,6},{5,7},{6,4},{7,5},{8,10},{9,11},{10,... | collective-permute-start | bytes 393224 | tf_op jit(solution)/shard_map/ppermute | solution.py:29
  41.8 0.5 collective-permute-start.2
  42.2 2.7 %collective-permute-done.refs_1_ = f32[128,256]{1,0:T(8,128)S(1)} collective-permute-done((f32[128,256]{1,0:T(8,128)S(1)}, f32[128,256]{1,0:T(8,128)S(1)}, u32[]{:S(2)}, u32[]{:S(2)}) %collective-permute-start) | collective-permute-done | bytes 131104 | tf_op jit(solution)/shard_map/ppermute | solution.py:29
  45.0 3.7 %collective-permute-done.1.refs_2_ = f32[128,256]{1,0:T(8,128)S(1)} collective-permute-done((f32[128,256]{1,0:T(8,128)S(1)}, f32[128,256]{1,0:T(8,128)S(1)}, u32[]{:S(2)}, u32[]{:S(2)}) %collective-permute-start.1) | collective-permute-done | bytes 131104 | tf_op jit(solution)/shard_map/ppermute | solution.py:29
  48.6 0.0 collective-permute-done.2.refs_3_
  48.6 0.0 copy-done.2
  48.6 0.0 copy-done.3
  48.6 0.9 shard_map.69
  49.6 20.3 %all-gather = s16[1664,256]{1,0:T(8,128)(2,1)S(1)} all-gather(s16[208,256]{1,0:T(8,128)(2,1)S(1)} %shard_map.69), channel_id=2, replica_groups=mesh['fsdp'=8,'tp'=4] {'fsdp'}, dimensions={0}, use_global_device_ids=true | all-gather | bytes 958464 | tf_op jit(solution)/shard_map/all_gather | solution.py:540
  69.9 0.0 all-to-all-done
  69.9 9.6 %shard_map.70 = (f32[256,1024]{1,0:T(8,128)S(1)}, f32[256,256]{1,0:T(8,128)S(1)}) custom-call(s16[8,208,256]{2,1,0:T(8,128)(2,1)S(1)} %bitcast.9), custom_call_target="tpu_custom_call" | custom-call | flops 805306368 | bytes 1703936 | tf_op jit(solution)/shard_map/pallas_call | solution.py:344
  79.5 0.0 copy-start.1
  79.5 2.4 %shard_map.71 = (s16[528,256]{1,0:T(8,128)(2,1)S(1)}, f32[128,256]{1,0:T(8,128)S(1)}) custom-call(s32[1]{0:T(128)} %bitcast.place_ref, s16[1024,512]{1,0:T(8,128)(2,1)S(1)} %bitcast.8, f32[256,1024]{1,0:T(8,128)S(1)} %get-tuple-element.23.turned_ref.own_ref, s16[8,208,256]{2,1,0:T(8,128)(2,1)S(1)} %bitcast.10, f32[256,256]{1,0:T(8,128)S(1)} %get-tuple-element.24.inverse_ref, ...), custom_call_target="tpu_custom_call" | custom-call | flops 805306368 | bytes 2097152 | tf_op jit(solution)/shard_map/pallas_call | solution.py:413
  81.9 0.0 copy-start
  81.9 23.8 %all-gather.5 = s16[4224,256]{1,0:T(8,128)(2,1)S(1)} all-gather(s16[528,256]{1,0:T(8,128)(2,1)S(1)} %get-tuple-element.25), channel_id=3, replica_groups=mesh['fsdp'=8,'tp'=4] {'fsdp'}, dimensions={0}, use_global_device_ids=true | all-gather | bytes 2433024 | tf_op jit(solution)/shard_map/all_gather | solution.py:544
  105.7 0.1 fusion.4
  105.8 1.6 %collective-permute-start.3 = (f32[1,256]{1,0:T(1,128)S(1)}, f32[1,256]{1,0:T(1,128)S(1)}, u32[]{:S(2)}, u32[]{:S(2)}) collective-permute-start(f32[1,256]{1,0:T(1,128)S(1)} %bitcast.11), channel_id=1, source_target_pairs={{0,1},{1,0},{2,3},{3,2},{4,5},{5,4},{6,7},{7,6},{8,9},{9,8},{10,11... | collective-permute-start | bytes 3080 | tf_op jit(solution)/shard_map/ppermute | solution.py:29
  107.3 1.5 %collective-permute-start.4 = (f32[1,256]{1,0:T(1,128)S(1)}, f32[1,256]{1,0:T(1,128)S(1)}, u32[]{:S(2)}, u32[]{:S(2)}) collective-permute-start(f32[1,256]{1,0:T(1,128)S(1)} %bitcast.12), channel_id=1, source_target_pairs={{0,2},{1,3},{2,0},{3,1},{4,6},{5,7},{6,4},{7,5},{8,10},{9,11},{10,... | collective-permute-start | bytes 3080 | tf_op jit(solution)/shard_map/ppermute | solution.py:29
  108.8 0.5 collective-permute-start.5
  109.3 0.0 copy-done.1
  109.3 0.0 copy-done
  109.3 2.9 %shard_map.72 = f32[128,4096]{1,0:T(8,128)} custom-call(f32[128,4096]{1,0:T(8,128)S(1)} %copy-done, bf16[128,4096]{1,0:T(8,128)(2,1)S(1)} %copy-done.1, s16[8,528,256]{2,1,0:T(8,128)(2,1)S(1)} %bitcast.6, f32[128,256]{1,0:T(8,128)S(1)} %get-tuple-element.26.ortho_ref), custom_call_target="tpu_custom_call" | custom-call | flops 805306368 | bytes 7340032 | tf_op jit(solution)/shard_map/pallas_call | solution.py:492
  112.2 0.0 collective-permute-done.3
  112.2 0.0 collective-permute-done.4
  112.2 1.1 collective-permute-done.5
  113.3 2.8 %shard_map.73 = (f32[4096,256]{1,0:T(8,128)}, bf16[128,4096]{1,0:T(8,128)(2,1)}) custom-call(s16[8,528,256]{2,1,0:T(8,128)(2,1)S(1)} %bitcast.7, f32[128,256]{1,0:T(8,128)S(1)} %get-tuple-element.26.ortho_ref, f32[1,256]{1,0:T(1,128)S(1)} %add_rsqrt_fusion.scale_ref), custom_call_target="tpu_custom_call" | custom-call | flops 805306368 | bytes 7340032 | tf_op jit(solution)/shard_map/pallas_call | solution.py:504
  (2 shorter events, 0.0 us)
Async XLA Ops:
  30.2 39.7 %all-to-all-start = ((s16[8,128,512]{2,1,0:T(8,128)(2,1)}), s16[8,128,512]{2,1,0:T(8,128)(2,1)S(1)}, u32[]{:S(2)}, u32[]{:S(2)}) async-start(s16[8,128,512]{2,1,0:T(8,128)(2,1)} %get-tuple-element.20), calls=%async_computation | async-start | bytes 2097152 | tf_op jit(solution)/shard_map/all_to_all | solution.py:533
  33.8 14.8 %copy-start.2 = (f32[2,128]{1,0:T(2,128)S(1)}, f32[2,128]{1,0:T(2,128)}, u32[]{:S(2)}) copy-start(f32[2,128]{1,0:T(2,128)} %get-tuple-element.16.unit_ref) | copy-start | bytes 3076
  33.8 14.8 %copy-start.3 = (s32[8]{0:T(128)S(1)}, s32[8]{0:T(128)}, u32[]{:S(2)}) copy-start(s32[8]{0:T(128)} %perm_ref.1) | copy-start | bytes 100
  38.7 6.3 %collective-permute-start = (f32[128,256]{1,0:T(8,128)S(1)}, f32[128,256]{1,0:T(8,128)S(1)}, u32[]{:S(2)}, u32[]{:S(2)}) collective-permute-start(f32[128,256]{1,0:T(8,128)S(1)} %shard_map.68.refs_0_), channel_id=1, source_target_pairs={{0,1},{1,0},{2,3},{3,2},{4,5},{5,4},{6,7},{7,6},{8,9},{9,8},{10,11... | collective-permute-start | bytes 393224 | tf_op jit(solution)/shard_map/ppermute | solution.py:29
  40.2 8.4 %collective-permute-start.1 = (f32[128,256]{1,0:T(8,128)S(1)}, f32[128,256]{1,0:T(8,128)S(1)}, u32[]{:S(2)}, u32[]{:S(2)}) collective-permute-start(f32[128,256]{1,0:T(8,128)S(1)} %shard_map.68.refs_0_), channel_id=1, source_target_pairs={{0,2},{1,3},{2,0},{3,1},{4,6},{5,7},{6,4},{7,5},{8,10},{9,11},{10,... | collective-permute-start | bytes 393224 | tf_op jit(solution)/shard_map/ppermute | solution.py:29
  41.8 6.9 %collective-permute-start.2 = (f32[128,256]{1,0:T(8,128)S(1)}, f32[128,256]{1,0:T(8,128)S(1)}, u32[]{:S(2)}, u32[]{:S(2)}) collective-permute-start(f32[128,256]{1,0:T(8,128)S(1)} %shard_map.68.refs_0_), channel_id=1, source_target_pairs={{0,3},{1,2},{2,1},{3,0},{4,7},{5,6},{6,5},{7,4},{8,11},{9,10},{10,... | collective-permute-start | bytes 393224 | tf_op jit(solution)/shard_map/ppermute | solution.py:29
  79.5 29.8 %copy-start.1 = (bf16[128,4096]{1,0:T(8,128)(2,1)S(1)}, bf16[128,4096]{1,0:T(8,128)(2,1)}, u32[]{:S(2)}) copy-start(bf16[128,4096]{1,0:T(8,128)(2,1)} %grad_ref.5) | copy-start | bytes 3145732
  81.9 27.4 %copy-start = (f32[128,4096]{1,0:T(8,128)S(1)}, f32[128,4096]{1,0:T(8,128)}, u32[]{:S(2)}) copy-start(f32[128,4096]{1,0:T(8,128)} %momentum_ref.5) | copy-start | bytes 6291460
  105.8 6.4 %collective-permute-start.3 = (f32[1,256]{1,0:T(1,128)S(1)}, f32[1,256]{1,0:T(1,128)S(1)}, u32[]{:S(2)}, u32[]{:S(2)}) collective-permute-start(f32[1,256]{1,0:T(1,128)S(1)} %bitcast.11), channel_id=1, source_target_pairs={{0,1},{1,0},{2,3},{3,2},{4,5},{5,4},{6,7},{7,6},{8,9},{9,8},{10,11... | collective-permute-start | bytes 3080 | tf_op jit(solution)/shard_map/ppermute | solution.py:29
  107.3 4.9 %collective-permute-start.4 = (f32[1,256]{1,0:T(1,128)S(1)}, f32[1,256]{1,0:T(1,128)S(1)}, u32[]{:S(2)}, u32[]{:S(2)}) collective-permute-start(f32[1,256]{1,0:T(1,128)S(1)} %bitcast.12), channel_id=1, source_target_pairs={{0,2},{1,3},{2,0},{3,1},{4,6},{5,7},{6,4},{7,5},{8,10},{9,11},{10,... | collective-permute-start | bytes 3080 | tf_op jit(solution)/shard_map/ppermute | solution.py:29
  108.8 4.5 %collective-permute-start.5 = (f32[1,256]{1,0:T(1,128)S(1)}, f32[1,256]{1,0:T(1,128)S(1)}, u32[]{:S(2)}, u32[]{:S(2)}) collective-permute-start(f32[1,256]{1,0:T(1,128)S(1)} %bitcast.13), channel_id=1, source_target_pairs={{0,3},{1,2},{2,1},{3,0},{4,7},{5,6},{6,5},{7,4},{8,11},{9,10},{10,... | collective-permute-start | bytes 3080 | tf_op jit(solution)/shard_map/ppermute | solution.py:29

commit v15 on v14

--- a/solution.py
+++ b/solution.py
@@ -23,24 +23,6 @@
 def halves(x):
     high = x.astype(jnp.bfloat16)
     return high, (x - high.astype(jnp.float32)).astype(jnp.bfloat16)
-
-
-def exchange(x, axis, k):
-    return lax.ppermute(x, axis, [(i, i ^ k) for i in range(lax.axis_size(axis))])
-
-
-def butterfly_sum(x, axis, step=1):
-    while step < lax.axis_size(axis):
-        x = x + exchange(x, axis, step)
-        step *= 2
-    return x
-
-
-def quad_sum(x, axis, step=1):
-    if lax.axis_size(axis) != 4 * step:
-        return butterfly_sum(x, axis, step)
-    near, far, across = [exchange(x, axis, k * step) for k in range(1, 4)]
-    return (x + near) + (far + across)
 
 
 def whole(x):
@@ -130,7 +112,7 @@
     )(momentum, grad, basis)
 
 
-def project_kernel(momentum_ref, grad_ref, code_ref, out_ref):
+def project_kernel(momentum_ref, grad_ref, code_ref, out_ref, total_ref):
     code = code_ref[...].astype(jnp.int32)
     power = jnp.exp2(((code >> 7) & 255).astype(jnp.float32) - 134.0)
     value = ((code & 127) | 128).astype(jnp.float32) * power
@@ -147,14 +129,19 @@
 
     @pl.when(pl.program_id(0) == 0)
     def _():
-        out_ref[...] = part
+        total_ref[...] = part
 
     @pl.when(pl.program_id(0) > 0)
     def _():
-        out_ref[...] += part
-
-
-def project(momentum, grad, codes):
+        total_ref[...] += part
+
+    @pl.when(pl.program_id(0) == pl.num_programs(0) - 1)
+    def _():
+        for k in range(out_ref.shape[0]):
+            out_ref[k] = total_ref[...]
+
+
+def project(momentum, grad, codes, copies):
     rows, cols = momentum.shape
     rank = codes.shape[0]
     block = min(1024, cols)
@@ -163,8 +150,9 @@
         project_kernel,
         grid=(cols // block,),
         in_specs=[wide, wide, pl.BlockSpec((rank, block), lambda i: (0, i))],
-        out_specs=pl.BlockSpec((rows, rank), lambda i: (0, 0)),
-        out_shape=jax.ShapeDtypeStruct((rows, rank), jnp.float32),
+        out_specs=pl.BlockSpec((copies, rows, rank), lambda i: (0, 0, 0)),
+        out_shape=jax.ShapeDtypeStruct((copies, rows, rank), jnp.float32),
+        scratch_shapes=[pltpu.VMEM((rows, rank), jnp.float32)],
         compiler_params=FLOW,
         cost_estimate=pl.CostEstimate(
             flops=4 * rows * cols * rank, bytes_accessed=rows * cols * 6 + rank * cols * 2, transcendentals=rank * cols
@@ -172,9 +160,8 @@
     )(momentum, grad, codes)
 
 
-def pack_kernel(perm_ref, unit_ref, *refs):
-    part_refs, out_ref = refs[:-1], refs[-1]
-    rows, rank = part_refs[0].shape
+def pack_kernel(perm_ref, unit_ref, part_ref, out_ref):
+    _, rows, rank = part_ref.shape
     blocks = perm_ref.shape[0]
     size = rank // blocks
     stored = lax.broadcasted_iota(jnp.int32, (rank, rank), 0)
@@ -182,7 +169,7 @@
     for s in range(blocks):
         target = jnp.where(stored // size == s, perm_ref[s] * size + stored % size, target)
     order = (target == lax.broadcasted_iota(jnp.int32, (rank, rank), 1)).astype(jnp.float32)
-    parts = [ref[...] for ref in part_refs]
+    parts = [part_ref[k] for k in range(part_ref.shape[0])]
     while len(parts) > 1:
         parts = [parts[k] + parts[k + 1] for k in range(0, len(parts), 2)]
     total = jnp.dot(parts[0], order, precision=HIGH, preferred_element_type=jnp.float32)
@@ -198,19 +185,19 @@
 
 
 def pack(perm, units, parts):
-    rows, rank = parts[0].shape
+    _, rows, rank = parts.shape
     return pl.pallas_call(
         pack_kernel,
         grid_spec=pltpu.PrefetchScalarGridSpec(
             num_scalar_prefetch=1,
             grid=(1,),
-            in_specs=[whole(x) for x in (units, *parts)],
+            in_specs=[whole(units), whole(parts)],
             out_specs=pl.BlockSpec((rows + rows // 2 + HEAD, rank), lambda *_: (0, 0)),
         ),
         out_shape=jax.ShapeDtypeStruct((rows + rows // 2 + HEAD, rank), jnp.int16),
         compiler_params=PARAMS,
         cost_estimate=pl.CostEstimate(flops=12 * rows * rank * rank, bytes_accessed=rank * rank * 4, transcendentals=0),
-    )(perm, units, *parts)
+    )(perm, units, parts)
 
 
 def spread(row):
@@ -532,11 +519,7 @@
     codes, basis = lax.optimization_barrier((codes, basis))
     codes = lax.all_to_all(codes, "fsdp", split_axis=0, concat_axis=0).reshape(row_total, share)
 
-    near, step = project(momentum, grad, basis), 1
-    while 4 * step < num_cols:
-        near = near + exchange(near, "tp", step)
-        step *= 2
-    parts = [near] + [exchange(near, "tp", k) for k in range(step, num_cols, step)]
+    parts = lax.all_to_all(project(momentum, grad, basis, num_cols), "tp", split_axis=0, concat_axis=0)
     packed = lax.all_gather(pack(perm, units, parts), "fsdp", axis=0)
     packed, codes = lax.optimization_barrier((packed, codes))
     turned, inverse_low = factor(packed)
@@ -544,7 +527,8 @@
     gathered = lax.all_gather(code, "fsdp", axis=0)
     head = gathered[:, share : share + 5].astype(jnp.float32)
     parts = (head[:, 3] + head[:, 4] * (1.0 / 16384.0)) * jnp.exp2(head[:, 2] - 13.0)
-    squares = quad_sum(jnp.sum(parts, axis=0, keepdims=True), "tp")
+    squares = jnp.broadcast_to(jnp.sum(parts, axis=0), (num_cols, 1, rank_total))
+    squares = jnp.sum(lax.all_to_all(squares, "tp", split_axis=0, concat_axis=0), axis=0)
     scale = lax.rsqrt(squares / col_total + EPSILON)
     return tuple(finish(momentum, grad, gathered, orthonormal, scale, math.sqrt(row_total / rank_total)))
 

time: 116 us -> 138 us (1.19)
  blocking collectives: 70.2 us -> 97.5 us
  waiting for transfers between devices: 7.52 us -> 0.16 us
  local copies, waits for them, and re-layouts: 0.03 us -> 5.17 us
  starting transfers between devices: 10.7 us -> 6.81 us
    all_gather x1, blocking collectives: 20.3 us -> 35.1 us  [on_device(): packed = lax.all_gather(pack(perm, units, parts), 'fsdp', axis=0)]
    all_to_all x0 -> x1, blocking collectives: none -> 12.6 us  [on_device(): lax.all_to_all(project(momentum, grad, basis, num_cols), 'tp', split_axis...]
    ppermute x6 -> x0, waiting for transfers between devices: 7.51 us -> none  [exchange(): lax.ppermute(x, axis, [(i, i ^ k) for i in range(lax.axis_size(axis))])]
    ppermute x6 -> x0, starting transfers between devices: 7.1 us -> none  [exchange(): lax.ppermute(x, axis, [(i, i ^ k) for i in range(lax.axis_size(axis))])]
    unnamed x8 -> x14, local copies, waits for them, and re-layouts: 0.03 us -> 4.57 us
    all_to_all x0 -> x1, starting transfers between devices: none -> 3.25 us  [on_device(): lax.all_to_all(squares, 'tp', split_axis=0, concat_axis=0)]
  transfers between devices with their start and end apart: 7 -> 2, of which waited for: 3 -> 1; matrix products, arithmetic and copies ran while one was open for 0% -> 0% of each run, Pallas kernels for 7% -> 3%
where the time goes in v15:
time: 138 us; the launch traced here: 137 us
  blocking collectives  97.5 us (71%)
  Pallas kernels  26.9 us (19%)
  starting transfers between devices  6.81 us (5%)
  local copies, waits for them, and re-layouts  5.17 us (4%)
    all_gather x1, blocking collectives, on_device(): packed = lax.all_gather(pack(perm, units, parts), 'fsdp', axis=0)  35.1 us
    all_gather x1, blocking collectives, on_device(): basis = lax.all_gather(basis, 'fsdp', axis=0, tiled=True)  26.1 us
    all_gather x1, blocking collectives, on_device(): gathered = lax.all_gather(code, 'fsdp', axis=0)  23.8 us
    all_to_all x1, blocking collectives, on_device(): lax.all_to_all(project(momentum, grad, basis, num_cols), 'tp', split_axis...  12.6 us
    pallas_call x1, Pallas kernels, factor(): pl.pallas_call(factor_kernel, grid=(devices // group,), in_specs=[pl.Bloc...  9.57 us
    pallas_call x1, Pallas kernels, project(): pl.pallas_call(project_kernel, grid=(cols // block,), in_specs=[wide, wid...  4.89 us
    unnamed x14, local copies, waits for them, and re-layouts  4.57 us
    all_to_all x1, starting transfers between devices, on_device(): lax.all_to_all(codes, 'fsdp', split_axis=0, concat_axis=0)  3.56 us
  transfers between devices with their start and end apart: 2, of which 1 were waited for; matrix products, arithmetic and copies ran while one was open for 0% of the time, Pallas kernels for 3%

profile of v15, /device:TPU:0, one launch (start us, length us, event | category | flops | bytes accessed | tf_op | source)
XLA Modules:
  0.0 137.5 jit_solution(2488315773490098199)
XLA Ops:
  0.6 3.5 %shard_map.67 = (s16[32,4096]{1,0:T(8,128)(2,1)}, s16[8,128,512]{2,1,0:T(8,128)(2,1)}, f32[2,128]{1,0:T(2,128)}) custom-call(f32[128,4096]{1,0:T(8,128)} %momentum_ref.5, bf16[128,4096]{1,0:T(8,128)(2,1)} %grad_ref.5, bf16[32,4096]{1,0:T(8,128)(2,1)} %basis_ref.1), custom_call_target="tpu_custom_call" | custom-call | flops 5242880 | bytes 4194304 | tf_op jit(solution)/shard_map/pallas_call | solution.py:95
  4.2 26.1 %all-gather.4.code_ref = s16[256,4096]{1,0:T(8,128)(2,1)} all-gather(s16[32,4096]{1,0:T(8,128)(2,1)} %get-tuple-element.18), channel_id=1, replica_groups=mesh['fsdp'=8,'tp'=4] {'fsdp'}, dimensions={0}, use_global_device_ids=true | all-gather | bytes 2359296 | tf_op jit(solution)/shard_map/all_gather | solution.py:518
  30.2 4.9 %shard_map.68 = f32[4,128,256]{2,1,0:T(8,128)S(1)} custom-call(f32[128,4096]{1,0:T(8,128)} %momentum_ref.5, bf16[128,4096]{1,0:T(8,128)(2,1)} %grad_ref.5, s16[256,4096]{1,0:T(8,128)(2,1)} %all-gather.4.code_ref), custom_call_target="tpu_custom_call" | custom-call | flops 536870912 | bytes 5242880 | tf_op jit(solution)/shard_map/pallas_call | solution.py:149
  35.1 0.0 copy-start.5
  35.1 0.0 copy-start.6
  35.2 12.6 %all_to_all.15.part_ref = f32[4,128,256]{2,1,0:T(8,128)S(1)} all-to-all(f32[4,128,256]{2,1,0:T(8,128)S(1)} %shard_map.68), channel_id=1, replica_groups=mesh['fsdp'=8,'tp'=4] {'tp'}, dimensions={0} | all-to-all | bytes 1048576 | tf_op jit(solution)/shard_map/all_to_all | solution.py:522
  47.7 3.6 %all-to-all-start.1 = ((s16[8,128,512]{2,1,0:T(8,128)(2,1)}), s16[8,128,512]{2,1,0:T(8,128)(2,1)S(1)}, u32[]{:S(2)}, u32[]{:S(2)}) async-start(s16[8,128,512]{2,1,0:T(8,128)(2,1)} %get-tuple-element.20), calls=%async_computation.1 | async-start | bytes 2097152 | tf_op jit(solution)/shard_map/all_to_all | solution.py:520
  51.3 0.0 copy-done.5
  51.3 0.0 copy-done.6
  51.3 0.9 shard_map.69
  52.3 35.1 %all-gather = s16[1664,256]{1,0:T(8,128)(2,1)S(1)} all-gather(s16[208,256]{1,0:T(8,128)(2,1)S(1)} %shard_map.69), channel_id=2, replica_groups=mesh['fsdp'=8,'tp'=4] {'fsdp'}, dimensions={0}, use_global_device_ids=true | all-gather | bytes 958464 | tf_op jit(solution)/shard_map/all_gather | solution.py:523
  87.4 0.0 all-to-all-done.1
  87.4 9.6 %shard_map.70 = (f32[256,1024]{1,0:T(8,128)S(1)}, f32[256,256]{1,0:T(8,128)S(1)}) custom-call(s16[8,208,256]{2,1,0:T(8,128)(2,1)S(1)} %bitcast.9), custom_call_target="tpu_custom_call" | custom-call | flops 805306368 | bytes 1703936 | tf_op jit(solution)/shard_map/pallas_call | solution.py:331
  97.0 0.0 copy-start.1
  97.0 2.4 %shard_map.71 = (s16[528,256]{1,0:T(8,128)(2,1)S(1)}, f32[128,256]{1,0:T(8,128)S(1)}) custom-call(s32[1]{0:T(128)} %bitcast.place_ref, s16[1024,512]{1,0:T(8,128)(2,1)S(1)} %bitcast.8, f32[256,1024]{1,0:T(8,128)S(1)} %get-tuple-element.23.turned_ref.own_ref, s16[8,208,256]{2,1,0:T(8,128)(2,1)S(1)} %bitcast.10, f32[256,256]{1,0:T(8,128)S(1)} %get-tuple-element.24.inverse_ref, ...), custom_call_target="tpu_custom_call" | custom-call | flops 805306368 | bytes 2097152 | tf_op jit(solution)/shard_map/pallas_call | solution.py:400
  99.4 0.0 copy-start
  99.4 23.8 %all-gather.5 = s16[4224,256]{1,0:T(8,128)(2,1)S(1)} all-gather(s16[528,256]{1,0:T(8,128)(2,1)S(1)} %get-tuple-element.25), channel_id=3, replica_groups=mesh['fsdp'=8,'tp'=4] {'fsdp'}, dimensions={0}, use_global_device_ids=true | all-gather | bytes 2433024 | tf_op jit(solution)/shard_map/all_gather | solution.py:527
  123.2 0.0 copy-start.2
  123.2 1.3 copy-done.2
  124.5 0.1 fusion.4
  124.6 0.6 broadcast_in_dim.3
  125.2 3.2 %all-to-all-start.2 = ((f32[4,1,256]{2,1,0:T(1,128)}), f32[4,1,256]{2,1,0:T(1,128)S(1)}, u32[]{:S(2)}, u32[]{:S(2)}) async-start(f32[4,1,256]{2,1,0:T(1,128)} %broadcast_in_dim.3), calls=%async_computation.2 | async-start | bytes 8192 | tf_op jit(solution)/shard_map/all_to_all | solution.py:531
  128.4 0.0 copy-done.1
  128.4 0.0 copy-done
  128.4 0.0 copy-start.3
  128.5 1.6 %copy-done.3 = s16[4224,256]{1,0:T(8,128)(2,1)S(1)} copy-done((s16[4224,256]{1,0:T(8,128)(2,1)S(1)}, s16[4224,256]{1,0:T(8,128)(2,1)}, u32[]{:S(2)}) %copy-start.3) | copy-done | bytes 2162712
  130.1 2.9 %shard_map.72 = f32[128,4096]{1,0:T(8,128)} custom-call(f32[128,4096]{1,0:T(8,128)S(1)} %copy-done, bf16[128,4096]{1,0:T(8,128)(2,1)S(1)} %copy-done.1, s16[8,528,256]{2,1,0:T(8,128)(2,1)S(1)} %bitcast.6, f32[128,256]{1,0:T(8,128)S(1)} %get-tuple-element.26.ortho_ref), custom_call_target="tpu_custom_call" | custom-call | flops 805306368 | bytes 7340032 | tf_op jit(solution)/shard_map/pallas_call | solution.py:479
  132.9 0.2 all-to-all-done.2
  133.1 0.0 copy-start.4
  133.1 1.6 %copy-done.4 = s16[4224,256]{1,0:T(8,128)(2,1)S(1)} copy-done((s16[4224,256]{1,0:T(8,128)(2,1)S(1)}, s16[4224,256]{1,0:T(8,128)(2,1)}, u32[]{:S(2)}) %copy-start.4) | copy-done | bytes 2162712
  134.7 2.8 %shard_map.73 = (f32[4096,256]{1,0:T(8,128)}, bf16[128,4096]{1,0:T(8,128)(2,1)}) custom-call(s16[8,528,256]{2,1,0:T(8,128)(2,1)S(1)} %bitcast.7, f32[128,256]{1,0:T(8,128)S(1)} %get-tuple-element.26.ortho_ref, f32[1,256]{1,0:T(1,128)S(1)} %bitcast.11), custom_call_target="tpu_custom_call" | custom-call | flops 805306368 | bytes 7340032 | tf_op jit(solution)/shard_map/pallas_call | solution.py:491
  (3 shorter events, 0.0 us)
Async XLA Ops:
  35.1 16.2 %copy-start.5 = (f32[2,128]{1,0:T(2,128)S(1)}, f32[2,128]{1,0:T(2,128)}, u32[]{:S(2)}) copy-start(f32[2,128]{1,0:T(2,128)} %get-tuple-element.16.unit_ref) | copy-start | bytes 3076
  35.1 16.2 %copy-start.6 = (s32[8]{0:T(128)S(1)}, s32[8]{0:T(128)}, u32[]{:S(2)}) copy-start(s32[8]{0:T(128)} %perm_ref.1) | copy-start | bytes 100
  47.7 39.7 %all-to-all-start.1 = ((s16[8,128,512]{2,1,0:T(8,128)(2,1)}), s16[8,128,512]{2,1,0:T(8,128)(2,1)S(1)}, u32[]{:S(2)}, u32[]{:S(2)}) async-start(s16[8,128,512]{2,1,0:T(8,128)(2,1)} %get-tuple-element.20), calls=%async_computation.1 | async-start | bytes 2097152 | tf_op jit(solution)/shard_map/all_to_all | solution.py:520
  97.0 31.5 %copy-start.1 = (bf16[128,4096]{1,0:T(8,128)(2,1)S(1)}, bf16[128,4096]{1,0:T(8,128)(2,1)}, u32[]{:S(2)}) copy-start(bf16[128,4096]{1,0:T(8,128)(2,1)} %grad_ref.5) | copy-start | bytes 3145732
  99.4 29.1 %copy-start = (f32[128,4096]{1,0:T(8,128)S(1)}, f32[128,4096]{1,0:T(8,128)}, u32[]{:S(2)}) copy-start(f32[128,4096]{1,0:T(8,128)} %momentum_ref.5) | copy-start | bytes 6291460
  123.2 1.3 copy-start.2
  125.2 7.9 %all-to-all-start.2 = ((f32[4,1,256]{2,1,0:T(1,128)}), f32[4,1,256]{2,1,0:T(1,128)S(1)}, u32[]{:S(2)}, u32[]{:S(2)}) async-start(f32[4,1,256]{2,1,0:T(1,128)} %broadcast_in_dim.3), calls=%async_computation.2 | async-start | bytes 8192 | tf_op jit(solution)/shard_map/all_to_all | solution.py:531
  128.4 1.6 %copy-start.3 = (s16[4224,256]{1,0:T(8,128)(2,1)S(1)}, s16[4224,256]{1,0:T(8,128)(2,1)}, u32[]{:S(2)}) copy-start(s16[4224,256]{1,0:T(8,128)(2,1)} %copy-done.2) | copy-start | bytes 6488068
  133.1 1.6 %copy-start.4 = (s16[4224,256]{1,0:T(8,128)(2,1)S(1)}, s16[4224,256]{1,0:T(8,128)(2,1)}, u32[]{:S(2)}) copy-start(s16[4224,256]{1,0:T(8,128)(2,1)} %copy-done.2) | copy-start | bytes 6488068

commit v16 on v14

--- a/solution.py
+++ b/solution.py
@@ -82,16 +82,22 @@
     return whole_number(jnp.where(normal, jnp.where(value < 0.0, code - 32768.0, code), 0.0))
 
 
-def prepare_kernel(momentum_ref, grad_ref, basis_ref, basis_code_ref, code_ref, unit_ref, column_ref):
+def prepare_kernel(momentum_ref, grad_ref, basis_ref, basis_code_ref, *refs):
+    code_refs, (unit_ref, column_ref) = refs[:-2], refs[-2:]
     rows, cols = momentum_ref.shape
-    width = code_ref.shape[-1]
+    width = sum(ref.shape[-1] for ref in code_refs)
     spans = [slice(i, i + width) for i in range(0, cols, width)]
     combined = lambda span: momentum_ref[:, span] + grad_ref[:, span].astype(jnp.float32)
     top = functools.reduce(jnp.maximum, [jnp.abs(combined(span)) for span in spans])
     exponent, mantissa = code_unit(jnp.max(top, axis=1, keepdims=True))
     inverse = 1.0 / unit_of(exponent, mantissa)
     for k, span in enumerate(spans):
-        code_ref[k] = whole_number(jnp.floor(combined(span) * inverse + 0.5))
+        code = whole_number(jnp.floor(combined(span) * inverse + 0.5))
+        start = 0
+        for ref in code_refs:
+            end = start + ref.shape[-1]
+            ref[k] = code[:, start:end]
+            start = end
         basis_code_ref[:, span] = code_basis(basis_ref[:, span])
     step = pl.program_id(0)
     here = pl.ds(pl.multiple_of(step * rows, rows), rows)
@@ -104,30 +110,27 @@
             unit_ref[k : k + 1, :] = column_ref[k].T[:1]
 
 
-def prepare(momentum, grad, basis, share):
+def prepare(momentum, grad, basis, widths):
     rows, cols = momentum.shape
-    width = share if share % 128 == 0 else cols
+    count = cols // sum(widths)
     steps = 2 if basis.shape[0] % 32 == 0 else 1
     wide = pl.BlockSpec((rows // steps, cols), lambda i: (i, 0))
     narrow = pl.BlockSpec((basis.shape[0] // steps, cols), lambda i: (i, 0))
-    return pl.pallas_call(
+    out = pl.pallas_call(
         prepare_kernel,
         grid=(steps,),
         in_specs=[wide, wide, narrow],
-        out_specs=[
-            narrow,
-            pl.BlockSpec((cols // width, rows // steps, width), lambda i: (0, i, 0)),
-            pl.BlockSpec((2, rows), lambda i: (0, 0)),
-        ],
-        out_shape=[
-            jax.ShapeDtypeStruct(basis.shape, jnp.int16),
-            jax.ShapeDtypeStruct((cols // width, rows, width), jnp.int16),
-            jax.ShapeDtypeStruct((2, rows), jnp.float32),
-        ],
+        out_specs=[narrow]
+        + [pl.BlockSpec((count, rows // steps, width), lambda i: (0, i, 0)) for width in widths]
+        + [pl.BlockSpec((2, rows), lambda i: (0, 0))],
+        out_shape=[jax.ShapeDtypeStruct(basis.shape, jnp.int16)]
+        + [jax.ShapeDtypeStruct((count, rows, width), jnp.int16) for width in widths]
+        + [jax.ShapeDtypeStruct((2, rows), jnp.float32)],
         scratch_shapes=[pltpu.VMEM((2, rows, 128), jnp.float32)],
         compiler_params=STREAM,
         cost_estimate=pl.CostEstimate(flops=10 * rows * cols, bytes_accessed=rows * cols * 8, transcendentals=0),
     )(momentum, grad, basis)
+    return out[0], out[1:-1], out[-1]
 
 
 def project_kernel(momentum_ref, grad_ref, code_ref, out_ref):
@@ -363,15 +366,18 @@
     )(codes)
 
 
-def encode_kernel(place_ref, source_ref, turned_ref, head_ref, inverse_ref, own_ref, code_ref, ortho_ref, mixed_ref):
+def encode_kernel(place_ref, *refs):
     def times(a, b):
         return jnp.dot(a, b, preferred_element_type=jnp.float32)
 
     def turned_dot(a, b):
         return lax.dot_general(a, b, (((0,), (1,)), ((), ())), precision=HIGH, preferred_element_type=jnp.float32)
 
+    source_refs = refs[:-7]
+    turned_ref, head_ref, inverse_ref, own_ref, code_ref, ortho_ref, mixed_ref = refs[-7:]
     rank = turned_ref.shape[0]
-    source_high, source_low = halves(source_ref[...].astype(jnp.int32).astype(jnp.float32))
+    source = jnp.concatenate([ref[...].astype(jnp.int32).astype(jnp.float32) for ref in source_refs], axis=1)
+    source_high, source_low = halves(source)
     head = head_ref[...].astype(jnp.int32).astype(jnp.float32)
     devices = head.shape[0]
     rows = turned_ref.shape[1] // devices
@@ -405,8 +411,8 @@
         set_head(code_ref.at[rows:], exponent, mantissa, square_exponent, square_high, square_low)
 
 
-def encode(place, source, turned, packed, inverse_low, rows):
-    total, share = source.shape
+def encode(place, sources, turned, packed, inverse_low, rows):
+    total, share = sources[0].shape[0], sum(x.shape[1] for x in sources)
     rank = turned.shape[0]
     block = min(1024, total)
     size = packed.shape[1]
@@ -416,7 +422,7 @@
             num_scalar_prefetch=1,
             grid=(total // block,),
             in_specs=[
-                pl.BlockSpec((block, share), lambda i, place: (i, 0)),
+                *[pl.BlockSpec((block, x.shape[1]), lambda i, place: (i, 0)) for x in sources],
                 pl.BlockSpec((rank, block), lambda i, place: (0, i)),
                 pl.BlockSpec((block // rows, HEAD, rank), lambda i, place: (i, size // HEAD - 1, 0)),
                 whole(inverse_low),
@@ -436,7 +442,7 @@
         cost_estimate=pl.CostEstimate(
             flops=6 * total * share * rank, bytes_accessed=total * (share * 2 + rank * 4), transcendentals=0
         ),
-    )(place, source, turned, packed, inverse_low, turned)
+    )(place, *sources, turned, packed, inverse_low, turned)
 
 
 def decode(code_ref):
@@ -526,11 +532,15 @@
     row_total, col_total = rows * num_blocks, cols * num_cols
     share = cols // num_blocks
 
-    basis, codes, units = prepare(momentum, grad, q_stored, share)
-    codes = codes.reshape(-1, rows, codes.shape[2] // share, share).swapaxes(1, 2).reshape(num_blocks, rows, share)
+    late = share // 4 if share % 512 == 0 else 0
+    widths = [share - late, late] if late else [share if share % 128 == 0 else cols]
+    basis, codes, units = prepare(momentum, grad, q_stored, widths)
+    if share % 128 != 0:
+        codes = [codes[0].reshape(rows, num_blocks, share).swapaxes(0, 1)]
+    trade = lambda x: lax.all_to_all(x, "fsdp", split_axis=0, concat_axis=0).reshape(row_total, x.shape[2])
     basis = lax.all_gather(basis, "fsdp", axis=0, tiled=True)
-    codes, basis = lax.optimization_barrier((codes, basis))
-    codes = lax.all_to_all(codes, "fsdp", split_axis=0, concat_axis=0).reshape(row_total, share)
+    first, basis = lax.optimization_barrier((codes[0], basis))
+    first = trade(first)
 
     near, step = project(momentum, grad, basis), 1
     while 4 * step < num_cols:
@@ -538,9 +548,10 @@
         step *= 2
     parts = [near] + [exchange(near, "tp", k) for k in range(step, num_cols, step)]
     packed = lax.all_gather(pack(perm, units, parts), "fsdp", axis=0)
-    packed, codes = lax.optimization_barrier((packed, codes))
+    packed, first, rest = lax.optimization_barrier((packed, first, codes[1:]))
+    sources = [first] + [trade(x) for x in rest]
     turned, inverse_low = factor(packed)
-    code, orthonormal = encode(lax.axis_index("fsdp").reshape(1), codes, turned, packed, inverse_low, rows)
+    code, orthonormal = encode(lax.axis_index("fsdp").reshape(1), sources, turned, packed, inverse_low, rows)
     gathered = lax.all_gather(code, "fsdp", axis=0)
     head = gathered[:, share : share + 5].astype(jnp.float32)
     parts = (head[:, 3] + head[:, 4] * (1.0 / 16384.0)) * jnp.exp2(head[:, 2] - 13.0)

time: 116 us -> 117 us (level)
  starting transfers between devices: 10.7 us -> 15.2 us
  blocking collectives: 70.2 us -> 66.6 us
    all_to_all x1 -> x2, starting transfers between devices: 3.56 us -> 8.08 us  [on_device(): lax.all_to_all(x, 'fsdp', split_axis=0, concat_axis=0)]
    all_gather x1, blocking collectives: 20.3 us -> 16.2 us  [on_device(): packed = lax.all_gather(pack(perm, units, parts), 'fsdp', axis=0)]
  transfers between devices with their start and end apart: 7 -> 8, of which waited for: 3 -> 4; matrix products, arithmetic and copies ran while one was open for 0% -> 0% of each run, Pallas kernels for 7% -> 16%
where the time goes in v16:
time: 117 us
  blocking collectives  66.6 us (57%)
  Pallas kernels  27.1 us (23%)
  starting transfers between devices  15.2 us (13%)
  waiting for transfers between devices  6.83 us (6%)
    all_gather x1, blocking collectives, on_device(): basis = lax.all_gather(basis, 'fsdp', axis=0, tiled=True)  26.1 us
    all_gather x1, blocking collectives, on_device(): gathered = lax.all_gather(code, 'fsdp', axis=0)  24.3 us
    all_gather x1, blocking collectives, on_device(): packed = lax.all_gather(pack(perm, units, parts), 'fsdp', axis=0)  16.2 us
    pallas_call x1, Pallas kernels, factor(): pl.pallas_call(factor_kernel, grid=(devices // group,), in_specs=[pl.Bloc...  9.57 us
    all_to_all x2, starting transfers between devices, on_device(): lax.all_to_all(x, 'fsdp', split_axis=0, concat_axis=0)  8.08 us
    ppermute x6, starting transfers between devices, exchange(): lax.ppermute(x, axis, [(i, i ^ k) for i in range(lax.axis_size(axis))])  7.1 us
    ppermute x6, waiting for transfers between devices, exchange(): lax.ppermute(x, axis, [(i, i ^ k) for i in range(lax.axis_size(axis))])  6.66 us
    pallas_call x1, Pallas kernels, project(): pl.pallas_call(project_kernel, grid=(cols // block,), in_specs=[wide, wid...  4.85 us
  transfers between devices with their start and end apart: 8, of which 4 were waited for; matrix products, arithmetic and copies ran while one was open for 0% of the time, Pallas kernels for 16%

profile of v16, /device:TPU:0, one launch (start us, length us, event | category | flops | bytes accessed | tf_op | source)
XLA Modules:
  0.0 116.5 jit_solution(8040608922608678773)
XLA Ops:
  0.6 3.7 %shard_map.67 = (s16[32,4096]{1,0:T(8,128)(2,1)}, s16[8,128,384]{2,1,0:T(8,128)(2,1)}, s16[8,128,128]{2,1,0:T(8,128)(2,1)}, f32[2,128]{1,0:T(2,128)}) custom-call(f32[128,4096]{1,0:T(8,128)} %momentum_ref.5, bf16[128,4096]{1,0:T(8,128)(2,1)} %grad_ref.5, bf16[32,4096]{1,0:T(8,128)(2,1)} %basis_ref.1), custom_call_target="tpu_custom_call" | custom-call | flops 5242880 | bytes 4194304 | tf_op jit(solution)/shard_map/pallas_call | solution.py:119
  4.3 26.1 %all-gather.4.code_ref = s16[256,4096]{1,0:T(8,128)(2,1)} all-gather(s16[32,4096]{1,0:T(8,128)(2,1)} %get-tuple-element.20), channel_id=1, replica_groups=mesh['fsdp'=8,'tp'=4] {'fsdp'}, dimensions={0}, use_global_device_ids=true | all-gather | bytes 2359296 | tf_op jit(solution)/shard_map/all_gather | solution.py:541
  30.4 3.5 %all-to-all-start = ((s16[8,128,384]{2,1,0:T(8,128)(2,1)}), s16[8,128,384]{2,1,0:T(8,128)(2,1)S(1)}, u32[]{:S(2)}, u32[]{:S(2)}) async-start(s16[8,128,384]{2,1,0:T(8,128)(2,1)} %get-tuple-element.22), calls=%async_computation | async-start | bytes 1572864 | tf_op jit(solution)/shard_map/all_to_all | solution.py:540
  34.0 0.0 copy-start.2
  34.0 0.0 copy-start.3
  34.0 4.9 %shard_map.68.refs_0_ = f32[128,256]{1,0:T(8,128)S(1)} custom-call(f32[128,4096]{1,0:T(8,128)} %momentum_ref.5, bf16[128,4096]{1,0:T(8,128)(2,1)} %grad_ref.5, s16[256,4096]{1,0:T(8,128)(2,1)} %all-gather.4.code_ref), custom_call_target="tpu_custom_call" | custom-call | flops 536870912 | bytes 5242880 | tf_op jit(solution)/shard_map/pallas_call | solution.py:165
  38.8 1.6 %collective-permute-start = (f32[128,256]{1,0:T(8,128)S(1)}, f32[128,256]{1,0:T(8,128)S(1)}, u32[]{:S(2)}, u32[]{:S(2)}) collective-permute-start(f32[128,256]{1,0:T(8,128)S(1)} %shard_map.68.refs_0_), channel_id=1, source_target_pairs={{0,1},{1,0},{2,3},{3,2},{4,5},{5,4},{6,7},{7,6},{8,9},{9,8},{10,11... | collective-permute-start | bytes 393224 | tf_op jit(solution)/shard_map/ppermute | solution.py:29
  40.4 1.5 %collective-permute-start.1 = (f32[128,256]{1,0:T(8,128)S(1)}, f32[128,256]{1,0:T(8,128)S(1)}, u32[]{:S(2)}, u32[]{:S(2)}) collective-permute-start(f32[128,256]{1,0:T(8,128)S(1)} %shard_map.68.refs_0_), channel_id=1, source_target_pairs={{0,2},{1,3},{2,0},{3,1},{4,6},{5,7},{6,4},{7,5},{8,10},{9,11},{10,... | collective-permute-start | bytes 393224 | tf_op jit(solution)/shard_map/ppermute | solution.py:29
  41.9 0.5 collective-permute-start.2
  42.4 2.7 %collective-permute-done.refs_1_ = f32[128,256]{1,0:T(8,128)S(1)} collective-permute-done((f32[128,256]{1,0:T(8,128)S(1)}, f32[128,256]{1,0:T(8,128)S(1)}, u32[]{:S(2)}, u32[]{:S(2)}) %collective-permute-start) | collective-permute-done | bytes 131104 | tf_op jit(solution)/shard_map/ppermute | solution.py:29
  45.1 3.7 %collective-permute-done.1.refs_2_ = f32[128,256]{1,0:T(8,128)S(1)} collective-permute-done((f32[128,256]{1,0:T(8,128)S(1)}, f32[128,256]{1,0:T(8,128)S(1)}, u32[]{:S(2)}, u32[]{:S(2)}) %collective-permute-start.1) | collective-permute-done | bytes 131104 | tf_op jit(solution)/shard_map/ppermute | solution.py:29
  48.8 0.0 collective-permute-done.2.refs_3_
  48.8 0.0 copy-done.2
  48.8 0.0 copy-done.3
  48.8 0.9 shard_map.69
  49.7 16.2 %all-gather = s16[1664,256]{1,0:T(8,128)(2,1)S(1)} all-gather(s16[208,256]{1,0:T(8,128)(2,1)S(1)} %shard_map.69), channel_id=2, replica_groups=mesh['fsdp'=8,'tp'=4] {'fsdp'}, dimensions={0}, use_global_device_ids=true | all-gather | bytes 958464 | tf_op jit(solution)/shard_map/all_gather | solution.py:550
  66.0 0.0 all-to-all-done
  66.0 4.5 %all-to-all-start.1 = ((s16[8,128,128]{2,1,0:T(8,128)(2,1)}), s16[8,128,128]{2,1,0:T(8,128)(2,1)S(1)}, u32[]{:S(2)}, u32[]{:S(2)}) async-start(s16[8,128,128]{2,1,0:T(8,128)(2,1)} %get-tuple-element.25), calls=%async_computation.1 | async-start | bytes 524288 | tf_op jit(solution)/shard_map/all_to_all | solution.py:540
  70.5 9.6 %shard_map.70 = (f32[256,1024]{1,0:T(8,128)S(1)}, f32[256,256]{1,0:T(8,128)S(1)}) custom-call(s16[8,208,256]{2,1,0:T(8,128)(2,1)S(1)} %bitcast.9), custom_call_target="tpu_custom_call" | custom-call | flops 805306368 | bytes 1703936 | tf_op jit(solution)/shard_map/pallas_call | solution.py:347
  80.1 0.2 all-to-all-done.1
  80.2 0.0 copy-start.1
  80.2 2.4 %shard_map.71 = (s16[528,256]{1,0:T(8,128)(2,1)S(1)}, f32[128,256]{1,0:T(8,128)S(1)}) custom-call(s32[1]{0:T(128)} %bitcast.place_ref, s16[1024,384]{1,0:T(8,128)(2,1)S(1)} %bitcast.11, s16[1024,128]{1,0:T(8,128)(2,1)S(1)} %bitcast.12, f32[256,1024]{1,0:T(8,128)S(1)} %get-tuple-element.27.refs_2_.refs_5_, s16[8,208,256]{2,1,0:T(8,128)(2,1)S(1)} %bitcast.10, ...), custom_call_target="tpu_custom_call" | custom-call | flops 805306368 | bytes 2097152 | tf_op jit(solution)/shard_map/pallas_call | solution.py:419
  82.6 0.0 copy-start
  82.6 24.3 %all-gather.5 = s16[4224,256]{1,0:T(8,128)(2,1)S(1)} all-gather(s16[528,256]{1,0:T(8,128)(2,1)S(1)} %get-tuple-element.29), channel_id=3, replica_groups=mesh['fsdp'=8,'tp'=4] {'fsdp'}, dimensions={0}, use_global_device_ids=true | all-gather | bytes 2433024 | tf_op jit(solution)/shard_map/all_gather | solution.py:555
  106.9 0.1 fusion.4
  107.0 1.2 %collective-permute-start.3 = (f32[1,256]{1,0:T(1,128)S(1)}, f32[1,256]{1,0:T(1,128)S(1)}, u32[]{:S(2)}, u32[]{:S(2)}) collective-permute-start(f32[1,256]{1,0:T(1,128)S(1)} %bitcast.13), channel_id=1, source_target_pairs={{0,1},{1,0},{2,3},{3,2},{4,5},{5,4},{6,7},{7,6},{8,9},{9,8},{10,11... | collective-permute-start | bytes 3080 | tf_op jit(solution)/shard_map/ppermute | solution.py:29
  108.2 1.0 collective-permute-start.4
  109.2 1.3 %collective-permute-start.5 = (f32[1,256]{1,0:T(1,128)S(1)}, f32[1,256]{1,0:T(1,128)S(1)}, u32[]{:S(2)}, u32[]{:S(2)}) collective-permute-start(f32[1,256]{1,0:T(1,128)S(1)} %bitcast.15), channel_id=1, source_target_pairs={{0,3},{1,2},{2,1},{3,0},{4,7},{5,6},{6,5},{7,4},{8,11},{9,10},{10,... | collective-permute-start | bytes 3080 | tf_op jit(solution)/shard_map/ppermute | solution.py:29
  110.5 0.0 copy-done.1
  110.5 0.0 copy-done
  110.6 2.9 %shard_map.72 = f32[128,4096]{1,0:T(8,128)} custom-call(f32[128,4096]{1,0:T(8,128)S(1)} %copy-done, bf16[128,4096]{1,0:T(8,128)(2,1)S(1)} %copy-done.1, s16[8,528,256]{2,1,0:T(8,128)(2,1)S(1)} %bitcast.7, f32[128,256]{1,0:T(8,128)S(1)} %get-tuple-element.30.ortho_ref), custom_call_target="tpu_custom_call" | custom-call | flops 805306368 | bytes 7340032 | tf_op jit(solution)/shard_map/pallas_call | solution.py:498
  113.4 0.0 collective-permute-done.3
  113.4 0.0 collective-permute-done.4
  113.4 0.3 collective-permute-done.5
  113.7 2.8 %shard_map.73 = (f32[4096,256]{1,0:T(8,128)}, bf16[128,4096]{1,0:T(8,128)(2,1)}) custom-call(s16[8,528,256]{2,1,0:T(8,128)(2,1)S(1)} %bitcast.8, f32[128,256]{1,0:T(8,128)S(1)} %get-tuple-element.30.ortho_ref, f32[1,256]{1,0:T(1,128)S(1)} %add_rsqrt_fusion.scale_ref), custom_call_target="tpu_custom_call" | custom-call | flops 805306368 | bytes 7340032 | tf_op jit(solution)/shard_map/pallas_call | solution.py:510
  (2 shorter events, 0.0 us)
Async XLA Ops:
  30.4 35.6 %all-to-all-start = ((s16[8,128,384]{2,1,0:T(8,128)(2,1)}), s16[8,128,384]{2,1,0:T(8,128)(2,1)S(1)}, u32[]{:S(2)}, u32[]{:S(2)}) async-start(s16[8,128,384]{2,1,0:T(8,128)(2,1)} %get-tuple-element.22), calls=%async_computation | async-start | bytes 1572864 | tf_op jit(solution)/shard_map/all_to_all | solution.py:540
  34.0 14.8 %copy-start.2 = (f32[2,128]{1,0:T(2,128)S(1)}, f32[2,128]{1,0:T(2,128)}, u32[]{:S(2)}) copy-start(f32[2,128]{1,0:T(2,128)} %get-tuple-element.18.unit_ref) | copy-start | bytes 3076
  34.0 14.8 %copy-start.3 = (s32[8]{0:T(128)S(1)}, s32[8]{0:T(128)}, u32[]{:S(2)}) copy-start(s32[8]{0:T(128)} %perm_ref.1) | copy-start | bytes 100
  38.8 6.3 %collective-permute-start = (f32[128,256]{1,0:T(8,128)S(1)}, f32[128,256]{1,0:T(8,128)S(1)}, u32[]{:S(2)}, u32[]{:S(2)}) collective-permute-start(f32[128,256]{1,0:T(8,128)S(1)} %shard_map.68.refs_0_), channel_id=1, source_target_pairs={{0,1},{1,0},{2,3},{3,2},{4,5},{5,4},{6,7},{7,6},{8,9},{9,8},{10,11... | collective-permute-start | bytes 393224 | tf_op jit(solution)/shard_map/ppermute | solution.py:29
  40.4 8.4 %collective-permute-start.1 = (f32[128,256]{1,0:T(8,128)S(1)}, f32[128,256]{1,0:T(8,128)S(1)}, u32[]{:S(2)}, u32[]{:S(2)}) collective-permute-start(f32[128,256]{1,0:T(8,128)S(1)} %shard_map.68.refs_0_), channel_id=1, source_target_pairs={{0,2},{1,3},{2,0},{3,1},{4,6},{5,7},{6,4},{7,5},{8,10},{9,11},{10,... | collective-permute-start | bytes 393224 | tf_op jit(solution)/shard_map/ppermute | solution.py:29
  41.9 6.9 %collective-permute-start.2 = (f32[128,256]{1,0:T(8,128)S(1)}, f32[128,256]{1,0:T(8,128)S(1)}, u32[]{:S(2)}, u32[]{:S(2)}) collective-permute-start(f32[128,256]{1,0:T(8,128)S(1)} %shard_map.68.refs_0_), channel_id=1, source_target_pairs={{0,3},{1,2},{2,1},{3,0},{4,7},{5,6},{6,5},{7,4},{8,11},{9,10},{10,... | collective-permute-start | bytes 393224 | tf_op jit(solution)/shard_map/ppermute | solution.py:29
  66.0 14.3 %all-to-all-start.1 = ((s16[8,128,128]{2,1,0:T(8,128)(2,1)}), s16[8,128,128]{2,1,0:T(8,128)(2,1)S(1)}, u32[]{:S(2)}, u32[]{:S(2)}) async-start(s16[8,128,128]{2,1,0:T(8,128)(2,1)} %get-tuple-element.25), calls=%async_computation.1 | async-start | bytes 524288 | tf_op jit(solution)/shard_map/all_to_all | solution.py:540
  80.2 30.3 %copy-start.1 = (bf16[128,4096]{1,0:T(8,128)(2,1)S(1)}, bf16[128,4096]{1,0:T(8,128)(2,1)}, u32[]{:S(2)}) copy-start(bf16[128,4096]{1,0:T(8,128)(2,1)} %grad_ref.5) | copy-start | bytes 3145732
  82.6 27.9 %copy-start = (f32[128,4096]{1,0:T(8,128)S(1)}, f32[128,4096]{1,0:T(8,128)}, u32[]{:S(2)}) copy-start(f32[128,4096]{1,0:T(8,128)} %momentum_ref.5) | copy-start | bytes 6291460
  107.0 6.4 %collective-permute-start.3 = (f32[1,256]{1,0:T(1,128)S(1)}, f32[1,256]{1,0:T(1,128)S(1)}, u32[]{:S(2)}, u32[]{:S(2)}) collective-permute-start(f32[1,256]{1,0:T(1,128)S(1)} %bitcast.13), channel_id=1, source_target_pairs={{0,1},{1,0},{2,3},{3,2},{4,5},{5,4},{6,7},{7,6},{8,9},{9,8},{10,11... | collective-permute-start | bytes 3080 | tf_op jit(solution)/shard_map/ppermute | solution.py:29
  108.2 5.2 %collective-permute-start.4 = (f32[1,256]{1,0:T(1,128)S(1)}, f32[1,256]{1,0:T(1,128)S(1)}, u32[]{:S(2)}, u32[]{:S(2)}) collective-permute-start(f32[1,256]{1,0:T(1,128)S(1)} %bitcast.14), channel_id=1, source_target_pairs={{0,2},{1,3},{2,0},{3,1},{4,6},{5,7},{6,4},{7,5},{8,10},{9,11},{10,... | collective-permute-start | bytes 3080 | tf_op jit(solution)/shard_map/ppermute | solution.py:29
  109.2 4.5 %collective-permute-start.5 = (f32[1,256]{1,0:T(1,128)S(1)}, f32[1,256]{1,0:T(1,128)S(1)}, u32[]{:S(2)}, u32[]{:S(2)}) collective-permute-start(f32[1,256]{1,0:T(1,128)S(1)} %bitcast.15), channel_id=1, source_target_pairs={{0,3},{1,2},{2,1},{3,0},{4,7},{5,6},{6,5},{7,4},{8,11},{9,10},{10,... | collective-permute-start | bytes 3080 | tf_op jit(solution)/shard_map/ppermute | solution.py:29

commit v17 on v14

--- a/solution.py
+++ b/solution.py
@@ -190,11 +190,14 @@
     value = total * (1.0 / unit_of(exponent, mantissa))
     high = jnp.floor(value + 0.5)
     out_ref[:rows] = whole_number(high)
-    low = jnp.minimum(jnp.floor((value - high) * 256.0 + 0.5), 127.0)
-    half = rows // 2
-    out_ref[rows : rows + half] = whole_number(low[:half] * 256.0 + (low[half:] + 128.0))
+    low = jnp.minimum(jnp.floor((value - high) * 16.0 + 0.5), 7.0)
+    part = rows // 4
+    packed = low[:part]
+    for k in range(1, 4):
+        packed = packed * 16.0 + (low[part * k : part * (k + 1)] + 8.0)
+    out_ref[rows : rows + part] = whole_number(packed)
     units = jnp.concatenate([unit_ref[...], jnp.zeros((2, rank - rows), jnp.float32)], axis=1)
-    set_head(out_ref.at[rows + half :], exponent, mantissa, units[:1], units[1:])
+    set_head(out_ref.at[rows + part :], exponent, mantissa, units[:1], units[1:])
 
 
 def pack(perm, units, parts):
@@ -205,9 +208,9 @@
             num_scalar_prefetch=1,
             grid=(1,),
             in_specs=[whole(x) for x in (units, *parts)],
-            out_specs=pl.BlockSpec((rows + rows // 2 + HEAD, rank), lambda *_: (0, 0)),
+            out_specs=pl.BlockSpec((rows + rows // 4 + HEAD, rank), lambda *_: (0, 0)),
         ),
-        out_shape=jax.ShapeDtypeStruct((rows + rows // 2 + HEAD, rank), jnp.int16),
+        out_shape=jax.ShapeDtypeStruct((rows + rows // 4 + HEAD, rank), jnp.int16),
         compiler_params=PARAMS,
         cost_estimate=pl.CostEstimate(flops=12 * rows * rank * rank, bytes_accessed=rank * rank * 4, transcendentals=0),
     )(perm, units, *parts)
@@ -289,10 +292,15 @@
     scale = lax.rsqrt(jnp.sum(diagonal, axis=0, keepdims=True))
     work[:, :rank] = gram * scale * lax.rsqrt(jnp.sum(diagonal, axis=1, keepdims=True))
     work[:, rank:] = (rows == cols).astype(jnp.float32)
+    block = work[:PANEL, :PANEL]
     for start in range(0, rank, PANEL):
         end = start + PANEL
         left, right = start // 128 * 128, rank + lanes_up(end)
-        inverse = panel_inverse(work[start:end, start:end], band)
+        inverse = panel_inverse(block, band)
+        if end < rank:
+            after = slice(end, end + PANEL)
+            ahead = short_dot(inverse, work[start:end, after])
+            block = work[after, after] - short_dot(ahead.T, ahead)
         scaled = short_dot(inverse, work[start:end, left:right])
         out_ref[start:end, : lanes_up(end)] = scaled[:, rank - left :] * scale[:, : lanes_up(end)]
         if lanes_up(end) < rank:
@@ -305,12 +313,13 @@
 
 def factor_kernel(code_ref, turned_ref, out_ref, gram_ref, mixed_ref, work, band):
     count, size, rank = code_ref.shape
-    size = (size - HEAD) * 2 // 3
+    size = (size - HEAD) * 4 // 5
     code = code_ref[...].astype(jnp.int32)
-    low = code[:, size : size + size // 2]
-    low = jnp.concatenate([low >> 8, (low & 255) - 128], axis=1).astype(jnp.float32)
-    head = code[:, size + size // 2 :].astype(jnp.float32)
-    part = (code[:, :size].astype(jnp.float32) + low * (1.0 / 256.0)) * unit_of(head[:, :1], head[:, 1:2])
+    low = code[:, size : size + size // 4]
+    low = jnp.concatenate([low >> 12, *[((low >> shift) & 15) - 8 for shift in (8, 4, 0)]], axis=1)
+    head = code[:, size + size // 4 :].astype(jnp.float32)
+    part = code[:, :size].astype(jnp.float32) + low.astype(jnp.float32) * (1.0 / 16.0)
+    part = part * unit_of(head[:, :1], head[:, 1:2])
     turned = part.reshape(count * size, rank).T
     turned_ref[...] = turned
 
@@ -339,7 +348,7 @@
 
 def factor(codes):
     devices, size, rank = codes.shape
-    rows = (size - HEAD) * 2 // 3
+    rows = (size - HEAD) * 4 // 5
     group = min(devices, max(1, 1024 // rows))
     return pl.pallas_call(
         factor_kernel,

time: 116 us -> 115 us (level)
  transfers between devices with their start and end apart: 7 -> 7, of which waited for: 3 -> 3; matrix products, arithmetic and copies ran while one was open for 0% -> 0% of each run, Pallas kernels for 7% -> 8%
where the time goes in v17:
time: 115 us
  blocking collectives  69.5 us (60%)
  Pallas kernels  26.7 us (23%)
  starting transfers between devices  10.7 us (9%)
  waiting for transfers between devices  7.51 us (7%)
    all_gather x1, blocking collectives, on_device(): basis = lax.all_gather(basis, 'fsdp', axis=0, tiled=True)  26.1 us
    all_gather x1, blocking collectives, on_device(): gathered = lax.all_gather(code, 'fsdp', axis=0)  23.7 us
    all_gather x1, blocking collectives, on_device(): packed = lax.all_gather(pack(perm, units, parts), 'fsdp', axis=0)  19.8 us
    pallas_call x1, Pallas kernels, factor(): pl.pallas_call(factor_kernel, grid=(devices // group,), in_specs=[pl.Bloc...  9.33 us
    ppermute x6, waiting for transfers between devices, exchange(): lax.ppermute(x, axis, [(i, i ^ k) for i in range(lax.axis_size(axis))])  7.51 us
    ppermute x6, starting transfers between devices, exchange(): lax.ppermute(x, axis, [(i, i ^ k) for i in range(lax.axis_size(axis))])  7.1 us
    pallas_call x1, Pallas kernels, project(): pl.pallas_call(project_kernel, grid=(cols // block,), in_specs=[wide, wid...  4.86 us
    all_to_all x1, starting transfers between devices, on_device(): lax.all_to_all(codes, 'fsdp', split_axis=0, concat_axis=0)  3.56 us
  transfers between devices with their start and end apart: 7, of which 3 were waited for; matrix products, arithmetic and copies ran while one was open for 0% of the time, Pallas kernels for 8%

profile of v17, /device:TPU:0, one launch (start us, length us, event | category | flops | bytes accessed | tf_op | source)
XLA Modules:
  0.0 115.2 jit_solution(16482928123847947705)
XLA Ops:
  0.6 3.5 %shard_map.67 = (s16[32,4096]{1,0:T(8,128)(2,1)}, s16[8,128,512]{2,1,0:T(8,128)(2,1)}, f32[2,128]{1,0:T(2,128)}) custom-call(f32[128,4096]{1,0:T(8,128)} %momentum_ref.5, bf16[128,4096]{1,0:T(8,128)(2,1)} %grad_ref.5, bf16[32,4096]{1,0:T(8,128)(2,1)} %basis_ref.1), custom_call_target="tpu_custom_call" | custom-call | flops 5242880 | bytes 4194304 | tf_op jit(solution)/shard_map/pallas_call | solution.py:113
  4.2 26.1 %all-gather.4.code_ref = s16[256,4096]{1,0:T(8,128)(2,1)} all-gather(s16[32,4096]{1,0:T(8,128)(2,1)} %get-tuple-element.18), channel_id=1, replica_groups=mesh['fsdp'=8,'tp'=4] {'fsdp'}, dimensions={0}, use_global_device_ids=true | all-gather | bytes 2359296 | tf_op jit(solution)/shard_map/all_gather | solution.py:540
  30.2 3.6 %all-to-all-start = ((s16[8,128,512]{2,1,0:T(8,128)(2,1)}), s16[8,128,512]{2,1,0:T(8,128)(2,1)S(1)}, u32[]{:S(2)}, u32[]{:S(2)}) async-start(s16[8,128,512]{2,1,0:T(8,128)(2,1)} %get-tuple-element.20), calls=%async_computation | async-start | bytes 2097152 | tf_op jit(solution)/shard_map/all_to_all | solution.py:542
  33.8 0.0 copy-start.2
  33.8 0.0 copy-start.3
  33.8 4.9 %shard_map.68.refs_0_ = f32[128,256]{1,0:T(8,128)S(1)} custom-call(f32[128,4096]{1,0:T(8,128)} %momentum_ref.5, bf16[128,4096]{1,0:T(8,128)(2,1)} %grad_ref.5, s16[256,4096]{1,0:T(8,128)(2,1)} %all-gather.4.code_ref), custom_call_target="tpu_custom_call" | custom-call | flops 536870912 | bytes 5242880 | tf_op jit(solution)/shard_map/pallas_call | solution.py:162
  38.7 1.6 %collective-permute-start = (f32[128,256]{1,0:T(8,128)S(1)}, f32[128,256]{1,0:T(8,128)S(1)}, u32[]{:S(2)}, u32[]{:S(2)}) collective-permute-start(f32[128,256]{1,0:T(8,128)S(1)} %shard_map.68.refs_0_), channel_id=1, source_target_pairs={{0,1},{1,0},{2,3},{3,2},{4,5},{5,4},{6,7},{7,6},{8,9},{9,8},{10,11... | collective-permute-start | bytes 393224 | tf_op jit(solution)/shard_map/ppermute | solution.py:29
  40.2 1.5 %collective-permute-start.1 = (f32[128,256]{1,0:T(8,128)S(1)}, f32[128,256]{1,0:T(8,128)S(1)}, u32[]{:S(2)}, u32[]{:S(2)}) collective-permute-start(f32[128,256]{1,0:T(8,128)S(1)} %shard_map.68.refs_0_), channel_id=1, source_target_pairs={{0,2},{1,3},{2,0},{3,1},{4,6},{5,7},{6,4},{7,5},{8,10},{9,11},{10,... | collective-permute-start | bytes 393224 | tf_op jit(solution)/shard_map/ppermute | solution.py:29
  41.8 0.5 collective-permute-start.2
  42.2 2.7 %collective-permute-done.refs_1_ = f32[128,256]{1,0:T(8,128)S(1)} collective-permute-done((f32[128,256]{1,0:T(8,128)S(1)}, f32[128,256]{1,0:T(8,128)S(1)}, u32[]{:S(2)}, u32[]{:S(2)}) %collective-permute-start) | collective-permute-done | bytes 131104 | tf_op jit(solution)/shard_map/ppermute | solution.py:29
  45.0 3.7 %collective-permute-done.1.refs_2_ = f32[128,256]{1,0:T(8,128)S(1)} collective-permute-done((f32[128,256]{1,0:T(8,128)S(1)}, f32[128,256]{1,0:T(8,128)S(1)}, u32[]{:S(2)}, u32[]{:S(2)}) %collective-permute-start.1) | collective-permute-done | bytes 131104 | tf_op jit(solution)/shard_map/ppermute | solution.py:29
  48.6 0.0 collective-permute-done.2.refs_3_
  48.6 0.0 copy-done.2
  48.6 0.0 copy-done.3
  48.6 0.9 shard_map.69
  49.6 19.8 %all-gather = s16[1408,256]{1,0:T(8,128)(2,1)S(1)} all-gather(s16[176,256]{1,0:T(8,128)(2,1)S(1)} %shard_map.69), channel_id=2, replica_groups=mesh['fsdp'=8,'tp'=4] {'fsdp'}, dimensions={0}, use_global_device_ids=true | all-gather | bytes 811008 | tf_op jit(solution)/shard_map/all_gather | solution.py:549
  69.4 0.0 all-to-all-done
  69.4 9.3 %shard_map.70 = (f32[256,1024]{1,0:T(8,128)S(1)}, f32[256,256]{1,0:T(8,128)S(1)}) custom-call(s16[8,176,256]{2,1,0:T(8,128)(2,1)S(1)} %bitcast.9), custom_call_target="tpu_custom_call" | custom-call | flops 805306368 | bytes 1441792 | tf_op jit(solution)/shard_map/pallas_call | solution.py:353
  78.7 0.0 copy-start.1
  78.7 2.4 %shard_map.71 = (s16[528,256]{1,0:T(8,128)(2,1)S(1)}, f32[128,256]{1,0:T(8,128)S(1)}) custom-call(s32[1]{0:T(128)} %bitcast.place_ref, s16[1024,512]{1,0:T(8,128)(2,1)S(1)} %bitcast.8, f32[256,1024]{1,0:T(8,128)S(1)} %get-tuple-element.23.turned_ref.own_ref, s16[8,176,256]{2,1,0:T(8,128)(2,1)S(1)} %bitcast.10, f32[256,256]{1,0:T(8,128)S(1)} %get-tuple-element.24.inverse_ref, ...), custom_call_target="tpu_custom_call" | custom-call | flops 805306368 | bytes 2097152 | tf_op jit(solution)/shard_map/pallas_call | solution.py:422
  81.1 0.0 copy-start
  81.1 23.7 %all-gather.5 = s16[4224,256]{1,0:T(8,128)(2,1)S(1)} all-gather(s16[528,256]{1,0:T(8,128)(2,1)S(1)} %get-tuple-element.25), channel_id=3, replica_groups=mesh['fsdp'=8,'tp'=4] {'fsdp'}, dimensions={0}, use_global_device_ids=true | all-gather | bytes 2433024 | tf_op jit(solution)/shard_map/all_gather | solution.py:553
  104.8 0.1 fusion.4
  104.8 1.6 %collective-permute-start.3 = (f32[1,256]{1,0:T(1,128)S(1)}, f32[1,256]{1,0:T(1,128)S(1)}, u32[]{:S(2)}, u32[]{:S(2)}) collective-permute-start(f32[1,256]{1,0:T(1,128)S(1)} %bitcast.11), channel_id=1, source_target_pairs={{0,1},{1,0},{2,3},{3,2},{4,5},{5,4},{6,7},{7,6},{8,9},{9,8},{10,11... | collective-permute-start | bytes 3080 | tf_op jit(solution)/shard_map/ppermute | solution.py:29
  106.4 1.5 %collective-permute-start.4 = (f32[1,256]{1,0:T(1,128)S(1)}, f32[1,256]{1,0:T(1,128)S(1)}, u32[]{:S(2)}, u32[]{:S(2)}) collective-permute-start(f32[1,256]{1,0:T(1,128)S(1)} %bitcast.12), channel_id=1, source_target_pairs={{0,2},{1,3},{2,0},{3,1},{4,6},{5,7},{6,4},{7,5},{8,10},{9,11},{10,... | collective-permute-start | bytes 3080 | tf_op jit(solution)/shard_map/ppermute | solution.py:29
  107.9 0.5 collective-permute-start.5
  108.4 0.0 copy-done.1
  108.4 0.0 copy-done
  108.4 2.9 %shard_map.72 = f32[128,4096]{1,0:T(8,128)} custom-call(f32[128,4096]{1,0:T(8,128)S(1)} %copy-done, bf16[128,4096]{1,0:T(8,128)(2,1)S(1)} %copy-done.1, s16[8,528,256]{2,1,0:T(8,128)(2,1)S(1)} %bitcast.6, f32[128,256]{1,0:T(8,128)S(1)} %get-tuple-element.26.ortho_ref), custom_call_target="tpu_custom_call" | custom-call | flops 805306368 | bytes 7340032 | tf_op jit(solution)/shard_map/pallas_call | solution.py:501
  111.3 0.0 collective-permute-done.3
  111.3 0.0 collective-permute-done.4
  111.3 1.1 collective-permute-done.5
  112.4 2.8 %shard_map.73 = (f32[4096,256]{1,0:T(8,128)}, bf16[128,4096]{1,0:T(8,128)(2,1)}) custom-call(s16[8,528,256]{2,1,0:T(8,128)(2,1)S(1)} %bitcast.7, f32[128,256]{1,0:T(8,128)S(1)} %get-tuple-element.26.ortho_ref, f32[1,256]{1,0:T(1,128)S(1)} %add_rsqrt_fusion.scale_ref), custom_call_target="tpu_custom_call" | custom-call | flops 805306368 | bytes 7340032 | tf_op jit(solution)/shard_map/pallas_call | solution.py:513
  (2 shorter events, 0.0 us)
Async XLA Ops:
  30.2 39.1 %all-to-all-start = ((s16[8,128,512]{2,1,0:T(8,128)(2,1)}), s16[8,128,512]{2,1,0:T(8,128)(2,1)S(1)}, u32[]{:S(2)}, u32[]{:S(2)}) async-start(s16[8,128,512]{2,1,0:T(8,128)(2,1)} %get-tuple-element.20), calls=%async_computation | async-start | bytes 2097152 | tf_op jit(solution)/shard_map/all_to_all | solution.py:542
  33.8 14.8 %copy-start.2 = (f32[2,128]{1,0:T(2,128)S(1)}, f32[2,128]{1,0:T(2,128)}, u32[]{:S(2)}) copy-start(f32[2,128]{1,0:T(2,128)} %get-tuple-element.16.unit_ref) | copy-start | bytes 3076
  33.8 14.8 %copy-start.3 = (s32[8]{0:T(128)S(1)}, s32[8]{0:T(128)}, u32[]{:S(2)}) copy-start(s32[8]{0:T(128)} %perm_ref.1) | copy-start | bytes 100
  38.7 6.3 %collective-permute-start = (f32[128,256]{1,0:T(8,128)S(1)}, f32[128,256]{1,0:T(8,128)S(1)}, u32[]{:S(2)}, u32[]{:S(2)}) collective-permute-start(f32[128,256]{1,0:T(8,128)S(1)} %shard_map.68.refs_0_), channel_id=1, source_target_pairs={{0,1},{1,0},{2,3},{3,2},{4,5},{5,4},{6,7},{7,6},{8,9},{9,8},{10,11... | collective-permute-start | bytes 393224 | tf_op jit(solution)/shard_map/ppermute | solution.py:29
  40.2 8.4 %collective-permute-start.1 = (f32[128,256]{1,0:T(8,128)S(1)}, f32[128,256]{1,0:T(8,128)S(1)}, u32[]{:S(2)}, u32[]{:S(2)}) collective-permute-start(f32[128,256]{1,0:T(8,128)S(1)} %shard_map.68.refs_0_), channel_id=1, source_target_pairs={{0,2},{1,3},{2,0},{3,1},{4,6},{5,7},{6,4},{7,5},{8,10},{9,11},{10,... | collective-permute-start | bytes 393224 | tf_op jit(solution)/shard_map/ppermute | solution.py:29
  41.8 6.9 %collective-permute-start.2 = (f32[128,256]{1,0:T(8,128)S(1)}, f32[128,256]{1,0:T(8,128)S(1)}, u32[]{:S(2)}, u32[]{:S(2)}) collective-permute-start(f32[128,256]{1,0:T(8,128)S(1)} %shard_map.68.refs_0_), channel_id=1, source_target_pairs={{0,3},{1,2},{2,1},{3,0},{4,7},{5,6},{6,5},{7,4},{8,11},{9,10},{10,... | collective-permute-start | bytes 393224 | tf_op jit(solution)/shard_map/ppermute | solution.py:29
  78.7 29.7 %copy-start.1 = (bf16[128,4096]{1,0:T(8,128)(2,1)S(1)}, bf16[128,4096]{1,0:T(8,128)(2,1)}, u32[]{:S(2)}) copy-start(bf16[128,4096]{1,0:T(8,128)(2,1)} %grad_ref.5) | copy-start | bytes 3145732
  81.1 27.3 %copy-start = (f32[128,4096]{1,0:T(8,128)S(1)}, f32[128,4096]{1,0:T(8,128)}, u32[]{:S(2)}) copy-start(f32[128,4096]{1,0:T(8,128)} %momentum_ref.5) | copy-start | bytes 6291460
  104.8 6.4 %collective-permute-start.3 = (f32[1,256]{1,0:T(1,128)S(1)}, f32[1,256]{1,0:T(1,128)S(1)}, u32[]{:S(2)}, u32[]{:S(2)}) collective-permute-start(f32[1,256]{1,0:T(1,128)S(1)} %bitcast.11), channel_id=1, source_target_pairs={{0,1},{1,0},{2,3},{3,2},{4,5},{5,4},{6,7},{7,6},{8,9},{9,8},{10,11... | collective-permute-start | bytes 3080 | tf_op jit(solution)/shard_map/ppermute | solution.py:29
  106.4 4.9 %collective-permute-start.4 = (f32[1,256]{1,0:T(1,128)S(1)}, f32[1,256]{1,0:T(1,128)S(1)}, u32[]{:S(2)}, u32[]{:S(2)}) collective-permute-start(f32[1,256]{1,0:T(1,128)S(1)} %bitcast.12), channel_id=1, source_target_pairs={{0,2},{1,3},{2,0},{3,1},{4,6},{5,7},{6,4},{7,5},{8,10},{9,11},{10,... | collective-permute-start | bytes 3080 | tf_op jit(solution)/shard_map/ppermute | solution.py:29
  107.9 4.5 %collective-permute-start.5 = (f32[1,256]{1,0:T(1,128)S(1)}, f32[1,256]{1,0:T(1,128)S(1)}, u32[]{:S(2)}, u32[]{:S(2)}) collective-permute-start(f32[1,256]{1,0:T(1,128)S(1)} %bitcast.13), channel_id=1, source_target_pairs={{0,3},{1,2},{2,1},{3,0},{4,7},{5,6},{6,5},{7,4},{8,11},{9,10},{10,... | collective-permute-start | bytes 3080 | tf_op jit(solution)/shard_map/ppermute | solution.py:29

commit v18 on v17

--- a/solution.py
+++ b/solution.py
@@ -466,64 +466,52 @@
     return most[:rows] + (most[rows:] + times(split[:rows], right_low))
 
 
-def set_split(split_ref, x):
-    rows = x.shape[0]
+def finish_kernel(
+    gain, momentum_ref, grad_ref, code_ref, ortho_ref, scale_ref, next_ref, basis_ref, update_ref, split_ref
+):
+    rows = momentum_ref.shape[0]
+    scale = scale_ref[...]
 
     @pl.when(pl.program_id(0) == 0)
     def _():
-        split_ref[:rows], split_ref[rows:] = halves(x)
-
-
-def momentum_kernel(momentum_ref, grad_ref, code_ref, ortho_ref, next_ref, split_ref):
-    set_split(split_ref, -KEEP_SHARE * ortho_ref[...])
-    change = times_rows(split_ref, decode(code_ref))
-    next_ref[...] = momentum_ref[...] + grad_ref[...].astype(jnp.float32) + change
-
-
-def update_kernel(gain, code_ref, ortho_ref, scale_ref, basis_ref, update_ref, split_ref):
-    set_split(split_ref, gain * ortho_ref[...])
-    basis = decode(code_ref) * scale_ref[...]
-    basis_ref[...] = basis
-    update_ref[...] = times_rows(split_ref, basis).astype(jnp.bfloat16)
+        ortho = ortho_ref[...]
+        for k, factor in enumerate((-KEEP_SHARE * ortho, gain * ortho * scale)):
+            high, low = halves(factor)
+            split_ref[rows * k : rows * (k + 1)] = high
+            split_ref[rows * (k + 2) : rows * (k + 3)] = low
+
+    right = decode(code_ref)
+    basis_ref[...] = right * scale
+    both = times_rows(split_ref, right)
+    next_ref[...] = momentum_ref[...] + grad_ref[...].astype(jnp.float32) + both[:rows]
+    update_ref[...] = both[rows:].astype(jnp.bfloat16)
 
 
 def finish(momentum, grad, codes, orthonormal, scale, gain):
     rows, cols = momentum.shape
     shares, share, rank = codes.shape
     share -= HEAD
-    group = max(1, min(2048 // share, shares))
+    group = max(1, min(1024 // share, shares))
     block = group * share
     wide = pl.BlockSpec((rows, block), lambda i: (0, i))
     tall = pl.BlockSpec((block, rank), lambda i: (i, 0))
     coded = pl.BlockSpec((group, share + HEAD, rank), lambda i: (i, 0, 0))
-    split = [pltpu.VMEM((2 * rows, rank), jnp.bfloat16)]
-    flops = 6 * rows * cols * rank
-    momentum_next = pl.pallas_call(
-        momentum_kernel,
+    return pl.pallas_call(
+        functools.partial(finish_kernel, gain),
         grid=(cols // block,),
-        in_specs=[wide, wide, coded, whole(orthonormal)],
-        out_specs=wide,
-        out_shape=jax.ShapeDtypeStruct((rows, cols), jnp.float32),
-        scratch_shapes=split,
-        compiler_params=PARAMS,
-        cost_estimate=pl.CostEstimate(
-            flops=flops, bytes_accessed=rows * cols * 10 + cols * rank * 2, transcendentals=0
-        ),
-    )(momentum, grad, codes, orthonormal)
-    q_next, update = pl.pallas_call(
-        functools.partial(update_kernel, gain),
-        grid=(cols // block,),
-        in_specs=[coded, whole(orthonormal), whole(scale)],
-        out_specs=[tall, wide],
+        in_specs=[wide, wide, coded, whole(orthonormal), whole(scale)],
+        out_specs=[wide, tall, wide],
         out_shape=[
+            jax.ShapeDtypeStruct((rows, cols), jnp.float32),
             jax.ShapeDtypeStruct((cols, rank), jnp.float32),
             jax.ShapeDtypeStruct((rows, cols), jnp.bfloat16),
         ],
-        scratch_shapes=split,
+        scratch_shapes=[pltpu.VMEM((4 * rows, rank), jnp.bfloat16)],
         compiler_params=PARAMS,
-        cost_estimate=pl.CostEstimate(flops=flops, bytes_accessed=rows * cols * 2 + cols * rank * 6, transcendentals=0),
-    )(codes, orthonormal, scale)
-    return momentum_next, q_next, update
+        cost_estimate=pl.CostEstimate(
+            flops=12 * rows * cols * rank, bytes_accessed=rows * cols * 12 + cols * rank * 6, transcendentals=0
+        ),
+    )(momentum, grad, codes, orthonormal, scale)
 
 
 def on_device(momentum, grad, q_stored, perm):

time: 115 us -> 115 us (level)
  Pallas kernels: 26.7 us -> 24.9 us
  waiting for transfers between devices: 7.51 us -> 9.19 us
    pallas_call x2 -> x1, Pallas kernels: 5.68 us -> 3.92 us  [finish(): pl.pallas_call(functools.partial(finish_kernel, gain), grid=(cols // bloc...]
    ppermute x6, waiting for transfers between devices: 7.51 us -> 9.19 us  [exchange(): lax.ppermute(x, axis, [(i, i ^ k) for i in range(lax.axis_size(axis))])]
  transfers between devices with their start and end apart: 7 -> 7, of which waited for: 3 -> 6; matrix products, arithmetic and copies ran while one was open for 0% -> 0% of each run, Pallas kernels for 8% -> 5%
where the time goes in v18:
time: 115 us
  blocking collectives  69.6 us (61%)
  Pallas kernels  24.9 us (22%)
  starting transfers between devices  10.7 us (9%)
  waiting for transfers between devices  9.19 us (8%)
    all_gather x1, blocking collectives, on_device(): basis = lax.all_gather(basis, 'fsdp', axis=0, tiled=True)  26.1 us
    all_gather x1, blocking collectives, on_device(): gathered = lax.all_gather(code, 'fsdp', axis=0)  23.5 us
    all_gather x1, blocking collectives, on_device(): packed = lax.all_gather(pack(perm, units, parts), 'fsdp', axis=0)  20 us
    pallas_call x1, Pallas kernels, factor(): pl.pallas_call(factor_kernel, grid=(devices // group,), in_specs=[pl.Bloc...  9.32 us
    ppermute x6, waiting for transfers between devices, exchange(): lax.ppermute(x, axis, [(i, i ^ k) for i in range(lax.axis_size(axis))])  9.19 us
    ppermute x6, starting transfers between devices, exchange(): lax.ppermute(x, axis, [(i, i ^ k) for i in range(lax.axis_size(axis))])  7.11 us
    pallas_call x1, Pallas kernels, project(): pl.pallas_call(project_kernel, grid=(cols // block,), in_specs=[wide, wid...  4.86 us
    pallas_call x1, Pallas kernels, finish(): pl.pallas_call(functools.partial(finish_kernel, gain), grid=(cols // bloc...  3.92 us
  transfers between devices with their start and end apart: 7, of which 6 were waited for; matrix products, arithmetic and copies ran while one was open for 0% of the time, Pallas kernels for 5%

profile of v18, /device:TPU:0, one launch (start us, length us, event | category | flops | bytes accessed | tf_op | source)
XLA Modules:
  0.0 115.2 jit_solution(13008142282822062612)
XLA Ops:
  0.6 3.5 %shard_map.67 = (s16[32,4096]{1,0:T(8,128)(2,1)}, s16[8,128,512]{2,1,0:T(8,128)(2,1)}, f32[2,128]{1,0:T(2,128)}) custom-call(f32[128,4096]{1,0:T(8,128)} %momentum_ref.5, bf16[128,4096]{1,0:T(8,128)(2,1)} %grad_ref.5, bf16[32,4096]{1,0:T(8,128)(2,1)} %basis_ref.1), custom_call_target="tpu_custom_call" | custom-call | flops 5242880 | bytes 4194304 | tf_op jit(solution)/shard_map/pallas_call | solution.py:113
  4.2 26.1 %all-gather.4.code_ref = s16[256,4096]{1,0:T(8,128)(2,1)} all-gather(s16[32,4096]{1,0:T(8,128)(2,1)} %get-tuple-element.16), channel_id=1, replica_groups=mesh['fsdp'=8,'tp'=4] {'fsdp'}, dimensions={0}, use_global_device_ids=true | all-gather | bytes 2359296 | tf_op jit(solution)/shard_map/all_gather | solution.py:528
  30.2 3.6 %all-to-all-start = ((s16[8,128,512]{2,1,0:T(8,128)(2,1)}), s16[8,128,512]{2,1,0:T(8,128)(2,1)S(1)}, u32[]{:S(2)}, u32[]{:S(2)}) async-start(s16[8,128,512]{2,1,0:T(8,128)(2,1)} %get-tuple-element.18), calls=%async_computation | async-start | bytes 2097152 | tf_op jit(solution)/shard_map/all_to_all | solution.py:530
  33.8 0.0 copy-start.2
  33.8 0.0 copy-start.3
  33.8 4.9 %shard_map.68.refs_0_ = f32[128,256]{1,0:T(8,128)S(1)} custom-call(f32[128,4096]{1,0:T(8,128)} %momentum_ref.5, bf16[128,4096]{1,0:T(8,128)(2,1)} %grad_ref.5, s16[256,4096]{1,0:T(8,128)(2,1)} %all-gather.4.code_ref), custom_call_target="tpu_custom_call" | custom-call | flops 536870912 | bytes 5242880 | tf_op jit(solution)/shard_map/pallas_call | solution.py:162
  38.7 2.5 %collective-permute-start.2 = (f32[128,256]{1,0:T(8,128)S(1)}, f32[128,256]{1,0:T(8,128)S(1)}, u32[]{:S(2)}, u32[]{:S(2)}) collective-permute-start(f32[128,256]{1,0:T(8,128)S(1)} %shard_map.68.refs_0_), channel_id=1, source_target_pairs={{0,3},{1,2},{2,1},{3,0},{4,7},{5,6},{6,5},{7,4},{8,11},{9,10},{10,... | collective-permute-start | bytes 393224 | tf_op jit(solution)/shard_map/ppermute | solution.py:29
  41.2 0.5 collective-permute-start.1
  41.7 0.5 collective-permute-start
  42.2 3.5 %collective-permute-done.2.refs_3_ = f32[128,256]{1,0:T(8,128)S(1)} collective-permute-done((f32[128,256]{1,0:T(8,128)S(1)}, f32[128,256]{1,0:T(8,128)S(1)}, u32[]{:S(2)}, u32[]{:S(2)}) %collective-permute-start.2) | collective-permute-done | bytes 131104 | tf_op jit(solution)/shard_map/ppermute | solution.py:29
  45.8 2.5 %collective-permute-done.1.refs_2_ = f32[128,256]{1,0:T(8,128)S(1)} collective-permute-done((f32[128,256]{1,0:T(8,128)S(1)}, f32[128,256]{1,0:T(8,128)S(1)}, u32[]{:S(2)}, u32[]{:S(2)}) %collective-permute-start.1) | collective-permute-done | bytes 131104 | tf_op jit(solution)/shard_map/ppermute | solution.py:29
  48.3 0.1 collective-permute-done.refs_1_
  48.4 0.0 copy-done.2
  48.4 0.0 copy-done.3
  48.4 0.9 shard_map.69
  49.4 20.0 %all-gather = s16[1408,256]{1,0:T(8,128)(2,1)S(1)} all-gather(s16[176,256]{1,0:T(8,128)(2,1)S(1)} %shard_map.69), channel_id=2, replica_groups=mesh['fsdp'=8,'tp'=4] {'fsdp'}, dimensions={0}, use_global_device_ids=true | all-gather | bytes 811008 | tf_op jit(solution)/shard_map/all_gather | solution.py:537
  69.4 0.0 all-to-all-done
  69.4 9.3 %shard_map.70 = (f32[256,1024]{1,0:T(8,128)S(1)}, f32[256,256]{1,0:T(8,128)S(1)}) custom-call(s16[8,176,256]{2,1,0:T(8,128)(2,1)S(1)} %bitcast.6), custom_call_target="tpu_custom_call" | custom-call | flops 805306368 | bytes 1441792 | tf_op jit(solution)/shard_map/pallas_call | solution.py:353
  78.7 0.0 copy-start.1
  78.7 2.4 %shard_map.71 = (s16[528,256]{1,0:T(8,128)(2,1)S(1)}, f32[128,256]{1,0:T(8,128)S(1)}) custom-call(s32[1]{0:T(128)} %bitcast.place_ref, s16[1024,512]{1,0:T(8,128)(2,1)S(1)} %bitcast.5, f32[256,1024]{1,0:T(8,128)S(1)} %get-tuple-element.21.turned_ref.own_ref, s16[8,176,256]{2,1,0:T(8,128)(2,1)S(1)} %bitcast.7, f32[256,256]{1,0:T(8,128)S(1)} %get-tuple-element.22.inverse_ref, ...), custom_call_target="tpu_custom_call" | custom-call | flops 805306368 | bytes 2097152 | tf_op jit(solution)/shard_map/pallas_call | solution.py:422
  81.1 0.0 copy-start
  81.1 23.5 %all-gather.5 = s16[4224,256]{1,0:T(8,128)(2,1)S(1)} all-gather(s16[528,256]{1,0:T(8,128)(2,1)S(1)} %get-tuple-element.23), channel_id=3, replica_groups=mesh['fsdp'=8,'tp'=4] {'fsdp'}, dimensions={0}, use_global_device_ids=true | all-gather | bytes 2433024 | tf_op jit(solution)/shard_map/all_gather | solution.py:541
  104.6 0.1 fusion.4
  104.7 2.5 %collective-permute-start.5 = (f32[1,256]{1,0:T(1,128)S(1)}, f32[1,256]{1,0:T(1,128)S(1)}, u32[]{:S(2)}, u32[]{:S(2)}) collective-permute-start(f32[1,256]{1,0:T(1,128)S(1)} %bitcast.10), channel_id=1, source_target_pairs={{0,3},{1,2},{2,1},{3,0},{4,7},{5,6},{6,5},{7,4},{8,11},{9,10},{10,... | collective-permute-start | bytes 3080 | tf_op jit(solution)/shard_map/ppermute | solution.py:29
  107.2 0.5 collective-permute-start.4
  107.7 0.5 collective-permute-start.3
  108.2 1.0 collective-permute-done.5
  109.2 1.5 %collective-permute-done.4 = f32[1,256]{1,0:T(1,128)S(1)} collective-permute-done((f32[1,256]{1,0:T(1,128)S(1)}, f32[1,256]{1,0:T(1,128)S(1)}, u32[]{:S(2)}, u32[]{:S(2)}) %collective-permute-start.4) | collective-permute-done | bytes 1056 | tf_op jit(solution)/shard_map/ppermute | solution.py:29
  110.7 0.5 collective-permute-done.3
  111.3 0.0 copy-done.1
  111.3 0.0 copy-done
  111.3 3.9 %shard_map.72 = (f32[128,4096]{1,0:T(8,128)}, f32[4096,256]{1,0:T(8,128)}, bf16[128,4096]{1,0:T(8,128)(2,1)}) custom-call(f32[128,4096]{1,0:T(8,128)S(1)} %copy-done, bf16[128,4096]{1,0:T(8,128)(2,1)S(1)} %copy-done.1, s16[8,528,256]{2,1,0:T(8,128)(2,1)S(1)} %bitcast.9, f32[128,256]{1,0:T(8,128)S(1)} %get-tuple-element.24.ortho_ref, ...), custom_call_target="tpu_custom_call" | custom-call | flops 1610612736 | bytes 12582912 | tf_op jit(solution)/shard_map/pallas_call | solution.py:499
  (2 shorter events, 0.0 us)
Async XLA Ops:
  30.2 39.1 %all-to-all-start = ((s16[8,128,512]{2,1,0:T(8,128)(2,1)}), s16[8,128,512]{2,1,0:T(8,128)(2,1)S(1)}, u32[]{:S(2)}, u32[]{:S(2)}) async-start(s16[8,128,512]{2,1,0:T(8,128)(2,1)} %get-tuple-element.18), calls=%async_computation | async-start | bytes 2097152 | tf_op jit(solution)/shard_map/all_to_all | solution.py:530
  33.8 14.6 %copy-start.2 = (f32[2,128]{1,0:T(2,128)S(1)}, f32[2,128]{1,0:T(2,128)}, u32[]{:S(2)}) copy-start(f32[2,128]{1,0:T(2,128)} %get-tuple-element.14.unit_ref) | copy-start | bytes 3076
  33.8 14.6 %copy-start.3 = (s32[8]{0:T(128)S(1)}, s32[8]{0:T(128)}, u32[]{:S(2)}) copy-start(s32[8]{0:T(128)} %perm_ref.1) | copy-start | bytes 100
  38.7 7.1 %collective-permute-start.2 = (f32[128,256]{1,0:T(8,128)S(1)}, f32[128,256]{1,0:T(8,128)S(1)}, u32[]{:S(2)}, u32[]{:S(2)}) collective-permute-start(f32[128,256]{1,0:T(8,128)S(1)} %shard_map.68.refs_0_), channel_id=1, source_target_pairs={{0,3},{1,2},{2,1},{3,0},{4,7},{5,6},{6,5},{7,4},{8,11},{9,10},{10,... | collective-permute-start | bytes 393224 | tf_op jit(solution)/shard_map/ppermute | solution.py:29
  41.2 7.1 %collective-permute-start.1 = (f32[128,256]{1,0:T(8,128)S(1)}, f32[128,256]{1,0:T(8,128)S(1)}, u32[]{:S(2)}, u32[]{:S(2)}) collective-permute-start(f32[128,256]{1,0:T(8,128)S(1)} %shard_map.68.refs_0_), channel_id=1, source_target_pairs={{0,2},{1,3},{2,0},{3,1},{4,6},{5,7},{6,4},{7,5},{8,10},{9,11},{10,... | collective-permute-start | bytes 393224 | tf_op jit(solution)/shard_map/ppermute | solution.py:29
  41.7 6.7 %collective-permute-start = (f32[128,256]{1,0:T(8,128)S(1)}, f32[128,256]{1,0:T(8,128)S(1)}, u32[]{:S(2)}, u32[]{:S(2)}) collective-permute-start(f32[128,256]{1,0:T(8,128)S(1)} %shard_map.68.refs_0_), channel_id=1, source_target_pairs={{0,1},{1,0},{2,3},{3,2},{4,5},{5,4},{6,7},{7,6},{8,9},{9,8},{10,11... | collective-permute-start | bytes 393224 | tf_op jit(solution)/shard_map/ppermute | solution.py:29
  78.7 32.6 %copy-start.1 = (bf16[128,4096]{1,0:T(8,128)(2,1)S(1)}, bf16[128,4096]{1,0:T(8,128)(2,1)}, u32[]{:S(2)}) copy-start(bf16[128,4096]{1,0:T(8,128)(2,1)} %grad_ref.5) | copy-start | bytes 3145732
  81.1 30.2 %copy-start = (f32[128,4096]{1,0:T(8,128)S(1)}, f32[128,4096]{1,0:T(8,128)}, u32[]{:S(2)}) copy-start(f32[128,4096]{1,0:T(8,128)} %momentum_ref.5) | copy-start | bytes 6291460
  104.7 4.5 %collective-permute-start.5 = (f32[1,256]{1,0:T(1,128)S(1)}, f32[1,256]{1,0:T(1,128)S(1)}, u32[]{:S(2)}, u32[]{:S(2)}) collective-permute-start(f32[1,256]{1,0:T(1,128)S(1)} %bitcast.10), channel_id=1, source_target_pairs={{0,3},{1,2},{2,1},{3,0},{4,7},{5,6},{6,5},{7,4},{8,11},{9,10},{10,... | collective-permute-start | bytes 3080 | tf_op jit(solution)/shard_map/ppermute | solution.py:29
  107.2 3.6 %collective-permute-start.4 = (f32[1,256]{1,0:T(1,128)S(1)}, f32[1,256]{1,0:T(1,128)S(1)}, u32[]{:S(2)}, u32[]{:S(2)}) collective-permute-start(f32[1,256]{1,0:T(1,128)S(1)} %bitcast.11), channel_id=1, source_target_pairs={{0,2},{1,3},{2,0},{3,1},{4,6},{5,7},{6,4},{7,5},{8,10},{9,11},{10,... | collective-permute-start | bytes 3080 | tf_op jit(solution)/shard_map/ppermute | solution.py:29
  107.7 3.6 %collective-permute-start.3 = (f32[1,256]{1,0:T(1,128)S(1)}, f32[1,256]{1,0:T(1,128)S(1)}, u32[]{:S(2)}, u32[]{:S(2)}) collective-permute-start(f32[1,256]{1,0:T(1,128)S(1)} %bitcast.12), channel_id=1, source_target_pairs={{0,1},{1,0},{2,3},{3,2},{4,5},{5,4},{6,7},{7,6},{8,9},{9,8},{10,11... | collective-permute-start | bytes 3080 | tf_op jit(solution)/shard_map/ppermute | solution.py:29

commit v19 on v18

--- a/solution.py
+++ b/solution.py
@@ -65,6 +65,27 @@
     return x.astype(jnp.int32).astype(jnp.int16)
 
 
+def cut(value, group):
+    step = 2.0 ** (16 // group)
+    high = jnp.floor(value + 0.5)
+    low = jnp.minimum(jnp.floor((value - high) * step + 0.5), 0.5 * step - 1.0)
+    part = value.shape[0] // group
+    packed = low[:part]
+    for k in range(1, group):
+        packed = packed * step + (low[part * k : part * (k + 1)] + 0.5 * step)
+    return jnp.concatenate([whole_number(high), whole_number(packed)], axis=0)
+
+
+def join(code, size, group):
+    bits = 16 // group
+    step = 2**bits
+    low = code[:, size : size + size // group]
+    shifts = [bits * k for k in reversed(range(group))]
+    lows = [low >> shifts[0]] + [((low >> shift) & (step - 1)) - step // 2 for shift in shifts[1:]]
+    low = jnp.concatenate(lows, axis=1).astype(jnp.float32)
+    return code[:, :size].astype(jnp.float32) + low * (1.0 / step)
+
+
 def set_head(head_ref, *rows):
     place = lax.broadcasted_iota(jnp.int32, head_ref.shape, 0)
     head = jnp.zeros(head_ref.shape, jnp.float32)
@@ -91,7 +112,7 @@
     exponent, mantissa = code_unit(jnp.max(top, axis=1, keepdims=True))
     inverse = 1.0 / unit_of(exponent, mantissa)
     for k, span in enumerate(spans):
-        code_ref[k] = whole_number(jnp.floor(combined(span) * inverse + 0.5))
+        code_ref[k] = cut(combined(span) * inverse, 4)
         basis_code_ref[:, span] = code_basis(basis_ref[:, span])
     step = pl.program_id(0)
     here = pl.ds(pl.multiple_of(step * rows, rows), rows)
@@ -104,10 +125,14 @@
             unit_ref[k : k + 1, :] = column_ref[k].T[:1]
 
 
+def row_steps(basis):
+    return 2 if basis.shape[0] % 32 == 0 else 1
+
+
 def prepare(momentum, grad, basis, share):
     rows, cols = momentum.shape
     width = share if share % 128 == 0 else cols
-    steps = 2 if basis.shape[0] % 32 == 0 else 1
+    steps = row_steps(basis)
     wide = pl.BlockSpec((rows // steps, cols), lambda i: (i, 0))
     narrow = pl.BlockSpec((basis.shape[0] // steps, cols), lambda i: (i, 0))
     return pl.pallas_call(
@@ -116,12 +141,12 @@
         in_specs=[wide, wide, narrow],
         out_specs=[
             narrow,
-            pl.BlockSpec((cols // width, rows // steps, width), lambda i: (0, i, 0)),
+            pl.BlockSpec((cols // width, rows // steps * 5 // 4, width), lambda i: (0, i, 0)),
             pl.BlockSpec((2, rows), lambda i: (0, 0)),
         ],
         out_shape=[
             jax.ShapeDtypeStruct(basis.shape, jnp.int16),
-            jax.ShapeDtypeStruct((cols // width, rows, width), jnp.int16),
+            jax.ShapeDtypeStruct((cols // width, rows * 5 // 4, width), jnp.int16),
             jax.ShapeDtypeStruct((2, rows), jnp.float32),
         ],
         scratch_shapes=[pltpu.VMEM((2, rows, 128), jnp.float32)],
@@ -138,12 +163,12 @@
     combined = momentum_ref[...] + grad_ref[...].astype(jnp.float32)
     rows = combined.shape[0]
     part = lax.dot_general(
-        jnp.concatenate(halves(combined), axis=0),
+        jnp.concatenate(split_three(combined), axis=0),
         basis,
         (((1,), (1,)), ((), ())),
         preferred_element_type=jnp.float32,
     )
-    part = part[:rows] + part[rows:]
+    part = part[:rows] + (part[rows : 2 * rows] + part[2 * rows :])
 
     @pl.when(pl.program_id(0) == 0)
     def _():
@@ -187,17 +212,10 @@
         parts = [parts[k] + parts[k + 1] for k in range(0, len(parts), 2)]
     total = jnp.dot(parts[0], order, precision=HIGH, preferred_element_type=jnp.float32)
     exponent, mantissa = code_unit(jnp.max(jnp.abs(total), axis=0, keepdims=True))
-    value = total * (1.0 / unit_of(exponent, mantissa))
-    high = jnp.floor(value + 0.5)
-    out_ref[:rows] = whole_number(high)
-    low = jnp.minimum(jnp.floor((value - high) * 16.0 + 0.5), 7.0)
-    part = rows // 4
-    packed = low[:part]
-    for k in range(1, 4):
-        packed = packed * 16.0 + (low[part * k : part * (k + 1)] + 8.0)
-    out_ref[rows : rows + part] = whole_number(packed)
+    coded = rows + rows // 2
+    out_ref[:coded] = cut(total * (1.0 / unit_of(exponent, mantissa)), 2)
     units = jnp.concatenate([unit_ref[...], jnp.zeros((2, rank - rows), jnp.float32)], axis=1)
-    set_head(out_ref.at[rows + part :], exponent, mantissa, units[:1], units[1:])
+    set_head(out_ref.at[coded:], exponent, mantissa, units[:1], units[1:])
 
 
 def pack(perm, units, parts):
@@ -208,9 +226,9 @@
             num_scalar_prefetch=1,
             grid=(1,),
             in_specs=[whole(x) for x in (units, *parts)],
-            out_specs=pl.BlockSpec((rows + rows // 4 + HEAD, rank), lambda *_: (0, 0)),
+            out_specs=pl.BlockSpec((rows + rows // 2 + HEAD, rank), lambda *_: (0, 0)),
         ),
-        out_shape=jax.ShapeDtypeStruct((rows + rows // 4 + HEAD, rank), jnp.int16),
+        out_shape=jax.ShapeDtypeStruct((rows + rows // 2 + HEAD, rank), jnp.int16),
         compiler_params=PARAMS,
         cost_estimate=pl.CostEstimate(flops=12 * rows * rank * rank, bytes_accessed=rank * rank * 4, transcendentals=0),
     )(perm, units, *parts)
@@ -313,13 +331,10 @@
 
 def factor_kernel(code_ref, turned_ref, out_ref, gram_ref, mixed_ref, work, band):
     count, size, rank = code_ref.shape
-    size = (size - HEAD) * 4 // 5
+    size = (size - HEAD) * 2 // 3
     code = code_ref[...].astype(jnp.int32)
-    low = code[:, size : size + size // 4]
-    low = jnp.concatenate([low >> 12, *[((low >> shift) & 15) - 8 for shift in (8, 4, 0)]], axis=1)
-    head = code[:, size + size // 4 :].astype(jnp.float32)
-    part = code[:, :size].astype(jnp.float32) + low.astype(jnp.float32) * (1.0 / 16.0)
-    part = part * unit_of(head[:, :1], head[:, 1:2])
+    head = code[:, size + size // 2 :].astype(jnp.float32)
+    part = join(code, size, 2) * unit_of(head[:, :1], head[:, 1:2])
     turned = part.reshape(count * size, rank).T
     turned_ref[...] = turned
 
@@ -348,7 +363,7 @@
 
 def factor(codes):
     devices, size, rank = codes.shape
-    rows = (size - HEAD) * 4 // 5
+    rows = (size - HEAD) * 2 // 3
     group = min(devices, max(1, 1024 // rows))
     return pl.pallas_call(
         factor_kernel,
@@ -372,7 +387,7 @@
     )(codes)
 
 
-def encode_kernel(place_ref, source_ref, turned_ref, head_ref, inverse_ref, own_ref, code_ref, ortho_ref, mixed_ref):
+def encode_kernel(chunk, place_ref, source_ref, turned_ref, head_ref, inverse_ref, own_ref, code_ref, ortho_ref, mixed_ref):
     def times(a, b):
         return jnp.dot(a, b, preferred_element_type=jnp.float32)
 
@@ -380,14 +395,17 @@
         return lax.dot_general(a, b, (((0,), (1,)), ((), ())), precision=HIGH, preferred_element_type=jnp.float32)
 
     rank = turned_ref.shape[0]
-    source_high, source_low = halves(source_ref[...].astype(jnp.int32).astype(jnp.float32))
+    code = source_ref[...].astype(jnp.int32)
+    share = code.shape[1]
+    source_high, source_low = halves(join(code.reshape(-1, chunk * 5 // 4, share), chunk, 4).reshape(-1, share))
     head = head_ref[...].astype(jnp.int32).astype(jnp.float32)
     devices = head.shape[0]
     rows = turned_ref.shape[1] // devices
     unit = jnp.concatenate([unit_of(head[k, 2:3, :rows], head[k, 3:4, :rows]) for k in range(devices)], axis=1)
-    scaled_high, scaled_low = halves(turned_ref[...] * unit)
-    most = times(jnp.concatenate([scaled_high, scaled_low], axis=0), source_high)
-    part = most[:rank] + (most[rank:] + times(scaled_high, source_low))
+    scaled = split_three(turned_ref[...] * unit)
+    most = times(jnp.concatenate(scaled, axis=0), source_high)
+    less = times(jnp.concatenate(scaled[:2], axis=0), source_low)
+    part = most[:rank] + (most[rank : 2 * rank] + less[:rank] + (most[2 * rank :] + less[rank:]))
     first, last = pl.program_id(0) == 0, pl.program_id(0) == pl.num_programs(0) - 1
 
     @pl.when(first)
@@ -414,18 +432,18 @@
         set_head(code_ref.at[rows:], exponent, mantissa, square_exponent, square_high, square_low)
 
 
-def encode(place, source, turned, packed, inverse_low, rows):
-    total, share = source.shape
-    rank = turned.shape[0]
+def encode(place, source, turned, packed, inverse_low, rows, chunk):
+    share = source.shape[1]
+    rank, total = turned.shape
     block = min(1024, total)
     size = packed.shape[1]
     return pl.pallas_call(
-        encode_kernel,
+        functools.partial(encode_kernel, chunk),
         grid_spec=pltpu.PrefetchScalarGridSpec(
             num_scalar_prefetch=1,
             grid=(total // block,),
             in_specs=[
-                pl.BlockSpec((block, share), lambda i, place: (i, 0)),
+                pl.BlockSpec((block * 5 // 4, share), lambda i, place: (i, 0)),
                 pl.BlockSpec((rank, block), lambda i, place: (0, i)),
                 pl.BlockSpec((block // rows, HEAD, rank), lambda i, place: (i, size // HEAD - 1, 0)),
                 whole(inverse_low),
@@ -524,10 +542,11 @@
     share = cols // num_blocks
 
     basis, codes, units = prepare(momentum, grad, q_stored, share)
-    codes = codes.reshape(-1, rows, codes.shape[2] // share, share).swapaxes(1, 2).reshape(num_blocks, rows, share)
+    coded = rows * 5 // 4
+    codes = codes.reshape(-1, coded, codes.shape[2] // share, share).swapaxes(1, 2).reshape(num_blocks, coded, share)
     basis = lax.all_gather(basis, "fsdp", axis=0, tiled=True)
     codes, basis = lax.optimization_barrier((codes, basis))
-    codes = lax.all_to_all(codes, "fsdp", split_axis=0, concat_axis=0).reshape(row_total, share)
+    codes = lax.all_to_all(codes, "fsdp", split_axis=0, concat_axis=0).reshape(num_blocks * coded, share)
 
     near, step = project(momentum, grad, basis), 1
     while 4 * step < num_cols:
@@ -537,7 +556,8 @@
     packed = lax.all_gather(pack(perm, units, parts), "fsdp", axis=0)
     packed, codes = lax.optimization_barrier((packed, codes))
     turned, inverse_low = factor(packed)
-    code, orthonormal = encode(lax.axis_index("fsdp").reshape(1), codes, turned, packed, inverse_low, rows)
+    chunk = rows // row_steps(q_stored)
+    code, orthonormal = encode(lax.axis_index("fsdp").reshape(1), codes, turned, packed, inverse_low, rows, chunk)
     gathered = lax.all_gather(code, "fsdp", axis=0)
     head = gathered[:, share : share + 5].astype(jnp.float32)
     parts = (head[:, 3] + head[:, 4] * (1.0 / 16384.0)) * jnp.exp2(head[:, 2] - 13.0)

time: 115 us -> 123 us (1.070)
  blocking collectives: 69.6 us -> 75.6 us
  Pallas kernels: 24.9 us -> 26.6 us
    all_gather x1, blocking collectives: 20 us -> 26 us  [on_device(): packed = lax.all_gather(pack(perm, units, parts), 'fsdp', axis=0)]
where the time goes in v19:
time: 123 us
  blocking collectives  75.6 us (61%)
  Pallas kernels  26.6 us (22%)
  starting transfers between devices  10.7 us (9%)
  waiting for transfers between devices  9.2 us (7%)
    all_gather x1, blocking collectives, on_device(): basis = lax.all_gather(basis, 'fsdp', axis=0, tiled=True)  26.1 us
    all_gather x1, blocking collectives, on_device(): packed = lax.all_gather(pack(perm, units, parts), 'fsdp', axis=0)  26 us
    all_gather x1, blocking collectives, on_device(): gathered = lax.all_gather(code, 'fsdp', axis=0)  23.6 us
    pallas_call x1, Pallas kernels, factor(): pl.pallas_call(factor_kernel, grid=(devices // group,), in_specs=[pl.Bloc...  9.31 us
    ppermute x6, waiting for transfers between devices, exchange(): lax.ppermute(x, axis, [(i, i ^ k) for i in range(lax.axis_size(axis))])  9.19 us
    ppermute x6, starting transfers between devices, exchange(): lax.ppermute(x, axis, [(i, i ^ k) for i in range(lax.axis_size(axis))])  7.11 us
    pallas_call x1, Pallas kernels, project(): pl.pallas_call(project_kernel, grid=(cols // block,), in_specs=[wide, wid...  5.03 us
    pallas_call x1, Pallas kernels, prepare(): pl.pallas_call(prepare_kernel, grid=(steps,), in_specs=[wide, wide, narro...  4.31 us
  transfers between devices with their start and end apart: 7, of which 6 were waited for; matrix products, arithmetic and copies ran while one was open for 0% of the time, Pallas kernels for 5%

profile of v19, /device:TPU:0, one launch (start us, length us, event | category | flops | bytes accessed | tf_op | source)
XLA Modules:
  0.0 122.9 jit_solution(13461697068379456025)
XLA Ops:
  0.6 4.3 %shard_map.67 = (s16[32,4096]{1,0:T(8,128)(2,1)}, s16[8,160,512]{2,1,0:T(8,128)(2,1)}, f32[2,128]{1,0:T(2,128)}) custom-call(f32[128,4096]{1,0:T(8,128)} %momentum_ref.5, bf16[128,4096]{1,0:T(8,128)(2,1)} %grad_ref.5, bf16[32,4096]{1,0:T(8,128)(2,1)} %basis_ref.1), custom_call_target="tpu_custom_call" | custom-call | flops 5242880 | bytes 4194304 | tf_op jit(solution)/shard_map/pallas_call | solution.py:138
  4.9 26.1 %all-gather.4.code_ref = s16[256,4096]{1,0:T(8,128)(2,1)} all-gather(s16[32,4096]{1,0:T(8,128)(2,1)} %get-tuple-element.16), channel_id=1, replica_groups=mesh['fsdp'=8,'tp'=4] {'fsdp'}, dimensions={0}, use_global_device_ids=true | all-gather | bytes 2359296 | tf_op jit(solution)/shard_map/all_gather | solution.py:547
  31.0 3.6 %all-to-all-start = ((s16[8,160,512]{2,1,0:T(8,128)(2,1)}), s16[8,160,512]{2,1,0:T(8,128)(2,1)S(1)}, u32[]{:S(2)}, u32[]{:S(2)}) async-start(s16[8,160,512]{2,1,0:T(8,128)(2,1)} %get-tuple-element.18), calls=%async_computation | async-start | bytes 2621440 | tf_op jit(solution)/shard_map/all_to_all | solution.py:549
  34.6 0.0 copy-start.2
  34.6 0.0 copy-start.3
  34.6 5.0 %shard_map.68.refs_0_ = f32[128,256]{1,0:T(8,128)S(1)} custom-call(f32[128,4096]{1,0:T(8,128)} %momentum_ref.5, bf16[128,4096]{1,0:T(8,128)(2,1)} %grad_ref.5, s16[256,4096]{1,0:T(8,128)(2,1)} %all-gather.4.code_ref), custom_call_target="tpu_custom_call" | custom-call | flops 536870912 | bytes 5242880 | tf_op jit(solution)/shard_map/pallas_call | solution.py:187
  39.7 2.5 %collective-permute-start.2 = (f32[128,256]{1,0:T(8,128)S(1)}, f32[128,256]{1,0:T(8,128)S(1)}, u32[]{:S(2)}, u32[]{:S(2)}) collective-permute-start(f32[128,256]{1,0:T(8,128)S(1)} %shard_map.68.refs_0_), channel_id=1, source_target_pairs={{0,3},{1,2},{2,1},{3,0},{4,7},{5,6},{6,5},{7,4},{8,11},{9,10},{10,... | collective-permute-start | bytes 393224 | tf_op jit(solution)/shard_map/ppermute | solution.py:29
  42.2 0.5 collective-permute-start.1
  42.7 0.5 collective-permute-start
  43.2 3.6 %collective-permute-done.2.refs_3_ = f32[128,256]{1,0:T(8,128)S(1)} collective-permute-done((f32[128,256]{1,0:T(8,128)S(1)}, f32[128,256]{1,0:T(8,128)S(1)}, u32[]{:S(2)}, u32[]{:S(2)}) %collective-permute-start.2) | collective-permute-done | bytes 131104 | tf_op jit(solution)/shard_map/ppermute | solution.py:29
  46.8 2.5 %collective-permute-done.1.refs_2_ = f32[128,256]{1,0:T(8,128)S(1)} collective-permute-done((f32[128,256]{1,0:T(8,128)S(1)}, f32[128,256]{1,0:T(8,128)S(1)}, u32[]{:S(2)}, u32[]{:S(2)}) %collective-permute-start.1) | collective-permute-done | bytes 131104 | tf_op jit(solution)/shard_map/ppermute | solution.py:29
  49.3 0.1 collective-permute-done.refs_1_
  49.4 0.0 copy-done.2
  49.4 0.0 copy-done.3
  49.4 0.9 shard_map.69
  50.3 26.0 %all-gather = s16[1664,256]{1,0:T(8,128)(2,1)S(1)} all-gather(s16[208,256]{1,0:T(8,128)(2,1)S(1)} %shard_map.69), channel_id=2, replica_groups=mesh['fsdp'=8,'tp'=4] {'fsdp'}, dimensions={0}, use_global_device_ids=true | all-gather | bytes 958464 | tf_op jit(solution)/shard_map/all_gather | solution.py:556
  76.3 0.0 all-to-all-done
  76.3 9.3 %shard_map.70 = (f32[256,1024]{1,0:T(8,128)S(1)}, f32[256,256]{1,0:T(8,128)S(1)}) custom-call(s16[8,208,256]{2,1,0:T(8,128)(2,1)S(1)} %bitcast.6), custom_call_target="tpu_custom_call" | custom-call | flops 805306368 | bytes 1703936 | tf_op jit(solution)/shard_map/pallas_call | solution.py:368
  85.6 0.0 copy-start.1
  85.7 3.0 %shard_map.71 = (s16[528,256]{1,0:T(8,128)(2,1)S(1)}, f32[128,256]{1,0:T(8,128)S(1)}) custom-call(s32[1]{0:T(128)} %bitcast.place_ref, s16[1280,512]{1,0:T(8,128)(2,1)S(1)} %bitcast.5, f32[256,1024]{1,0:T(8,128)S(1)} %get-tuple-element.21.turned_ref.own_ref, s16[8,208,256]{2,1,0:T(8,128)(2,1)S(1)} %bitcast.7, f32[256,256]{1,0:T(8,128)S(1)} %get-tuple-element.22.inverse_ref, ...), custom_call_target="tpu_custom_call" | custom-call | flops 805306368 | bytes 2097152 | tf_op jit(solution)/shard_map/pallas_call | solution.py:440
  88.7 0.0 copy-start
  88.7 23.6 %all-gather.5 = s16[4224,256]{1,0:T(8,128)(2,1)S(1)} all-gather(s16[528,256]{1,0:T(8,128)(2,1)S(1)} %get-tuple-element.23), channel_id=3, replica_groups=mesh['fsdp'=8,'tp'=4] {'fsdp'}, dimensions={0}, use_global_device_ids=true | all-gather | bytes 2433024 | tf_op jit(solution)/shard_map/all_gather | solution.py:561
  112.3 0.1 fusion.4
  112.4 2.5 %collective-permute-start.5 = (f32[1,256]{1,0:T(1,128)S(1)}, f32[1,256]{1,0:T(1,128)S(1)}, u32[]{:S(2)}, u32[]{:S(2)}) collective-permute-start(f32[1,256]{1,0:T(1,128)S(1)} %bitcast.10), channel_id=1, source_target_pairs={{0,3},{1,2},{2,1},{3,0},{4,7},{5,6},{6,5},{7,4},{8,11},{9,10},{10,... | collective-permute-start | bytes 3080 | tf_op jit(solution)/shard_map/ppermute | solution.py:29
  114.9 0.5 collective-permute-start.4
  115.4 0.5 collective-permute-start.3
  115.9 1.0 collective-permute-done.5
  116.9 1.6 %collective-permute-done.4 = f32[1,256]{1,0:T(1,128)S(1)} collective-permute-done((f32[1,256]{1,0:T(1,128)S(1)}, f32[1,256]{1,0:T(1,128)S(1)}, u32[]{:S(2)}, u32[]{:S(2)}) %collective-permute-start.4) | collective-permute-done | bytes 1056 | tf_op jit(solution)/shard_map/ppermute | solution.py:29
  118.5 0.5 collective-permute-done.3
  119.0 0.0 copy-done.1
  119.0 0.0 copy-done
  119.0 3.9 %shard_map.72 = (f32[128,4096]{1,0:T(8,128)}, f32[4096,256]{1,0:T(8,128)}, bf16[128,4096]{1,0:T(8,128)(2,1)}) custom-call(f32[128,4096]{1,0:T(8,128)S(1)} %copy-done, bf16[128,4096]{1,0:T(8,128)(2,1)S(1)} %copy-done.1, s16[8,528,256]{2,1,0:T(8,128)(2,1)S(1)} %bitcast.9, f32[128,256]{1,0:T(8,128)S(1)} %get-tuple-element.24.ortho_ref, ...), custom_call_target="tpu_custom_call" | custom-call | flops 1610612736 | bytes 12582912 | tf_op jit(solution)/shard_map/pallas_call | solution.py:517
  (2 shorter events, 0.0 us)
Async XLA Ops:
  31.0 45.3 %all-to-all-start = ((s16[8,160,512]{2,1,0:T(8,128)(2,1)}), s16[8,160,512]{2,1,0:T(8,128)(2,1)S(1)}, u32[]{:S(2)}, u32[]{:S(2)}) async-start(s16[8,160,512]{2,1,0:T(8,128)(2,1)} %get-tuple-element.18), calls=%async_computation | async-start | bytes 2621440 | tf_op jit(solution)/shard_map/all_to_all | solution.py:549
  34.6 14.8 %copy-start.2 = (f32[2,128]{1,0:T(2,128)S(1)}, f32[2,128]{1,0:T(2,128)}, u32[]{:S(2)}) copy-start(f32[2,128]{1,0:T(2,128)} %get-tuple-element.14.unit_ref) | copy-start | bytes 3076
  34.6 14.8 %copy-start.3 = (s32[8]{0:T(128)S(1)}, s32[8]{0:T(128)}, u32[]{:S(2)}) copy-start(s32[8]{0:T(128)} %perm_ref.1) | copy-start | bytes 100
  39.7 7.1 %collective-permute-start.2 = (f32[128,256]{1,0:T(8,128)S(1)}, f32[128,256]{1,0:T(8,128)S(1)}, u32[]{:S(2)}, u32[]{:S(2)}) collective-permute-start(f32[128,256]{1,0:T(8,128)S(1)} %shard_map.68.refs_0_), channel_id=1, source_target_pairs={{0,3},{1,2},{2,1},{3,0},{4,7},{5,6},{6,5},{7,4},{8,11},{9,10},{10,... | collective-permute-start | bytes 393224 | tf_op jit(solution)/shard_map/ppermute | solution.py:29
  42.2 7.1 %collective-permute-start.1 = (f32[128,256]{1,0:T(8,128)S(1)}, f32[128,256]{1,0:T(8,128)S(1)}, u32[]{:S(2)}, u32[]{:S(2)}) collective-permute-start(f32[128,256]{1,0:T(8,128)S(1)} %shard_map.68.refs_0_), channel_id=1, source_target_pairs={{0,2},{1,3},{2,0},{3,1},{4,6},{5,7},{6,4},{7,5},{8,10},{9,11},{10,... | collective-permute-start | bytes 393224 | tf_op jit(solution)/shard_map/ppermute | solution.py:29
  42.7 6.7 %collective-permute-start = (f32[128,256]{1,0:T(8,128)S(1)}, f32[128,256]{1,0:T(8,128)S(1)}, u32[]{:S(2)}, u32[]{:S(2)}) collective-permute-start(f32[128,256]{1,0:T(8,128)S(1)} %shard_map.68.refs_0_), channel_id=1, source_target_pairs={{0,1},{1,0},{2,3},{3,2},{4,5},{5,4},{6,7},{7,6},{8,9},{9,8},{10,11... | collective-permute-start | bytes 393224 | tf_op jit(solution)/shard_map/ppermute | solution.py:29
  85.6 33.3 %copy-start.1 = (bf16[128,4096]{1,0:T(8,128)(2,1)S(1)}, bf16[128,4096]{1,0:T(8,128)(2,1)}, u32[]{:S(2)}) copy-start(bf16[128,4096]{1,0:T(8,128)(2,1)} %grad_ref.5) | copy-start | bytes 3145732
  88.7 30.3 %copy-start = (f32[128,4096]{1,0:T(8,128)S(1)}, f32[128,4096]{1,0:T(8,128)}, u32[]{:S(2)}) copy-start(f32[128,4096]{1,0:T(8,128)} %momentum_ref.5) | copy-start | bytes 6291460
  112.4 4.5 %collective-permute-start.5 = (f32[1,256]{1,0:T(1,128)S(1)}, f32[1,256]{1,0:T(1,128)S(1)}, u32[]{:S(2)}, u32[]{:S(2)}) collective-permute-start(f32[1,256]{1,0:T(1,128)S(1)} %bitcast.10), channel_id=1, source_target_pairs={{0,3},{1,2},{2,1},{3,0},{4,7},{5,6},{6,5},{7,4},{8,11},{9,10},{10,... | collective-permute-start | bytes 3080 | tf_op jit(solution)/shard_map/ppermute | solution.py:29
  114.9 3.6 %collective-permute-start.4 = (f32[1,256]{1,0:T(1,128)S(1)}, f32[1,256]{1,0:T(1,128)S(1)}, u32[]{:S(2)}, u32[]{:S(2)}) collective-permute-start(f32[1,256]{1,0:T(1,128)S(1)} %bitcast.11), channel_id=1, source_target_pairs={{0,2},{1,3},{2,0},{3,1},{4,6},{5,7},{6,4},{7,5},{8,10},{9,11},{10,... | collective-permute-start | bytes 3080 | tf_op jit(solution)/shard_map/ppermute | solution.py:29
  115.4 3.6 %collective-permute-start.3 = (f32[1,256]{1,0:T(1,128)S(1)}, f32[1,256]{1,0:T(1,128)S(1)}, u32[]{:S(2)}, u32[]{:S(2)}) collective-permute-start(f32[1,256]{1,0:T(1,128)S(1)} %bitcast.12), channel_id=1, source_target_pairs={{0,1},{1,0},{2,3},{3,2},{4,5},{5,4},{6,7},{7,6},{8,9},{9,8},{10,11... | collective-permute-start | bytes 3080 | tf_op jit(solution)/shard_map/ppermute | solution.py:29

commit v20 on v19

--- a/solution.py
+++ b/solution.py
@@ -73,17 +73,16 @@
     packed = low[:part]
     for k in range(1, group):
         packed = packed * step + (low[part * k : part * (k + 1)] + 0.5 * step)
-    return jnp.concatenate([whole_number(high), whole_number(packed)], axis=0)
-
-
-def join(code, size, group):
+    return whole_number(high), whole_number(packed)
+
+
+def join(high, low, group):
     bits = 16 // group
     step = 2**bits
-    low = code[:, size : size + size // group]
     shifts = [bits * k for k in reversed(range(group))]
     lows = [low >> shifts[0]] + [((low >> shift) & (step - 1)) - step // 2 for shift in shifts[1:]]
     low = jnp.concatenate(lows, axis=1).astype(jnp.float32)
-    return code[:, :size].astype(jnp.float32) + low * (1.0 / step)
+    return high.astype(jnp.float32) + low * (1.0 / step)
 
 
 def set_head(head_ref, *rows):
@@ -103,7 +102,7 @@
     return whole_number(jnp.where(normal, jnp.where(value < 0.0, code - 32768.0, code), 0.0))
 
 
-def prepare_kernel(momentum_ref, grad_ref, basis_ref, basis_code_ref, code_ref, unit_ref, column_ref):
+def prepare_kernel(momentum_ref, grad_ref, basis_ref, basis_code_ref, code_ref, low_ref, unit_ref, column_ref):
     rows, cols = momentum_ref.shape
     width = code_ref.shape[-1]
     spans = [slice(i, i + width) for i in range(0, cols, width)]
@@ -112,7 +111,7 @@
     exponent, mantissa = code_unit(jnp.max(top, axis=1, keepdims=True))
     inverse = 1.0 / unit_of(exponent, mantissa)
     for k, span in enumerate(spans):
-        code_ref[k] = cut(combined(span) * inverse, 4)
+        code_ref[k], low_ref[k] = cut(combined(span) * inverse, 4)
         basis_code_ref[:, span] = code_basis(basis_ref[:, span])
     step = pl.program_id(0)
     here = pl.ds(pl.multiple_of(step * rows, rows), rows)
@@ -141,12 +140,14 @@
         in_specs=[wide, wide, narrow],
         out_specs=[
             narrow,
-            pl.BlockSpec((cols // width, rows // steps * 5 // 4, width), lambda i: (0, i, 0)),
+            pl.BlockSpec((cols // width, rows // steps, width), lambda i: (0, i, 0)),
+            pl.BlockSpec((cols // width, rows // steps // 4, width), lambda i: (0, i, 0)),
             pl.BlockSpec((2, rows), lambda i: (0, 0)),
         ],
         out_shape=[
             jax.ShapeDtypeStruct(basis.shape, jnp.int16),
-            jax.ShapeDtypeStruct((cols // width, rows * 5 // 4, width), jnp.int16),
+            jax.ShapeDtypeStruct((cols // width, rows, width), jnp.int16),
+            jax.ShapeDtypeStruct((cols // width, rows // 4, width), jnp.int16),
             jax.ShapeDtypeStruct((2, rows), jnp.float32),
         ],
         scratch_shapes=[pltpu.VMEM((2, rows, 128), jnp.float32)],
@@ -213,7 +214,7 @@
     total = jnp.dot(parts[0], order, precision=HIGH, preferred_element_type=jnp.float32)
     exponent, mantissa = code_unit(jnp.max(jnp.abs(total), axis=0, keepdims=True))
     coded = rows + rows // 2
-    out_ref[:coded] = cut(total * (1.0 / unit_of(exponent, mantissa)), 2)
+    out_ref[:rows], out_ref[rows:coded] = cut(total * (1.0 / unit_of(exponent, mantissa)), 2)
     units = jnp.concatenate([unit_ref[...], jnp.zeros((2, rank - rows), jnp.float32)], axis=1)
     set_head(out_ref.at[coded:], exponent, mantissa, units[:1], units[1:])
 
@@ -334,7 +335,7 @@
     size = (size - HEAD) * 2 // 3
     code = code_ref[...].astype(jnp.int32)
     head = code[:, size + size // 2 :].astype(jnp.float32)
-    part = join(code, size, 2) * unit_of(head[:, :1], head[:, 1:2])
+    part = join(code[:, :size], code[:, size : size + size // 2], 2) * unit_of(head[:, :1], head[:, 1:2])
     turned = part.reshape(count * size, rank).T
     turned_ref[...] = turned
 
@@ -387,7 +388,7 @@
     )(codes)
 
 
-def encode_kernel(chunk, place_ref, source_ref, turned_ref, head_ref, inverse_ref, own_ref, code_ref, ortho_ref, mixed_ref):
+def encode_kernel(chunk, place_ref, source_ref, low_ref, turned_ref, head_ref, inverse_ref, own_ref, code_ref, ortho_ref, mixed_ref):
     def times(a, b):
         return jnp.dot(a, b, preferred_element_type=jnp.float32)
 
@@ -395,9 +396,10 @@
         return lax.dot_general(a, b, (((0,), (1,)), ((), ())), precision=HIGH, preferred_element_type=jnp.float32)
 
     rank = turned_ref.shape[0]
-    code = source_ref[...].astype(jnp.int32)
-    share = code.shape[1]
-    source_high, source_low = halves(join(code.reshape(-1, chunk * 5 // 4, share), chunk, 4).reshape(-1, share))
+    share = source_ref.shape[1]
+    high, low = source_ref[...].astype(jnp.int32), low_ref[...].astype(jnp.int32)
+    source = join(high.reshape(-1, chunk, share), low.reshape(-1, chunk // 4, share), 4)
+    source_high, source_low = halves(source.reshape(-1, share))
     head = head_ref[...].astype(jnp.int32).astype(jnp.float32)
     devices = head.shape[0]
     rows = turned_ref.shape[1] // devices
@@ -432,7 +434,7 @@
         set_head(code_ref.at[rows:], exponent, mantissa, square_exponent, square_high, square_low)
 
 
-def encode(place, source, turned, packed, inverse_low, rows, chunk):
+def encode(place, source, low, turned, packed, inverse_low, rows, chunk):
     share = source.shape[1]
     rank, total = turned.shape
     block = min(1024, total)
@@ -443,7 +445,8 @@
             num_scalar_prefetch=1,
             grid=(total // block,),
             in_specs=[
-                pl.BlockSpec((block * 5 // 4, share), lambda i, place: (i, 0)),
+                pl.BlockSpec((block, share), lambda i, place: (i, 0)),
+                pl.BlockSpec((block // 4, share), lambda i, place: (i, 0)),
                 pl.BlockSpec((rank, block), lambda i, place: (0, i)),
                 pl.BlockSpec((block // rows, HEAD, rank), lambda i, place: (i, size // HEAD - 1, 0)),
                 whole(inverse_low),
@@ -463,7 +466,7 @@
         cost_estimate=pl.CostEstimate(
             flops=6 * total * share * rank, bytes_accessed=total * (share * 2 + rank * 4), transcendentals=0
         ),
-    )(place, source, turned, packed, inverse_low, turned)
+    )(place, source, low, turned, packed, inverse_low, turned)
 
 
 def decode(code_ref):
@@ -541,12 +544,15 @@
     row_total, col_total = rows * num_blocks, cols * num_cols
     share = cols // num_blocks
 
-    basis, codes, units = prepare(momentum, grad, q_stored, share)
-    coded = rows * 5 // 4
-    codes = codes.reshape(-1, coded, codes.shape[2] // share, share).swapaxes(1, 2).reshape(num_blocks, coded, share)
+    basis, codes, lows, units = prepare(momentum, grad, q_stored, share)
+
+    def trade(x):
+        x = x.reshape(-1, x.shape[1], x.shape[2] // share, share).swapaxes(1, 2).reshape(num_blocks, -1, share)
+        return lax.all_to_all(x, "fsdp", split_axis=0, concat_axis=0).reshape(-1, share)
+
     basis = lax.all_gather(basis, "fsdp", axis=0, tiled=True)
     codes, basis = lax.optimization_barrier((codes, basis))
-    codes = lax.all_to_all(codes, "fsdp", split_axis=0, concat_axis=0).reshape(num_blocks * coded, share)
+    codes = trade(codes)
 
     near, step = project(momentum, grad, basis), 1
     while 4 * step < num_cols:
@@ -554,10 +560,11 @@
         step *= 2
     parts = [near] + [exchange(near, "tp", k) for k in range(step, num_cols, step)]
     packed = lax.all_gather(pack(perm, units, parts), "fsdp", axis=0)
-    packed, codes = lax.optimization_barrier((packed, codes))
+    packed, codes, lows = lax.optimization_barrier((packed, codes, lows))
+    lows = trade(lows)
     turned, inverse_low = factor(packed)
     chunk = rows // row_steps(q_stored)
-    code, orthonormal = encode(lax.axis_index("fsdp").reshape(1), codes, turned, packed, inverse_low, rows, chunk)
+    code, orthonormal = encode(lax.axis_index("fsdp").reshape(1), codes, lows, turned, packed, inverse_low, rows, chunk)
     gathered = lax.all_gather(code, "fsdp", axis=0)
     head = gathered[:, share : share + 5].astype(jnp.float32)
     parts = (head[:, 3] + head[:, 4] * (1.0 / 16384.0)) * jnp.exp2(head[:, 2] - 13.0)

time: 123 us -> 123 us (level)
  blocking collectives: 75.6 us -> 70.5 us
  starting transfers between devices: 10.7 us -> 15 us
    all_gather x1, blocking collectives: 26 us -> 20.4 us  [on_device(): packed = lax.all_gather(pack(perm, units, parts), 'fsdp', axis=0)]
    all_to_all x1 -> x2, starting transfers between devices: 3.57 us -> 7.87 us  [trade(): lax.all_to_all(x, 'fsdp', split_axis=0, concat_axis=0).reshape(-1, share)]
  transfers between devices with their start and end apart: 7 -> 8, of which waited for: 6 -> 7; matrix products, arithmetic and copies ran while one was open for 0% -> 0% of each run, Pallas kernels for 5% -> 12%
where the time goes in v20:
time: 123 us; the launch traced here: 122 us
  blocking collectives  70.5 us (57%)
  Pallas kernels  26.6 us (22%)
  starting transfers between devices  15 us (12%)
  waiting for transfers between devices  9.62 us (8%)
    all_gather x1, blocking collectives, on_device(): basis = lax.all_gather(basis, 'fsdp', axis=0, tiled=True)  26.1 us
    all_gather x1, blocking collectives, on_device(): gathered = lax.all_gather(code, 'fsdp', axis=0)  24 us
    all_gather x1, blocking collectives, on_device(): packed = lax.all_gather(pack(perm, units, parts), 'fsdp', axis=0)  20.4 us
    pallas_call x1, Pallas kernels, factor(): pl.pallas_call(factor_kernel, grid=(devices // group,), in_specs=[pl.Bloc...  9.31 us
    ppermute x6, waiting for transfers between devices, exchange(): lax.ppermute(x, axis, [(i, i ^ k) for i in range(lax.axis_size(axis))])  9.19 us
    all_to_all x2, starting transfers between devices, trade(): lax.all_to_all(x, 'fsdp', split_axis=0, concat_axis=0).reshape(-1, share)  7.87 us
    ppermute x6, starting transfers between devices, exchange(): lax.ppermute(x, axis, [(i, i ^ k) for i in range(lax.axis_size(axis))])  7.11 us
    pallas_call x1, Pallas kernels, project(): pl.pallas_call(project_kernel, grid=(cols // block,), in_specs=[wide, wid...  5.03 us
  transfers between devices with their start and end apart: 8, of which 7 were waited for; matrix products, arithmetic and copies ran while one was open for 0% of the time, Pallas kernels for 12%

profile of v20, /device:TPU:0, one launch (start us, length us, event | category | flops | bytes accessed | tf_op | source)
XLA Modules:
  0.0 122.4 jit_solution(8180331754514016916)
XLA Ops:
  0.6 4.3 %shard_map.67 = (s16[32,4096]{1,0:T(8,128)(2,1)}, s16[8,128,512]{2,1,0:T(8,128)(2,1)}, s16[8,32,512]{2,1,0:T(8,128)(2,1)}, f32[2,128]{1,0:T(2,128)}) custom-call(f32[128,4096]{1,0:T(8,128)} %momentum_ref.5, bf16[128,4096]{1,0:T(8,128)(2,1)} %grad_ref.5, bf16[32,4096]{1,0:T(8,128)(2,1)} %basis_ref.1), custom_call_target="tpu_custom_call" | custom-call | flops 5242880 | bytes 4194304 | tf_op jit(solution)/shard_map/pallas_call | solution.py:137
  4.9 26.1 %all-gather.4.code_ref = s16[256,4096]{1,0:T(8,128)(2,1)} all-gather(s16[32,4096]{1,0:T(8,128)(2,1)} %get-tuple-element.18), channel_id=1, replica_groups=mesh['fsdp'=8,'tp'=4] {'fsdp'}, dimensions={0}, use_global_device_ids=true | all-gather | bytes 2359296 | tf_op jit(solution)/shard_map/all_gather | solution.py:553
  31.0 3.6 %all-to-all-start = ((s16[8,128,512]{2,1,0:T(8,128)(2,1)}), s16[8,128,512]{2,1,0:T(8,128)(2,1)S(1)}, u32[]{:S(2)}, u32[]{:S(2)}) async-start(s16[8,128,512]{2,1,0:T(8,128)(2,1)} %get-tuple-element.20), calls=%async_computation | async-start | bytes 2097152 | tf_op jit(solution)/shard_map/all_to_all | solution.py:551
  34.6 0.0 copy-start.2
  34.6 0.0 copy-start.3
  34.6 5.0 %shard_map.68.refs_0_ = f32[128,256]{1,0:T(8,128)S(1)} custom-call(f32[128,4096]{1,0:T(8,128)} %momentum_ref.5, bf16[128,4096]{1,0:T(8,128)(2,1)} %grad_ref.5, s16[256,4096]{1,0:T(8,128)(2,1)} %all-gather.4.code_ref), custom_call_target="tpu_custom_call" | custom-call | flops 536870912 | bytes 5242880 | tf_op jit(solution)/shard_map/pallas_call | solution.py:188
  39.6 2.5 %collective-permute-start.2 = (f32[128,256]{1,0:T(8,128)S(1)}, f32[128,256]{1,0:T(8,128)S(1)}, u32[]{:S(2)}, u32[]{:S(2)}) collective-permute-start(f32[128,256]{1,0:T(8,128)S(1)} %shard_map.68.refs_0_), channel_id=1, source_target_pairs={{0,3},{1,2},{2,1},{3,0},{4,7},{5,6},{6,5},{7,4},{8,11},{9,10},{10,... | collective-permute-start | bytes 393224 | tf_op jit(solution)/shard_map/ppermute | solution.py:29
  42.2 0.5 collective-permute-start.1
  42.7 0.5 collective-permute-start
  43.2 3.5 %collective-permute-done.2.refs_3_ = f32[128,256]{1,0:T(8,128)S(1)} collective-permute-done((f32[128,256]{1,0:T(8,128)S(1)}, f32[128,256]{1,0:T(8,128)S(1)}, u32[]{:S(2)}, u32[]{:S(2)}) %collective-permute-start.2) | collective-permute-done | bytes 131104 | tf_op jit(solution)/shard_map/ppermute | solution.py:29
  46.7 2.5 %collective-permute-done.1.refs_2_ = f32[128,256]{1,0:T(8,128)S(1)} collective-permute-done((f32[128,256]{1,0:T(8,128)S(1)}, f32[128,256]{1,0:T(8,128)S(1)}, u32[]{:S(2)}, u32[]{:S(2)}) %collective-permute-start.1) | collective-permute-done | bytes 131104 | tf_op jit(solution)/shard_map/ppermute | solution.py:29
  49.3 0.1 collective-permute-done.refs_1_
  49.4 0.0 copy-done.2
  49.4 0.0 copy-done.3
  49.4 0.9 shard_map.69
  50.3 20.4 %all-gather = s16[1664,256]{1,0:T(8,128)(2,1)S(1)} all-gather(s16[208,256]{1,0:T(8,128)(2,1)S(1)} %shard_map.69), channel_id=2, replica_groups=mesh['fsdp'=8,'tp'=4] {'fsdp'}, dimensions={0}, use_global_device_ids=true | all-gather | bytes 958464 | tf_op jit(solution)/shard_map/all_gather | solution.py:562
  70.7 0.0 all-to-all-done
  70.7 4.3 %all-to-all-start.1 = ((s16[8,32,512]{2,1,0:T(8,128)(2,1)}), s16[8,32,512]{2,1,0:T(8,128)(2,1)S(1)}, u32[]{:S(2)}, u32[]{:S(2)}) async-start(s16[8,32,512]{2,1,0:T(8,128)(2,1)} %get-tuple-element.23), calls=%async_computation.1 | async-start | bytes 524288 | tf_op jit(solution)/shard_map/all_to_all | solution.py:551
  75.0 9.3 %shard_map.70 = (f32[256,1024]{1,0:T(8,128)S(1)}, f32[256,256]{1,0:T(8,128)S(1)}) custom-call(s16[8,208,256]{2,1,0:T(8,128)(2,1)S(1)} %bitcast.7), custom_call_target="tpu_custom_call" | custom-call | flops 805306368 | bytes 1703936 | tf_op jit(solution)/shard_map/pallas_call | solution.py:369
  84.3 0.4 all-to-all-done.1
  84.8 0.0 copy-start.1
  84.8 3.0 %shard_map.71 = (s16[528,256]{1,0:T(8,128)(2,1)S(1)}, f32[128,256]{1,0:T(8,128)S(1)}) custom-call(s32[1]{0:T(128)} %bitcast.place_ref, s16[1024,512]{1,0:T(8,128)(2,1)S(1)} %bitcast.6, s16[256,512]{1,0:T(8,128)(2,1)S(1)} %bitcast.11, f32[256,1024]{1,0:T(8,128)S(1)} %get-tuple-element.25.turned_ref.own_ref, s16[8,208,256]{2,1,0:T(8,128)(2,1)S(1)} %bitcast.8, ...), custom_call_target="tpu_custom_call" | custom-call | flops 805306368 | bytes 2097152 | tf_op jit(solution)/shard_map/pallas_call | solution.py:442
  87.8 0.0 copy-start
  87.8 24.0 %all-gather.5 = s16[4224,256]{1,0:T(8,128)(2,1)S(1)} all-gather(s16[528,256]{1,0:T(8,128)(2,1)S(1)} %get-tuple-element.27), channel_id=3, replica_groups=mesh['fsdp'=8,'tp'=4] {'fsdp'}, dimensions={0}, use_global_device_ids=true | all-gather | bytes 2433024 | tf_op jit(solution)/shard_map/all_gather | solution.py:568
  111.9 0.1 fusion.4
  111.9 2.5 %collective-permute-start.5 = (f32[1,256]{1,0:T(1,128)S(1)}, f32[1,256]{1,0:T(1,128)S(1)}, u32[]{:S(2)}, u32[]{:S(2)}) collective-permute-start(f32[1,256]{1,0:T(1,128)S(1)} %bitcast.12), channel_id=1, source_target_pairs={{0,3},{1,2},{2,1},{3,0},{4,7},{5,6},{6,5},{7,4},{8,11},{9,10},{10,... | collective-permute-start | bytes 3080 | tf_op jit(solution)/shard_map/ppermute | solution.py:29
  114.4 0.5 collective-permute-start.4
  114.9 0.5 collective-permute-start.3
  115.5 1.0 collective-permute-done.5
  116.4 1.6 %collective-permute-done.4 = f32[1,256]{1,0:T(1,128)S(1)} collective-permute-done((f32[1,256]{1,0:T(1,128)S(1)}, f32[1,256]{1,0:T(1,128)S(1)}, u32[]{:S(2)}, u32[]{:S(2)}) %collective-permute-start.4) | collective-permute-done | bytes 1056 | tf_op jit(solution)/shard_map/ppermute | solution.py:29
  118.0 0.5 collective-permute-done.3
  118.5 0.0 copy-done.1
  118.5 0.0 copy-done
  118.5 3.9 %shard_map.72 = (f32[128,4096]{1,0:T(8,128)}, f32[4096,256]{1,0:T(8,128)}, bf16[128,4096]{1,0:T(8,128)(2,1)}) custom-call(f32[128,4096]{1,0:T(8,128)S(1)} %copy-done, bf16[128,4096]{1,0:T(8,128)(2,1)S(1)} %copy-done.1, s16[8,528,256]{2,1,0:T(8,128)(2,1)S(1)} %bitcast.10, f32[128,256]{1,0:T(8,128)S(1)} %get-tuple-element.28.ortho_ref, ...), custom_call_target="tpu_custom_call" | custom-call | flops 1610612736 | bytes 12582912 | tf_op jit(solution)/shard_map/pallas_call | solution.py:520
  (2 shorter events, 0.0 us)
Async XLA Ops:
  31.0 39.7 %all-to-all-start = ((s16[8,128,512]{2,1,0:T(8,128)(2,1)}), s16[8,128,512]{2,1,0:T(8,128)(2,1)S(1)}, u32[]{:S(2)}, u32[]{:S(2)}) async-start(s16[8,128,512]{2,1,0:T(8,128)(2,1)} %get-tuple-element.20), calls=%async_computation | async-start | bytes 2097152 | tf_op jit(solution)/shard_map/all_to_all | solution.py:551
  34.6 14.8 %copy-start.2 = (f32[2,128]{1,0:T(2,128)S(1)}, f32[2,128]{1,0:T(2,128)}, u32[]{:S(2)}) copy-start(f32[2,128]{1,0:T(2,128)} %get-tuple-element.16.unit_ref) | copy-start | bytes 3076
  34.6 14.8 %copy-start.3 = (s32[8]{0:T(128)S(1)}, s32[8]{0:T(128)}, u32[]{:S(2)}) copy-start(s32[8]{0:T(128)} %perm_ref.1) | copy-start | bytes 100
  39.6 7.1 %collective-permute-start.2 = (f32[128,256]{1,0:T(8,128)S(1)}, f32[128,256]{1,0:T(8,128)S(1)}, u32[]{:S(2)}, u32[]{:S(2)}) collective-permute-start(f32[128,256]{1,0:T(8,128)S(1)} %shard_map.68.refs_0_), channel_id=1, source_target_pairs={{0,3},{1,2},{2,1},{3,0},{4,7},{5,6},{6,5},{7,4},{8,11},{9,10},{10,... | collective-permute-start | bytes 393224 | tf_op jit(solution)/shard_map/ppermute | solution.py:29
  42.2 7.1 %collective-permute-start.1 = (f32[128,256]{1,0:T(8,128)S(1)}, f32[128,256]{1,0:T(8,128)S(1)}, u32[]{:S(2)}, u32[]{:S(2)}) collective-permute-start(f32[128,256]{1,0:T(8,128)S(1)} %shard_map.68.refs_0_), channel_id=1, source_target_pairs={{0,2},{1,3},{2,0},{3,1},{4,6},{5,7},{6,4},{7,5},{8,10},{9,11},{10,... | collective-permute-start | bytes 393224 | tf_op jit(solution)/shard_map/ppermute | solution.py:29
  42.7 6.7 %collective-permute-start = (f32[128,256]{1,0:T(8,128)S(1)}, f32[128,256]{1,0:T(8,128)S(1)}, u32[]{:S(2)}, u32[]{:S(2)}) collective-permute-start(f32[128,256]{1,0:T(8,128)S(1)} %shard_map.68.refs_0_), channel_id=1, source_target_pairs={{0,1},{1,0},{2,3},{3,2},{4,5},{5,4},{6,7},{7,6},{8,9},{9,8},{10,11... | collective-permute-start | bytes 393224 | tf_op jit(solution)/shard_map/ppermute | solution.py:29
  70.7 14.0 %all-to-all-start.1 = ((s16[8,32,512]{2,1,0:T(8,128)(2,1)}), s16[8,32,512]{2,1,0:T(8,128)(2,1)S(1)}, u32[]{:S(2)}, u32[]{:S(2)}) async-start(s16[8,32,512]{2,1,0:T(8,128)(2,1)} %get-tuple-element.23), calls=%async_computation.1 | async-start | bytes 524288 | tf_op jit(solution)/shard_map/all_to_all | solution.py:551
  84.8 33.7 %copy-start.1 = (bf16[128,4096]{1,0:T(8,128)(2,1)S(1)}, bf16[128,4096]{1,0:T(8,128)(2,1)}, u32[]{:S(2)}) copy-start(bf16[128,4096]{1,0:T(8,128)(2,1)} %grad_ref.5) | copy-start | bytes 3145732
  87.8 30.7 %copy-start = (f32[128,4096]{1,0:T(8,128)S(1)}, f32[128,4096]{1,0:T(8,128)}, u32[]{:S(2)}) copy-start(f32[128,4096]{1,0:T(8,128)} %momentum_ref.5) | copy-start | bytes 6291460
  111.9 4.5 %collective-permute-start.5 = (f32[1,256]{1,0:T(1,128)S(1)}, f32[1,256]{1,0:T(1,128)S(1)}, u32[]{:S(2)}, u32[]{:S(2)}) collective-permute-start(f32[1,256]{1,0:T(1,128)S(1)} %bitcast.12), channel_id=1, source_target_pairs={{0,3},{1,2},{2,1},{3,0},{4,7},{5,6},{6,5},{7,4},{8,11},{9,10},{10,... | collective-permute-start | bytes 3080 | tf_op jit(solution)/shard_map/ppermute | solution.py:29
  114.4 3.6 %collective-permute-start.4 = (f32[1,256]{1,0:T(1,128)S(1)}, f32[1,256]{1,0:T(1,128)S(1)}, u32[]{:S(2)}, u32[]{:S(2)}) collective-permute-start(f32[1,256]{1,0:T(1,128)S(1)} %bitcast.13), channel_id=1, source_target_pairs={{0,2},{1,3},{2,0},{3,1},{4,6},{5,7},{6,4},{7,5},{8,10},{9,11},{10,... | collective-permute-start | bytes 3080 | tf_op jit(solution)/shard_map/ppermute | solution.py:29
  114.9 3.6 %collective-permute-start.3 = (f32[1,256]{1,0:T(1,128)S(1)}, f32[1,256]{1,0:T(1,128)S(1)}, u32[]{:S(2)}, u32[]{:S(2)}) collective-permute-start(f32[1,256]{1,0:T(1,128)S(1)} %bitcast.14), channel_id=1, source_target_pairs={{0,1},{1,0},{2,3},{3,2},{4,5},{5,4},{6,7},{7,6},{8,9},{9,8},{10,11... | collective-permute-start | bytes 3080 | tf_op jit(solution)/shard_map/ppermute | solution.py:29

commit v21 on v20

--- a/solution.py
+++ b/solution.py
@@ -213,8 +213,8 @@
         parts = [parts[k] + parts[k + 1] for k in range(0, len(parts), 2)]
     total = jnp.dot(parts[0], order, precision=HIGH, preferred_element_type=jnp.float32)
     exponent, mantissa = code_unit(jnp.max(jnp.abs(total), axis=0, keepdims=True))
-    coded = rows + rows // 2
-    out_ref[:rows], out_ref[rows:coded] = cut(total * (1.0 / unit_of(exponent, mantissa)), 2)
+    coded = rows + rows // 4
+    out_ref[:rows], out_ref[rows:coded] = cut(total * (1.0 / unit_of(exponent, mantissa)), 4)
     units = jnp.concatenate([unit_ref[...], jnp.zeros((2, rank - rows), jnp.float32)], axis=1)
     set_head(out_ref.at[coded:], exponent, mantissa, units[:1], units[1:])
 
@@ -227,9 +227,9 @@
             num_scalar_prefetch=1,
             grid=(1,),
             in_specs=[whole(x) for x in (units, *parts)],
-            out_specs=pl.BlockSpec((rows + rows // 2 + HEAD, rank), lambda *_: (0, 0)),
+            out_specs=pl.BlockSpec((rows + rows // 4 + HEAD, rank), lambda *_: (0, 0)),
         ),
-        out_shape=jax.ShapeDtypeStruct((rows + rows // 2 + HEAD, rank), jnp.int16),
+        out_shape=jax.ShapeDtypeStruct((rows + rows // 4 + HEAD, rank), jnp.int16),
         compiler_params=PARAMS,
         cost_estimate=pl.CostEstimate(flops=12 * rows * rank * rank, bytes_accessed=rank * rank * 4, transcendentals=0),
     )(perm, units, *parts)
@@ -332,10 +332,10 @@
 
 def factor_kernel(code_ref, turned_ref, out_ref, gram_ref, mixed_ref, work, band):
     count, size, rank = code_ref.shape
-    size = (size - HEAD) * 2 // 3
+    size = (size - HEAD) * 4 // 5
     code = code_ref[...].astype(jnp.int32)
-    head = code[:, size + size // 2 :].astype(jnp.float32)
-    part = join(code[:, :size], code[:, size : size + size // 2], 2) * unit_of(head[:, :1], head[:, 1:2])
+    head = code[:, size + size // 4 :].astype(jnp.float32)
+    part = join(code[:, :size], code[:, size : size + size // 4], 4) * unit_of(head[:, :1], head[:, 1:2])
     turned = part.reshape(count * size, rank).T
     turned_ref[...] = turned
 
@@ -364,7 +364,7 @@
 
 def factor(codes):
     devices, size, rank = codes.shape
-    rows = (size - HEAD) * 2 // 3
+    rows = (size - HEAD) * 4 // 5
     group = min(devices, max(1, 1024 // rows))
     return pl.pallas_call(
         factor_kernel,
@@ -512,7 +512,7 @@
     rows, cols = momentum.shape
     shares, share, rank = codes.shape
     share -= HEAD
-    group = max(1, min(1024 // share, shares))
+    group = max(1, min(2048 // share, shares))
     block = group * share
     wide = pl.BlockSpec((rows, block), lambda i: (0, i))
     tall = pl.BlockSpec((block, rank), lambda i: (i, 0))

time: 123 us -> 122 us (level)
  transfers between devices with their start and end apart: 8 -> 8, of which waited for: 7 -> 7; matrix products, arithmetic and copies ran while one was open for 0% -> 0% of each run, Pallas kernels for 12% -> 13%
where the time goes in v21:
time: 122 us
  blocking collectives  69.9 us (57%)
  Pallas kernels  26.4 us (22%)
  starting transfers between devices  14.9 us (12%)
  waiting for transfers between devices  9.63 us (8%)
    all_gather x1, blocking collectives, on_device(): basis = lax.all_gather(basis, 'fsdp', axis=0, tiled=True)  26.1 us
    all_gather x1, blocking collectives, on_device(): gathered = lax.all_gather(code, 'fsdp', axis=0)  24 us
    all_gather x1, blocking collectives, on_device(): packed = lax.all_gather(pack(perm, units, parts), 'fsdp', axis=0)  19.8 us
    pallas_call x1, Pallas kernels, factor(): pl.pallas_call(factor_kernel, grid=(devices // group,), in_specs=[pl.Bloc...  9.3 us
    ppermute x6, waiting for transfers between devices, exchange(): lax.ppermute(x, axis, [(i, i ^ k) for i in range(lax.axis_size(axis))])  9.19 us
    all_to_all x2, starting transfers between devices, trade(): lax.all_to_all(x, 'fsdp', split_axis=0, concat_axis=0).reshape(-1, share)  7.77 us
    ppermute x6, starting transfers between devices, exchange(): lax.ppermute(x, axis, [(i, i ^ k) for i in range(lax.axis_size(axis))])  7.11 us
    pallas_call x1, Pallas kernels, project(): pl.pallas_call(project_kernel, grid=(cols // block,), in_specs=[wide, wid...  5.03 us
  transfers between devices with their start and end apart: 8, of which 7 were waited for; matrix products, arithmetic and copies ran while one was open for 0% of the time, Pallas kernels for 13%

profile of v21, /device:TPU:0, one launch (start us, length us, event | category | flops | bytes accessed | tf_op | source)
XLA Modules:
  0.0 121.6 jit_solution(739579890031860367)
XLA Ops:
  0.6 4.3 %shard_map.67 = (s16[32,4096]{1,0:T(8,128)(2,1)}, s16[8,128,512]{2,1,0:T(8,128)(2,1)}, s16[8,32,512]{2,1,0:T(8,128)(2,1)}, f32[2,128]{1,0:T(2,128)}) custom-call(f32[128,4096]{1,0:T(8,128)} %momentum_ref.5, bf16[128,4096]{1,0:T(8,128)(2,1)} %grad_ref.5, bf16[32,4096]{1,0:T(8,128)(2,1)} %basis_ref.1), custom_call_target="tpu_custom_call" | custom-call | flops 5242880 | bytes 4194304 | tf_op jit(solution)/shard_map/pallas_call | solution.py:137
  4.9 26.1 %all-gather.4.code_ref = s16[256,4096]{1,0:T(8,128)(2,1)} all-gather(s16[32,4096]{1,0:T(8,128)(2,1)} %get-tuple-element.18), channel_id=1, replica_groups=mesh['fsdp'=8,'tp'=4] {'fsdp'}, dimensions={0}, use_global_device_ids=true | all-gather | bytes 2359296 | tf_op jit(solution)/shard_map/all_gather | solution.py:553
  31.0 3.6 %all-to-all-start = ((s16[8,128,512]{2,1,0:T(8,128)(2,1)}), s16[8,128,512]{2,1,0:T(8,128)(2,1)S(1)}, u32[]{:S(2)}, u32[]{:S(2)}) async-start(s16[8,128,512]{2,1,0:T(8,128)(2,1)} %get-tuple-element.20), calls=%async_computation | async-start | bytes 2097152 | tf_op jit(solution)/shard_map/all_to_all | solution.py:551
  34.6 0.0 copy-start.2
  34.6 0.0 copy-start.3
  34.6 5.0 %shard_map.68.refs_0_ = f32[128,256]{1,0:T(8,128)S(1)} custom-call(f32[128,4096]{1,0:T(8,128)} %momentum_ref.5, bf16[128,4096]{1,0:T(8,128)(2,1)} %grad_ref.5, s16[256,4096]{1,0:T(8,128)(2,1)} %all-gather.4.code_ref), custom_call_target="tpu_custom_call" | custom-call | flops 536870912 | bytes 5242880 | tf_op jit(solution)/shard_map/pallas_call | solution.py:188
  39.6 2.5 %collective-permute-start.2 = (f32[128,256]{1,0:T(8,128)S(1)}, f32[128,256]{1,0:T(8,128)S(1)}, u32[]{:S(2)}, u32[]{:S(2)}) collective-permute-start(f32[128,256]{1,0:T(8,128)S(1)} %shard_map.68.refs_0_), channel_id=1, source_target_pairs={{0,3},{1,2},{2,1},{3,0},{4,7},{5,6},{6,5},{7,4},{8,11},{9,10},{10,... | collective-permute-start | bytes 393224 | tf_op jit(solution)/shard_map/ppermute | solution.py:29
  42.2 0.5 collective-permute-start.1
  42.7 0.5 collective-permute-start
  43.2 3.5 %collective-permute-done.2.refs_3_ = f32[128,256]{1,0:T(8,128)S(1)} collective-permute-done((f32[128,256]{1,0:T(8,128)S(1)}, f32[128,256]{1,0:T(8,128)S(1)}, u32[]{:S(2)}, u32[]{:S(2)}) %collective-permute-start.2) | collective-permute-done | bytes 131104 | tf_op jit(solution)/shard_map/ppermute | solution.py:29
  46.7 2.5 %collective-permute-done.1.refs_2_ = f32[128,256]{1,0:T(8,128)S(1)} collective-permute-done((f32[128,256]{1,0:T(8,128)S(1)}, f32[128,256]{1,0:T(8,128)S(1)}, u32[]{:S(2)}, u32[]{:S(2)}) %collective-permute-start.1) | collective-permute-done | bytes 131104 | tf_op jit(solution)/shard_map/ppermute | solution.py:29
  49.3 0.1 collective-permute-done.refs_1_
  49.4 0.0 copy-done.2
  49.4 0.0 copy-done.3
  49.4 0.9 shard_map.69
  50.3 19.8 %all-gather = s16[1408,256]{1,0:T(8,128)(2,1)S(1)} all-gather(s16[176,256]{1,0:T(8,128)(2,1)S(1)} %shard_map.69), channel_id=2, replica_groups=mesh['fsdp'=8,'tp'=4] {'fsdp'}, dimensions={0}, use_global_device_ids=true | all-gather | bytes 811008 | tf_op jit(solution)/shard_map/all_gather | solution.py:562
  70.1 0.0 all-to-all-done
  70.1 4.2 %all-to-all-start.1 = ((s16[8,32,512]{2,1,0:T(8,128)(2,1)}), s16[8,32,512]{2,1,0:T(8,128)(2,1)S(1)}, u32[]{:S(2)}, u32[]{:S(2)}) async-start(s16[8,32,512]{2,1,0:T(8,128)(2,1)} %get-tuple-element.23), calls=%async_computation.1 | async-start | bytes 524288 | tf_op jit(solution)/shard_map/all_to_all | solution.py:551
  74.4 9.3 %shard_map.70 = (f32[256,1024]{1,0:T(8,128)S(1)}, f32[256,256]{1,0:T(8,128)S(1)}) custom-call(s16[8,176,256]{2,1,0:T(8,128)(2,1)S(1)} %bitcast.7), custom_call_target="tpu_custom_call" | custom-call | flops 805306368 | bytes 1441792 | tf_op jit(solution)/shard_map/pallas_call | solution.py:369
  83.7 0.4 all-to-all-done.1
  84.1 0.0 copy-start.1
  84.1 3.0 %shard_map.71 = (s16[528,256]{1,0:T(8,128)(2,1)S(1)}, f32[128,256]{1,0:T(8,128)S(1)}) custom-call(s32[1]{0:T(128)} %bitcast.place_ref, s16[1024,512]{1,0:T(8,128)(2,1)S(1)} %bitcast.6, s16[256,512]{1,0:T(8,128)(2,1)S(1)} %bitcast.11, f32[256,1024]{1,0:T(8,128)S(1)} %get-tuple-element.25.turned_ref.own_ref, s16[8,176,256]{2,1,0:T(8,128)(2,1)S(1)} %bitcast.8, ...), custom_call_target="tpu_custom_call" | custom-call | flops 805306368 | bytes 2097152 | tf_op jit(solution)/shard_map/pallas_call | solution.py:442
  87.1 0.0 copy-start
  87.2 24.0 %all-gather.5 = s16[4224,256]{1,0:T(8,128)(2,1)S(1)} all-gather(s16[528,256]{1,0:T(8,128)(2,1)S(1)} %get-tuple-element.27), channel_id=3, replica_groups=mesh['fsdp'=8,'tp'=4] {'fsdp'}, dimensions={0}, use_global_device_ids=true | all-gather | bytes 2433024 | tf_op jit(solution)/shard_map/all_gather | solution.py:568
  111.2 0.1 fusion.4
  111.2 2.5 %collective-permute-start.5 = (f32[1,256]{1,0:T(1,128)S(1)}, f32[1,256]{1,0:T(1,128)S(1)}, u32[]{:S(2)}, u32[]{:S(2)}) collective-permute-start(f32[1,256]{1,0:T(1,128)S(1)} %bitcast.12), channel_id=1, source_target_pairs={{0,3},{1,2},{2,1},{3,0},{4,7},{5,6},{6,5},{7,4},{8,11},{9,10},{10,... | collective-permute-start | bytes 3080 | tf_op jit(solution)/shard_map/ppermute | solution.py:29
  113.7 0.5 collective-permute-start.4
  114.3 0.5 collective-permute-start.3
  114.8 1.0 collective-permute-done.5
  115.8 1.5 %collective-permute-done.4 = f32[1,256]{1,0:T(1,128)S(1)} collective-permute-done((f32[1,256]{1,0:T(1,128)S(1)}, f32[1,256]{1,0:T(1,128)S(1)}, u32[]{:S(2)}, u32[]{:S(2)}) %collective-permute-start.4) | collective-permute-done | bytes 1056 | tf_op jit(solution)/shard_map/ppermute | solution.py:29
  117.3 0.5 collective-permute-done.3
  117.8 0.0 copy-done.1
  117.8 0.0 copy-done
  117.9 3.8 %shard_map.72 = (f32[128,4096]{1,0:T(8,128)}, f32[4096,256]{1,0:T(8,128)}, bf16[128,4096]{1,0:T(8,128)(2,1)}) custom-call(f32[128,4096]{1,0:T(8,128)S(1)} %copy-done, bf16[128,4096]{1,0:T(8,128)(2,1)S(1)} %copy-done.1, s16[8,528,256]{2,1,0:T(8,128)(2,1)S(1)} %bitcast.10, f32[128,256]{1,0:T(8,128)S(1)} %get-tuple-element.28.ortho_ref, ...), custom_call_target="tpu_custom_call" | custom-call | flops 1610612736 | bytes 12582912 | tf_op jit(solution)/shard_map/pallas_call | solution.py:520
  (2 shorter events, 0.0 us)
Async XLA Ops:
  31.0 39.1 %all-to-all-start = ((s16[8,128,512]{2,1,0:T(8,128)(2,1)}), s16[8,128,512]{2,1,0:T(8,128)(2,1)S(1)}, u32[]{:S(2)}, u32[]{:S(2)}) async-start(s16[8,128,512]{2,1,0:T(8,128)(2,1)} %get-tuple-element.20), calls=%async_computation | async-start | bytes 2097152 | tf_op jit(solution)/shard_map/all_to_all | solution.py:551
  34.6 14.8 %copy-start.2 = (f32[2,128]{1,0:T(2,128)S(1)}, f32[2,128]{1,0:T(2,128)}, u32[]{:S(2)}) copy-start(f32[2,128]{1,0:T(2,128)} %get-tuple-element.16.unit_ref) | copy-start | bytes 3076
  34.6 14.8 %copy-start.3 = (s32[8]{0:T(128)S(1)}, s32[8]{0:T(128)}, u32[]{:S(2)}) copy-start(s32[8]{0:T(128)} %perm_ref.1) | copy-start | bytes 100
  39.6 7.1 %collective-permute-start.2 = (f32[128,256]{1,0:T(8,128)S(1)}, f32[128,256]{1,0:T(8,128)S(1)}, u32[]{:S(2)}, u32[]{:S(2)}) collective-permute-start(f32[128,256]{1,0:T(8,128)S(1)} %shard_map.68.refs_0_), channel_id=1, source_target_pairs={{0,3},{1,2},{2,1},{3,0},{4,7},{5,6},{6,5},{7,4},{8,11},{9,10},{10,... | collective-permute-start | bytes 393224 | tf_op jit(solution)/shard_map/ppermute | solution.py:29
  42.2 7.1 %collective-permute-start.1 = (f32[128,256]{1,0:T(8,128)S(1)}, f32[128,256]{1,0:T(8,128)S(1)}, u32[]{:S(2)}, u32[]{:S(2)}) collective-permute-start(f32[128,256]{1,0:T(8,128)S(1)} %shard_map.68.refs_0_), channel_id=1, source_target_pairs={{0,2},{1,3},{2,0},{3,1},{4,6},{5,7},{6,4},{7,5},{8,10},{9,11},{10,... | collective-permute-start | bytes 393224 | tf_op jit(solution)/shard_map/ppermute | solution.py:29
  42.7 6.7 %collective-permute-start = (f32[128,256]{1,0:T(8,128)S(1)}, f32[128,256]{1,0:T(8,128)S(1)}, u32[]{:S(2)}, u32[]{:S(2)}) collective-permute-start(f32[128,256]{1,0:T(8,128)S(1)} %shard_map.68.refs_0_), channel_id=1, source_target_pairs={{0,1},{1,0},{2,3},{3,2},{4,5},{5,4},{6,7},{7,6},{8,9},{9,8},{10,11... | collective-permute-start | bytes 393224 | tf_op jit(solution)/shard_map/ppermute | solution.py:29
  70.1 14.0 %all-to-all-start.1 = ((s16[8,32,512]{2,1,0:T(8,128)(2,1)}), s16[8,32,512]{2,1,0:T(8,128)(2,1)S(1)}, u32[]{:S(2)}, u32[]{:S(2)}) async-start(s16[8,32,512]{2,1,0:T(8,128)(2,1)} %get-tuple-element.23), calls=%async_computation.1 | async-start | bytes 524288 | tf_op jit(solution)/shard_map/all_to_all | solution.py:551
  84.1 33.7 %copy-start.1 = (bf16[128,4096]{1,0:T(8,128)(2,1)S(1)}, bf16[128,4096]{1,0:T(8,128)(2,1)}, u32[]{:S(2)}) copy-start(bf16[128,4096]{1,0:T(8,128)(2,1)} %grad_ref.5) | copy-start | bytes 3145732
  87.1 30.7 %copy-start = (f32[128,4096]{1,0:T(8,128)S(1)}, f32[128,4096]{1,0:T(8,128)}, u32[]{:S(2)}) copy-start(f32[128,4096]{1,0:T(8,128)} %momentum_ref.5) | copy-start | bytes 6291460
  111.2 4.5 %collective-permute-start.5 = (f32[1,256]{1,0:T(1,128)S(1)}, f32[1,256]{1,0:T(1,128)S(1)}, u32[]{:S(2)}, u32[]{:S(2)}) collective-permute-start(f32[1,256]{1,0:T(1,128)S(1)} %bitcast.12), channel_id=1, source_target_pairs={{0,3},{1,2},{2,1},{3,0},{4,7},{5,6},{6,5},{7,4},{8,11},{9,10},{10,... | collective-permute-start | bytes 3080 | tf_op jit(solution)/shard_map/ppermute | solution.py:29
  113.7 3.6 %collective-permute-start.4 = (f32[1,256]{1,0:T(1,128)S(1)}, f32[1,256]{1,0:T(1,128)S(1)}, u32[]{:S(2)}, u32[]{:S(2)}) collective-permute-start(f32[1,256]{1,0:T(1,128)S(1)} %bitcast.13), channel_id=1, source_target_pairs={{0,2},{1,3},{2,0},{3,1},{4,6},{5,7},{6,4},{7,5},{8,10},{9,11},{10,... | collective-permute-start | bytes 3080 | tf_op jit(solution)/shard_map/ppermute | solution.py:29
  114.3 3.6 %collective-permute-start.3 = (f32[1,256]{1,0:T(1,128)S(1)}, f32[1,256]{1,0:T(1,128)S(1)}, u32[]{:S(2)}, u32[]{:S(2)}) collective-permute-start(f32[1,256]{1,0:T(1,128)S(1)} %bitcast.14), channel_id=1, source_target_pairs={{0,1},{1,0},{2,3},{3,2},{4,5},{5,4},{6,7},{7,6},{8,9},{9,8},{10,11... | collective-permute-start | bytes 3080 | tf_op jit(solution)/shard_map/ppermute | solution.py:29
